TPU v7x, 512 devices: a whole 4x8x8 slice. The times are simulated.
512 devices in a mesh: tm: 16 (over y, core), space: 32 (over z, x).
Axes of the slice: x: 4, y: 8, z: 8, core: 2. Of those that a mesh axis runs over, the one named last changes fastest.
Arguments:
- right_side: float32 [128, 256, 1024], P('tm', 'space'), may hold values from -50 to 50
- kappa: float32 [256, 1024], P('space'), may hold values from 0.05 to 1
- velocity: int32 [2, 256, 1024], P(None, 'space'), may hold values from -2 to 2
Outputs:
- solution: float32 [128, 256, 1024], P('tm', 'space')
- residual: float32 [128, 256, 1024], P('tm', 'space')
All inputs are finite; a program needn't handle non-finite values.
Results may differ from a plain program's by a relative error of at most 0.013.
Values sent between devices are 32-bit elements; how exact they have to be, the bound alone decides.
No kernel may reach another device: no remote copies, remote signals or barrier semaphores. Data moves between devices by JAX's collectives and lax.ppermute only.
A program may use at most 64 MiB of HBM per device.

v0:
```python
import math

import jax
import jax.numpy as jnp
from jax import lax
from jax.sharding import PartitionSpec as P

CHEB = 4
ITERS = 2


time_coupling = 2.0
kappa_low = 0.05
kappa_high = 1.0
stencil_reach = 16.0


def padded(block, sides, width):
    for axis, dim in sides:
        count = lax.axis_size(axis)
        forward = [(i, i + 1) for i in range(count - 1)]
        forward.append((count - 1, 0))
        backward = [(target, source) for source, target in forward]
        low = lax.ppermute(
            lax.slice_in_dim(block, block.shape[dim] - width, None, axis=dim), axis, forward
        )
        high = lax.ppermute(lax.slice_in_dim(block, 0, width, axis=dim), axis, backward)
        block = jnp.concatenate([low, block, high], axis=dim)
    return block


def hartley_table(length):
    index = jnp.arange(length, dtype=jnp.int32)
    product = index[:, None] * index[None, :] % length
    angle = product.astype(jnp.float32) * (2.0 * math.pi / length)
    return (jnp.cos(angle) + jnp.sin(angle)) / math.sqrt(length)


def spectral_shift(length):
    index = jnp.arange(length, dtype=jnp.int32)
    angle = index.astype(jnp.float32) * (2.0 * math.pi / length)
    return (time_coupling * (2.0 - 2.0 * jnp.cos(angle))).reshape(length, 1, 1)


def transform(cas_table, field):
    return jnp.einsum("kt,txy->kxy", cas_table, field, precision=lax.Precision.HIGHEST)


def chebyshev(source, freq_shift, apply_space):
    half_width = 0.5 * (kappa_high + stencil_reach - kappa_low)
    middle = 0.5 * (kappa_low + kappa_high + stencil_reach) + freq_shift
    spread_ratio = middle / half_width
    damping = 1.0 / spread_ratio
    step_dir = source / middle
    solved = jnp.zeros_like(source)
    remain = source
    for _ in range(CHEB):
        solved = solved + step_dir
        remain = remain - (apply_space(step_dir) + freq_shift * step_dir)
        damp_next = 1.0 / (2.0 * spread_ratio - damping)
        step_dir = damp_next * damping * step_dir + 2.0 * damp_next / half_width * remain
        damping = damp_next
    return solved + step_dir


def inner(left, right):
    return lax.psum(jnp.sum(left * right), ("tm", "space"))


def solve(source, apply_full, precondition):
    solution = jnp.zeros_like(source)
    residual = source
    search = precondition(residual)
    direction = search
    gamma = inner(residual, search)
    for iteration in range(ITERS):
        curved = apply_full(direction)
        step_len = gamma / inner(direction, curved)
        solution = solution + step_len * direction
        residual = residual - step_len * curved
        if iteration + 1 < ITERS:
            search = precondition(residual)
            gamma_next = inner(residual, search)
            direction = search + gamma_next / gamma * direction
            gamma = gamma_next
    return (solution, residual)


def shards(right_side, kappa, velocity):
    tm_count = lax.axis_size("tm")
    length = right_side.shape[0] * tm_count
    y_block = right_side.shape[2] // tm_count
    cas_table = hartley_table(length)
    freq_shift = spectral_shift(length)
    squares = velocity.astype(jnp.float32) ** 2
    rimmed = padded(squares[0], (("space", 0),), 1)
    east_edge = 1.0 + 0.125 * (rimmed[1:-1] + rimmed[2:])
    west_edge = 1.0 + 0.125 * (rimmed[:-2] + rimmed[1:-1])
    north_edge = 1.0 + 0.125 * (squares[1] + jnp.roll(squares[1], -1, 1))
    south_edge = jnp.roll(north_edge, 1, 1)
    centre = kappa + east_edge + west_edge + north_edge + south_edge
    weights_full = (centre, east_edge, west_edge, north_edge, south_edge)
    y_offset = lax.axis_index("tm") * y_block
    weights_tile = tuple(
        (lax.dynamic_slice_in_dim(weight, y_offset, y_block, 1) for weight in weights_full)
    )

    def space_tile(field):
        tile_centre, tile_east, tile_west, tile_north, tile_south = weights_tile
        extended = padded(field, (("tm", 2), ("space", 1)), 1)
        middle = extended[:, 1:-1, 1:-1]
        return (
            tile_centre * middle
            - tile_east * extended[:, 2:, 1:-1]
            - tile_west * extended[:, :-2, 1:-1]
            - tile_north * extended[:, 1:-1, 2:]
            - tile_south * extended[:, 1:-1, :-2]
        )

    def full_time(field):
        extended = padded(field, (("tm", 0), ("space", 1)), 1)
        middle = extended[1:-1, 1:-1]
        spatial = (
            centre * middle
            - east_edge * extended[1:-1, 2:]
            - west_edge * extended[1:-1, :-2]
            - north_edge * jnp.roll(middle, -1, 2)
            - south_edge * jnp.roll(middle, 1, 2)
        )
        return spatial + time_coupling * (2.0 * middle - extended[2:, 1:-1] - extended[:-2, 1:-1])

    def to_frequency(field):
        return transform(
            cas_table, lax.all_to_all(field, "tm", split_axis=2, concat_axis=0, tiled=True)
        )

    def precondition_time(field):
        filtered = transform(cas_table, chebyshev(to_frequency(field), freq_shift, space_tile))
        return lax.all_to_all(filtered, "tm", split_axis=0, concat_axis=2, tiled=True)

    solution, residual = solve(right_side, full_time, precondition_time)
    return (solution, residual)


def solution(mesh):
    placed = (P("tm", "space", None), P("space", None), P(None, "space", None))
    return jax.shard_map(
        shards,
        mesh=mesh,
        in_specs=placed,
        out_specs=(P("tm", "space", None), P("tm", "space", None)),
        check_vma=False,
    )
```

profile of v0, /device:TPU:1, one launch (start us, length us, event | category | flops | bytes accessed | tf_op | source)
XLA Modules:
  0.0 580.7 jit_solution(15501276765867989606)
XLA Ops:
  1.5 3.9 collective-permute-start.1
  5.5 11.7 %collective-permute-start = (f32[1,1024]{1,0:T(1,128)S(1)}, f32[1,1024]{1,0:T(1,128)S(1)}, u32[]{:S(2)}, u32[]{:S(2)}) collective-permute-start(f32[1,1024]{1,0:T(1,128)S(1)} %get-tuple-element.68), channel_id=1, source_target_pairs={{1,0},{2,1},{3,2},{4,3},{5,4},{6,5},{7,6},{8,7},{9,8},{10,9},{11,1... | collective-permute-start | bytes 12296 | tf_op jit(solution)/shard_map/ppermute | solution.py:27
  17.1 3.5 copy.30
  20.6 4.4 reshape.99
  25.1 8.1 %all-to-all-start = ((f32[16,1,4096]{2,1,0:T(1,128)}), f32[16,1,4096]{2,1,0:T(1,128)S(1)}, u32[]{:S(2)}, u32[]{:S(2)}) async-start(f32[16,1,4096]{2,1,0:T(1,128)} %reshape.99), calls=%async_computation | async-start | bytes 524288 | tf_op jit(solution)/shard_map/all_to_all | solution.py:134
  33.8 11.0 %all-to-all-done = f32[16,1,4096]{2,1,0:T(1,128)S(1)} async-done(((f32[16,1,4096]{2,1,0:T(1,128)}), f32[16,1,4096]{2,1,0:T(1,128)S(1)}, u32[]{:S(2)}, u32[]{:S(2)}) %all-to-all-start) | async-done | bytes 262176 | tf_op jit(solution)/shard_map/all_to_all | solution.py:134
  46.6 3.7 reshape.100
  50.3 2.8 copy.31
  54.0 1.7 collective-permute-start.2
  55.8 1.5 collective-permute-done.3
  57.4 3.6 collective-permute-start.4
  61.0 1.9 collective-permute-start.5
  63.0 6.0 %collective-permute-done.5 = f32[128,1,66]{0,2,1:T(8,128)S(1)} collective-permute-done((f32[128,1,66]{0,2,1:T(8,128)S(1)}, f32[128,1,66]{0,2,1:T(8,128)S(1)}, u32[]{:S(2)}, u32[]{:S(2)}) %collective-permute-start.5) | collective-permute-done | bytes 33824 | tf_op jit(solution)/shard_map/ppermute | solution.py:24
  69.5 2.1 collective-permute-start.7
  72.4 1.3 collective-permute-done.7
  73.7 1.9 collective-permute-start.8
  75.6 3.4 collective-permute-start.9
  79.1 4.6 collective-permute-done.9
  84.1 3.3 collective-permute-start.11
  88.6 1.9 collective-permute-start.12
  90.5 3.4 collective-permute-start.13
  94.0 4.6 collective-permute-done.13
  99.0 4.3 collective-permute-start.15
  104.5 1.9 collective-permute-start.16
  106.4 3.4 collective-permute-start.17
  109.8 4.6 collective-permute-done.17
  116.2 21.2 %all_to_all.72 = f32[16,1,4096]{2,1,0:T(1,128)S(1)} all-to-all(f32[16,1,4096]{2,1,0:T(1,128)S(1)} %reshape.101), channel_id=1, replica_groups=mesh['tm'=16,'space'=32] {'tm'}, dimensions={0} | all-to-all | bytes 524288 | tf_op jit(solution)/shard_map/all_to_all | solution.py:139
  137.4 1.3 reduce.1
  139.6 1.7 collective-permute-start.18
  143.2 1.9 collective-permute-start.20
  145.1 3.4 collective-permute-start.21
  148.5 4.6 collective-permute-done.21
  154.0 94.5 %all-reduce = (f32[]{:T(128)}, f32[]{:T(128)}) all-reduce(f32[]{:T(128)} %get-tuple-element.3, f32[]{:T(128)} %get-tuple-element.2), channel_id=1, replica_groups=mesh['tm'=16,'space'=32] {'tm','space'}, use_global_device_ids=true, to_apply=%region_1.2 | all-reduce | flops 2 | bytes 16 | tf_op jit(solution)/shard_map/psum | solution.py:67
  249.9 2.6 copy.38
  252.6 3.8 reshape.103
  256.3 17.6 %all_to_all.73 = f32[16,1,4096]{2,1,0:T(1,128)S(1)} all-to-all(f32[16,1,4096]{2,1,0:T(1,128)S(1)} %reshape.103), channel_id=1, replica_groups=mesh['tm'=16,'space'=32] {'tm'}, dimensions={0} | all-to-all | bytes 524288 | tf_op jit(solution)/shard_map/all_to_all | solution.py:134
  274.0 1.3 reduce.2
  275.2 3.7 reshape.104
  278.9 2.8 copy.39
  282.7 1.7 collective-permute-start.22
  284.4 1.6 collective-permute-done.23
  286.0 6.0 %collective-permute-start.24 = (f32[128,1,66]{0,2,1:T(8,128)S(1)}, f32[128,1,66]{0,2,1:T(8,128)S(1)}, u32[]{:S(2)}, u32[]{:S(2)}) collective-permute-start(f32[128,1,66]{0,2,1:T(8,128)S(1)} %get-tuple-element.29), channel_id=1, source_target_pairs={{1,0},{2,1},{3,2},{4,3},{5,4},{6,5},{7,6},{8,7},{9,8},{10,9},{11,1... | collective-permute-start | bytes 101384 | tf_op jit(solution)/shard_map/ppermute | solution.py:27
  292.0 1.9 collective-permute-start.25
  293.9 6.1 %collective-permute-done.25 = f32[128,1,66]{0,2,1:T(8,128)S(1)} collective-permute-done((f32[128,1,66]{0,2,1:T(8,128)S(1)}, f32[128,1,66]{0,2,1:T(8,128)S(1)}, u32[]{:S(2)}, u32[]{:S(2)}) %collective-permute-start.25) | collective-permute-done | bytes 33824 | tf_op jit(solution)/shard_map/ppermute | solution.py:24
  300.4 2.1 collective-permute-start.27
  303.3 1.3 collective-permute-done.27
  304.6 1.9 collective-permute-start.28
  306.6 3.4 collective-permute-start.29
  309.9 4.6 collective-permute-done.29
  315.0 3.3 collective-permute-start.31
  319.6 1.9 collective-permute-start.32
  321.5 3.4 collective-permute-start.33
  324.9 4.6 collective-permute-done.33
  329.9 4.3 collective-permute-start.35
  335.4 1.9 collective-permute-start.36
  337.3 3.4 collective-permute-start.37
  340.7 4.6 collective-permute-done.37
  347.1 21.2 %all_to_all.74 = f32[16,1,4096]{2,1,0:T(1,128)S(1)} all-to-all(f32[16,1,4096]{2,1,0:T(1,128)S(1)} %reshape.105), channel_id=1, replica_groups=mesh['tm'=16,'space'=32] {'tm'}, dimensions={0} | all-to-all | bytes 524288 | tf_op jit(solution)/shard_map/all_to_all | solution.py:139
  370.9 93.2 %psum.30 = f32[]{:T(128)} all-reduce(f32[]{:T(128)} %multiply_reduce_fusion.1), channel_id=1, replica_groups=mesh['tm'=16,'space'=32] {'tm','space'}, use_global_device_ids=true, to_apply=%region_5.6 | all-reduce | flops 1 | bytes 8 | tf_op jit(solution)/shard_map/psum | solution.py:67
  467.5 1.5 collective-permute-done.39
  469.0 4.7 collective-permute-start.40
  473.7 1.9 collective-permute-start.41
  475.7 6.1 %collective-permute-done.41 = f32[10,1,1024]{2,1,0:T(1,128)S(1)} collective-permute-done((f32[10,1,1024]{2,1,0:T(1,128)S(1)}, f32[10,1,1024]{2,1,0:T(1,128)S(1)}, u32[]{:S(2)}, u32[]{:S(2)}) %collective-permute-start.41) | collective-permute-done | bytes 40992 | tf_op jit(solution)/shard_map/ppermute | solution.py:24
  482.6 95.3 %psum.31 = f32[]{:T(128)} all-reduce(f32[]{:T(128)} %get-tuple-element.6), channel_id=1, replica_groups=mesh['tm'=16,'space'=32] {'tm','space'}, use_global_device_ids=true, to_apply=%region_7.8 | all-reduce | flops 1 | bytes 8 | tf_op jit(solution)/shard_map/psum | solution.py:67
  (127 shorter events, 28.6 us)
Async XLA Ops:
  1.5 32.2 %collective-permute-start.1 = (f32[1,1024]{1,0:T(1,128)S(1)}, f32[1,1024]{1,0:T(1,128)S(1)}, u32[]{:S(2)}, u32[]{:S(2)}) collective-permute-start(f32[1,1024]{1,0:T(1,128)S(1)} %get-tuple-element.67), channel_id=1, source_target_pairs={{0,1},{1,2},{2,3},{3,4},{4,5},{5,6},{6,7},{7,8},{8,9},{9,10},{10,1... | collective-permute-start | bytes 12296 | tf_op jit(solution)/shard_map/ppermute | solution.py:24
  5.4 28.3 %copy-start.1 = (f32[8,1024]{1,0:T(8,128)S(1)}, f32[8,1024]{1,0:T(8,128)}, u32[]{:S(2)}) copy-start(f32[8,1024]{1,0:T(8,128)} %param.4) | copy-start | bytes 98308
  5.5 28.3 %collective-permute-start = (f32[1,1024]{1,0:T(1,128)S(1)}, f32[1,1024]{1,0:T(1,128)S(1)}, u32[]{:S(2)}, u32[]{:S(2)}) collective-permute-start(f32[1,1024]{1,0:T(1,128)S(1)} %get-tuple-element.68), channel_id=1, source_target_pairs={{1,0},{2,1},{3,2},{4,3},{5,4},{6,5},{7,6},{8,7},{9,8},{10,9},{11,1... | collective-permute-start | bytes 12296 | tf_op jit(solution)/shard_map/ppermute | solution.py:27
  25.1 19.8 %all-to-all-start = ((f32[16,1,4096]{2,1,0:T(1,128)}), f32[16,1,4096]{2,1,0:T(1,128)S(1)}, u32[]{:S(2)}, u32[]{:S(2)}) async-start(f32[16,1,4096]{2,1,0:T(1,128)} %reshape.99), calls=%async_computation | async-start | bytes 524288 | tf_op jit(solution)/shard_map/all_to_all | solution.py:134
  54.0 3.3 collective-permute-start.3
  54.0 3.3 collective-permute-start.2
  57.4 5.7 collective-permute-start.4
  61.0 8.0 %collective-permute-start.5 = (f32[128,1,66]{0,2,1:T(8,128)S(1)}, f32[128,1,66]{0,2,1:T(8,128)S(1)}, u32[]{:S(2)}, u32[]{:S(2)}) collective-permute-start(f32[128,1,66]{0,2,1:T(8,128)S(1)} %get-tuple-element.38), channel_id=1, source_target_pairs={{0,1},{1,2},{2,3},{3,4},{4,5},{5,6},{6,7},{7,8},{8,9},{9,10},{10,1... | collective-permute-start | bytes 101384 | tf_op jit(solution)/shard_map/ppermute | solution.py:24
  69.5 4.2 collective-permute-start.7
  71.6 2.1 collective-permute-start.6
  73.7 5.4 collective-permute-start.8
  75.6 8.0 %collective-permute-start.9 = (f32[128,1,66]{0,2,1:T(8,128)S(1)}, f32[128,1,66]{0,2,1:T(8,128)S(1)}, u32[]{:S(2)}, u32[]{:S(2)}) collective-permute-start(f32[128,1,66]{0,2,1:T(8,128)S(1)} %get-tuple-element.36), channel_id=1, source_target_pairs={{0,1},{1,2},{2,3},{3,4},{4,5},{5,6},{6,7},{7,8},{8,9},{9,10},{10,1... | collective-permute-start | bytes 101384 | tf_op jit(solution)/shard_map/ppermute | solution.py:24
  84.1 4.2 collective-permute-start.11
  87.4 1.2 collective-permute-start.10
  88.6 5.4 collective-permute-start.12
  90.5 8.0 %collective-permute-start.13 = (f32[128,1,66]{0,2,1:T(8,128)S(1)}, f32[128,1,66]{0,2,1:T(8,128)S(1)}, u32[]{:S(2)}, u32[]{:S(2)}) collective-permute-start(f32[128,1,66]{0,2,1:T(8,128)S(1)} %get-tuple-element.34), channel_id=1, source_target_pairs={{0,1},{1,2},{2,3},{3,4},{4,5},{5,6},{6,7},{7,8},{8,9},{9,10},{10,1... | collective-permute-start | bytes 101384 | tf_op jit(solution)/shard_map/ppermute | solution.py:24
  99.0 5.1 collective-permute-start.15
  103.3 1.2 collective-permute-start.14
  104.5 5.4 collective-permute-start.16
  106.4 8.0 %collective-permute-start.17 = (f32[128,1,66]{0,2,1:T(8,128)S(1)}, f32[128,1,66]{0,2,1:T(8,128)S(1)}, u32[]{:S(2)}, u32[]{:S(2)}) collective-permute-start(f32[128,1,66]{0,2,1:T(8,128)S(1)} %get-tuple-element.32), channel_id=1, source_target_pairs={{0,1},{1,2},{2,3},{3,4},{4,5},{5,6},{6,7},{7,8},{8,9},{9,10},{10,1... | collective-permute-start | bytes 101384 | tf_op jit(solution)/shard_map/ppermute | solution.py:24
  114.9 38.2 %copy-start = (f32[8,8,1024]{2,1,0:T(8,128)S(1)}, f32[8,8,1024]{2,1,0:T(8,128)}, u32[]{:S(2)}) copy-start(f32[8,8,1024]{2,1,0:T(8,128)} %param.3) | copy-start | bytes 786436
  139.5 3.6 collective-permute-start.19
  139.6 2.8 collective-permute-start.18
  143.2 5.4 collective-permute-start.20
  145.1 8.1 %collective-permute-start.21 = (f32[10,1,1024]{2,1,0:T(1,128)S(1)}, f32[10,1,1024]{2,1,0:T(1,128)S(1)}, u32[]{:S(2)}, u32[]{:S(2)}) collective-permute-start(f32[10,1,1024]{2,1,0:T(1,128)S(1)} %get-tuple-element.22), channel_id=1, source_target_pairs={{0,1},{1,2},{2,3},{3,4},{4,5},{5,6},{6,7},{7,8},{8,9},{9,10},{10,1... | collective-permute-start | bytes 122888 | tf_op jit(solution)/shard_map/ppermute | solution.py:24
  282.6 3.3 collective-permute-start.23
  282.7 3.3 collective-permute-start.22
  286.0 7.9 %collective-permute-start.24 = (f32[128,1,66]{0,2,1:T(8,128)S(1)}, f32[128,1,66]{0,2,1:T(8,128)S(1)}, u32[]{:S(2)}, u32[]{:S(2)}) collective-permute-start(f32[128,1,66]{0,2,1:T(8,128)S(1)} %get-tuple-element.29), channel_id=1, source_target_pairs={{1,0},{2,1},{3,2},{4,3},{5,4},{6,5},{7,6},{8,7},{9,8},{10,9},{11,1... | collective-permute-start | bytes 101384 | tf_op jit(solution)/shard_map/ppermute | solution.py:27
  292.0 8.0 %collective-permute-start.25 = (f32[128,1,66]{0,2,1:T(8,128)S(1)}, f32[128,1,66]{0,2,1:T(8,128)S(1)}, u32[]{:S(2)}, u32[]{:S(2)}) collective-permute-start(f32[128,1,66]{0,2,1:T(8,128)S(1)} %get-tuple-element.30), channel_id=1, source_target_pairs={{0,1},{1,2},{2,3},{3,4},{4,5},{5,6},{6,7},{7,8},{8,9},{9,10},{10,1... | collective-permute-start | bytes 101384 | tf_op jit(solution)/shard_map/ppermute | solution.py:24
  300.4 4.2 collective-permute-start.27
  302.5 2.1 collective-permute-start.26
  304.6 5.3 collective-permute-start.28
  306.6 8.0 %collective-permute-start.29 = (f32[128,1,66]{0,2,1:T(8,128)S(1)}, f32[128,1,66]{0,2,1:T(8,128)S(1)}, u32[]{:S(2)}, u32[]{:S(2)}) collective-permute-start(f32[128,1,66]{0,2,1:T(8,128)S(1)} %get-tuple-element.28), channel_id=1, source_target_pairs={{0,1},{1,2},{2,3},{3,4},{4,5},{5,6},{6,7},{7,8},{8,9},{9,10},{10,1... | collective-permute-start | bytes 101384 | tf_op jit(solution)/shard_map/ppermute | solution.py:24
  315.0 4.2 collective-permute-start.31
  318.4 1.2 collective-permute-start.30
  319.6 5.3 collective-permute-start.32
  321.5 8.0 %collective-permute-start.33 = (f32[128,1,66]{0,2,1:T(8,128)S(1)}, f32[128,1,66]{0,2,1:T(8,128)S(1)}, u32[]{:S(2)}, u32[]{:S(2)}) collective-permute-start(f32[128,1,66]{0,2,1:T(8,128)S(1)} %get-tuple-element.26), channel_id=1, source_target_pairs={{0,1},{1,2},{2,3},{3,4},{4,5},{5,6},{6,7},{7,8},{8,9},{9,10},{10,1... | collective-permute-start | bytes 101384 | tf_op jit(solution)/shard_map/ppermute | solution.py:24
  329.9 5.1 collective-permute-start.35
  334.2 1.2 collective-permute-start.34
  335.4 5.3 collective-permute-start.36
  337.3 8.0 %collective-permute-start.37 = (f32[128,1,66]{0,2,1:T(8,128)S(1)}, f32[128,1,66]{0,2,1:T(8,128)S(1)}, u32[]{:S(2)}, u32[]{:S(2)}) collective-permute-start(f32[128,1,66]{0,2,1:T(8,128)S(1)} %get-tuple-element.24), channel_id=1, source_target_pairs={{0,1},{1,2},{2,3},{3,4},{4,5},{5,6},{6,7},{7,8},{8,9},{9,10},{10,1... | collective-permute-start | bytes 101384 | tf_op jit(solution)/shard_map/ppermute | solution.py:24
  465.6 3.4 collective-permute-start.39
  466.2 2.7 collective-permute-start.38
  469.0 6.7 %collective-permute-start.40 = (f32[10,1,1024]{2,1,0:T(1,128)S(1)}, f32[10,1,1024]{2,1,0:T(1,128)S(1)}, u32[]{:S(2)}, u32[]{:S(2)}) collective-permute-start(f32[10,1,1024]{2,1,0:T(1,128)S(1)} %get-tuple-element.19), channel_id=1, source_target_pairs={{1,0},{2,1},{3,2},{4,3},{5,4},{6,5},{7,6},{8,7},{9,8},{10,9},{11,1... | collective-permute-start | bytes 122888 | tf_op jit(solution)/shard_map/ppermute | solution.py:27
  473.7 8.1 %collective-permute-start.41 = (f32[10,1,1024]{2,1,0:T(1,128)S(1)}, f32[10,1,1024]{2,1,0:T(1,128)S(1)}, u32[]{:S(2)}, u32[]{:S(2)}) collective-permute-start(f32[10,1,1024]{2,1,0:T(1,128)S(1)} %get-tuple-element.20), channel_id=1, source_target_pairs={{0,1},{1,2},{2,3},{3,4},{4,5},{5,6},{6,7},{7,8},{8,9},{9,10},{10,1... | collective-permute-start | bytes 122888 | tf_op jit(solution)/shard_map/ppermute | solution.py:24
where the time goes:
time: 583 us; the launch traced here: 581 us
  blocking collectives  343 us (59%)
  starting transfers between devices  109 us (19%)
  waiting for transfers between devices  74.9 us (13%)
  local copies, waits for them, and re-layouts  31.8 us (5%)
  other arithmetic  14.2 us (2%)
    psum x3, blocking collectives, inner(): return lax.psum(jnp.sum(left * right), ('tm', 'space'))  283 us
    ppermute x21, starting transfers between devices, padded(): lax.ppermute(lax.slice_in_dim(block, 0, width, axis=dim), axis, backward)  59.5 us
    ppermute x21, waiting for transfers between devices, padded(): lax.ppermute(lax.slice_in_dim(block, block.shape[dim] - width, None, axis...  52.6 us
    all_to_all x2, blocking collectives, precondition_time(): lax.all_to_all(filtered, 'tm', split_axis=0, concat_axis=2, tiled=True)  42.4 us
    ppermute x21, starting transfers between devices, padded(): lax.ppermute(lax.slice_in_dim(block, block.shape[dim] - width, None, axis...  41.2 us
    unnamed x15, local copies, waits for them, and re-layouts  20.1 us
    all_to_all x1, blocking collectives, to_frequency(): lax.all_to_all(field, 'tm', split_axis=2, concat_axis=0, tiled=True)  17.6 us
  transfers between devices with their start and end apart: 43, of which 26 were waited for; matrix products, arithmetic and copies ran while one was open for 2% of the time, Pallas kernels for 0%

commit v1 on v0

v1 whole, which is shorter than its diff:
```python
import functools
import math

import jax
import jax.numpy as jnp
import numpy as np
from jax import lax
from jax.experimental import pallas as pl
from jax.experimental.pallas import tpu as pltpu
from jax.sharding import PartitionSpec as P

CHEB = 4
COUPLING = 2.0
KAPPA_LOW = 0.05
KAPPA_HIGH = 1.0
REACH = 16.0

LANES = 128
HALO = CHEB + 1
PARAMS = pltpu.CompilerParams(vmem_limit_bytes=24 * 1024 * 1024)


def hartley_table(length):
    index = np.arange(length)
    angle = (index[:, None] * index[None, :] % length) * (2.0 * math.pi / length)
    return ((np.cos(angle) + np.sin(angle)) / math.sqrt(length)).astype(np.float32)


def chebyshev_table(length):
    shift = COUPLING * (2.0 - 2.0 * np.cos(2.0 * math.pi * np.arange(length) / length))
    half = 0.5 * (KAPPA_HIGH + REACH - KAPPA_LOW)
    mid = 0.5 * (KAPPA_LOW + KAPPA_HIGH + REACH) + shift
    ratio = mid / half
    damp = 1.0 / ratio
    columns = [shift, 1.0 / mid]
    for _ in range(CHEB):
        damp_next = 1.0 / (2.0 * ratio - damp)
        columns += [damp_next * damp, 2.0 * damp_next / half]
        damp = damp_next
    table = np.zeros((length, LANES), np.float32)
    table[:, : len(columns)] = np.stack(columns, 1)
    return table


def lane_index(shape):
    return lax.broadcasted_iota(jnp.int32, shape, len(shape) - 1)


def exact_dot(left, right):
    return lax.dot_general(
        left,
        right,
        (((1,), (0,)), ((), ())),
        precision=lax.Precision.HIGHEST,
        preferred_element_type=jnp.float32,
    )


def window_kernel(rows, times, tiles, source_ref, out_ref, scratch_ref):
    quarter = LANES // 4
    width = source_ref.shape[1]
    for part in range(width // LANES):
        scratch_ref[part] = source_ref[:, part * LANES : (part + 1) * LANES]
    for row in range(rows):
        place = pl.ds(row, times, stride=rows)
        field = jnp.concatenate(
            [scratch_ref[part, place, :] for part in range(width // LANES)], axis=1
        )
        even = pltpu.roll(field, quarter, 1)
        odd = pltpu.roll(field, width - quarter, 1)
        for tile in range(tiles):
            picked = even if tile % 2 == 0 else odd
            start = tile // 2 * LANES
            out_ref[tile, row * times : (row + 1) * times, :] = picked[:, start : start + LANES]


def forward_kernel(rows, times, length, cas_ref, field_ref, weight_ref, out_ref, low_ref, high_ref):
    for row in range(rows):
        block = field_ref[:, row * times : (row + 1) * times, :].reshape(length, LANES)
        freq = exact_dot(cas_ref[...], block)
        out_ref[row * length : (row + 1) * length, :] = freq
        if row < HALO:
            low_ref[row * length : (row + 1) * length, :] = freq
        if row >= rows - HALO:
            place = row - (rows - HALO)
            high_ref[place * length : (place + 1) * length, :] = freq
    low_ref[HALO * length :, :] = weight_ref[...]
    high_ref[HALO * length :, :] = weight_ref[...]


def passes(source, weights, coef, rows):
    shift, scale = coef[0], coef[1]
    total = rows + 2 * HALO
    step = [scale * field for field in source]
    remain = list(source)
    solved = [None] * total
    for turn in range(CHEB + 1):
        first, last = turn + 1, total - turn - 1
        flux = None
        new_step = [None] * total
        for row in range(first - 1, last):
            here = step[row]
            ahead = weights(1, row) * (here - step[row + 1])
            if row >= first:
                side = weights(2, row) * (here - pltpu.roll(here, LANES - 1, 1))
                applied = (
                    (weights(0, row) + shift) * here
                    + (ahead - flux)
                    + (side - pltpu.roll(side, 1, 1))
                )
                remain[row] = remain[row] - applied
                if HALO <= row < rows + HALO:
                    solved[row] = here if turn == 0 else solved[row] + here
                if turn < CHEB:
                    new_step[row] = coef[2 + 2 * turn] * here + coef[3 + 2 * turn] * remain[row]
            flux = ahead
        step = new_step
    inside = range(HALO, rows + HALO)
    return [solved[row] for row in inside], [source[row] - remain[row] for row in inside]


def read_coef(coef_ref, block):
    return [
        jnp.broadcast_to(coef_ref[block, index : index + 1], (8, LANES))
        for index in range(2 + 2 * CHEB)
    ]


def own(field):
    lane = lane_index(field.shape)
    return jnp.where((lane >= LANES // 4) & (lane < 3 * LANES // 4), field, 0.0)


def first_kernel(
    rows, length, field_ref, top_ref, bottom_ref, weight_ref, coef_ref,
    solved_ref, applied_ref, low_ref, high_ref, wide_ref, sums_ref,
):
    edge = HALO * length
    planes = []
    for plane in range(3):
        start = plane * rows
        planes.append(
            jnp.concatenate(
                [
                    top_ref[edge + start + rows - HALO : edge + start + rows, :],
                    weight_ref[start : start + rows, :],
                    bottom_ref[edge + start : edge + start + HALO, :],
                ],
                axis=0,
            )
        )
    east = 1.0 + 0.125 * (planes[1][:-1] + planes[1][1:])
    north = 1.0 + 0.125 * (planes[2] + pltpu.roll(planes[2], LANES - 1, 1))
    total = rows + 2 * HALO
    for plane, weight in enumerate((planes[0], east, north)):
        for row in range(weight.shape[0]):
            wide_ref[plane * total + row] = jnp.broadcast_to(weight[row : row + 1], (8, LANES))

    def weights(plane, row):
        return wide_ref[plane * total + row]

    def block_step(index, sums):
        gamma, curved = sums
        start = pl.multiple_of(index * 8, 8)
        source = (
            [top_ref[pl.ds(row * length + start, 8), :] for row in range(HALO)]
            + [field_ref[pl.ds(row * length + start, 8), :] for row in range(rows)]
            + [bottom_ref[pl.ds(row * length + start, 8), :] for row in range(HALO)]
        )
        coef = read_coef(coef_ref, pl.ds(start, 8))
        solved, applied = passes(source, weights, coef, rows)
        for row in range(rows):
            place = pl.ds(row * length + start, 8)
            solved_ref[place, :] = solved[row]
            applied_ref[place, :] = applied[row]
            if row < HALO:
                low_ref[place, :] = applied[row]
            if row >= rows - HALO:
                high_ref[pl.ds((row - rows + HALO) * length + start, 8), :] = applied[row]
            gamma = gamma + source[row + HALO] * solved[row]
            curved = curved + solved[row] * applied[row]
        return gamma, curved

    zero = jnp.zeros((8, LANES), jnp.float32)
    gamma, curved = lax.fori_loop(0, length // 8, block_step, (zero, zero))
    sums_ref[0] = gamma
    sums_ref[1] = curved


def second_kernel(
    rows, times, length, field_ref, top_ref, bottom_ref, earlier_ref, wide_ref, coef_ref, cas_ref,
    early_ref, out_ref, sums_ref, packed_ref,
):
    total = rows + 2 * HALO
    quarter = LANES // 4

    def weights(plane, row):
        return wide_ref[plane * total + row]

    def pack(left, right):
        return jnp.where(
            lane_index(left.shape) < LANES // 2,
            pltpu.roll(left, LANES - quarter, 1),
            pltpu.roll(right, quarter, 1),
        )

    def block_step(index, sums):
        cross, curved = sums
        start = pl.multiple_of(index * 8, 8)
        source = (
            [top_ref[pl.ds(row * length + start, 8), :] for row in range(HALO)]
            + [field_ref[pl.ds(row * length + start, 8), :] for row in range(rows)]
            + [bottom_ref[pl.ds(row * length + start, 8), :] for row in range(HALO)]
        )
        coef = read_coef(coef_ref, pl.ds(start, 8))
        solved, applied = passes(source, weights, coef, rows)
        for row in range(rows):
            place = pl.ds(row * length + start, 8)
            here = source[row + HALO]
            packed_ref[pl.ds(start, 8), row * LANES : (row + 1) * LANES] = pack(
                earlier_ref[place, :], solved[row]
            )
            packed_ref[pl.ds(start, 8), (rows + row) * LANES : (rows + row + 1) * LANES] = pack(
                here, applied[row]
            )
            cross = cross + here * solved[row]
            curved = curved + solved[row] * applied[row]
        return cross, curved

    zero = jnp.zeros((8, LANES), jnp.float32)
    cross, curved = lax.fori_loop(0, length // 8, block_step, (zero, zero))
    values = [jnp.sum(own(field)) for field in (early_ref[0], early_ref[1], cross, curved)]
    lane = lane_index((1, LANES))
    line = jnp.zeros((1, LANES), jnp.float32)
    for index, value in enumerate(values):
        line = jnp.where(lane == index, value, line)
    sums_ref[...] = jnp.broadcast_to(line[None], sums_ref.shape)
    for place in range(rows):
        wide = slice(place * 2 * LANES, (place + 1) * 2 * LANES)
        back = exact_dot(cas_ref[...], packed_ref[:, wide])
        for part in range(2):
            piece = back[:, part * LANES : (part + 1) * LANES].reshape(length // times, times, LANES)
            start = (2 * place + part) * times
            out_ref[:, start : start + times, :] = piece


def final_kernel(rows, times, tiles, source_ref, field_ref, sums_ref, solution_ref, residual_ref):
    line = jnp.sum(sums_ref[...].reshape(tiles, LANES), axis=0, keepdims=True)
    gamma, curved, cross, last = (
        jnp.broadcast_to(line[:, index : index + 1], (times, LANES)) for index in range(4)
    )
    step = gamma / curved
    gamma_next = step * step * cross - gamma
    turn = gamma_next / gamma
    grown = 1.0 + turn
    next_curved = grown * grown * curved - 2.0 * step * grown * cross + step * step * last
    next_step = gamma_next / next_curved
    low = lane_index((times, LANES)) < LANES // 2
    scale = jnp.where(low, step + next_step * grown, -next_step * step)
    for time in range(times):
        place = slice(time * rows, (time + 1) * rows)
        for pair in range(tiles // 2):
            columns = slice(pair * LANES, (pair + 1) * LANES)
            merged = []
            for part in range(2):
                taken = pl.ds(part * rows * times + time, rows, stride=times)
                left = scale * source_ref[2 * pair, taken, :]
                right = scale * source_ref[2 * pair + 1, taken, :]
                left = left + pltpu.roll(left, LANES // 2, 1)
                right = right + pltpu.roll(right, LANES // 2, 1)
                merged.append(jnp.where(low, left, right))
            solution_ref[place, columns] = merged[0]
            residual_ref[place, columns] = field_ref[place, columns] - merged[1]


def call(kernel, out_shape, scratch=()):
    shapes = [jax.ShapeDtypeStruct(shape, jnp.float32) for shape in out_shape]
    return pl.pallas_call(
        kernel,
        out_shape=shapes[0] if len(shapes) == 1 else shapes,
        scratch_shapes=[pltpu.VMEM(shape, jnp.float32) for shape in scratch],
        compiler_params=PARAMS,
    )


def shards(right_side, kappa, velocity):
    tiles = lax.axis_size("tm")
    spaces = lax.axis_size("space")
    times, rows, width = right_side.shape
    length = times * tiles
    tile = width // tiles
    quarter = LANES // 4
    cas_table = jnp.asarray(hartley_table(length))
    coef_table = jnp.asarray(chebyshev_table(length))
    up = [(i, (i + 1) % spaces) for i in range(spaces)]
    down = [(i, (i - 1) % spaces) for i in range(spaces)]

    field = right_side.reshape(times * rows, width)
    windows = call(
        functools.partial(window_kernel, rows, times, tiles),
        [(tiles, rows * times, LANES)],
        [(width // LANES, times * rows, LANES)],
    )(field)
    gathered = lax.all_to_all(windows, "tm", 0, 0)

    squares = velocity.astype(jnp.float32) ** 2
    planes = jnp.concatenate([kappa, squares[0], squares[1]], axis=0)
    planes = jnp.concatenate([planes[:, -quarter:], planes, planes[:, :quarter]], axis=1)
    local = lax.dynamic_slice_in_dim(planes, lax.axis_index("tm") * tile, LANES, 1)

    halo_shape = (HALO * length + 3 * rows, LANES)
    freq, low, high = call(
        functools.partial(forward_kernel, rows, times, length),
        [(rows * length, LANES), halo_shape, halo_shape],
    )(cas_table, gathered, local)
    top = lax.ppermute(high, "space", up)
    bottom = lax.ppermute(low, "space", down)

    total = rows + 2 * HALO
    halo_shape = (HALO * length, LANES)
    solved, applied, low, high, wide, early = call(
        functools.partial(first_kernel, rows, length),
        [
            (rows * length, LANES),
            (rows * length, LANES),
            halo_shape,
            halo_shape,
            (3 * total, 8, LANES),
            (2, 8, LANES),
        ],
    )(freq, top, bottom, local, coef_table)
    top = lax.ppermute(high, "space", up)
    bottom = lax.ppermute(low, "space", down)

    packed, sums = call(
        functools.partial(second_kernel, rows, times, length),
        [(tiles, 2 * rows * times, LANES), (spaces, 1, LANES)],
        [(length, 2 * rows * LANES)],
    )(applied, top, bottom, solved, wide, coef_table, cas_table, early)
    returned = lax.all_to_all(packed, "tm", 0, 0)
    sums = jnp.sum(lax.all_to_all(sums, "space", 0, 0), axis=0)
    sums = lax.all_to_all(jnp.broadcast_to(sums[None], (tiles, 1, LANES)), "tm", 0, 0)

    solution, residual = call(
        functools.partial(final_kernel, rows, times, tiles),
        [(times * rows, width), (times * rows, width)],
    )(returned, field, sums)
    shape = right_side.shape
    return solution.reshape(shape), residual.reshape(shape)


def solution(mesh):
    placed = (P("tm", "space", None), P("space", None), P(None, "space", None))
    return jax.shard_map(
        shards,
        mesh=mesh,
        in_specs=placed,
        out_specs=(P("tm", "space", None), P("tm", "space", None)),
        check_vma=False,
    )
```

time: 583 us -> 157 us (0.27)
  blocking collectives: 343 us -> 59.5 us
  starting transfers between devices: 109 us -> 32.6 us
  waiting for transfers between devices: 74.9 us -> 30.4 us
  Pallas kernels: 0 us -> 31 us
  local copies, waits for them, and re-layouts: 31.8 us -> 1.98 us
  other arithmetic: 14.2 us -> 0.07 us
    psum x3 -> x0, blocking collectives: 283 us -> none  [inner(): return lax.psum(jnp.sum(left * right), ('tm', 'space'))]
    ppermute x42 -> x4, starting transfers between devices: 101 us -> 22.2 us  [the longest x2 18.3 us: shards(): bottom = lax.ppermute(low, 'space', down)]
    ppermute x42 -> x4, waiting for transfers between devices: 63.8 us -> 14.2 us  [the longest x2 11.4 us: shards(): top = lax.ppermute(high, 'space', up)]
    pallas_call x0 -> x5, Pallas kernels: none -> 31 us  [the longest x1 15.2 us: shards(): call(functools.partial(second_kernel, rows, times, length), [(tiles, 2 *...]
    unnamed x15 -> x12, local copies, waits for them, and re-layouts: 20.1 us -> 1.7 us
    all_to_all x9 -> x0, local copies, waits for them, and re-layouts: 7.51 us -> none  [the longest x5 6.54 us: to_frequency(): lax.all_to_all(field, 'tm', split_axis=2, concat_axis=0, tiled=True)]
  transfers between devices with their start and end apart: 43 -> 5, of which waited for: 26 -> 5; matrix products, arithmetic and copies ran while one was open for 2% -> 0% of each run, Pallas kernels for 0% -> 0%
where the time goes in v1:
time: 157 us; the launch traced here: 156 us
  blocking collectives  59.5 us (38%)
  starting transfers between devices  32.6 us (21%)
  Pallas kernels  31 us (20%)
  waiting for transfers between devices  30.4 us (19%)
  local copies, waits for them, and re-layouts  1.98 us (1%)
    all_to_all x1, blocking collectives, shards(): returned = lax.all_to_all(packed, 'tm', 0, 0)  31.8 us
    ppermute x2, starting transfers between devices, shards(): bottom = lax.ppermute(low, 'space', down)  18.3 us
    all_to_all x1, waiting for transfers between devices, shards(): gathered = lax.all_to_all(windows, 'tm', 0, 0)  16.3 us
    all_to_all x1, blocking collectives, shards(): sums = jnp.sum(lax.all_to_all(sums, 'space', 0, 0), axis=0)  15.6 us
    pallas_call x1, Pallas kernels, shards(): call(functools.partial(second_kernel, rows, times, length), [(tiles, 2 *...  15.2 us
    pallas_call x1, Pallas kernels, shards(): call(functools.partial(first_kernel, rows, length), [(rows * length, LANE...  12.9 us
    all_to_all x1, blocking collectives, shards(): lax.all_to_all(jnp.broadcast_to(sums[None], (tiles, 1, LANES)), 'tm', 0, 0)  12 us
    ppermute x2, waiting for transfers between devices, shards(): top = lax.ppermute(high, 'space', up)  11.4 us
  transfers between devices with their start and end apart: 5, of which 5 were waited for; matrix products, arithmetic and copies ran while one was open for 0% of the time, Pallas kernels for 0%

profile of v1, /device:TPU:1, one launch (start us, length us, event | category | flops | bytes accessed | tf_op | source)
XLA Modules:
  0.0 156.2 jit_solution(16821843658558522823)
XLA Ops:
  0.6 0.0 copy-start
  0.6 0.9 copy-done
  1.6 1.0 shard_map.68
  2.6 0.0 copy-start.4
  2.6 10.4 %all-to-all-start = ((f32[16,64,128]{2,1,0:T(8,128)}), f32[16,64,128]{2,1,0:T(8,128)S(1)}, u32[]{:S(2)}, u32[]{:S(2)}) async-start(f32[16,64,128]{2,1,0:T(8,128)} %shard_map.68), calls=%async_computation | async-start | bytes 1048576 | tf_op jit(solution)/shard_map/all_to_all | solution.py:304
  13.0 0.0 copy-done.4
  13.0 0.0 copy-start.5
  13.0 0.7 copy-done.5
  13.8 0.1 fusion
  13.8 0.0 copy-start.2
  13.8 0.1 concatenate.7
  14.0 0.1 constant_dynamic-slice_fusion.weight_ref
  14.0 0.0 copy-start.3
  14.0 16.3 %all-to-all-done.field_ref = f32[16,64,128]{2,1,0:T(8,128)S(1)} async-done(((f32[16,64,128]{2,1,0:T(8,128)}), f32[16,64,128]{2,1,0:T(8,128)S(1)}, u32[]{:S(2)}, u32[]{:S(2)}) %all-to-all-start) | async-done | bytes 524320 | tf_op jit(solution)/shard_map/all_to_all | solution.py:304
  30.3 0.0 copy-done.2
  30.3 0.6 shard_map.69
  30.9 1.9 %collective-permute-start = (f32[664,128]{1,0:T(8,128)S(1)}, f32[664,128]{1,0:T(8,128)S(1)}, u32[]{:S(2)}, u32[]{:S(2)}) collective-permute-start(f32[664,128]{1,0:T(8,128)S(1)} %get-tuple-element.16), channel_id=1, source_target_pairs={{0,1},{1,2},{2,3},{3,4},{4,5},{5,6},{6,7},{7,8},{8,9},{9,10},{10,1... | collective-permute-start | bytes 1019912 | tf_op jit(solution)/shard_map/ppermute | solution.py:316
  32.9 11.2 %collective-permute-start.1 = (f32[664,128]{1,0:T(8,128)S(1)}, f32[664,128]{1,0:T(8,128)S(1)}, u32[]{:S(2)}, u32[]{:S(2)}) collective-permute-start(f32[664,128]{1,0:T(8,128)S(1)} %get-tuple-element.17), channel_id=1, source_target_pairs={{0,31},{1,0},{2,1},{3,2},{4,3},{5,4},{6,5},{7,6},{8,7},{9,8},{10,9... | collective-permute-start | bytes 1019912 | tf_op jit(solution)/shard_map/ppermute | solution.py:317
  44.1 5.3 %collective-permute-done.top_ref = f32[664,128]{1,0:T(8,128)S(1)} collective-permute-done((f32[664,128]{1,0:T(8,128)S(1)}, f32[664,128]{1,0:T(8,128)S(1)}, u32[]{:S(2)}, u32[]{:S(2)}) %collective-permute-start) | collective-permute-done | bytes 340000 | tf_op jit(solution)/shard_map/ppermute | solution.py:316
  49.4 1.8 %collective-permute-done.1.bottom_ref = f32[664,128]{1,0:T(8,128)S(1)} collective-permute-done((f32[664,128]{1,0:T(8,128)S(1)}, f32[664,128]{1,0:T(8,128)S(1)}, u32[]{:S(2)}, u32[]{:S(2)}) %collective-permute-start.1) | collective-permute-done | bytes 340000 | tf_op jit(solution)/shard_map/ppermute | solution.py:317
  51.1 0.0 copy-done.3
  51.1 12.9 %shard_map.70 = (f32[1024,128]{1,0:T(8,128)S(1)}, f32[1024,128]{1,0:T(8,128)S(1)}, f32[640,128]{1,0:T(8,128)S(1)}, f32[640,128]{1,0:T(8,128)S(1)}, f32[54,8,128]{2,1,0:T(8,128)S(1)}, /*index=5*/f32[2,8,128]{2,1,0:T(8,128)S(1)}) custom-call(f32[1024,128]{1,0:T(8,128)S(1)} %get-tuple-element.15.field_ref, f32[664,128]{1,0:T(8,128)S(1)} %collective-permute-done.top_ref, ...), custom_call_target="tpu_custom_call" | custom-call | tf_op jit(solution)/shard_map/pallas_call | solution.py:321
  64.0 1.9 %collective-permute-start.2 = (f32[640,128]{1,0:T(8,128)S(1)}, f32[640,128]{1,0:T(8,128)S(1)}, u32[]{:S(2)}, u32[]{:S(2)}) collective-permute-start(f32[640,128]{1,0:T(8,128)S(1)} %get-tuple-element.19), channel_id=1, source_target_pairs={{0,1},{1,2},{2,3},{3,4},{4,5},{5,6},{6,7},{7,8},{8,9},{9,10},{10,1... | collective-permute-start | bytes 983048 | tf_op jit(solution)/shard_map/ppermute | solution.py:332
  66.0 7.1 %collective-permute-start.3 = (f32[640,128]{1,0:T(8,128)S(1)}, f32[640,128]{1,0:T(8,128)S(1)}, u32[]{:S(2)}, u32[]{:S(2)}) collective-permute-start(f32[640,128]{1,0:T(8,128)S(1)} %get-tuple-element.20), channel_id=1, source_target_pairs={{0,31},{1,0},{2,1},{3,2},{4,3},{5,4},{6,5},{7,6},{8,7},{9,8},{10,9... | collective-permute-start | bytes 983048 | tf_op jit(solution)/shard_map/ppermute | solution.py:333
  73.1 6.2 %collective-permute-done.2.top_ref = f32[640,128]{1,0:T(8,128)S(1)} collective-permute-done((f32[640,128]{1,0:T(8,128)S(1)}, f32[640,128]{1,0:T(8,128)S(1)}, u32[]{:S(2)}, u32[]{:S(2)}) %collective-permute-start.2) | collective-permute-done | bytes 327712 | tf_op jit(solution)/shard_map/ppermute | solution.py:332
  79.3 1.0 collective-permute-done.3.bottom_ref
  80.2 15.2 %shard_map.71 = (f32[16,128,128]{2,1,0:T(8,128)S(1)}, f32[32,1,128]{2,1,0:T(1,128)S(1)}) custom-call(f32[1024,128]{1,0:T(8,128)S(1)} %get-tuple-element.18.field_ref, f32[640,128]{1,0:T(8,128)S(1)} %collective-permute-done.2.top_ref, f32[640,128]{1,0:T(8,128)S(1)} %collective-permute-done.3.bottom_ref, f32[1024,128]{1,0:T(8,128)S(1)} %get-tuple-element.21.earlier_ref, ...), custom_call_target="tpu_custom_call" | custom-call | tf_op jit(solution)/shard_map/pallas_call | solution.py:335
  95.5 15.6 %all_to_all.20 = f32[32,1,128]{2,1,0:T(1,128)S(1)} all-to-all(f32[32,1,128]{2,1,0:T(1,128)S(1)} %get-tuple-element.25), channel_id=1, replica_groups=mesh['tm'=16,'space'=32] {'space'}, dimensions={0} | all-to-all | bytes 32768 | tf_op jit(solution)/shard_map/all_to_all | solution.py:341
  111.1 0.1 reduce_sum.9
  111.1 12.0 %all_to_all.21.sums_ref = f32[16,1,128]{2,1,0:T(1,128)S(1)} all-to-all(f32[16,1,128]{2,1,0:T(1,128)S(1)} %broadcast_in_dim.2), channel_id=1, replica_groups=mesh['tm'=16,'space'=32] {'tm'}, dimensions={0} | all-to-all | bytes 16384 | tf_op jit(solution)/shard_map/all_to_all | solution.py:342
  123.2 0.0 copy-start.1
  123.2 31.8 %all_to_all.22.source_ref = f32[16,128,128]{2,1,0:T(8,128)S(1)} all-to-all(f32[16,128,128]{2,1,0:T(8,128)S(1)} %get-tuple-element.24), channel_id=1, replica_groups=mesh['tm'=16,'space'=32] {'tm'}, dimensions={0} | all-to-all | bytes 2097152 | tf_op jit(solution)/shard_map/all_to_all | solution.py:340
  155.0 0.0 copy-done.1
  155.0 1.2 shard_map.72
  (4 shorter events, 0.0 us)
Async XLA Ops:
  0.6 1.0 copy-start
  2.6 10.4 %copy-start.4 = (s32[2,8,1024]{2,1,0:T(8,128)S(1)}, s32[2,8,1024]{2,1,0:T(8,128)}, u32[]{:S(2)}) copy-start(s32[2,8,1024]{2,1,0:T(8,128)} %param.7) | copy-start | bytes 196612
  2.6 27.7 %all-to-all-start = ((f32[16,64,128]{2,1,0:T(8,128)}), f32[16,64,128]{2,1,0:T(8,128)S(1)}, u32[]{:S(2)}, u32[]{:S(2)}) async-start(f32[16,64,128]{2,1,0:T(8,128)} %shard_map.68), calls=%async_computation | async-start | bytes 1048576 | tf_op jit(solution)/shard_map/all_to_all | solution.py:304
  13.0 0.8 copy-start.5
  13.8 16.5 %copy-start.2 = (f32[128,128]{1,0:T(8,128)S(1)}, f32[128,128]{1,0:T(8,128)}, u32[]{:S(2)}) copy-start(f32[128,128]{1,0:T(8,128)} %constant.18.clone.cas_ref) | copy-start | bytes 196612
  14.0 37.1 %copy-start.3 = (f32[128,128]{1,0:T(8,128)S(1)}, f32[128,128]{1,0:T(8,128)}, u32[]{:S(2)}) copy-start(f32[128,128]{1,0:T(8,128)} %constant.19.clone.coef_ref) | copy-start | bytes 196612
  30.9 18.4 %collective-permute-start = (f32[664,128]{1,0:T(8,128)S(1)}, f32[664,128]{1,0:T(8,128)S(1)}, u32[]{:S(2)}, u32[]{:S(2)}) collective-permute-start(f32[664,128]{1,0:T(8,128)S(1)} %get-tuple-element.16), channel_id=1, source_target_pairs={{0,1},{1,2},{2,3},{3,4},{4,5},{5,6},{6,7},{7,8},{8,9},{9,10},{10,1... | collective-permute-start | bytes 1019912 | tf_op jit(solution)/shard_map/ppermute | solution.py:316
  32.9 18.3 %collective-permute-start.1 = (f32[664,128]{1,0:T(8,128)S(1)}, f32[664,128]{1,0:T(8,128)S(1)}, u32[]{:S(2)}, u32[]{:S(2)}) collective-permute-start(f32[664,128]{1,0:T(8,128)S(1)} %get-tuple-element.17), channel_id=1, source_target_pairs={{0,31},{1,0},{2,1},{3,2},{4,3},{5,4},{6,5},{7,6},{8,7},{9,8},{10,9... | collective-permute-start | bytes 1019912 | tf_op jit(solution)/shard_map/ppermute | solution.py:317
  64.0 15.2 %collective-permute-start.2 = (f32[640,128]{1,0:T(8,128)S(1)}, f32[640,128]{1,0:T(8,128)S(1)}, u32[]{:S(2)}, u32[]{:S(2)}) collective-permute-start(f32[640,128]{1,0:T(8,128)S(1)} %get-tuple-element.19), channel_id=1, source_target_pairs={{0,1},{1,2},{2,3},{3,4},{4,5},{5,6},{6,7},{7,8},{8,9},{9,10},{10,1... | collective-permute-start | bytes 983048 | tf_op jit(solution)/shard_map/ppermute | solution.py:332
  66.0 14.3 %collective-permute-start.3 = (f32[640,128]{1,0:T(8,128)S(1)}, f32[640,128]{1,0:T(8,128)S(1)}, u32[]{:S(2)}, u32[]{:S(2)}) collective-permute-start(f32[640,128]{1,0:T(8,128)S(1)} %get-tuple-element.20), channel_id=1, source_target_pairs={{0,31},{1,0},{2,1},{3,2},{4,3},{5,4},{6,5},{7,6},{8,7},{9,8},{10,9... | collective-permute-start | bytes 983048 | tf_op jit(solution)/shard_map/ppermute | solution.py:333
  123.2 31.8 %copy-start.1 = (f32[8,8,1024]{2,1,0:T(8,128)S(1)}, f32[8,8,1024]{2,1,0:T(8,128)}, u32[]{:S(2)}) copy-start(f32[8,8,1024]{2,1,0:T(8,128)} %param.5) | copy-start | bytes 786436

commit v2 on v1

v2 whole, which is shorter than its diff:
```python
import functools
import math

import jax
import jax.numpy as jnp
import numpy as np
from jax import lax
from jax.experimental import pallas as pl
from jax.experimental.pallas import tpu as pltpu
from jax.sharding import PartitionSpec as P

CHEB = 4
COUPLING = 2.0
KAPPA_LOW = 0.05
KAPPA_HIGH = 1.0
REACH = 16.0

LANES = 128
SUB = 8
HALO = CHEB + 1
SIDE = 16
BLOCK = 11
WINDOW = SUB * BLOCK
PARAMS = pltpu.CompilerParams(vmem_limit_bytes=24 * 1024 * 1024)


def hartley_table(length):
    index = np.arange(length)
    angle = (index[:, None] * index[None, :] % length) * (2.0 * math.pi / length)
    return ((np.cos(angle) + np.sin(angle)) / math.sqrt(length)).astype(np.float32)


def chebyshev_table(length):
    shift = COUPLING * (2.0 - 2.0 * np.cos(2.0 * math.pi * np.arange(length) / length))
    half = 0.5 * (KAPPA_HIGH + REACH - KAPPA_LOW)
    mid = 0.5 * (KAPPA_LOW + KAPPA_HIGH + REACH) + shift
    ratio = mid / half
    damp = 1.0 / ratio
    lines = [shift, 1.0 / mid]
    for _ in range(CHEB):
        damp_next = 1.0 / (2.0 * ratio - damp)
        lines += [damp_next * damp, 2.0 * damp_next / half]
        damp = damp_next
    return np.repeat(np.stack(lines).astype(np.float32)[:, None], SUB, 1)


def lane_index(shape):
    return lax.broadcasted_iota(jnp.int32, shape, len(shape) - 1)


def exact_dot(left, right, left_dim, right_dim):
    return lax.dot_general(
        left,
        right,
        (((left_dim,), (right_dim,)), ((), ())),
        precision=lax.Precision.HIGHEST,
        preferred_element_type=jnp.float32,
    )


def window_kernel(rows, times, tiles, source_ref, out_ref, scratch_ref):
    half = LANES // 2
    parts = source_ref.shape[1] // LANES
    for part in range(parts):
        scratch_ref[part] = source_ref[:, part * LANES : (part + 1) * LANES]
    lane = lane_index((times, LANES))
    fields = [
        [scratch_ref[part, pl.ds(row, times, stride=rows), :] for part in range(parts)]
        for row in range(rows)
    ]
    for pair in range(rows // 2):
        for part in range(parts):
            one, two = fields[2 * pair][part], fields[2 * pair + 1][part]
            place = slice(pair * times, (pair + 1) * times)
            out_ref[2 * part, place, :] = jnp.where(lane < half, one, pltpu.roll(two, half, 1))
            out_ref[2 * part + 1, place, :] = jnp.where(lane < half, pltpu.roll(one, half, 1), two)
    spread = 2 * SIDE
    group = LANES // spread
    for quad in range(rows // group):
        even = [None] * parts
        odd = [None] * parts
        for index in range(group):
            row = quad * group + index
            wide = jnp.concatenate(fields[row], axis=1)
            near = pltpu.roll(wide, spread * index + SIDE, 1)
            away = pltpu.roll(wide, (spread * index - half + SIDE) % wide.shape[1], 1)
            left = (lane >= spread * index) & (lane < spread * index + SIDE)
            right = (lane >= spread * index + SIDE) & (lane < spread * (index + 1))
            for part in range(parts):
                here = slice(part * LANES, (part + 1) * LANES)
                then = (part + 1) % parts
                then = slice(then * LANES, (then + 1) * LANES)
                if index == 0:
                    even[part] = jnp.where(left, near[:, here], away[:, here])
                    odd[part] = jnp.where(left, away[:, here], near[:, then])
                else:
                    even[part] = jnp.where(
                        left, near[:, here], jnp.where(right, away[:, here], even[part])
                    )
                    odd[part] = jnp.where(
                        left, away[:, here], jnp.where(right, near[:, then], odd[part])
                    )
        start = (rows // 2 + quad) * times
        for part in range(parts):
            out_ref[2 * part, start : start + times, :] = even[part]
            out_ref[2 * part + 1, start : start + times, :] = odd[part]


def forward_kernel(rows, times, length, cas_ref, field_ref, out_ref, low_ref, high_ref, line_ref):
    half = LANES // 2
    span = half + 2 * SIDE
    pieces = field_ref.shape[1] // times
    group = LANES // (2 * SIDE)
    for piece in range(pieces):
        block = field_ref[:, piece * times : (piece + 1) * times, :].reshape(length, LANES)
        freq = exact_dot(block, cas_ref[...], 0, 0)
        if piece < rows // 2:
            for part in range(2):
                start = (2 * piece + part) * span + SIDE
                line_ref[start : start + half, :] = freq[part * half : (part + 1) * half]
        else:
            for index in range(group):
                start = ((piece - rows // 2) * group + index) * span
                place = 2 * SIDE * index
                line_ref[start : start + SIDE, :] = freq[place : place + SIDE]
                line_ref[start + SIDE + half : start + span, :] = freq[
                    place + SIDE : place + 2 * SIDE
                ]
    skip = (span - WINDOW) // 2
    for row in range(rows):
        for column in range(BLOCK):
            value = line_ref[pl.ds(row * span + skip + column, SUB, stride=BLOCK), :]
            out_ref[row, column] = value
            if row < HALO:
                low_ref[row, column] = value
            if row >= rows - HALO:
                high_ref[row - (rows - HALO), column] = value


def weight_kernel(rows, local_ref, top_ref, bottom_ref, wide_ref, scratch_ref):
    planes = []
    for plane in range(3):
        start = plane * rows
        planes.append(
            jnp.concatenate(
                [
                    top_ref[start + rows - HALO : start + rows, :],
                    local_ref[start : start + rows, :],
                    bottom_ref[start : start + HALO, :],
                ],
                axis=0,
            )
        )
    east = 1.0 + 0.125 * (planes[1] + jnp.concatenate([planes[1][1:], planes[1][:1]], axis=0))
    north = 1.0 + 0.125 * (planes[2] + pltpu.roll(planes[2], LANES - 1, 1))
    total = rows + 2 * HALO
    zero = jnp.zeros((LANES - 3 * total, LANES), jnp.float32)
    scratch_ref[...] = jnp.transpose(jnp.concatenate([planes[0], east, north, zero], axis=0))
    skip = (LANES - WINDOW) // 2
    for column in range(BLOCK):
        lines = scratch_ref[pl.ds(skip + column, SUB, stride=BLOCK), :]
        for row in range(total):
            for plane in range(3):
                index = plane * total + row
                wide_ref[row, plane * BLOCK + column] = jnp.broadcast_to(
                    lines[:, index : index + 1], (SUB, LANES)
                )


def own_columns(column):
    place = lax.broadcasted_iota(jnp.int32, (SUB, LANES), 0) * BLOCK + column
    first = (WINDOW - LANES // 2) // 2
    return (place >= first) & (place < first + LANES // 2)


def passes(
    rows, top_ref, field_ref, bottom_ref, wide_ref, coef_ref, step_ref, remain_ref, solved_ref, emit
):
    total = rows + 2 * HALO
    columns = range(BLOCK)

    def begin(source_ref, offset, count):
        scale = coef_ref[1]

        @pl.loop(0, count)
        def _(row):
            for column in columns:
                value = source_ref[row, column]
                remain_ref[offset + row, column] = value
                step_ref[offset + row, column] = scale * value

    begin(top_ref, 0, HALO)
    begin(field_ref, HALO, rows)
    begin(bottom_ref, HALO + rows, HALO)

    for turn in range(CHEB + 1):
        first, last = turn + 1, total - turn - 1
        shift = coef_ref[0]

        def row_step(row, carry, *, turn=turn, inside=False, shift=shift):
            here, flux = carry[:BLOCK], carry[BLOCK:]
            after = [step_ref[row + 1, column] for column in columns]
            ahead = [wide_ref[row, BLOCK + column] * (here[column] - after[column]) for column in columns]
            beside = list(here[1:]) + [pltpu.roll(here[0], SUB - 1, 0)]
            side = [wide_ref[row, 2 * BLOCK + column] * (here[column] - beside[column]) for column in columns]
            behind = [pltpu.roll(side[-1], 1, 0)] + side[:-1]
            for column in columns:
                applied = (
                    (wide_ref[row, column] + shift) * here[column]
                    + (ahead[column] - flux[column])
                    + (side[column] - behind[column])
                )
                left = remain_ref[row, column] - applied
                if turn < CHEB:
                    remain_ref[row, column] = left
                    step_ref[row, column] = (
                        coef_ref[2 + 2 * turn] * here[column] + coef_ref[3 + 2 * turn] * left
                    )
                if inside:
                    own = row - HALO
                    if turn == 0:
                        solved_ref[own, column] = here[column]
                    elif turn < CHEB:
                        solved_ref[own, column] = solved_ref[own, column] + here[column]
                    else:
                        source = field_ref[own, column]
                        emit(own, column, source, solved_ref[own, column] + here[column], source - left)
            return (*after, *ahead)

        here = [step_ref[first, column] for column in columns]
        flux = [
            wide_ref[first - 1, BLOCK + column] * (step_ref[first - 1, column] - here[column])
            for column in columns
        ]
        carry = (*here, *flux)
        if first < HALO:
            carry = lax.fori_loop(first, HALO, row_step, carry)
        carry = lax.fori_loop(HALO, HALO + rows, functools.partial(row_step, inside=True), carry)
        if HALO + rows < last:
            lax.fori_loop(HALO + rows, last, row_step, carry)


def first_kernel(
    rows, top_ref, field_ref, bottom_ref, wide_ref, coef_ref,
    solved_ref, applied_ref, low_ref, high_ref, sums_ref, step_ref, remain_ref, part_ref,
):
    sums_ref[...] = jnp.zeros_like(sums_ref)

    def emit(row, column, source, solved, applied):
        solved_ref[row, column] = solved
        applied_ref[row, column] = applied
        inside = jnp.where(own_columns(column), solved, 0.0)
        sums_ref[0] = sums_ref[0] + source * inside
        sums_ref[1] = sums_ref[1] + applied * inside

    passes(
        rows, top_ref, field_ref, bottom_ref, wide_ref, coef_ref, step_ref, remain_ref, part_ref, emit
    )
    for row in range(HALO):
        for column in range(BLOCK):
            low_ref[row, column] = applied_ref[row, column]
            high_ref[row, column] = applied_ref[rows - HALO + row, column]


def second_kernel(
    rows, top_ref, field_ref, bottom_ref, wide_ref, coef_ref, early_ref,
    solved_ref, applied_ref, sums_ref, step_ref, remain_ref, part_ref, late_ref,
):
    late_ref[...] = jnp.zeros_like(late_ref)

    def emit(row, column, source, solved, applied):
        solved_ref[row, column] = solved
        applied_ref[row, column] = applied
        inside = jnp.where(own_columns(column), solved, 0.0)
        late_ref[0] = late_ref[0] + source * inside
        late_ref[1] = late_ref[1] + applied * inside

    passes(
        rows, top_ref, field_ref, bottom_ref, wide_ref, coef_ref, step_ref, remain_ref, part_ref, emit
    )
    values = [jnp.sum(ref[index]) for ref in (early_ref, late_ref) for index in range(2)]
    lane = lane_index((1, LANES))
    line = jnp.zeros((1, LANES), jnp.float32)
    for index, value in enumerate(values):
        line = jnp.where(lane == index, value, line)
    sums_ref[...] = jnp.broadcast_to(line[None], sums_ref.shape)


def inverse_kernel(rows, times, length, cas_ref, one_ref, two_ref, three_ref, four_ref, out_ref, line_ref):
    half = LANES // 2
    span = half + 2 * SIDE
    skip = (span - WINDOW) // 2
    refs = (one_ref, two_ref, three_ref, four_ref)
    for row in range(rows):
        for index, ref in enumerate(refs):
            for column in range(BLOCK):
                start = (row * len(refs) + index) * span + skip + column
                line_ref[pl.ds(start, SUB, stride=BLOCK), :] = ref[row, column]
    for row in range(rows):
        for pair in range(2):
            start = (row * len(refs) + 2 * pair) * span + SIDE
            points = jnp.concatenate(
                [line_ref[start : start + half, :], line_ref[start + span : start + span + half, :]],
                axis=0,
            )
            back = exact_dot(cas_ref[...], points, 1, 1).reshape(length // times, times, LANES)
            place = (pair * rows + row) * times
            out_ref[:, place : place + times, :] = back


def final_kernel(rows, times, tiles, source_ref, field_ref, sums_ref, solution_ref, residual_ref):
    line = sums_ref[...]
    gamma, curved, cross, last = (
        jnp.broadcast_to(line[:, index : index + 1], (times, LANES)) for index in range(4)
    )
    step = gamma / curved
    gamma_next = step * step * cross - gamma
    turn = gamma_next / gamma
    grown = 1.0 + turn
    next_curved = grown * grown * curved - 2.0 * step * grown * cross + step * step * last
    next_step = gamma_next / next_curved
    low = lane_index((times, LANES)) < LANES // 2
    scale = jnp.where(low, step + next_step * grown, -next_step * step)
    for time in range(times):
        place = slice(time * rows, (time + 1) * rows)
        for pair in range(tiles // 2):
            columns = slice(pair * LANES, (pair + 1) * LANES)
            merged = []
            for part in range(2):
                taken = pl.ds(part * rows * times + time, rows, stride=times)
                left = scale * source_ref[2 * pair, taken, :]
                right = scale * source_ref[2 * pair + 1, taken, :]
                left = left + pltpu.roll(left, LANES // 2, 1)
                right = right + pltpu.roll(right, LANES // 2, 1)
                merged.append(jnp.where(low, left, right))
            solution_ref[place, columns] = merged[0]
            residual_ref[place, columns] = field_ref[place, columns] - merged[1]


def call(kernel, out_shape, scratch=()):
    shapes = [jax.ShapeDtypeStruct(shape, jnp.float32) for shape in out_shape]
    return pl.pallas_call(
        kernel,
        out_shape=shapes[0] if len(shapes) == 1 else shapes,
        scratch_shapes=[pltpu.VMEM(shape, jnp.float32) for shape in scratch],
        compiler_params=PARAMS,
    )


def exchange(low, high, spaces):
    up = [(i, (i + 1) % spaces) for i in range(spaces)]
    down = [(i, (i - 1) % spaces) for i in range(spaces)]
    return lax.ppermute(high, "space", up), lax.ppermute(low, "space", down)


def shards(right_side, kappa, velocity):
    tiles = lax.axis_size("tm")
    spaces = lax.axis_size("space")
    times, rows, width = right_side.shape
    length = times * tiles
    tile = width // tiles
    around = (LANES - tile) // 2
    cas_table = jnp.asarray(hartley_table(length))
    coef_table = jnp.asarray(chebyshev_table(length))

    field = right_side.reshape(times * rows, width)
    windows = call(
        functools.partial(window_kernel, rows, times, tiles),
        [(tiles, 6 * times, LANES)],
        [(width // LANES, times * rows, LANES)],
    )(field)
    gathered = lax.all_to_all(windows, "tm", 0, 0)

    squares = velocity.astype(jnp.float32) ** 2
    planes = jnp.concatenate([kappa, squares[0], squares[1]], axis=0)
    planes = jnp.concatenate([planes[:, -around:], planes, planes[:, :around]], axis=1)
    local = lax.dynamic_slice_in_dim(planes, lax.axis_index("tm") * tile, LANES, 1)
    top, bottom = exchange(local, local, spaces)
    total = rows + 2 * HALO
    wide = call(
        functools.partial(weight_kernel, rows),
        [(total, 3 * BLOCK, SUB, LANES)],
        [(LANES, LANES)],
    )(local, top, bottom)

    tile_shape = (rows, BLOCK, SUB, LANES)
    edge_shape = (HALO, BLOCK, SUB, LANES)
    work = [(total, BLOCK, SUB, LANES), (total, BLOCK, SUB, LANES), tile_shape]
    span = LANES // 2 + 2 * SIDE
    freq, low, high = call(
        functools.partial(forward_kernel, rows, times, length),
        [tile_shape, edge_shape, edge_shape],
        [(rows * span, LANES)],
    )(cas_table, gathered)
    top, bottom = exchange(low, high, spaces)

    solved, applied, low, high, early = call(
        functools.partial(first_kernel, rows),
        [tile_shape, tile_shape, edge_shape, edge_shape, (2, SUB, LANES)],
        work,
    )(top, freq, bottom, wide, coef_table)
    top, bottom = exchange(low, high, spaces)

    solved_two, applied_two, sums = call(
        functools.partial(second_kernel, rows),
        [tile_shape, tile_shape, (tiles, 1, LANES)],
        [*work, (2, SUB, LANES)],
    )(top, applied, bottom, wide, coef_table, early)
    packed = call(
        functools.partial(inverse_kernel, rows, times, length),
        [(tiles, 2 * rows * times, LANES)],
        [(rows * 4 * span, LANES)],
    )(cas_table, solved, solved_two, applied, applied_two)
    sums = jnp.sum(lax.all_to_all(sums, "tm", 0, 0), axis=0)
    returned = lax.all_to_all(packed, "tm", 0, 0)
    distance = 1
    while distance < spaces:
        pairs = [(i, i ^ distance) for i in range(spaces)]
        sums = sums + lax.ppermute(sums, "space", pairs)
        distance *= 2

    solution, residual = call(
        functools.partial(final_kernel, rows, times, tiles),
        [(times * rows, width), (times * rows, width)],
    )(returned, field, sums)
    shape = right_side.shape
    return solution.reshape(shape), residual.reshape(shape)


def solution(mesh):
    placed = (P("tm", "space", None), P("space", None), P(None, "space", None))
    return jax.shard_map(
        shards,
        mesh=mesh,
        in_specs=placed,
        out_specs=(P("tm", "space", None), P("tm", "space", None)),
        check_vma=False,
    )
```

time: 157 us -> 123 us (0.78)
  the two profiles are of different devices: /device:TPU:1 before, /device:TPU:8 now
where the time goes in v2:
time: 123 us; the launch traced here: 122 us
  starting transfers between devices  59.4 us (48%)
  waiting for transfers between devices  45.9 us (37%)
  Pallas kernels  12.5 us (10%)
  local copies, waits for them, and re-layouts  2.07 us (2%)
  other arithmetic  1.66 us (1%)
    ppermute x6, starting transfers between devices, exchange(): return (lax.ppermute(high, 'space', up), lax.ppermute(low, 'space', down))  28.7 us
    ppermute x5, waiting for transfers between devices, shards(): sums = sums + lax.ppermute(sums, 'space', pairs)  22.5 us
    ppermute x5, starting transfers between devices, shards(): sums = sums + lax.ppermute(sums, 'space', pairs)  10.9 us
    ppermute x6, waiting for transfers between devices, exchange(): return (lax.ppermute(high, 'space', up), lax.ppermute(low, 'space', down))  10.5 us
    all_to_all x1, waiting for transfers between devices, shards(): gathered = lax.all_to_all(windows, 'tm', 0, 0)  10.2 us
    all_to_all x1, starting transfers between devices, shards(): gathered = lax.all_to_all(windows, 'tm', 0, 0)  9.17 us
    all_to_all x1, starting transfers between devices, shards(): sums = jnp.sum(lax.all_to_all(sums, 'tm', 0, 0), axis=0)  5.76 us
    all_to_all x1, starting transfers between devices, shards(): returned = lax.all_to_all(packed, 'tm', 0, 0)  4.92 us
  transfers between devices with their start and end apart: 14, of which 10 were waited for; matrix products, arithmetic and copies ran while one was open for 2% of the time, Pallas kernels for 4%

profile of v2, /device:TPU:8, one launch (start us, length us, event | category | flops | bytes accessed | tf_op | source)
XLA Modules:
  0.0 122.4 jit_solution(4612357553579961828)
XLA Ops:
  0.6 0.0 copy-start
  0.6 0.9 copy-done
  1.6 0.0 copy-start.4
  1.6 1.0 shard_map.68
  2.6 9.2 %all-to-all-start = ((f32[16,48,128]{2,1,0:T(8,128)}), f32[16,48,128]{2,1,0:T(8,128)S(1)}, u32[]{:S(2)}, u32[]{:S(2)}) async-start(f32[16,48,128]{2,1,0:T(8,128)} %shard_map.68), calls=%async_computation | async-start | bytes 786432 | tf_op jit(solution)/shard_map/all_to_all | solution.py:372
  11.8 0.8 convert_multiply_fusion
  12.6 0.8 pad_maximum_fusion
  13.4 10.2 %all-to-all-done.field_ref = f32[16,48,128]{2,1,0:T(8,128)S(1)} async-done(((f32[16,48,128]{2,1,0:T(8,128)}), f32[16,48,128]{2,1,0:T(8,128)S(1)}, u32[]{:S(2)}, u32[]{:S(2)}) %all-to-all-start) | async-done | bytes 393248 | tf_op jit(solution)/shard_map/all_to_all | solution.py:372
  23.6 0.0 copy-start.2
  23.6 0.8 copy-done.2
  24.4 0.6 shard_map.69
  25.0 1.9 %collective-permute-start = (f32[5,11,8,128]{3,2,1,0:T(8,128)S(1)}, f32[5,11,8,128]{3,2,1,0:T(8,128)S(1)}, u32[]{:S(2)}, u32[]{:S(2)}) collective-permute-start(f32[5,11,8,128]{3,2,1,0:T(8,128)S(1)} %get-tuple-element.15), channel_id=1, source_target_pairs={{0,1},{1,2},{2,3},{3,4},{4,5},{5,6},{6,7},{7,8},{8,9},{9,10},{10,1... | collective-permute-start | bytes 675848 | tf_op jit(solution)/shard_map/ppermute | solution.py:353
  26.9 11.6 %collective-permute-start.1 = (f32[5,11,8,128]{3,2,1,0:T(8,128)S(1)}, f32[5,11,8,128]{3,2,1,0:T(8,128)S(1)}, u32[]{:S(2)}, u32[]{:S(2)}) collective-permute-start(f32[5,11,8,128]{3,2,1,0:T(8,128)S(1)} %get-tuple-element.17), channel_id=1, source_target_pairs={{0,31},{1,0},{2,1},{3,2},{4,3},{5,4},{6,5},{7,6},{8,7},{9,8},{10,9... | collective-permute-start | bytes 675848 | tf_op jit(solution)/shard_map/ppermute | solution.py:353
  38.6 0.1 fusion
  38.7 0.1 concatenate.7
  38.8 0.1 constant_dynamic-slice_fusion.local_ref
  38.8 3.9 %collective-permute-start.3 = (f32[24,128]{1,0:T(8,128)S(1)}, f32[24,128]{1,0:T(8,128)S(1)}, u32[]{:S(2)}, u32[]{:S(2)}) collective-permute-start(f32[24,128]{1,0:T(8,128)S(1)} %constant_dynamic-slice_fusion.local_ref), channel_id=1, source_target_pairs={{0,31},{1,0},{2,1},{3,2},{4,3},{5,4},{6,5},{7,6},{8,7},{9,8},{10,9... | collective-permute-start | bytes 36872 | tf_op jit(solution)/shard_map/ppermute | solution.py:353
  42.8 1.9 %collective-permute-start.2 = (f32[24,128]{1,0:T(8,128)S(1)}, f32[24,128]{1,0:T(8,128)S(1)}, u32[]{:S(2)}, u32[]{:S(2)}) collective-permute-start(f32[24,128]{1,0:T(8,128)S(1)} %constant_dynamic-slice_fusion.local_ref), channel_id=1, source_target_pairs={{0,1},{1,2},{2,3},{3,4},{4,5},{5,6},{6,7},{7,8},{8,9},{9,10},{10,1... | collective-permute-start | bytes 36872 | tf_op jit(solution)/shard_map/ppermute | solution.py:353
  44.7 0.0 collective-permute-done.3.bottom_ref
  44.7 7.0 %collective-permute-done.2.top_ref = f32[24,128]{1,0:T(8,128)S(1)} collective-permute-done((f32[24,128]{1,0:T(8,128)S(1)}, f32[24,128]{1,0:T(8,128)S(1)}, u32[]{:S(2)}, u32[]{:S(2)}) %collective-permute-start.2) | collective-permute-done | bytes 12320 | tf_op jit(solution)/shard_map/ppermute | solution.py:353
  51.7 1.2 %shard_map.70.wide_ref = f32[18,33,8,128]{3,2,1,0:T(8,128)S(1)} custom-call(f32[24,128]{1,0:T(8,128)S(1)} %constant_dynamic-slice_fusion.local_ref, f32[24,128]{1,0:T(8,128)S(1)} %collective-permute-done.2.top_ref, f32[24,128]{1,0:T(8,128)S(1)} %collective-permute-done.3.bottom_ref), custom_call_target="tpu_custom_call" | custom-call | tf_op jit(solution)/shard_map/pallas_call | solution.py:380
  52.9 0.0 collective-permute-done.top_ref
  52.9 0.0 collective-permute-done.1.bottom_ref
  52.9 0.0 copy-done.4
  52.9 2.2 %shard_map.71 = (f32[8,11,8,128]{3,2,1,0:T(8,128)S(1)}, f32[8,11,8,128]{3,2,1,0:T(8,128)S(1)}, f32[5,11,8,128]{3,2,1,0:T(8,128)S(1)}, f32[5,11,8,128]{3,2,1,0:T(8,128)S(1)}, f32[2,8,128]{2,1,0:T(8,128)S(1)}) custom-call(f32[5,11,8,128]{3,2,1,0:T(8,128)S(1)} %collective-permute-done.top_ref, f32[8,11,8,128]{3,2,1,0:T(8,128)S(1)} %get-tuple-element.16.field_ref, ...), custom_call_target="tpu_custom_call" | custom-call | tf_op jit(solution)/shard_map/pallas_call | solution.py:397
  55.1 0.0 copy-start.3
  55.2 2.1 %collective-permute-start.4 = (f32[5,11,8,128]{3,2,1,0:T(8,128)S(1)}, f32[5,11,8,128]{3,2,1,0:T(8,128)S(1)}, u32[]{:S(2)}, u32[]{:S(2)}) collective-permute-start(f32[5,11,8,128]{3,2,1,0:T(8,128)S(1)} %get-tuple-element.19), channel_id=1, source_target_pairs={{0,1},{1,2},{2,3},{3,4},{4,5},{5,6},{6,7},{7,8},{8,9},{9,10},{10,1... | collective-permute-start | bytes 675848 | tf_op jit(solution)/shard_map/ppermute | solution.py:353
  57.2 7.2 %collective-permute-start.5 = (f32[5,11,8,128]{3,2,1,0:T(8,128)S(1)}, f32[5,11,8,128]{3,2,1,0:T(8,128)S(1)}, u32[]{:S(2)}, u32[]{:S(2)}) collective-permute-start(f32[5,11,8,128]{3,2,1,0:T(8,128)S(1)} %get-tuple-element.21), channel_id=1, source_target_pairs={{0,31},{1,0},{2,1},{3,2},{4,3},{5,4},{6,5},{7,6},{8,7},{9,8},{10,9... | collective-permute-start | bytes 675848 | tf_op jit(solution)/shard_map/ppermute | solution.py:353
  64.5 2.0 %collective-permute-done.4.top_ref = f32[5,11,8,128]{3,2,1,0:T(8,128)S(1)} collective-permute-done((f32[5,11,8,128]{3,2,1,0:T(8,128)S(1)}, f32[5,11,8,128]{3,2,1,0:T(8,128)S(1)}, u32[]{:S(2)}, u32[]{:S(2)}) %collective-permute-start.4) | collective-permute-done | bytes 225312 | tf_op jit(solution)/shard_map/ppermute | solution.py:353
  66.5 1.5 %collective-permute-done.5.bottom_ref = f32[5,11,8,128]{3,2,1,0:T(8,128)S(1)} collective-permute-done((f32[5,11,8,128]{3,2,1,0:T(8,128)S(1)}, f32[5,11,8,128]{3,2,1,0:T(8,128)S(1)}, u32[]{:S(2)}, u32[]{:S(2)}) %collective-permute-start.5) | collective-permute-done | bytes 225312 | tf_op jit(solution)/shard_map/ppermute | solution.py:353
  67.9 2.9 %shard_map.72 = (f32[8,11,8,128]{3,2,1,0:T(8,128)S(1)}, f32[8,11,8,128]{3,2,1,0:T(8,128)S(1)}, f32[16,1,128]{2,1,0:T(1,128)}) custom-call(f32[5,11,8,128]{3,2,1,0:T(8,128)S(1)} %collective-permute-done.4.top_ref, f32[8,11,8,128]{3,2,1,0:T(8,128)S(1)} %get-tuple-element.20.field_ref.three_ref, f32[5,11,8,128]{3,2,1,0:T(8,128)S(1)} %collective-permute-done.5.bottom_ref, ...), custom_call_target="tpu_custom_call" | custom-call | tf_op jit(solution)/shard_map/pallas_call | solution.py:404
  70.8 0.0 copy-start.1
  70.8 5.8 %all-to-all-start.2 = ((f32[16,1,128]{2,1,0:T(1,128)}), f32[16,1,128]{2,1,0:T(1,128)S(1)}, u32[]{:S(2)}, u32[]{:S(2)}) async-start(f32[16,1,128]{2,1,0:T(1,128)} %get-tuple-element.25), calls=%async_computation.2 | async-start | bytes 16384 | tf_op jit(solution)/shard_map/all_to_all | solution.py:414
  76.6 0.0 copy-done.3
  76.6 3.3 %shard_map.73 = f32[16,128,128]{2,1,0:T(8,128)} custom-call(f32[128,128]{1,0:T(8,128)S(1)} %copy-done.3, f32[8,11,8,128]{3,2,1,0:T(8,128)S(1)} %get-tuple-element.18.one_ref, f32[8,11,8,128]{3,2,1,0:T(8,128)S(1)} %get-tuple-element.23.two_ref, f32[8,11,8,128]{3,2,1,0:T(8,128)S(1)} %get-tuple-element.20.field_ref.three_ref, ...), custom_call_target="tpu_custom_call" | custom-call | tf_op jit(solution)/shard_map/pallas_call | solution.py:409
  79.9 2.8 %all-to-all-done.2 = f32[16,1,128]{2,1,0:T(1,128)S(1)} async-done(((f32[16,1,128]{2,1,0:T(1,128)}), f32[16,1,128]{2,1,0:T(1,128)S(1)}, u32[]{:S(2)}, u32[]{:S(2)}) %all-to-all-start.2) | async-done | bytes 8224 | tf_op jit(solution)/shard_map/all_to_all | solution.py:414
  82.8 4.9 %all-to-all-start.1 = ((f32[16,128,128]{2,1,0:T(8,128)}), f32[16,128,128]{2,1,0:T(8,128)S(1)}, u32[]{:S(2)}, u32[]{:S(2)}) async-start(f32[16,128,128]{2,1,0:T(8,128)} %shard_map.73), calls=%async_computation.1 | async-start | bytes 2097152 | tf_op jit(solution)/shard_map/all_to_all | solution.py:415
  87.7 1.9 %collective-permute-start.6 = (f32[1,128]{1,0:T(1,128)S(1)}, f32[1,128]{1,0:T(1,128)S(1)}, u32[]{:S(2)}, u32[]{:S(2)}) collective-permute-start(f32[1,128]{1,0:T(1,128)S(1)} %bitcast.11), channel_id=1, source_target_pairs={{0,1},{1,0},{2,3},{3,2},{4,5},{5,4},{6,7},{7,6},{8,9},{9,8},{10,11... | collective-permute-start | bytes 1544 | tf_op jit(solution)/shard_map/ppermute | solution.py:419
  89.6 3.5 %collective-permute-done.6 = f32[1,128]{1,0:T(1,128)S(1)} collective-permute-done((f32[1,128]{1,0:T(1,128)S(1)}, f32[1,128]{1,0:T(1,128)S(1)}, u32[]{:S(2)}, u32[]{:S(2)}) %collective-permute-start.6) | collective-permute-done | bytes 544 | tf_op jit(solution)/shard_map/ppermute | solution.py:419
  93.1 1.9 %collective-permute-start.7 = (f32[1,128]{1,0:T(1,128)S(1)}, f32[1,128]{1,0:T(1,128)S(1)}, u32[]{:S(2)}, u32[]{:S(2)}) collective-permute-start(f32[1,128]{1,0:T(1,128)S(1)} %bitcast_add_fusion), channel_id=1, source_target_pairs={{0,2},{1,3},{2,0},{3,1},{4,6},{5,7},{6,4},{7,5},{8,10},{9,11},{10,... | collective-permute-start | bytes 1544 | tf_op jit(solution)/shard_map/ppermute | solution.py:419
  95.1 5.0 %collective-permute-done.7 = f32[1,128]{1,0:T(1,128)S(1)} collective-permute-done((f32[1,128]{1,0:T(1,128)S(1)}, f32[1,128]{1,0:T(1,128)S(1)}, u32[]{:S(2)}, u32[]{:S(2)}) %collective-permute-start.7) | collective-permute-done | bytes 544 | tf_op jit(solution)/shard_map/ppermute | solution.py:419
  100.1 1.9 %collective-permute-start.8 = (f32[1,128]{1,0:T(1,128)S(1)}, f32[1,128]{1,0:T(1,128)S(1)}, u32[]{:S(2)}, u32[]{:S(2)}) collective-permute-start(f32[1,128]{1,0:T(1,128)S(1)} %add.20), channel_id=1, source_target_pairs={{0,4},{1,5},{2,6},{3,7},{4,0},{5,1},{6,2},{7,3},{8,12},{9,13},{10,... | collective-permute-start | bytes 1544 | tf_op jit(solution)/shard_map/ppermute | solution.py:419
  102.0 3.5 %collective-permute-done.8 = f32[1,128]{1,0:T(1,128)S(1)} collective-permute-done((f32[1,128]{1,0:T(1,128)S(1)}, f32[1,128]{1,0:T(1,128)S(1)}, u32[]{:S(2)}, u32[]{:S(2)}) %collective-permute-start.8) | collective-permute-done | bytes 544 | tf_op jit(solution)/shard_map/ppermute | solution.py:419
  105.5 1.9 %collective-permute-start.9 = (f32[1,128]{1,0:T(1,128)S(1)}, f32[1,128]{1,0:T(1,128)S(1)}, u32[]{:S(2)}, u32[]{:S(2)}) collective-permute-start(f32[1,128]{1,0:T(1,128)S(1)} %add.21), channel_id=1, source_target_pairs={{0,8},{1,9},{2,10},{3,11},{4,12},{5,13},{6,14},{7,15},{8,0},{9,1},... | collective-permute-start | bytes 1544 | tf_op jit(solution)/shard_map/ppermute | solution.py:419
  107.4 4.4 %collective-permute-done.9 = f32[1,128]{1,0:T(1,128)S(1)} collective-permute-done((f32[1,128]{1,0:T(1,128)S(1)}, f32[1,128]{1,0:T(1,128)S(1)}, u32[]{:S(2)}, u32[]{:S(2)}) %collective-permute-start.9) | collective-permute-done | bytes 544 | tf_op jit(solution)/shard_map/ppermute | solution.py:419
  111.8 3.3 %collective-permute-start.10 = (f32[1,128]{1,0:T(1,128)S(1)}, f32[1,128]{1,0:T(1,128)S(1)}, u32[]{:S(2)}, u32[]{:S(2)}) collective-permute-start(f32[1,128]{1,0:T(1,128)S(1)} %add.22), channel_id=1, source_target_pairs={{0,16},{1,17},{2,18},{3,19},{4,20},{5,21},{6,22},{7,23},{8,24},{9,... | collective-permute-start | bytes 1544 | tf_op jit(solution)/shard_map/ppermute | solution.py:419
  115.1 6.1 %collective-permute-done.10 = f32[1,128]{1,0:T(1,128)S(1)} collective-permute-done((f32[1,128]{1,0:T(1,128)S(1)}, f32[1,128]{1,0:T(1,128)S(1)}, u32[]{:S(2)}, u32[]{:S(2)}) %collective-permute-start.10) | collective-permute-done | bytes 544 | tf_op jit(solution)/shard_map/ppermute | solution.py:419
  121.2 0.0 all-to-all-done.1.source_ref
  121.2 0.0 copy-done.1
  121.2 1.2 %shard_map.74 = (f32[64,1024]{1,0:T(8,128)}, f32[64,1024]{1,0:T(8,128)}) custom-call(f32[16,128,128]{2,1,0:T(8,128)S(1)} %all-to-all-done.1.source_ref, f32[64,1024]{1,0:T(8,128)S(1)} %bitcast.10, f32[1,128]{1,0:T(1,128)S(1)} %add.23.sums_ref), custom_call_target="tpu_custom_call" | custom-call | tf_op jit(solution)/shard_map/pallas_call | solution.py:422
  (7 shorter events, 0.1 us)
Async XLA Ops:
  0.6 1.0 copy-start
  1.6 51.4 %copy-start.4 = (f32[10,8,128]{2,1,0:T(8,128)S(1)}, f32[10,8,128]{2,1,0:T(8,128)}, u32[]{:S(2)}) copy-start(f32[10,8,128]{2,1,0:T(8,128)} %constant.19.clone.coef_ref) | copy-start | bytes 122884
  2.6 21.0 %all-to-all-start = ((f32[16,48,128]{2,1,0:T(8,128)}), f32[16,48,128]{2,1,0:T(8,128)S(1)}, u32[]{:S(2)}, u32[]{:S(2)}) async-start(f32[16,48,128]{2,1,0:T(8,128)} %shard_map.68), calls=%async_computation | async-start | bytes 786432 | tf_op jit(solution)/shard_map/all_to_all | solution.py:372
  23.6 0.8 copy-start.2
  25.0 27.9 %collective-permute-start = (f32[5,11,8,128]{3,2,1,0:T(8,128)S(1)}, f32[5,11,8,128]{3,2,1,0:T(8,128)S(1)}, u32[]{:S(2)}, u32[]{:S(2)}) collective-permute-start(f32[5,11,8,128]{3,2,1,0:T(8,128)S(1)} %get-tuple-element.15), channel_id=1, source_target_pairs={{0,1},{1,2},{2,3},{3,4},{4,5},{5,6},{6,7},{7,8},{8,9},{9,10},{10,1... | collective-permute-start | bytes 675848 | tf_op jit(solution)/shard_map/ppermute | solution.py:353
  26.9 26.0 %collective-permute-start.1 = (f32[5,11,8,128]{3,2,1,0:T(8,128)S(1)}, f32[5,11,8,128]{3,2,1,0:T(8,128)S(1)}, u32[]{:S(2)}, u32[]{:S(2)}) collective-permute-start(f32[5,11,8,128]{3,2,1,0:T(8,128)S(1)} %get-tuple-element.17), channel_id=1, source_target_pairs={{0,31},{1,0},{2,1},{3,2},{4,3},{5,4},{6,5},{7,6},{8,7},{9,8},{10,9... | collective-permute-start | bytes 675848 | tf_op jit(solution)/shard_map/ppermute | solution.py:353
  38.8 5.9 %collective-permute-start.3 = (f32[24,128]{1,0:T(8,128)S(1)}, f32[24,128]{1,0:T(8,128)S(1)}, u32[]{:S(2)}, u32[]{:S(2)}) collective-permute-start(f32[24,128]{1,0:T(8,128)S(1)} %constant_dynamic-slice_fusion.local_ref), channel_id=1, source_target_pairs={{0,31},{1,0},{2,1},{3,2},{4,3},{5,4},{6,5},{7,6},{8,7},{9,8},{10,9... | collective-permute-start | bytes 36872 | tf_op jit(solution)/shard_map/ppermute | solution.py:353
  42.8 8.9 %collective-permute-start.2 = (f32[24,128]{1,0:T(8,128)S(1)}, f32[24,128]{1,0:T(8,128)S(1)}, u32[]{:S(2)}, u32[]{:S(2)}) collective-permute-start(f32[24,128]{1,0:T(8,128)S(1)} %constant_dynamic-slice_fusion.local_ref), channel_id=1, source_target_pairs={{0,1},{1,2},{2,3},{3,4},{4,5},{5,6},{6,7},{7,8},{8,9},{9,10},{10,1... | collective-permute-start | bytes 36872 | tf_op jit(solution)/shard_map/ppermute | solution.py:353
  55.1 21.4 %copy-start.3 = (f32[128,128]{1,0:T(8,128)S(1)}, f32[128,128]{1,0:T(8,128)}, u32[]{:S(2)}) copy-start(f32[128,128]{1,0:T(8,128)} %constant.18.clone.cas_ref) | copy-start | bytes 196612
  55.2 11.3 %collective-permute-start.4 = (f32[5,11,8,128]{3,2,1,0:T(8,128)S(1)}, f32[5,11,8,128]{3,2,1,0:T(8,128)S(1)}, u32[]{:S(2)}, u32[]{:S(2)}) collective-permute-start(f32[5,11,8,128]{3,2,1,0:T(8,128)S(1)} %get-tuple-element.19), channel_id=1, source_target_pairs={{0,1},{1,2},{2,3},{3,4},{4,5},{5,6},{6,7},{7,8},{8,9},{9,10},{10,1... | collective-permute-start | bytes 675848 | tf_op jit(solution)/shard_map/ppermute | solution.py:353
  57.2 10.7 %collective-permute-start.5 = (f32[5,11,8,128]{3,2,1,0:T(8,128)S(1)}, f32[5,11,8,128]{3,2,1,0:T(8,128)S(1)}, u32[]{:S(2)}, u32[]{:S(2)}) collective-permute-start(f32[5,11,8,128]{3,2,1,0:T(8,128)S(1)} %get-tuple-element.21), channel_id=1, source_target_pairs={{0,31},{1,0},{2,1},{3,2},{4,3},{5,4},{6,5},{7,6},{8,7},{9,8},{10,9... | collective-permute-start | bytes 675848 | tf_op jit(solution)/shard_map/ppermute | solution.py:353
  70.8 50.3 %copy-start.1 = (f32[8,8,1024]{2,1,0:T(8,128)S(1)}, f32[8,8,1024]{2,1,0:T(8,128)}, u32[]{:S(2)}) copy-start(f32[8,8,1024]{2,1,0:T(8,128)} %param.5) | copy-start | bytes 786436
  70.8 11.9 %all-to-all-start.2 = ((f32[16,1,128]{2,1,0:T(1,128)}), f32[16,1,128]{2,1,0:T(1,128)S(1)}, u32[]{:S(2)}, u32[]{:S(2)}) async-start(f32[16,1,128]{2,1,0:T(1,128)} %get-tuple-element.25), calls=%async_computation.2 | async-start | bytes 16384 | tf_op jit(solution)/shard_map/all_to_all | solution.py:414
  82.8 38.4 %all-to-all-start.1 = ((f32[16,128,128]{2,1,0:T(8,128)}), f32[16,128,128]{2,1,0:T(8,128)S(1)}, u32[]{:S(2)}, u32[]{:S(2)}) async-start(f32[16,128,128]{2,1,0:T(8,128)} %shard_map.73), calls=%async_computation.1 | async-start | bytes 2097152 | tf_op jit(solution)/shard_map/all_to_all | solution.py:415
  87.7 5.4 %collective-permute-start.6 = (f32[1,128]{1,0:T(1,128)S(1)}, f32[1,128]{1,0:T(1,128)S(1)}, u32[]{:S(2)}, u32[]{:S(2)}) collective-permute-start(f32[1,128]{1,0:T(1,128)S(1)} %bitcast.11), channel_id=1, source_target_pairs={{0,1},{1,0},{2,3},{3,2},{4,5},{5,4},{6,7},{7,6},{8,9},{9,8},{10,11... | collective-permute-start | bytes 1544 | tf_op jit(solution)/shard_map/ppermute | solution.py:419
  93.1 6.9 %collective-permute-start.7 = (f32[1,128]{1,0:T(1,128)S(1)}, f32[1,128]{1,0:T(1,128)S(1)}, u32[]{:S(2)}, u32[]{:S(2)}) collective-permute-start(f32[1,128]{1,0:T(1,128)S(1)} %bitcast_add_fusion), channel_id=1, source_target_pairs={{0,2},{1,3},{2,0},{3,1},{4,6},{5,7},{6,4},{7,5},{8,10},{9,11},{10,... | collective-permute-start | bytes 1544 | tf_op jit(solution)/shard_map/ppermute | solution.py:419
  100.1 5.4 %collective-permute-start.8 = (f32[1,128]{1,0:T(1,128)S(1)}, f32[1,128]{1,0:T(1,128)S(1)}, u32[]{:S(2)}, u32[]{:S(2)}) collective-permute-start(f32[1,128]{1,0:T(1,128)S(1)} %add.20), channel_id=1, source_target_pairs={{0,4},{1,5},{2,6},{3,7},{4,0},{5,1},{6,2},{7,3},{8,12},{9,13},{10,... | collective-permute-start | bytes 1544 | tf_op jit(solution)/shard_map/ppermute | solution.py:419
  105.5 6.3 %collective-permute-start.9 = (f32[1,128]{1,0:T(1,128)S(1)}, f32[1,128]{1,0:T(1,128)S(1)}, u32[]{:S(2)}, u32[]{:S(2)}) collective-permute-start(f32[1,128]{1,0:T(1,128)S(1)} %add.21), channel_id=1, source_target_pairs={{0,8},{1,9},{2,10},{3,11},{4,12},{5,13},{6,14},{7,15},{8,0},{9,1},... | collective-permute-start | bytes 1544 | tf_op jit(solution)/shard_map/ppermute | solution.py:419
  111.8 9.3 %collective-permute-start.10 = (f32[1,128]{1,0:T(1,128)S(1)}, f32[1,128]{1,0:T(1,128)S(1)}, u32[]{:S(2)}, u32[]{:S(2)}) collective-permute-start(f32[1,128]{1,0:T(1,128)S(1)} %add.22), channel_id=1, source_target_pairs={{0,16},{1,17},{2,18},{3,19},{4,20},{5,21},{6,22},{7,23},{8,24},{9,... | collective-permute-start | bytes 1544 | tf_op jit(solution)/shard_map/ppermute | solution.py:419

commit v3 on v2

--- a/solution.py
+++ b/solution.py
@@ -21,6 +21,7 @@
 SIDE = 16
 BLOCK = 11
 WINDOW = SUB * BLOCK
+NEAR = 4
 PARAMS = pltpu.CompilerParams(vmem_limit_bytes=24 * 1024 * 1024)
 
 
@@ -401,9 +402,13 @@
     )(top, freq, bottom, wide, coef_table)
     top, bottom = exchange(low, high, spaces)
 
+    groups = [
+        [i * spaces + first + j for i in range(tiles) for j in range(NEAR)]
+        for first in range(0, spaces, NEAR)
+    ]
     solved_two, applied_two, sums = call(
         functools.partial(second_kernel, rows),
-        [tile_shape, tile_shape, (tiles, 1, LANES)],
+        [tile_shape, tile_shape, (tiles * NEAR, 1, LANES)],
         [*work, (2, SUB, LANES)],
     )(top, applied, bottom, wide, coef_table, early)
     packed = call(
@@ -411,9 +416,10 @@
         [(tiles, 2 * rows * times, LANES)],
         [(rows * 4 * span, LANES)],
     )(cas_table, solved, solved_two, applied, applied_two)
-    sums = jnp.sum(lax.all_to_all(sums, "tm", 0, 0), axis=0)
+    sums = lax.all_to_all(sums, ("tm", "space"), 0, 0, axis_index_groups=groups)
+    sums = jnp.sum(sums, axis=0)
     returned = lax.all_to_all(packed, "tm", 0, 0)
-    distance = 1
+    distance = NEAR
     while distance < spaces:
         pairs = [(i, i ^ distance) for i in range(spaces)]
         sums = sums + lax.ppermute(sums, "space", pairs)

time: 123 us -> 122 us (level)
  the two profiles are of different devices: /device:TPU:8 before, /device:TPU:1 now
where the time goes in v3:
time: 122 us; the launch traced here: 121 us
  starting transfers between devices  61.3 us (50%)
  waiting for transfers between devices  42.8 us (35%)
  Pallas kernels  12.5 us (10%)
  local copies, waits for them, and re-layouts  2.07 us (2%)
  other arithmetic  1.71 us (1%)
    ppermute x6, starting transfers between devices, exchange(): return (lax.ppermute(high, 'space', up), lax.ppermute(low, 'space', down))  27.2 us
    ppermute x3, starting transfers between devices, shards(): sums = sums + lax.ppermute(sums, 'space', pairs)  12.9 us
    all_to_all x1, waiting for transfers between devices, shards(): gathered = lax.all_to_all(windows, 'tm', 0, 0)  12.9 us
    all_to_all x1, starting transfers between devices, shards(): gathered = lax.all_to_all(windows, 'tm', 0, 0)  10.2 us
    all_to_all x1, waiting for transfers between devices, shards(): returned = lax.all_to_all(packed, 'tm', 0, 0)  9.63 us
    ppermute x6, waiting for transfers between devices, exchange(): return (lax.ppermute(high, 'space', up), lax.ppermute(low, 'space', down))  9.11 us
    all_to_all x1, starting transfers between devices, shards(): sums = lax.all_to_all(sums, ('tm', 'space'), 0, 0, axis_index_groups=groups)  6.6 us
    all_to_all x1, waiting for transfers between devices, shards(): sums = lax.all_to_all(sums, ('tm', 'space'), 0, 0, axis_index_groups=groups)  5.86 us
  transfers between devices with their start and end apart: 12, of which 9 were waited for; matrix products, arithmetic and copies ran while one was open for 2% of the time, Pallas kernels for 4%

profile of v3, /device:TPU:1, one launch (start us, length us, event | category | flops | bytes accessed | tf_op | source)
XLA Modules:
  0.0 121.2 jit_solution(15312020157768347088)
XLA Ops:
  0.6 0.0 copy-start
  0.6 0.9 copy-done
  1.6 0.0 copy-start.4
  1.6 1.0 shard_map.68
  2.6 10.2 %all-to-all-start = ((f32[16,48,128]{2,1,0:T(8,128)}), f32[16,48,128]{2,1,0:T(8,128)S(1)}, u32[]{:S(2)}, u32[]{:S(2)}) async-start(f32[16,48,128]{2,1,0:T(8,128)} %shard_map.68), calls=%async_computation | async-start | bytes 786432 | tf_op jit(solution)/shard_map/all_to_all | solution.py:373
  12.8 0.8 convert_multiply_fusion
  13.7 0.8 pad_maximum_fusion
  14.5 12.9 %all-to-all-done.field_ref = f32[16,48,128]{2,1,0:T(8,128)S(1)} async-done(((f32[16,48,128]{2,1,0:T(8,128)}), f32[16,48,128]{2,1,0:T(8,128)S(1)}, u32[]{:S(2)}, u32[]{:S(2)}) %all-to-all-start) | async-done | bytes 393248 | tf_op jit(solution)/shard_map/all_to_all | solution.py:373
  27.4 0.0 copy-start.2
  27.4 0.8 copy-done.2
  28.2 0.6 shard_map.69
  28.8 1.9 %collective-permute-start = (f32[5,11,8,128]{3,2,1,0:T(8,128)S(1)}, f32[5,11,8,128]{3,2,1,0:T(8,128)S(1)}, u32[]{:S(2)}, u32[]{:S(2)}) collective-permute-start(f32[5,11,8,128]{3,2,1,0:T(8,128)S(1)} %get-tuple-element.15), channel_id=1, source_target_pairs={{0,1},{1,2},{2,3},{3,4},{4,5},{5,6},{6,7},{7,8},{8,9},{9,10},{10,1... | collective-permute-start | bytes 675848 | tf_op jit(solution)/shard_map/ppermute | solution.py:354
  30.8 11.3 %collective-permute-start.1 = (f32[5,11,8,128]{3,2,1,0:T(8,128)S(1)}, f32[5,11,8,128]{3,2,1,0:T(8,128)S(1)}, u32[]{:S(2)}, u32[]{:S(2)}) collective-permute-start(f32[5,11,8,128]{3,2,1,0:T(8,128)S(1)} %get-tuple-element.17), channel_id=1, source_target_pairs={{0,31},{1,0},{2,1},{3,2},{4,3},{5,4},{6,5},{7,6},{8,7},{9,8},{10,9... | collective-permute-start | bytes 675848 | tf_op jit(solution)/shard_map/ppermute | solution.py:354
  42.0 0.1 fusion
  42.1 0.1 concatenate.7
  42.2 0.1 constant_dynamic-slice_fusion.local_ref
  42.3 3.4 %collective-permute-start.3 = (f32[24,128]{1,0:T(8,128)S(1)}, f32[24,128]{1,0:T(8,128)S(1)}, u32[]{:S(2)}, u32[]{:S(2)}) collective-permute-start(f32[24,128]{1,0:T(8,128)S(1)} %constant_dynamic-slice_fusion.local_ref), channel_id=1, source_target_pairs={{0,31},{1,0},{2,1},{3,2},{4,3},{5,4},{6,5},{7,6},{8,7},{9,8},{10,9... | collective-permute-start | bytes 36872 | tf_op jit(solution)/shard_map/ppermute | solution.py:354
  45.7 1.9 %collective-permute-start.2 = (f32[24,128]{1,0:T(8,128)S(1)}, f32[24,128]{1,0:T(8,128)S(1)}, u32[]{:S(2)}, u32[]{:S(2)}) collective-permute-start(f32[24,128]{1,0:T(8,128)S(1)} %constant_dynamic-slice_fusion.local_ref), channel_id=1, source_target_pairs={{0,1},{1,2},{2,3},{3,4},{4,5},{5,6},{6,7},{7,8},{8,9},{9,10},{10,1... | collective-permute-start | bytes 36872 | tf_op jit(solution)/shard_map/ppermute | solution.py:354
  47.6 0.0 collective-permute-done.3.bottom_ref
  47.6 5.8 %collective-permute-done.2.top_ref = f32[24,128]{1,0:T(8,128)S(1)} collective-permute-done((f32[24,128]{1,0:T(8,128)S(1)}, f32[24,128]{1,0:T(8,128)S(1)}, u32[]{:S(2)}, u32[]{:S(2)}) %collective-permute-start.2) | collective-permute-done | bytes 12320 | tf_op jit(solution)/shard_map/ppermute | solution.py:354
  53.4 1.2 %shard_map.70.wide_ref = f32[18,33,8,128]{3,2,1,0:T(8,128)S(1)} custom-call(f32[24,128]{1,0:T(8,128)S(1)} %constant_dynamic-slice_fusion.local_ref, f32[24,128]{1,0:T(8,128)S(1)} %collective-permute-done.2.top_ref, f32[24,128]{1,0:T(8,128)S(1)} %collective-permute-done.3.bottom_ref), custom_call_target="tpu_custom_call" | custom-call | tf_op jit(solution)/shard_map/pallas_call | solution.py:381
  54.7 0.0 collective-permute-done.top_ref
  54.7 0.0 collective-permute-done.1.bottom_ref
  54.7 0.0 copy-done.4
  54.7 2.2 %shard_map.71 = (f32[8,11,8,128]{3,2,1,0:T(8,128)S(1)}, f32[8,11,8,128]{3,2,1,0:T(8,128)S(1)}, f32[5,11,8,128]{3,2,1,0:T(8,128)S(1)}, f32[5,11,8,128]{3,2,1,0:T(8,128)S(1)}, f32[2,8,128]{2,1,0:T(8,128)S(1)}) custom-call(f32[5,11,8,128]{3,2,1,0:T(8,128)S(1)} %collective-permute-done.top_ref, f32[8,11,8,128]{3,2,1,0:T(8,128)S(1)} %get-tuple-element.16.field_ref, ...), custom_call_target="tpu_custom_call" | custom-call | tf_op jit(solution)/shard_map/pallas_call | solution.py:398
  56.9 0.0 copy-start.3
  56.9 2.1 %collective-permute-start.4 = (f32[5,11,8,128]{3,2,1,0:T(8,128)S(1)}, f32[5,11,8,128]{3,2,1,0:T(8,128)S(1)}, u32[]{:S(2)}, u32[]{:S(2)}) collective-permute-start(f32[5,11,8,128]{3,2,1,0:T(8,128)S(1)} %get-tuple-element.19), channel_id=1, source_target_pairs={{0,1},{1,2},{2,3},{3,4},{4,5},{5,6},{6,7},{7,8},{8,9},{9,10},{10,1... | collective-permute-start | bytes 675848 | tf_op jit(solution)/shard_map/ppermute | solution.py:354
  59.0 6.7 %collective-permute-start.5 = (f32[5,11,8,128]{3,2,1,0:T(8,128)S(1)}, f32[5,11,8,128]{3,2,1,0:T(8,128)S(1)}, u32[]{:S(2)}, u32[]{:S(2)}) collective-permute-start(f32[5,11,8,128]{3,2,1,0:T(8,128)S(1)} %get-tuple-element.21), channel_id=1, source_target_pairs={{0,31},{1,0},{2,1},{3,2},{4,3},{5,4},{6,5},{7,6},{8,7},{9,8},{10,9... | collective-permute-start | bytes 675848 | tf_op jit(solution)/shard_map/ppermute | solution.py:354
  65.6 2.4 %collective-permute-done.4.top_ref = f32[5,11,8,128]{3,2,1,0:T(8,128)S(1)} collective-permute-done((f32[5,11,8,128]{3,2,1,0:T(8,128)S(1)}, f32[5,11,8,128]{3,2,1,0:T(8,128)S(1)}, u32[]{:S(2)}, u32[]{:S(2)}) %collective-permute-start.4) | collective-permute-done | bytes 225312 | tf_op jit(solution)/shard_map/ppermute | solution.py:354
  68.0 0.9 collective-permute-done.5.bottom_ref
  68.9 2.9 %shard_map.72 = (f32[8,11,8,128]{3,2,1,0:T(8,128)S(1)}, f32[8,11,8,128]{3,2,1,0:T(8,128)S(1)}, f32[64,1,128]{2,1,0:T(1,128)}) custom-call(f32[5,11,8,128]{3,2,1,0:T(8,128)S(1)} %collective-permute-done.4.top_ref, f32[8,11,8,128]{3,2,1,0:T(8,128)S(1)} %get-tuple-element.20.field_ref.three_ref, f32[5,11,8,128]{3,2,1,0:T(8,128)S(1)} %collective-permute-done.5.bottom_ref, ...), custom_call_target="tpu_custom_call" | custom-call | tf_op jit(solution)/shard_map/pallas_call | solution.py:409
  71.8 0.0 copy-start.1
  71.8 6.6 %all-to-all-start.2 = ((f32[64,1,128]{2,1,0:T(1,128)}), f32[64,1,128]{2,1,0:T(1,128)S(1)}, u32[]{:S(2)}, u32[]{:S(2)}) async-start(f32[64,1,128]{2,1,0:T(1,128)} %get-tuple-element.25), calls=%async_computation.2 | async-start | bytes 65536 | tf_op jit(solution)/shard_map/all_to_all | solution.py:419
  78.4 0.0 copy-done.3
  78.5 3.3 %shard_map.73 = f32[16,128,128]{2,1,0:T(8,128)} custom-call(f32[128,128]{1,0:T(8,128)S(1)} %copy-done.3, f32[8,11,8,128]{3,2,1,0:T(8,128)S(1)} %get-tuple-element.18.one_ref, f32[8,11,8,128]{3,2,1,0:T(8,128)S(1)} %get-tuple-element.23.two_ref, f32[8,11,8,128]{3,2,1,0:T(8,128)S(1)} %get-tuple-element.20.field_ref.three_ref, ...), custom_call_target="tpu_custom_call" | custom-call | tf_op jit(solution)/shard_map/pallas_call | solution.py:414
  81.8 5.9 %all-to-all-done.2 = f32[64,1,128]{2,1,0:T(1,128)S(1)} async-done(((f32[64,1,128]{2,1,0:T(1,128)}), f32[64,1,128]{2,1,0:T(1,128)S(1)}, u32[]{:S(2)}, u32[]{:S(2)}) %all-to-all-start.2) | async-done | bytes 32800 | tf_op jit(solution)/shard_map/all_to_all | solution.py:419
  87.7 4.3 %all-to-all-start.1 = ((f32[16,128,128]{2,1,0:T(8,128)}), f32[16,128,128]{2,1,0:T(8,128)S(1)}, u32[]{:S(2)}, u32[]{:S(2)}) async-start(f32[16,128,128]{2,1,0:T(8,128)} %shard_map.73), calls=%async_computation.1 | async-start | bytes 2097152 | tf_op jit(solution)/shard_map/all_to_all | solution.py:421
  92.0 0.1 reduce_sum.11
  92.1 1.9 %collective-permute-start.6 = (f32[1,128]{1,0:T(1,128)S(1)}, f32[1,128]{1,0:T(1,128)S(1)}, u32[]{:S(2)}, u32[]{:S(2)}) collective-permute-start(f32[1,128]{1,0:T(1,128)S(1)} %bitcast.11), channel_id=1, source_target_pairs={{0,4},{1,5},{2,6},{3,7},{4,0},{5,1},{6,2},{7,3},{8,12},{9,13},{10,... | collective-permute-start | bytes 1544 | tf_op jit(solution)/shard_map/ppermute | solution.py:425
  94.0 2.4 %collective-permute-done.6 = f32[1,128]{1,0:T(1,128)S(1)} collective-permute-done((f32[1,128]{1,0:T(1,128)S(1)}, f32[1,128]{1,0:T(1,128)S(1)}, u32[]{:S(2)}, u32[]{:S(2)}) %collective-permute-start.6) | collective-permute-done | bytes 544 | tf_op jit(solution)/shard_map/ppermute | solution.py:425
  96.4 4.6 %collective-permute-start.7 = (f32[1,128]{1,0:T(1,128)S(1)}, f32[1,128]{1,0:T(1,128)S(1)}, u32[]{:S(2)}, u32[]{:S(2)}) collective-permute-start(f32[1,128]{1,0:T(1,128)S(1)} %bitcast_add_fusion), channel_id=1, source_target_pairs={{0,8},{1,9},{2,10},{3,11},{4,12},{5,13},{6,14},{7,15},{8,0},{9,1},... | collective-permute-start | bytes 1544 | tf_op jit(solution)/shard_map/ppermute | solution.py:425
  100.9 1.2 collective-permute-done.7
  102.2 6.4 %collective-permute-start.8 = (f32[1,128]{1,0:T(1,128)S(1)}, f32[1,128]{1,0:T(1,128)S(1)}, u32[]{:S(2)}, u32[]{:S(2)}) collective-permute-start(f32[1,128]{1,0:T(1,128)S(1)} %add.14), channel_id=1, source_target_pairs={{0,16},{1,17},{2,18},{3,19},{4,20},{5,21},{6,22},{7,23},{8,24},{9,... | collective-permute-start | bytes 1544 | tf_op jit(solution)/shard_map/ppermute | solution.py:425
  108.6 1.7 %collective-permute-done.8 = f32[1,128]{1,0:T(1,128)S(1)} collective-permute-done((f32[1,128]{1,0:T(1,128)S(1)}, f32[1,128]{1,0:T(1,128)S(1)}, u32[]{:S(2)}, u32[]{:S(2)}) %collective-permute-start.8) | collective-permute-done | bytes 544 | tf_op jit(solution)/shard_map/ppermute | solution.py:425
  110.3 9.6 %all-to-all-done.1.source_ref = f32[16,128,128]{2,1,0:T(8,128)S(1)} async-done(((f32[16,128,128]{2,1,0:T(8,128)}), f32[16,128,128]{2,1,0:T(8,128)S(1)}, u32[]{:S(2)}, u32[]{:S(2)}) %all-to-all-start.1) | async-done | bytes 1048608 | tf_op jit(solution)/shard_map/all_to_all | solution.py:421
  120.0 0.0 copy-done.1
  120.0 1.2 %shard_map.74 = (f32[64,1024]{1,0:T(8,128)}, f32[64,1024]{1,0:T(8,128)}) custom-call(f32[16,128,128]{2,1,0:T(8,128)S(1)} %all-to-all-done.1.source_ref, f32[64,1024]{1,0:T(8,128)S(1)} %bitcast.10, f32[1,128]{1,0:T(1,128)S(1)} %add.15.sums_ref), custom_call_target="tpu_custom_call" | custom-call | tf_op jit(solution)/shard_map/pallas_call | solution.py:428
  (4 shorter events, 0.0 us)
Async XLA Ops:
  0.6 1.0 copy-start
  1.6 53.1 %copy-start.4 = (f32[10,8,128]{2,1,0:T(8,128)S(1)}, f32[10,8,128]{2,1,0:T(8,128)}, u32[]{:S(2)}) copy-start(f32[10,8,128]{2,1,0:T(8,128)} %constant.19.clone.coef_ref) | copy-start | bytes 122884
  2.6 24.8 %all-to-all-start = ((f32[16,48,128]{2,1,0:T(8,128)}), f32[16,48,128]{2,1,0:T(8,128)S(1)}, u32[]{:S(2)}, u32[]{:S(2)}) async-start(f32[16,48,128]{2,1,0:T(8,128)} %shard_map.68), calls=%async_computation | async-start | bytes 786432 | tf_op jit(solution)/shard_map/all_to_all | solution.py:373
  27.4 0.8 copy-start.2
  28.8 25.8 %collective-permute-start = (f32[5,11,8,128]{3,2,1,0:T(8,128)S(1)}, f32[5,11,8,128]{3,2,1,0:T(8,128)S(1)}, u32[]{:S(2)}, u32[]{:S(2)}) collective-permute-start(f32[5,11,8,128]{3,2,1,0:T(8,128)S(1)} %get-tuple-element.15), channel_id=1, source_target_pairs={{0,1},{1,2},{2,3},{3,4},{4,5},{5,6},{6,7},{7,8},{8,9},{9,10},{10,1... | collective-permute-start | bytes 675848 | tf_op jit(solution)/shard_map/ppermute | solution.py:354
  30.8 23.9 %collective-permute-start.1 = (f32[5,11,8,128]{3,2,1,0:T(8,128)S(1)}, f32[5,11,8,128]{3,2,1,0:T(8,128)S(1)}, u32[]{:S(2)}, u32[]{:S(2)}) collective-permute-start(f32[5,11,8,128]{3,2,1,0:T(8,128)S(1)} %get-tuple-element.17), channel_id=1, source_target_pairs={{0,31},{1,0},{2,1},{3,2},{4,3},{5,4},{6,5},{7,6},{8,7},{9,8},{10,9... | collective-permute-start | bytes 675848 | tf_op jit(solution)/shard_map/ppermute | solution.py:354
  42.3 5.3 %collective-permute-start.3 = (f32[24,128]{1,0:T(8,128)S(1)}, f32[24,128]{1,0:T(8,128)S(1)}, u32[]{:S(2)}, u32[]{:S(2)}) collective-permute-start(f32[24,128]{1,0:T(8,128)S(1)} %constant_dynamic-slice_fusion.local_ref), channel_id=1, source_target_pairs={{0,31},{1,0},{2,1},{3,2},{4,3},{5,4},{6,5},{7,6},{8,7},{9,8},{10,9... | collective-permute-start | bytes 36872 | tf_op jit(solution)/shard_map/ppermute | solution.py:354
  45.7 7.8 %collective-permute-start.2 = (f32[24,128]{1,0:T(8,128)S(1)}, f32[24,128]{1,0:T(8,128)S(1)}, u32[]{:S(2)}, u32[]{:S(2)}) collective-permute-start(f32[24,128]{1,0:T(8,128)S(1)} %constant_dynamic-slice_fusion.local_ref), channel_id=1, source_target_pairs={{0,1},{1,2},{2,3},{3,4},{4,5},{5,6},{6,7},{7,8},{8,9},{9,10},{10,1... | collective-permute-start | bytes 36872 | tf_op jit(solution)/shard_map/ppermute | solution.py:354
  56.9 21.6 %copy-start.3 = (f32[128,128]{1,0:T(8,128)S(1)}, f32[128,128]{1,0:T(8,128)}, u32[]{:S(2)}) copy-start(f32[128,128]{1,0:T(8,128)} %constant.18.clone.cas_ref) | copy-start | bytes 196612
  56.9 11.1 %collective-permute-start.4 = (f32[5,11,8,128]{3,2,1,0:T(8,128)S(1)}, f32[5,11,8,128]{3,2,1,0:T(8,128)S(1)}, u32[]{:S(2)}, u32[]{:S(2)}) collective-permute-start(f32[5,11,8,128]{3,2,1,0:T(8,128)S(1)} %get-tuple-element.19), channel_id=1, source_target_pairs={{0,1},{1,2},{2,3},{3,4},{4,5},{5,6},{6,7},{7,8},{8,9},{9,10},{10,1... | collective-permute-start | bytes 675848 | tf_op jit(solution)/shard_map/ppermute | solution.py:354
  59.0 10.0 %collective-permute-start.5 = (f32[5,11,8,128]{3,2,1,0:T(8,128)S(1)}, f32[5,11,8,128]{3,2,1,0:T(8,128)S(1)}, u32[]{:S(2)}, u32[]{:S(2)}) collective-permute-start(f32[5,11,8,128]{3,2,1,0:T(8,128)S(1)} %get-tuple-element.21), channel_id=1, source_target_pairs={{0,31},{1,0},{2,1},{3,2},{4,3},{5,4},{6,5},{7,6},{8,7},{9,8},{10,9... | collective-permute-start | bytes 675848 | tf_op jit(solution)/shard_map/ppermute | solution.py:354
  71.8 48.1 %copy-start.1 = (f32[8,8,1024]{2,1,0:T(8,128)S(1)}, f32[8,8,1024]{2,1,0:T(8,128)}, u32[]{:S(2)}) copy-start(f32[8,8,1024]{2,1,0:T(8,128)} %param.5) | copy-start | bytes 786436
  71.8 15.8 %all-to-all-start.2 = ((f32[64,1,128]{2,1,0:T(1,128)}), f32[64,1,128]{2,1,0:T(1,128)S(1)}, u32[]{:S(2)}, u32[]{:S(2)}) async-start(f32[64,1,128]{2,1,0:T(1,128)} %get-tuple-element.25), calls=%async_computation.2 | async-start | bytes 65536 | tf_op jit(solution)/shard_map/all_to_all | solution.py:419
  87.7 32.3 %all-to-all-start.1 = ((f32[16,128,128]{2,1,0:T(8,128)}), f32[16,128,128]{2,1,0:T(8,128)S(1)}, u32[]{:S(2)}, u32[]{:S(2)}) async-start(f32[16,128,128]{2,1,0:T(8,128)} %shard_map.73), calls=%async_computation.1 | async-start | bytes 2097152 | tf_op jit(solution)/shard_map/all_to_all | solution.py:421
  92.1 4.3 %collective-permute-start.6 = (f32[1,128]{1,0:T(1,128)S(1)}, f32[1,128]{1,0:T(1,128)S(1)}, u32[]{:S(2)}, u32[]{:S(2)}) collective-permute-start(f32[1,128]{1,0:T(1,128)S(1)} %bitcast.11), channel_id=1, source_target_pairs={{0,4},{1,5},{2,6},{3,7},{4,0},{5,1},{6,2},{7,3},{8,12},{9,13},{10,... | collective-permute-start | bytes 1544 | tf_op jit(solution)/shard_map/ppermute | solution.py:425
  96.4 5.8 %collective-permute-start.7 = (f32[1,128]{1,0:T(1,128)S(1)}, f32[1,128]{1,0:T(1,128)S(1)}, u32[]{:S(2)}, u32[]{:S(2)}) collective-permute-start(f32[1,128]{1,0:T(1,128)S(1)} %bitcast_add_fusion), channel_id=1, source_target_pairs={{0,8},{1,9},{2,10},{3,11},{4,12},{5,13},{6,14},{7,15},{8,0},{9,1},... | collective-permute-start | bytes 1544 | tf_op jit(solution)/shard_map/ppermute | solution.py:425
  102.2 8.2 %collective-permute-start.8 = (f32[1,128]{1,0:T(1,128)S(1)}, f32[1,128]{1,0:T(1,128)S(1)}, u32[]{:S(2)}, u32[]{:S(2)}) collective-permute-start(f32[1,128]{1,0:T(1,128)S(1)} %add.14), channel_id=1, source_target_pairs={{0,16},{1,17},{2,18},{3,19},{4,20},{5,21},{6,22},{7,23},{8,24},{9,... | collective-permute-start | bytes 1544 | tf_op jit(solution)/shard_map/ppermute | solution.py:425

commit v4 on v3

--- a/solution.py
+++ b/solution.py
@@ -18,6 +18,7 @@
 LANES = 128
 SUB = 8
 HALO = CHEB + 1
+FAR = 2
 SIDE = 16
 BLOCK = 11
 WINDOW = SUB * BLOCK
@@ -107,7 +108,10 @@
             out_ref[2 * part + 1, start : start + times, :] = odd[part]
 
 
-def forward_kernel(rows, times, length, cas_ref, field_ref, out_ref, low_ref, high_ref, line_ref):
+def forward_kernel(
+    rows, times, length, cas_ref, field_ref, *refs
+):
+    out_ref, low_ref, high_ref, line_ref = refs[-4:]
     half = LANES // 2
     span = half + 2 * SIDE
     pieces = field_ref.shape[1] // times
@@ -132,29 +136,33 @@
         for column in range(BLOCK):
             value = line_ref[pl.ds(row * span + skip + column, SUB, stride=BLOCK), :]
             out_ref[row, column] = value
-            if row < HALO:
+            if row < FAR:
                 low_ref[row, column] = value
-            if row >= rows - HALO:
-                high_ref[row - (rows - HALO), column] = value
-
-
-def weight_kernel(rows, local_ref, top_ref, bottom_ref, wide_ref, scratch_ref):
+            if row >= rows - FAR:
+                high_ref[row - (rows - FAR), column] = value
+
+
+def weight_kernel(
+    rows, local_ref, top_ref, bottom_ref, top_far_ref, bottom_far_ref, wide_ref, scratch_ref
+):
     planes = []
     for plane in range(3):
         start = plane * rows
         planes.append(
             jnp.concatenate(
                 [
-                    top_ref[start + rows - HALO : start + rows, :],
+                    top_far_ref[start + rows - FAR : start + rows, :],
+                    top_ref[start : start + rows, :],
                     local_ref[start : start + rows, :],
-                    bottom_ref[start : start + HALO, :],
+                    bottom_ref[start : start + rows, :],
+                    bottom_far_ref[start : start + FAR, :],
                 ],
                 axis=0,
             )
         )
     east = 1.0 + 0.125 * (planes[1] + jnp.concatenate([planes[1][1:], planes[1][:1]], axis=0))
     north = 1.0 + 0.125 * (planes[2] + pltpu.roll(planes[2], LANES - 1, 1))
-    total = rows + 2 * HALO
+    total = planes[0].shape[0]
     zero = jnp.zeros((LANES - 3 * total, LANES), jnp.float32)
     scratch_ref[...] = jnp.transpose(jnp.concatenate([planes[0], east, north, zero], axis=0))
     skip = (LANES - WINDOW) // 2
@@ -174,40 +182,25 @@
     return (place >= first) & (place < first + LANES // 2)
 
 
-def passes(
-    rows, top_ref, field_ref, bottom_ref, wide_ref, coef_ref, step_ref, remain_ref, solved_ref, emit
-):
-    total = rows + 2 * HALO
+def passes(edge, own, sources, wide_ref, coef_ref, step_ref, remain_ref, solved_ref, emit):
+    total = step_ref.shape[0]
     columns = range(BLOCK)
 
-    def begin(source_ref, offset, count):
-        scale = coef_ref[1]
-
-        @pl.loop(0, count)
-        def _(row):
-            for column in columns:
-                value = source_ref[row, column]
-                remain_ref[offset + row, column] = value
-                step_ref[offset + row, column] = scale * value
-
-    begin(top_ref, 0, HALO)
-    begin(field_ref, HALO, rows)
-    begin(bottom_ref, HALO + rows, HALO)
-
     for turn in range(CHEB + 1):
-        first, last = turn + 1, total - turn - 1
-        shift = coef_ref[0]
-
-        def row_step(row, carry, *, turn=turn, inside=False, shift=shift):
+        first, last = edge + turn + 1, total - edge - turn - 1
+
+        def row_step(row, carry, *, turn, place):
             here, flux = carry[:BLOCK], carry[BLOCK:]
             after = [step_ref[row + 1, column] for column in columns]
             ahead = [wide_ref[row, BLOCK + column] * (here[column] - after[column]) for column in columns]
             beside = list(here[1:]) + [pltpu.roll(here[0], SUB - 1, 0)]
             side = [wide_ref[row, 2 * BLOCK + column] * (here[column] - beside[column]) for column in columns]
             behind = [pltpu.roll(side[-1], 1, 0)] + side[:-1]
+            inside = place == 1
+            results = []
             for column in columns:
                 applied = (
-                    (wide_ref[row, column] + shift) * here[column]
+                    (wide_ref[row, column] + coef_ref[0]) * here[column]
                     + (ahead[column] - flux[column])
                     + (side[column] - behind[column])
                 )
@@ -217,15 +210,16 @@
                     step_ref[row, column] = (
                         coef_ref[2 + 2 * turn] * here[column] + coef_ref[3 + 2 * turn] * left
                     )
-                if inside:
-                    own = row - HALO
-                    if turn == 0:
-                        solved_ref[own, column] = here[column]
-                    elif turn < CHEB:
-                        solved_ref[own, column] = solved_ref[own, column] + here[column]
-                    else:
-                        source = field_ref[own, column]
-                        emit(own, column, source, solved_ref[own, column] + here[column], source - left)
+                solved = here[column]
+                if inside and turn > 0:
+                    solved = solved_ref[row - own[0], column] + solved
+                if inside and turn < CHEB:
+                    solved_ref[row - own[0], column] = solved
+                if turn == CHEB:
+                    source = sources[place](row, column)
+                    results.append((source, solved, source - left))
+            if turn == CHEB:
+                emit(row, inside, *zip(*results))
             return (*after, *ahead)
 
         here = [step_ref[first, column] for column in columns]
@@ -234,56 +228,72 @@
             for column in columns
         ]
         carry = (*here, *flux)
-        if first < HALO:
-            carry = lax.fori_loop(first, HALO, row_step, carry)
-        carry = lax.fori_loop(HALO, HALO + rows, functools.partial(row_step, inside=True), carry)
-        if HALO + rows < last:
-            lax.fori_loop(HALO + rows, last, row_step, carry)
-
-
-def first_kernel(
-    rows, top_ref, field_ref, bottom_ref, wide_ref, coef_ref,
-    solved_ref, applied_ref, low_ref, high_ref, sums_ref, step_ref, remain_ref, part_ref,
+        for place, (low, high) in enumerate(((first, own[0]), own, (own[1], last))):
+            if low < high:
+                step = functools.partial(row_step, turn=turn, place=place)
+                carry = lax.fori_loop(low, high, step, carry)
+
+
+def stencil_kernel(
+    rows, top_far_ref, top_ref, field_ref, bottom_ref, bottom_far_ref, wide_ref, coef_ref,
+    solved_ref, applied_ref, solved_two_ref, applied_two_ref, sums_ref,
+    step_ref, remain_ref, part_ref, line_ref,
 ):
-    sums_ref[...] = jnp.zeros_like(sums_ref)
-
-    def emit(row, column, source, solved, applied):
-        solved_ref[row, column] = solved
-        applied_ref[row, column] = applied
-        inside = jnp.where(own_columns(column), solved, 0.0)
-        sums_ref[0] = sums_ref[0] + source * inside
-        sums_ref[1] = sums_ref[1] + applied * inside
-
-    passes(
-        rows, top_ref, field_ref, bottom_ref, wide_ref, coef_ref, step_ref, remain_ref, part_ref, emit
+    columns = range(BLOCK)
+    offset = 0
+    for ref in (top_far_ref, top_ref, field_ref, bottom_ref, bottom_far_ref):
+
+        @pl.loop(0, ref.shape[0])
+        def _(row, ref=ref, offset=offset):
+            for column in columns:
+                value = ref[row, column]
+                remain_ref[offset + row, column] = value
+                step_ref[offset + row, column] = coef_ref[1] * value
+
+        offset += ref.shape[0]
+
+    own = (FAR + rows, FAR + 2 * rows)
+    line_ref[...] = jnp.zeros_like(line_ref)
+
+    def add(index, one, two):
+        total = None
+        for column in columns:
+            product = jnp.where(own_columns(column), one[column] * two[column], 0.0)
+            total = product if total is None else total + product
+        line_ref[index] = line_ref[index] + total
+
+    def emit_first(row, inside, source, solved, applied):
+        for column in columns:
+            remain_ref[row, column] = applied[column]
+            step_ref[row, column] = coef_ref[1] * applied[column]
+        if inside:
+            for column in columns:
+                solved_ref[row - own[0], column] = solved[column]
+                applied_ref[row - own[0], column] = applied[column]
+            add(0, source, solved)
+            add(1, solved, applied)
+
+    def emit_second(row, inside, source, solved, applied):
+        for column in columns:
+            solved_two_ref[row - own[0], column] = solved[column]
+            applied_two_ref[row - own[0], column] = applied[column]
+        add(2, source, solved)
+        add(3, solved, applied)
+
+    work = (wide_ref, coef_ref, step_ref, remain_ref, part_ref)
+    sources = (
+        lambda row, column: top_ref[row - FAR, column],
+        lambda row, column: field_ref[row - own[0], column],
+        lambda row, column: bottom_ref[row - own[1], column],
     )
-    for row in range(HALO):
-        for column in range(BLOCK):
-            low_ref[row, column] = applied_ref[row, column]
-            high_ref[row, column] = applied_ref[rows - HALO + row, column]
-
-
-def second_kernel(
-    rows, top_ref, field_ref, bottom_ref, wide_ref, coef_ref, early_ref,
-    solved_ref, applied_ref, sums_ref, step_ref, remain_ref, part_ref, late_ref,
-):
-    late_ref[...] = jnp.zeros_like(late_ref)
-
-    def emit(row, column, source, solved, applied):
-        solved_ref[row, column] = solved
-        applied_ref[row, column] = applied
-        inside = jnp.where(own_columns(column), solved, 0.0)
-        late_ref[0] = late_ref[0] + source * inside
-        late_ref[1] = late_ref[1] + applied * inside
-
-    passes(
-        rows, top_ref, field_ref, bottom_ref, wide_ref, coef_ref, step_ref, remain_ref, part_ref, emit
-    )
-    values = [jnp.sum(ref[index]) for ref in (early_ref, late_ref) for index in range(2)]
+    passes(0, own, sources, *work, emit_first)
+    sources = (None, lambda row, column: applied_ref[row - own[0], column], None)
+    passes(HALO, own, sources, *work, emit_second)
+
     lane = lane_index((1, LANES))
     line = jnp.zeros((1, LANES), jnp.float32)
-    for index, value in enumerate(values):
-        line = jnp.where(lane == index, value, line)
+    for index in range(4):
+        line = jnp.where(lane == index, jnp.sum(line_ref[index]), line)
     sums_ref[...] = jnp.broadcast_to(line[None], sums_ref.shape)
 
 
@@ -338,20 +348,23 @@
             residual_ref[place, columns] = field_ref[place, columns] - merged[1]
 
 
-def call(kernel, out_shape, scratch=()):
+def call(kernel, out_shape, scratch=(), unread=0, inputs=0):
     shapes = [jax.ShapeDtypeStruct(shape, jnp.float32) for shape in out_shape]
+    specs = {}
+    if unread:
+        whole = pl.BlockSpec(memory_space=pltpu.VMEM)
+        specs["in_specs"] = [whole] * (inputs - unread) + [pl.BlockSpec(memory_space=pl.ANY)] * unread
     return pl.pallas_call(
         kernel,
         out_shape=shapes[0] if len(shapes) == 1 else shapes,
         scratch_shapes=[pltpu.VMEM(shape, jnp.float32) for shape in scratch],
         compiler_params=PARAMS,
+        **specs,
     )
 
 
-def exchange(low, high, spaces):
-    up = [(i, (i + 1) % spaces) for i in range(spaces)]
-    down = [(i, (i - 1) % spaces) for i in range(spaces)]
-    return lax.ppermute(high, "space", up), lax.ppermute(low, "space", down)
+def shift(value, distance, spaces):
+    return lax.ppermute(value, "space", [(i, (i + distance) % spaces) for i in range(spaces)])
 
 
 def shards(right_side, kappa, velocity):
@@ -376,41 +389,37 @@
     planes = jnp.concatenate([kappa, squares[0], squares[1]], axis=0)
     planes = jnp.concatenate([planes[:, -around:], planes, planes[:, :around]], axis=1)
     local = lax.dynamic_slice_in_dim(planes, lax.axis_index("tm") * tile, LANES, 1)
-    top, bottom = exchange(local, local, spaces)
-    total = rows + 2 * HALO
+    edges = [shift(local, distance, spaces) for distance in (1, -1, 2, -2)]
+    total = 3 * rows + 2 * FAR
     wide = call(
         functools.partial(weight_kernel, rows),
         [(total, 3 * BLOCK, SUB, LANES)],
         [(LANES, LANES)],
-    )(local, top, bottom)
+    )(local, *edges)
 
     tile_shape = (rows, BLOCK, SUB, LANES)
-    edge_shape = (HALO, BLOCK, SUB, LANES)
-    work = [(total, BLOCK, SUB, LANES), (total, BLOCK, SUB, LANES), tile_shape]
+    far_shape = (FAR, BLOCK, SUB, LANES)
     span = LANES // 2 + 2 * SIDE
     freq, low, high = call(
         functools.partial(forward_kernel, rows, times, length),
-        [tile_shape, edge_shape, edge_shape],
+        [tile_shape, far_shape, far_shape],
         [(rows * span, LANES)],
-    )(cas_table, gathered)
-    top, bottom = exchange(low, high, spaces)
-
-    solved, applied, low, high, early = call(
-        functools.partial(first_kernel, rows),
-        [tile_shape, tile_shape, edge_shape, edge_shape, (2, SUB, LANES)],
-        work,
-    )(top, freq, bottom, wide, coef_table)
-    top, bottom = exchange(low, high, spaces)
+        unread=len(edges),
+        inputs=2 + len(edges),
+    )(cas_table, gathered, *edges)
+    top, bottom = shift(freq, 1, spaces), shift(freq, -1, spaces)
+    top_far, bottom_far = shift(high, 2, spaces), shift(low, -2, spaces)
 
     groups = [
         [i * spaces + first + j for i in range(tiles) for j in range(NEAR)]
         for first in range(0, spaces, NEAR)
     ]
-    solved_two, applied_two, sums = call(
-        functools.partial(second_kernel, rows),
-        [tile_shape, tile_shape, (tiles * NEAR, 1, LANES)],
-        [*work, (2, SUB, LANES)],
-    )(top, applied, bottom, wide, coef_table, early)
+    work = (total, BLOCK, SUB, LANES)
+    solved, applied, solved_two, applied_two, sums = call(
+        functools.partial(stencil_kernel, rows),
+        [tile_shape] * 4 + [(tiles * NEAR, 1, LANES)],
+        [work, work, tile_shape, (4, SUB, LANES)],
+    )(top_far, top, freq, bottom, bottom_far, wide, coef_table)
     packed = call(
         functools.partial(inverse_kernel, rows, times, length),
         [(tiles, 2 * rows * times, LANES)],

time: 122 us -> 123 us (level)
  waiting for transfers between devices: 42.8 us -> 31.1 us
  starting transfers between devices: 61.3 us -> 72.3 us
  Pallas kernels: 12.5 us -> 14.4 us
    all_to_all x1, waiting for transfers between devices: 12.9 us -> 0.01 us  [shards(): gathered = lax.all_to_all(windows, 'tm', 0, 0)]
    ppermute x6 -> x8, starting transfers between devices: 27.2 us -> 36.4 us  [shift(): lax.ppermute(value, 'space', [(i, (i + distance) % spaces) for i in range...]
    all_to_all x1, starting transfers between devices: 6.6 us -> 12 us  [shards(): sums = lax.all_to_all(sums, ('tm', 'space'), 0, 0, axis_index_groups=groups)]
    ppermute x3, starting transfers between devices: 12.9 us -> 9.3 us  [shards(): sums = sums + lax.ppermute(sums, 'space', pairs)]
    ppermute x3, waiting for transfers between devices: 5.29 us -> 8.6 us  [shards(): sums = sums + lax.ppermute(sums, 'space', pairs)]
    ppermute x6 -> x8, waiting for transfers between devices: 9.11 us -> 6.83 us  [shift(): lax.ppermute(value, 'space', [(i, (i + distance) % spaces) for i in range...]
    pallas_call x2 -> x1, Pallas kernels: 5.1 us -> 6.39 us  [shards(): call(functools.partial(stencil_kernel, rows), [tile_shape] * 4 + [(tiles...]
  transfers between devices with their start and end apart: 12 -> 14, of which waited for: 9 -> 7; matrix products, arithmetic and copies ran while one was open for 2% -> 2% of each run, Pallas kernels for 4% -> 4%
where the time goes in v4:
time: 123 us; the launch traced here: 122 us
  starting transfers between devices  72.3 us (59%)
  waiting for transfers between devices  31.1 us (25%)
  Pallas kernels  14.4 us (12%)
  local copies, waits for them, and re-layouts  2.07 us (2%)
  other arithmetic  1.71 us (1%)
    ppermute x8, starting transfers between devices, shift(): lax.ppermute(value, 'space', [(i, (i + distance) % spaces) for i in range...  36.4 us
    all_to_all x1, starting transfers between devices, shards(): sums = lax.all_to_all(sums, ('tm', 'space'), 0, 0, axis_index_groups=groups)  12 us
    all_to_all x1, starting transfers between devices, shards(): gathered = lax.all_to_all(windows, 'tm', 0, 0)  10.2 us
    all_to_all x1, waiting for transfers between devices, shards(): returned = lax.all_to_all(packed, 'tm', 0, 0)  9.96 us
    ppermute x3, starting transfers between devices, shards(): sums = sums + lax.ppermute(sums, 'space', pairs)  9.3 us
    ppermute x3, waiting for transfers between devices, shards(): sums = sums + lax.ppermute(sums, 'space', pairs)  8.6 us
    ppermute x8, waiting for transfers between devices, shift(): lax.ppermute(value, 'space', [(i, (i + distance) % spaces) for i in range...  6.83 us
    pallas_call x1, Pallas kernels, shards(): call(functools.partial(stencil_kernel, rows), [tile_shape] * 4 + [(tiles...  6.39 us
  transfers between devices with their start and end apart: 14, of which 7 were waited for; matrix products, arithmetic and copies ran while one was open for 2% of the time, Pallas kernels for 4%

profile of v4, /device:TPU:1, one launch (start us, length us, event | category | flops | bytes accessed | tf_op | source)
XLA Modules:
  0.0 122.4 jit_solution(8726813260329180075)
XLA Ops:
  0.6 0.0 copy-start
  0.6 0.9 copy-done
  1.6 0.0 copy-start.4
  1.6 1.0 shard_map.68
  2.6 10.2 %all-to-all-start = ((f32[16,48,128]{2,1,0:T(8,128)}), f32[16,48,128]{2,1,0:T(8,128)S(1)}, u32[]{:S(2)}, u32[]{:S(2)}) async-start(f32[16,48,128]{2,1,0:T(8,128)} %shard_map.68), calls=%async_computation | async-start | bytes 786432 | tf_op jit(solution)/shard_map/all_to_all | solution.py:386
  12.8 0.8 convert_multiply_fusion
  13.7 0.8 pad_maximum_fusion
  14.5 0.1 fusion
  14.5 0.1 concatenate.7
  14.7 0.1 constant_dynamic-slice_fusion.local_ref
  14.7 11.5 %collective-permute-start.3 = (f32[24,128]{1,0:T(8,128)S(1)}, f32[24,128]{1,0:T(8,128)S(1)}, u32[]{:S(2)}, u32[]{:S(2)}) collective-permute-start(f32[24,128]{1,0:T(8,128)S(1)} %constant_dynamic-slice_fusion.local_ref), channel_id=1, source_target_pairs={{0,30},{1,31},{2,0},{3,1},{4,2},{5,3},{6,4},{7,5},{8,6},{9,7},{10,... | collective-permute-start | bytes 36872 | tf_op jit(solution)/shard_map/ppermute | solution.py:367
  26.3 1.9 %collective-permute-start.2 = (f32[24,128]{1,0:T(8,128)S(1)}, f32[24,128]{1,0:T(8,128)S(1)}, u32[]{:S(2)}, u32[]{:S(2)}) collective-permute-start(f32[24,128]{1,0:T(8,128)S(1)} %constant_dynamic-slice_fusion.local_ref), channel_id=1, source_target_pairs={{0,2},{1,3},{2,4},{3,5},{4,6},{5,7},{6,8},{7,9},{8,10},{9,11},{10,... | collective-permute-start | bytes 36872 | tf_op jit(solution)/shard_map/ppermute | solution.py:367
  28.2 6.7 %collective-permute-start.1 = (f32[24,128]{1,0:T(8,128)S(1)}, f32[24,128]{1,0:T(8,128)S(1)}, u32[]{:S(2)}, u32[]{:S(2)}) collective-permute-start(f32[24,128]{1,0:T(8,128)S(1)} %constant_dynamic-slice_fusion.local_ref), channel_id=1, source_target_pairs={{0,31},{1,0},{2,1},{3,2},{4,3},{5,4},{6,5},{7,6},{8,7},{9,8},{10,9... | collective-permute-start | bytes 36872 | tf_op jit(solution)/shard_map/ppermute | solution.py:367
  34.9 1.9 %collective-permute-start = (f32[24,128]{1,0:T(8,128)S(1)}, f32[24,128]{1,0:T(8,128)S(1)}, u32[]{:S(2)}, u32[]{:S(2)}) collective-permute-start(f32[24,128]{1,0:T(8,128)S(1)} %constant_dynamic-slice_fusion.local_ref), channel_id=1, source_target_pairs={{0,1},{1,2},{2,3},{3,4},{4,5},{5,6},{6,7},{7,8},{8,9},{9,10},{10,1... | collective-permute-start | bytes 36872 | tf_op jit(solution)/shard_map/ppermute | solution.py:367
  36.9 0.0 collective-permute-done.3.refs_3_.bottom_far_ref
  36.9 0.0 collective-permute-done.2.refs_2_.top_far_ref
  36.9 0.0 collective-permute-done.1.refs_1_.bottom_ref
  36.9 5.8 %collective-permute-done.refs_0_.top_ref = f32[24,128]{1,0:T(8,128)S(1)} collective-permute-done((f32[24,128]{1,0:T(8,128)S(1)}, f32[24,128]{1,0:T(8,128)S(1)}, u32[]{:S(2)}, u32[]{:S(2)}) %collective-permute-start) | collective-permute-done | bytes 12320 | tf_op jit(solution)/shard_map/ppermute | solution.py:367
  42.7 0.0 all-to-all-done.field_ref
  42.7 0.0 copy-start.2
  42.7 0.8 copy-done.2
  43.5 0.6 shard_map.69
  44.1 1.9 %collective-permute-start.6 = (f32[8,11,8,128]{3,2,1,0:T(8,128)S(1)}, f32[8,11,8,128]{3,2,1,0:T(8,128)S(1)}, u32[]{:S(2)}, u32[]{:S(2)}) collective-permute-start(f32[8,11,8,128]{3,2,1,0:T(8,128)S(1)} %get-tuple-element.13.field_ref), channel_id=1, source_target_pairs={{0,31},{1,0},{2,1},{3,2},{4,3},{5,4},{6,5},{7,6},{8,7},{9,8},{10,9... | collective-permute-start | bytes 1081352 | tf_op jit(solution)/shard_map/ppermute | solution.py:367
  46.0 3.4 %collective-permute-start.5 = (f32[8,11,8,128]{3,2,1,0:T(8,128)S(1)}, f32[8,11,8,128]{3,2,1,0:T(8,128)S(1)}, u32[]{:S(2)}, u32[]{:S(2)}) collective-permute-start(f32[8,11,8,128]{3,2,1,0:T(8,128)S(1)} %get-tuple-element.13.field_ref), channel_id=1, source_target_pairs={{0,1},{1,2},{2,3},{3,4},{4,5},{5,6},{6,7},{7,8},{8,9},{9,10},{10,1... | collective-permute-start | bytes 1081352 | tf_op jit(solution)/shard_map/ppermute | solution.py:367
  49.4 1.9 %collective-permute-start.4 = (f32[2,11,8,128]{3,2,1,0:T(8,128)S(1)}, f32[2,11,8,128]{3,2,1,0:T(8,128)S(1)}, u32[]{:S(2)}, u32[]{:S(2)}) collective-permute-start(f32[2,11,8,128]{3,2,1,0:T(8,128)S(1)} %get-tuple-element.12), channel_id=1, source_target_pairs={{0,2},{1,3},{2,4},{3,5},{4,6},{5,7},{6,8},{7,9},{8,10},{9,11},{10,... | collective-permute-start | bytes 270344 | tf_op jit(solution)/shard_map/ppermute | solution.py:367
  51.3 0.0 copy-start.3
  51.4 7.1 %collective-permute-start.7 = (f32[2,11,8,128]{3,2,1,0:T(8,128)S(1)}, f32[2,11,8,128]{3,2,1,0:T(8,128)S(1)}, u32[]{:S(2)}, u32[]{:S(2)}) collective-permute-start(f32[2,11,8,128]{3,2,1,0:T(8,128)S(1)} %get-tuple-element.14), channel_id=1, source_target_pairs={{0,30},{1,31},{2,0},{3,1},{4,2},{5,3},{6,4},{7,5},{8,6},{9,7},{10,... | collective-permute-start | bytes 270344 | tf_op jit(solution)/shard_map/ppermute | solution.py:367
  58.5 1.9 %shard_map.70.wide_ref = f32[28,33,8,128]{3,2,1,0:T(8,128)S(1)} custom-call(f32[24,128]{1,0:T(8,128)S(1)} %constant_dynamic-slice_fusion.local_ref, f32[24,128]{1,0:T(8,128)S(1)} %collective-permute-done.refs_0_.top_ref, f32[24,128]{1,0:T(8,128)S(1)} %collective-permute-done.1.refs_1_.bottom_ref, f32[24,128]{1,0:T(8,128)S(1)} %collective-permute-done.2.refs_2_.top_far_ref, ...), custom_call_target="tpu_custom_call" | custom-call | tf_op jit(solution)/shard_map/pallas_call | solution.py:394
  60.3 0.0 copy-start.1
  60.3 0.0 collective-permute-done.4.top_far_ref
  60.4 1.0 collective-permute-done.7.bottom_far_ref
  61.4 0.0 collective-permute-done.6.bottom_ref
  61.4 0.0 collective-permute-done.5.top_ref
  61.4 0.0 copy-done.4
  61.4 6.4 %shard_map.71 = (f32[8,11,8,128]{3,2,1,0:T(8,128)S(1)}, f32[8,11,8,128]{3,2,1,0:T(8,128)S(1)}, f32[8,11,8,128]{3,2,1,0:T(8,128)S(1)}, f32[8,11,8,128]{3,2,1,0:T(8,128)S(1)}, f32[64,1,128]{2,1,0:T(1,128)}) custom-call(f32[2,11,8,128]{3,2,1,0:T(8,128)S(1)} %collective-permute-done.4.top_far_ref, f32[8,11,8,128]{3,2,1,0:T(8,128)S(1)} %collective-permute-done.5.top_ref, ...), custom_call_target="tpu_custom_call" | custom-call | tf_op jit(solution)/shard_map/pallas_call | solution.py:418
  67.8 12.0 %all-to-all-start.2 = ((f32[64,1,128]{2,1,0:T(1,128)}), f32[64,1,128]{2,1,0:T(1,128)S(1)}, u32[]{:S(2)}, u32[]{:S(2)}) async-start(f32[64,1,128]{2,1,0:T(1,128)} %get-tuple-element.19), calls=%async_computation.2 | async-start | bytes 65536 | tf_op jit(solution)/shard_map/all_to_all | solution.py:428
  79.7 0.0 copy-done.3
  79.8 3.3 %shard_map.72 = f32[16,128,128]{2,1,0:T(8,128)} custom-call(f32[128,128]{1,0:T(8,128)S(1)} %copy-done.3, f32[8,11,8,128]{3,2,1,0:T(8,128)S(1)} %get-tuple-element.15.one_ref, f32[8,11,8,128]{3,2,1,0:T(8,128)S(1)} %get-tuple-element.16.two_ref, f32[8,11,8,128]{3,2,1,0:T(8,128)S(1)} %get-tuple-element.17.three_ref, ...), custom_call_target="tpu_custom_call" | custom-call | tf_op jit(solution)/shard_map/pallas_call | solution.py:423
  83.1 5.7 %all-to-all-done.2 = f32[64,1,128]{2,1,0:T(1,128)S(1)} async-done(((f32[64,1,128]{2,1,0:T(1,128)}), f32[64,1,128]{2,1,0:T(1,128)S(1)}, u32[]{:S(2)}, u32[]{:S(2)}) %all-to-all-start.2) | async-done | bytes 32800 | tf_op jit(solution)/shard_map/all_to_all | solution.py:428
  88.8 4.4 %all-to-all-start.1 = ((f32[16,128,128]{2,1,0:T(8,128)}), f32[16,128,128]{2,1,0:T(8,128)S(1)}, u32[]{:S(2)}, u32[]{:S(2)}) async-start(f32[16,128,128]{2,1,0:T(8,128)} %shard_map.72), calls=%async_computation.1 | async-start | bytes 2097152 | tf_op jit(solution)/shard_map/all_to_all | solution.py:430
  93.2 0.1 reduce_sum.11
  93.3 1.9 %collective-permute-start.8 = (f32[1,128]{1,0:T(1,128)S(1)}, f32[1,128]{1,0:T(1,128)S(1)}, u32[]{:S(2)}, u32[]{:S(2)}) collective-permute-start(f32[1,128]{1,0:T(1,128)S(1)} %bitcast.11), channel_id=1, source_target_pairs={{0,4},{1,5},{2,6},{3,7},{4,0},{5,1},{6,2},{7,3},{8,12},{9,13},{10,... | collective-permute-start | bytes 1544 | tf_op jit(solution)/shard_map/ppermute | solution.py:434
  95.2 2.4 %collective-permute-done.8 = f32[1,128]{1,0:T(1,128)S(1)} collective-permute-done((f32[1,128]{1,0:T(1,128)S(1)}, f32[1,128]{1,0:T(1,128)S(1)}, u32[]{:S(2)}, u32[]{:S(2)}) %collective-permute-start.8) | collective-permute-done | bytes 544 | tf_op jit(solution)/shard_map/ppermute | solution.py:434
  97.6 1.9 %collective-permute-start.9 = (f32[1,128]{1,0:T(1,128)S(1)}, f32[1,128]{1,0:T(1,128)S(1)}, u32[]{:S(2)}, u32[]{:S(2)}) collective-permute-start(f32[1,128]{1,0:T(1,128)S(1)} %bitcast_add_fusion), channel_id=1, source_target_pairs={{0,8},{1,9},{2,10},{3,11},{4,12},{5,13},{6,14},{7,15},{8,0},{9,1},... | collective-permute-start | bytes 1544 | tf_op jit(solution)/shard_map/ppermute | solution.py:434
  99.5 3.5 %collective-permute-done.9 = f32[1,128]{1,0:T(1,128)S(1)} collective-permute-done((f32[1,128]{1,0:T(1,128)S(1)}, f32[1,128]{1,0:T(1,128)S(1)}, u32[]{:S(2)}, u32[]{:S(2)}) %collective-permute-start.9) | collective-permute-done | bytes 544 | tf_op jit(solution)/shard_map/ppermute | solution.py:434
  103.0 5.5 %collective-permute-start.10 = (f32[1,128]{1,0:T(1,128)S(1)}, f32[1,128]{1,0:T(1,128)S(1)}, u32[]{:S(2)}, u32[]{:S(2)}) collective-permute-start(f32[1,128]{1,0:T(1,128)S(1)} %add.14), channel_id=1, source_target_pairs={{0,16},{1,17},{2,18},{3,19},{4,20},{5,21},{6,22},{7,23},{8,24},{9,... | collective-permute-start | bytes 1544 | tf_op jit(solution)/shard_map/ppermute | solution.py:434
  108.5 2.7 %collective-permute-done.10 = f32[1,128]{1,0:T(1,128)S(1)} collective-permute-done((f32[1,128]{1,0:T(1,128)S(1)}, f32[1,128]{1,0:T(1,128)S(1)}, u32[]{:S(2)}, u32[]{:S(2)}) %collective-permute-start.10) | collective-permute-done | bytes 544 | tf_op jit(solution)/shard_map/ppermute | solution.py:434
  111.2 10.0 %all-to-all-done.1.source_ref = f32[16,128,128]{2,1,0:T(8,128)S(1)} async-done(((f32[16,128,128]{2,1,0:T(8,128)}), f32[16,128,128]{2,1,0:T(8,128)S(1)}, u32[]{:S(2)}, u32[]{:S(2)}) %all-to-all-start.1) | async-done | bytes 1048608 | tf_op jit(solution)/shard_map/all_to_all | solution.py:430
  121.2 0.0 copy-done.1
  121.2 1.2 %shard_map.73 = (f32[64,1024]{1,0:T(8,128)}, f32[64,1024]{1,0:T(8,128)}) custom-call(f32[16,128,128]{2,1,0:T(8,128)S(1)} %all-to-all-done.1.source_ref, f32[64,1024]{1,0:T(8,128)S(1)} %bitcast.10, f32[1,128]{1,0:T(1,128)S(1)} %add.15.sums_ref), custom_call_target="tpu_custom_call" | custom-call | tf_op jit(solution)/shard_map/pallas_call | solution.py:437
  (4 shorter events, 0.0 us)
Async XLA Ops:
  0.6 1.0 copy-start
  1.6 59.8 %copy-start.4 = (f32[10,8,128]{2,1,0:T(8,128)S(1)}, f32[10,8,128]{2,1,0:T(8,128)}, u32[]{:S(2)}) copy-start(f32[10,8,128]{2,1,0:T(8,128)} %constant.19.clone.coef_ref) | copy-start | bytes 122884
  2.6 40.1 %all-to-all-start = ((f32[16,48,128]{2,1,0:T(8,128)}), f32[16,48,128]{2,1,0:T(8,128)S(1)}, u32[]{:S(2)}, u32[]{:S(2)}) async-start(f32[16,48,128]{2,1,0:T(8,128)} %shard_map.68), calls=%async_computation | async-start | bytes 786432 | tf_op jit(solution)/shard_map/all_to_all | solution.py:386
  14.7 22.1 %collective-permute-start.3 = (f32[24,128]{1,0:T(8,128)S(1)}, f32[24,128]{1,0:T(8,128)S(1)}, u32[]{:S(2)}, u32[]{:S(2)}) collective-permute-start(f32[24,128]{1,0:T(8,128)S(1)} %constant_dynamic-slice_fusion.local_ref), channel_id=1, source_target_pairs={{0,30},{1,31},{2,0},{3,1},{4,2},{5,3},{6,4},{7,5},{8,6},{9,7},{10,... | collective-permute-start | bytes 36872 | tf_op jit(solution)/shard_map/ppermute | solution.py:367
  26.3 10.6 %collective-permute-start.2 = (f32[24,128]{1,0:T(8,128)S(1)}, f32[24,128]{1,0:T(8,128)S(1)}, u32[]{:S(2)}, u32[]{:S(2)}) collective-permute-start(f32[24,128]{1,0:T(8,128)S(1)} %constant_dynamic-slice_fusion.local_ref), channel_id=1, source_target_pairs={{0,2},{1,3},{2,4},{3,5},{4,6},{5,7},{6,8},{7,9},{8,10},{9,11},{10,... | collective-permute-start | bytes 36872 | tf_op jit(solution)/shard_map/ppermute | solution.py:367
  28.2 8.7 %collective-permute-start.1 = (f32[24,128]{1,0:T(8,128)S(1)}, f32[24,128]{1,0:T(8,128)S(1)}, u32[]{:S(2)}, u32[]{:S(2)}) collective-permute-start(f32[24,128]{1,0:T(8,128)S(1)} %constant_dynamic-slice_fusion.local_ref), channel_id=1, source_target_pairs={{0,31},{1,0},{2,1},{3,2},{4,3},{5,4},{6,5},{7,6},{8,7},{9,8},{10,9... | collective-permute-start | bytes 36872 | tf_op jit(solution)/shard_map/ppermute | solution.py:367
  34.9 7.8 %collective-permute-start = (f32[24,128]{1,0:T(8,128)S(1)}, f32[24,128]{1,0:T(8,128)S(1)}, u32[]{:S(2)}, u32[]{:S(2)}) collective-permute-start(f32[24,128]{1,0:T(8,128)S(1)} %constant_dynamic-slice_fusion.local_ref), channel_id=1, source_target_pairs={{0,1},{1,2},{2,3},{3,4},{4,5},{5,6},{6,7},{7,8},{8,9},{9,10},{10,1... | collective-permute-start | bytes 36872 | tf_op jit(solution)/shard_map/ppermute | solution.py:367
  42.7 0.8 copy-start.2
  44.1 17.3 %collective-permute-start.6 = (f32[8,11,8,128]{3,2,1,0:T(8,128)S(1)}, f32[8,11,8,128]{3,2,1,0:T(8,128)S(1)}, u32[]{:S(2)}, u32[]{:S(2)}) collective-permute-start(f32[8,11,8,128]{3,2,1,0:T(8,128)S(1)} %get-tuple-element.13.field_ref), channel_id=1, source_target_pairs={{0,31},{1,0},{2,1},{3,2},{4,3},{5,4},{6,5},{7,6},{8,7},{9,8},{10,9... | collective-permute-start | bytes 1081352 | tf_op jit(solution)/shard_map/ppermute | solution.py:367
  46.0 15.3 %collective-permute-start.5 = (f32[8,11,8,128]{3,2,1,0:T(8,128)S(1)}, f32[8,11,8,128]{3,2,1,0:T(8,128)S(1)}, u32[]{:S(2)}, u32[]{:S(2)}) collective-permute-start(f32[8,11,8,128]{3,2,1,0:T(8,128)S(1)} %get-tuple-element.13.field_ref), channel_id=1, source_target_pairs={{0,1},{1,2},{2,3},{3,4},{4,5},{5,6},{6,7},{7,8},{8,9},{9,10},{10,1... | collective-permute-start | bytes 1081352 | tf_op jit(solution)/shard_map/ppermute | solution.py:367
  49.4 10.9 %collective-permute-start.4 = (f32[2,11,8,128]{3,2,1,0:T(8,128)S(1)}, f32[2,11,8,128]{3,2,1,0:T(8,128)S(1)}, u32[]{:S(2)}, u32[]{:S(2)}) collective-permute-start(f32[2,11,8,128]{3,2,1,0:T(8,128)S(1)} %get-tuple-element.12), channel_id=1, source_target_pairs={{0,2},{1,3},{2,4},{3,5},{4,6},{5,7},{6,8},{7,9},{8,10},{9,11},{10,... | collective-permute-start | bytes 270344 | tf_op jit(solution)/shard_map/ppermute | solution.py:367
  51.3 28.4 %copy-start.3 = (f32[128,128]{1,0:T(8,128)S(1)}, f32[128,128]{1,0:T(8,128)}, u32[]{:S(2)}) copy-start(f32[128,128]{1,0:T(8,128)} %constant.18.clone.cas_ref) | copy-start | bytes 196612
  51.4 10.0 %collective-permute-start.7 = (f32[2,11,8,128]{3,2,1,0:T(8,128)S(1)}, f32[2,11,8,128]{3,2,1,0:T(8,128)S(1)}, u32[]{:S(2)}, u32[]{:S(2)}) collective-permute-start(f32[2,11,8,128]{3,2,1,0:T(8,128)S(1)} %get-tuple-element.14), channel_id=1, source_target_pairs={{0,30},{1,31},{2,0},{3,1},{4,2},{5,3},{6,4},{7,5},{8,6},{9,7},{10,... | collective-permute-start | bytes 270344 | tf_op jit(solution)/shard_map/ppermute | solution.py:367
  60.3 60.9 %copy-start.1 = (f32[8,8,1024]{2,1,0:T(8,128)S(1)}, f32[8,8,1024]{2,1,0:T(8,128)}, u32[]{:S(2)}) copy-start(f32[8,8,1024]{2,1,0:T(8,128)} %param.5) | copy-start | bytes 786436
  67.8 21.1 %all-to-all-start.2 = ((f32[64,1,128]{2,1,0:T(1,128)}), f32[64,1,128]{2,1,0:T(1,128)S(1)}, u32[]{:S(2)}, u32[]{:S(2)}) async-start(f32[64,1,128]{2,1,0:T(1,128)} %get-tuple-element.19), calls=%async_computation.2 | async-start | bytes 65536 | tf_op jit(solution)/shard_map/all_to_all | solution.py:428
  88.8 32.4 %all-to-all-start.1 = ((f32[16,128,128]{2,1,0:T(8,128)}), f32[16,128,128]{2,1,0:T(8,128)S(1)}, u32[]{:S(2)}, u32[]{:S(2)}) async-start(f32[16,128,128]{2,1,0:T(8,128)} %shard_map.72), calls=%async_computation.1 | async-start | bytes 2097152 | tf_op jit(solution)/shard_map/all_to_all | solution.py:430
  93.3 4.3 %collective-permute-start.8 = (f32[1,128]{1,0:T(1,128)S(1)}, f32[1,128]{1,0:T(1,128)S(1)}, u32[]{:S(2)}, u32[]{:S(2)}) collective-permute-start(f32[1,128]{1,0:T(1,128)S(1)} %bitcast.11), channel_id=1, source_target_pairs={{0,4},{1,5},{2,6},{3,7},{4,0},{5,1},{6,2},{7,3},{8,12},{9,13},{10,... | collective-permute-start | bytes 1544 | tf_op jit(solution)/shard_map/ppermute | solution.py:434
  97.6 5.5 %collective-permute-start.9 = (f32[1,128]{1,0:T(1,128)S(1)}, f32[1,128]{1,0:T(1,128)S(1)}, u32[]{:S(2)}, u32[]{:S(2)}) collective-permute-start(f32[1,128]{1,0:T(1,128)S(1)} %bitcast_add_fusion), channel_id=1, source_target_pairs={{0,8},{1,9},{2,10},{3,11},{4,12},{5,13},{6,14},{7,15},{8,0},{9,1},... | collective-permute-start | bytes 1544 | tf_op jit(solution)/shard_map/ppermute | solution.py:434
  103.0 8.2 %collective-permute-start.10 = (f32[1,128]{1,0:T(1,128)S(1)}, f32[1,128]{1,0:T(1,128)S(1)}, u32[]{:S(2)}, u32[]{:S(2)}) collective-permute-start(f32[1,128]{1,0:T(1,128)S(1)} %add.14), channel_id=1, source_target_pairs={{0,16},{1,17},{2,18},{3,19},{4,20},{5,21},{6,22},{7,23},{8,24},{9,... | collective-permute-start | bytes 1544 | tf_op jit(solution)/shard_map/ppermute | solution.py:434

commit v5 on v4

--- a/solution.py
+++ b/solution.py
@@ -109,9 +109,8 @@
 
 
 def forward_kernel(
-    rows, times, length, cas_ref, field_ref, *refs
+    rows, times, length, cas_ref, field_ref, local_ref, out_ref, low_ref, high_ref, line_ref
 ):
-    out_ref, low_ref, high_ref, line_ref = refs[-4:]
     half = LANES // 2
     span = half + 2 * SIDE
     pieces = field_ref.shape[1] // times
@@ -135,31 +134,24 @@
     for row in range(rows):
         for column in range(BLOCK):
             value = line_ref[pl.ds(row * span + skip + column, SUB, stride=BLOCK), :]
-            out_ref[row, column] = value
+            out_ref[row * BLOCK + column] = value
             if row < FAR:
-                low_ref[row, column] = value
+                low_ref[row * BLOCK + column] = value
             if row >= rows - FAR:
-                high_ref[row - (rows - FAR), column] = value
-
-
-def weight_kernel(
-    rows, local_ref, top_ref, bottom_ref, top_far_ref, bottom_far_ref, wide_ref, scratch_ref
-):
+                high_ref[(row - (rows - FAR)) * BLOCK + column] = value
+    for ref in (out_ref, low_ref, high_ref):
+        first = ref.shape[0] - 3
+        for plane in range(3):
+            ref[first + plane] = local_ref[plane * rows : (plane + 1) * rows, :]
+
+
+def weight_step(rows, refs, wide_ref, scratch_ref):
     planes = []
     for plane in range(3):
-        start = plane * rows
-        planes.append(
-            jnp.concatenate(
-                [
-                    top_far_ref[start + rows - FAR : start + rows, :],
-                    top_ref[start : start + rows, :],
-                    local_ref[start : start + rows, :],
-                    bottom_ref[start : start + rows, :],
-                    bottom_far_ref[start : start + FAR, :],
-                ],
-                axis=0,
-            )
-        )
+        blocks = [ref[ref.shape[0] - 3 + plane] for ref in refs]
+        blocks[0] = blocks[0][rows - FAR :]
+        blocks[-1] = blocks[-1][:FAR]
+        planes.append(jnp.concatenate(blocks, axis=0))
     east = 1.0 + 0.125 * (planes[1] + jnp.concatenate([planes[1][1:], planes[1][:1]], axis=0))
     north = 1.0 + 0.125 * (planes[2] + pltpu.roll(planes[2], LANES - 1, 1))
     total = planes[0].shape[0]
@@ -235,22 +227,25 @@
 
 
 def stencil_kernel(
-    rows, top_far_ref, top_ref, field_ref, bottom_ref, bottom_far_ref, wide_ref, coef_ref,
+    rows, top_far_ref, top_ref, field_ref, bottom_ref, bottom_far_ref, coef_ref,
     solved_ref, applied_ref, solved_two_ref, applied_two_ref, sums_ref,
-    step_ref, remain_ref, part_ref, line_ref,
+    step_ref, remain_ref, part_ref, line_ref, wide_ref, scratch_ref,
 ):
     columns = range(BLOCK)
+    refs = (top_far_ref, top_ref, field_ref, bottom_ref, bottom_far_ref)
+    weight_step(rows, refs, wide_ref, scratch_ref)
     offset = 0
-    for ref in (top_far_ref, top_ref, field_ref, bottom_ref, bottom_far_ref):
-
-        @pl.loop(0, ref.shape[0])
+    for ref in refs:
+        count = (ref.shape[0] - 3) // BLOCK
+
+        @pl.loop(0, count)
         def _(row, ref=ref, offset=offset):
             for column in columns:
-                value = ref[row, column]
+                value = ref[row * BLOCK + column]
                 remain_ref[offset + row, column] = value
                 step_ref[offset + row, column] = coef_ref[1] * value
 
-        offset += ref.shape[0]
+        offset += count
 
     own = (FAR + rows, FAR + 2 * rows)
     line_ref[...] = jnp.zeros_like(line_ref)
@@ -282,9 +277,9 @@
 
     work = (wide_ref, coef_ref, step_ref, remain_ref, part_ref)
     sources = (
-        lambda row, column: top_ref[row - FAR, column],
-        lambda row, column: field_ref[row - own[0], column],
-        lambda row, column: bottom_ref[row - own[1], column],
+        lambda row, column: top_ref[(row - FAR) * BLOCK + column],
+        lambda row, column: field_ref[(row - own[0]) * BLOCK + column],
+        lambda row, column: bottom_ref[(row - own[1]) * BLOCK + column],
     )
     passes(0, own, sources, *work, emit_first)
     sources = (None, lambda row, column: applied_ref[row - own[0], column], None)
@@ -348,18 +343,13 @@
             residual_ref[place, columns] = field_ref[place, columns] - merged[1]
 
 
-def call(kernel, out_shape, scratch=(), unread=0, inputs=0):
+def call(kernel, out_shape, scratch=()):
     shapes = [jax.ShapeDtypeStruct(shape, jnp.float32) for shape in out_shape]
-    specs = {}
-    if unread:
-        whole = pl.BlockSpec(memory_space=pltpu.VMEM)
-        specs["in_specs"] = [whole] * (inputs - unread) + [pl.BlockSpec(memory_space=pl.ANY)] * unread
     return pl.pallas_call(
         kernel,
         out_shape=shapes[0] if len(shapes) == 1 else shapes,
         scratch_shapes=[pltpu.VMEM(shape, jnp.float32) for shape in scratch],
         compiler_params=PARAMS,
-        **specs,
     )
 
 
@@ -389,24 +379,16 @@
     planes = jnp.concatenate([kappa, squares[0], squares[1]], axis=0)
     planes = jnp.concatenate([planes[:, -around:], planes, planes[:, :around]], axis=1)
     local = lax.dynamic_slice_in_dim(planes, lax.axis_index("tm") * tile, LANES, 1)
-    edges = [shift(local, distance, spaces) for distance in (1, -1, 2, -2)]
     total = 3 * rows + 2 * FAR
-    wide = call(
-        functools.partial(weight_kernel, rows),
-        [(total, 3 * BLOCK, SUB, LANES)],
-        [(LANES, LANES)],
-    )(local, *edges)
-
     tile_shape = (rows, BLOCK, SUB, LANES)
-    far_shape = (FAR, BLOCK, SUB, LANES)
+    row_shape = (rows * BLOCK + 3, SUB, LANES)
+    far_shape = (FAR * BLOCK + 3, SUB, LANES)
     span = LANES // 2 + 2 * SIDE
     freq, low, high = call(
         functools.partial(forward_kernel, rows, times, length),
-        [tile_shape, far_shape, far_shape],
+        [row_shape, far_shape, far_shape],
         [(rows * span, LANES)],
-        unread=len(edges),
-        inputs=2 + len(edges),
-    )(cas_table, gathered, *edges)
+    )(cas_table, gathered, local)
     top, bottom = shift(freq, 1, spaces), shift(freq, -1, spaces)
     top_far, bottom_far = shift(high, 2, spaces), shift(low, -2, spaces)
 
@@ -418,8 +400,15 @@
     solved, applied, solved_two, applied_two, sums = call(
         functools.partial(stencil_kernel, rows),
         [tile_shape] * 4 + [(tiles * NEAR, 1, LANES)],
-        [work, work, tile_shape, (4, SUB, LANES)],
-    )(top_far, top, freq, bottom, bottom_far, wide, coef_table)
+        [
+            work,
+            work,
+            tile_shape,
+            (4, SUB, LANES),
+            (total, 3 * BLOCK, SUB, LANES),
+            (LANES, LANES),
+        ],
+    )(top_far, top, freq, bottom, bottom_far, coef_table)
     packed = call(
         functools.partial(inverse_kernel, rows, times, length),
         [(tiles, 2 * rows * times, LANES)],

time: 123 us -> 116 us (0.943)
  starting transfers between devices: 72.3 us -> 47.2 us
  waiting for transfers between devices: 31.1 us -> 50.6 us
  other arithmetic: 1.71 us -> 0.11 us
    ppermute x8 -> x4, starting transfers between devices: 36.4 us -> 22.1 us  [shift(): lax.ppermute(value, 'space', [(i, (i + distance) % spaces) for i in range...]
    all_to_all x1, waiting for transfers between devices: 0.01 us -> 13.5 us  [shards(): gathered = lax.all_to_all(windows, 'tm', 0, 0)]
    all_to_all x1, starting transfers between devices: 12 us -> 4.71 us  [shards(): sums = lax.all_to_all(sums, ('tm', 'space'), 0, 0, axis_index_groups=groups)]
    ppermute x3, waiting for transfers between devices: 8.6 us -> 12.2 us  [shards(): sums = sums + lax.ppermute(sums, 'space', pairs)]
    ppermute x3, starting transfers between devices: 9.3 us -> 5.73 us  [shards(): sums = sums + lax.ppermute(sums, 'space', pairs)]
    ppermute x8 -> x4, waiting for transfers between devices: 6.83 us -> 9.14 us  [shift(): lax.ppermute(value, 'space', [(i, (i + distance) % spaces) for i in range...]
    pallas_call x1, Pallas kernels: 6.39 us -> 8.26 us  [shards(): call(functools.partial(stencil_kernel, rows), [tile_shape] * 4 + [(tiles...]
    pallas_call x2 -> x1, Pallas kernels: 2.44 us -> 0.57 us  [shards(): call(functools.partial(forward_kernel, rows, times, length), [row_shape,...]
  transfers between devices with their start and end apart: 14 -> 10, of which waited for: 7 -> 9; matrix products, arithmetic and copies ran while one was open for 2% -> 0% of each run, Pallas kernels for 4% -> 3%
where the time goes in v5:
time: 116 us; the launch traced here: 115 us
  waiting for transfers between devices  50.6 us (44%)
  starting transfers between devices  47.2 us (41%)
  Pallas kernels  14.4 us (12%)
  local copies, waits for them, and re-layouts  1.97 us (2%)
    ppermute x4, starting transfers between devices, shift(): lax.ppermute(value, 'space', [(i, (i + distance) % spaces) for i in range...  22.1 us
    all_to_all x1, waiting for transfers between devices, shards(): gathered = lax.all_to_all(windows, 'tm', 0, 0)  13.5 us
    ppermute x3, waiting for transfers between devices, shards(): sums = sums + lax.ppermute(sums, 'space', pairs)  12.2 us
    all_to_all x1, starting transfers between devices, shards(): gathered = lax.all_to_all(windows, 'tm', 0, 0)  10.3 us
    all_to_all x1, waiting for transfers between devices, shards(): returned = lax.all_to_all(packed, 'tm', 0, 0)  9.96 us
    ppermute x4, waiting for transfers between devices, shift(): lax.ppermute(value, 'space', [(i, (i + distance) % spaces) for i in range...  9.14 us
    pallas_call x1, Pallas kernels, shards(): call(functools.partial(stencil_kernel, rows), [tile_shape] * 4 + [(tiles...  8.26 us
    all_to_all x1, waiting for transfers between devices, shards(): sums = lax.all_to_all(sums, ('tm', 'space'), 0, 0, axis_index_groups=groups)  5.88 us
  transfers between devices with their start and end apart: 10, of which 9 were waited for; matrix products, arithmetic and copies ran while one was open for 0% of the time, Pallas kernels for 3%

profile of v5, /device:TPU:1, one launch (start us, length us, event | category | flops | bytes accessed | tf_op | source)
XLA Modules:
  0.0 115.1 jit_solution(18343096605117831953)
XLA Ops:
  0.6 0.0 copy-start
  0.6 0.9 copy-done
  1.6 1.0 shard_map.68
  2.6 0.0 copy-start.4
  2.6 10.3 %all-to-all-start = ((f32[16,48,128]{2,1,0:T(8,128)}), f32[16,48,128]{2,1,0:T(8,128)S(1)}, u32[]{:S(2)}, u32[]{:S(2)}) async-start(f32[16,48,128]{2,1,0:T(8,128)} %shard_map.68), calls=%async_computation | async-start | bytes 786432 | tf_op jit(solution)/shard_map/all_to_all | solution.py:376
  13.0 0.0 copy-done.4
  13.0 0.0 copy-start.5
  13.0 0.7 copy-done.5
  13.8 0.1 fusion
  13.8 0.0 copy-start.2
  13.9 0.1 concatenate.7
  14.0 0.1 constant_dynamic-slice_fusion.local_ref
  14.0 0.0 copy-start.3
  14.0 13.5 %all-to-all-done.field_ref = f32[16,48,128]{2,1,0:T(8,128)S(1)} async-done(((f32[16,48,128]{2,1,0:T(8,128)}), f32[16,48,128]{2,1,0:T(8,128)S(1)}, u32[]{:S(2)}, u32[]{:S(2)}) %all-to-all-start) | async-done | bytes 393248 | tf_op jit(solution)/shard_map/all_to_all | solution.py:376
  27.5 0.0 copy-done.2
  27.5 0.6 shard_map.69
  28.1 11.3 %collective-permute-start.2 = (f32[91,8,128]{2,1,0:T(8,128)S(1)}, f32[91,8,128]{2,1,0:T(8,128)S(1)}, u32[]{:S(2)}, u32[]{:S(2)}) collective-permute-start(f32[91,8,128]{2,1,0:T(8,128)S(1)} %get-tuple-element.13.field_ref), channel_id=1, source_target_pairs={{0,31},{1,0},{2,1},{3,2},{4,3},{5,4},{6,5},{7,6},{8,7},{9,8},{10,9... | collective-permute-start | bytes 1118216 | tf_op jit(solution)/shard_map/ppermute | solution.py:357
  39.4 1.9 %collective-permute-start.1 = (f32[91,8,128]{2,1,0:T(8,128)S(1)}, f32[91,8,128]{2,1,0:T(8,128)S(1)}, u32[]{:S(2)}, u32[]{:S(2)}) collective-permute-start(f32[91,8,128]{2,1,0:T(8,128)S(1)} %get-tuple-element.13.field_ref), channel_id=1, source_target_pairs={{0,1},{1,2},{2,3},{3,4},{4,5},{5,6},{6,7},{7,8},{8,9},{9,10},{10,1... | collective-permute-start | bytes 1118216 | tf_op jit(solution)/shard_map/ppermute | solution.py:357
  41.3 1.9 %collective-permute-start = (f32[25,8,128]{2,1,0:T(8,128)S(1)}, f32[25,8,128]{2,1,0:T(8,128)S(1)}, u32[]{:S(2)}, u32[]{:S(2)}) collective-permute-start(f32[25,8,128]{2,1,0:T(8,128)S(1)} %get-tuple-element.12), channel_id=1, source_target_pairs={{0,2},{1,3},{2,4},{3,5},{4,6},{5,7},{6,8},{7,9},{8,10},{9,11},{10,... | collective-permute-start | bytes 307208 | tf_op jit(solution)/shard_map/ppermute | solution.py:357
  43.2 7.0 %collective-permute-start.3 = (f32[25,8,128]{2,1,0:T(8,128)S(1)}, f32[25,8,128]{2,1,0:T(8,128)S(1)}, u32[]{:S(2)}, u32[]{:S(2)}) collective-permute-start(f32[25,8,128]{2,1,0:T(8,128)S(1)} %get-tuple-element.14), channel_id=1, source_target_pairs={{0,30},{1,31},{2,0},{3,1},{4,2},{5,3},{6,4},{7,5},{8,6},{9,7},{10,... | collective-permute-start | bytes 307208 | tf_op jit(solution)/shard_map/ppermute | solution.py:357
  50.2 4.0 %collective-permute-done.top_far_ref = f32[25,8,128]{2,1,0:T(8,128)S(1)} collective-permute-done((f32[25,8,128]{2,1,0:T(8,128)S(1)}, f32[25,8,128]{2,1,0:T(8,128)S(1)}, u32[]{:S(2)}, u32[]{:S(2)}) %collective-permute-start) | collective-permute-done | bytes 102432 | tf_op jit(solution)/shard_map/ppermute | solution.py:357
  54.2 5.1 %collective-permute-done.3.bottom_far_ref = f32[25,8,128]{2,1,0:T(8,128)S(1)} collective-permute-done((f32[25,8,128]{2,1,0:T(8,128)S(1)}, f32[25,8,128]{2,1,0:T(8,128)S(1)}, u32[]{:S(2)}, u32[]{:S(2)}) %collective-permute-start.3) | collective-permute-done | bytes 102432 | tf_op jit(solution)/shard_map/ppermute | solution.py:357
  59.3 0.0 collective-permute-done.2.bottom_ref
  59.3 0.1 collective-permute-done.1.top_ref
  59.4 0.0 copy-done.3
  59.4 8.3 %shard_map.70 = (f32[8,11,8,128]{3,2,1,0:T(8,128)S(1)}, f32[8,11,8,128]{3,2,1,0:T(8,128)S(1)}, f32[8,11,8,128]{3,2,1,0:T(8,128)S(1)}, f32[8,11,8,128]{3,2,1,0:T(8,128)S(1)}, f32[64,1,128]{2,1,0:T(1,128)}) custom-call(f32[25,8,128]{2,1,0:T(8,128)S(1)} %collective-permute-done.top_far_ref, f32[91,8,128]{2,1,0:T(8,128)S(1)} %collective-permute-done.1.top_ref, ...), custom_call_target="tpu_custom_call" | custom-call | tf_op jit(solution)/shard_map/pallas_call | solution.py:400
  67.6 4.7 %all-to-all-start.2 = ((f32[64,1,128]{2,1,0:T(1,128)}), f32[64,1,128]{2,1,0:T(1,128)S(1)}, u32[]{:S(2)}, u32[]{:S(2)}) async-start(f32[64,1,128]{2,1,0:T(1,128)} %get-tuple-element.19), calls=%async_computation.2 | async-start | bytes 65536 | tf_op jit(solution)/shard_map/all_to_all | solution.py:417
  72.3 3.3 %shard_map.71 = f32[16,128,128]{2,1,0:T(8,128)} custom-call(f32[128,128]{1,0:T(8,128)S(1)} %copy-done.2, f32[8,11,8,128]{3,2,1,0:T(8,128)S(1)} %get-tuple-element.15.one_ref, f32[8,11,8,128]{3,2,1,0:T(8,128)S(1)} %get-tuple-element.16.two_ref, f32[8,11,8,128]{3,2,1,0:T(8,128)S(1)} %get-tuple-element.17.three_ref, ...), custom_call_target="tpu_custom_call" | custom-call | tf_op jit(solution)/shard_map/pallas_call | solution.py:412
  75.7 0.0 copy-start.1
  75.7 5.9 %all-to-all-done.2 = f32[64,1,128]{2,1,0:T(1,128)S(1)} async-done(((f32[64,1,128]{2,1,0:T(1,128)}), f32[64,1,128]{2,1,0:T(1,128)S(1)}, u32[]{:S(2)}, u32[]{:S(2)}) %all-to-all-start.2) | async-done | bytes 32800 | tf_op jit(solution)/shard_map/all_to_all | solution.py:417
  81.6 4.3 %all-to-all-start.1 = ((f32[16,128,128]{2,1,0:T(8,128)}), f32[16,128,128]{2,1,0:T(8,128)S(1)}, u32[]{:S(2)}, u32[]{:S(2)}) async-start(f32[16,128,128]{2,1,0:T(8,128)} %shard_map.71), calls=%async_computation.1 | async-start | bytes 2097152 | tf_op jit(solution)/shard_map/all_to_all | solution.py:419
  85.9 0.1 reduce_sum.11
  86.0 1.9 %collective-permute-start.4 = (f32[1,128]{1,0:T(1,128)S(1)}, f32[1,128]{1,0:T(1,128)S(1)}, u32[]{:S(2)}, u32[]{:S(2)}) collective-permute-start(f32[1,128]{1,0:T(1,128)S(1)} %bitcast.11), channel_id=1, source_target_pairs={{0,4},{1,5},{2,6},{3,7},{4,0},{5,1},{6,2},{7,3},{8,12},{9,13},{10,... | collective-permute-start | bytes 1544 | tf_op jit(solution)/shard_map/ppermute | solution.py:423
  87.9 2.4 %collective-permute-done.4 = f32[1,128]{1,0:T(1,128)S(1)} collective-permute-done((f32[1,128]{1,0:T(1,128)S(1)}, f32[1,128]{1,0:T(1,128)S(1)}, u32[]{:S(2)}, u32[]{:S(2)}) %collective-permute-start.4) | collective-permute-done | bytes 544 | tf_op jit(solution)/shard_map/ppermute | solution.py:423
  90.3 1.9 %collective-permute-start.5 = (f32[1,128]{1,0:T(1,128)S(1)}, f32[1,128]{1,0:T(1,128)S(1)}, u32[]{:S(2)}, u32[]{:S(2)}) collective-permute-start(f32[1,128]{1,0:T(1,128)S(1)} %bitcast_add_fusion), channel_id=1, source_target_pairs={{0,8},{1,9},{2,10},{3,11},{4,12},{5,13},{6,14},{7,15},{8,0},{9,1},... | collective-permute-start | bytes 1544 | tf_op jit(solution)/shard_map/ppermute | solution.py:423
  92.2 3.5 %collective-permute-done.5 = f32[1,128]{1,0:T(1,128)S(1)} collective-permute-done((f32[1,128]{1,0:T(1,128)S(1)}, f32[1,128]{1,0:T(1,128)S(1)}, u32[]{:S(2)}, u32[]{:S(2)}) %collective-permute-start.5) | collective-permute-done | bytes 544 | tf_op jit(solution)/shard_map/ppermute | solution.py:423
  95.7 1.9 %collective-permute-start.6 = (f32[1,128]{1,0:T(1,128)S(1)}, f32[1,128]{1,0:T(1,128)S(1)}, u32[]{:S(2)}, u32[]{:S(2)}) collective-permute-start(f32[1,128]{1,0:T(1,128)S(1)} %add.14), channel_id=1, source_target_pairs={{0,16},{1,17},{2,18},{3,19},{4,20},{5,21},{6,22},{7,23},{8,24},{9,... | collective-permute-start | bytes 1544 | tf_op jit(solution)/shard_map/ppermute | solution.py:423
  97.6 6.3 %collective-permute-done.6 = f32[1,128]{1,0:T(1,128)S(1)} collective-permute-done((f32[1,128]{1,0:T(1,128)S(1)}, f32[1,128]{1,0:T(1,128)S(1)}, u32[]{:S(2)}, u32[]{:S(2)}) %collective-permute-start.6) | collective-permute-done | bytes 544 | tf_op jit(solution)/shard_map/ppermute | solution.py:423
  103.9 10.0 %all-to-all-done.1.source_ref = f32[16,128,128]{2,1,0:T(8,128)S(1)} async-done(((f32[16,128,128]{2,1,0:T(8,128)}), f32[16,128,128]{2,1,0:T(8,128)S(1)}, u32[]{:S(2)}, u32[]{:S(2)}) %all-to-all-start.1) | async-done | bytes 1048608 | tf_op jit(solution)/shard_map/all_to_all | solution.py:419
  113.9 0.0 copy-done.1
  113.9 1.2 %shard_map.72 = (f32[64,1024]{1,0:T(8,128)}, f32[64,1024]{1,0:T(8,128)}) custom-call(f32[16,128,128]{2,1,0:T(8,128)S(1)} %all-to-all-done.1.source_ref, f32[64,1024]{1,0:T(8,128)S(1)} %bitcast.10, f32[1,128]{1,0:T(1,128)S(1)} %add.15.sums_ref), custom_call_target="tpu_custom_call" | custom-call | tf_op jit(solution)/shard_map/pallas_call | solution.py:426
  (6 shorter events, 0.0 us)
Async XLA Ops:
  0.6 1.0 copy-start
  2.6 10.4 %copy-start.4 = (s32[2,8,1024]{2,1,0:T(8,128)S(1)}, s32[2,8,1024]{2,1,0:T(8,128)}, u32[]{:S(2)}) copy-start(s32[2,8,1024]{2,1,0:T(8,128)} %param.7) | copy-start | bytes 196612
  2.6 24.9 %all-to-all-start = ((f32[16,48,128]{2,1,0:T(8,128)}), f32[16,48,128]{2,1,0:T(8,128)S(1)}, u32[]{:S(2)}, u32[]{:S(2)}) async-start(f32[16,48,128]{2,1,0:T(8,128)} %shard_map.68), calls=%async_computation | async-start | bytes 786432 | tf_op jit(solution)/shard_map/all_to_all | solution.py:376
  13.0 0.8 copy-start.5
  13.8 13.7 %copy-start.2 = (f32[128,128]{1,0:T(8,128)S(1)}, f32[128,128]{1,0:T(8,128)}, u32[]{:S(2)}) copy-start(f32[128,128]{1,0:T(8,128)} %constant.18.clone.cas_ref) | copy-start | bytes 196612
  14.0 45.3 %copy-start.3 = (f32[10,8,128]{2,1,0:T(8,128)S(1)}, f32[10,8,128]{2,1,0:T(8,128)}, u32[]{:S(2)}) copy-start(f32[10,8,128]{2,1,0:T(8,128)} %constant.19.clone.coef_ref) | copy-start | bytes 122884
  28.1 31.2 %collective-permute-start.2 = (f32[91,8,128]{2,1,0:T(8,128)S(1)}, f32[91,8,128]{2,1,0:T(8,128)S(1)}, u32[]{:S(2)}, u32[]{:S(2)}) collective-permute-start(f32[91,8,128]{2,1,0:T(8,128)S(1)} %get-tuple-element.13.field_ref), channel_id=1, source_target_pairs={{0,31},{1,0},{2,1},{3,2},{4,3},{5,4},{6,5},{7,6},{8,7},{9,8},{10,9... | collective-permute-start | bytes 1118216 | tf_op jit(solution)/shard_map/ppermute | solution.py:357
  39.4 20.0 %collective-permute-start.1 = (f32[91,8,128]{2,1,0:T(8,128)S(1)}, f32[91,8,128]{2,1,0:T(8,128)S(1)}, u32[]{:S(2)}, u32[]{:S(2)}) collective-permute-start(f32[91,8,128]{2,1,0:T(8,128)S(1)} %get-tuple-element.13.field_ref), channel_id=1, source_target_pairs={{0,1},{1,2},{2,3},{3,4},{4,5},{5,6},{6,7},{7,8},{8,9},{9,10},{10,1... | collective-permute-start | bytes 1118216 | tf_op jit(solution)/shard_map/ppermute | solution.py:357
  41.3 12.9 %collective-permute-start = (f32[25,8,128]{2,1,0:T(8,128)S(1)}, f32[25,8,128]{2,1,0:T(8,128)S(1)}, u32[]{:S(2)}, u32[]{:S(2)}) collective-permute-start(f32[25,8,128]{2,1,0:T(8,128)S(1)} %get-tuple-element.12), channel_id=1, source_target_pairs={{0,2},{1,3},{2,4},{3,5},{4,6},{5,7},{6,8},{7,9},{8,10},{9,11},{10,... | collective-permute-start | bytes 307208 | tf_op jit(solution)/shard_map/ppermute | solution.py:357
  43.2 16.0 %collective-permute-start.3 = (f32[25,8,128]{2,1,0:T(8,128)S(1)}, f32[25,8,128]{2,1,0:T(8,128)S(1)}, u32[]{:S(2)}, u32[]{:S(2)}) collective-permute-start(f32[25,8,128]{2,1,0:T(8,128)S(1)} %get-tuple-element.14), channel_id=1, source_target_pairs={{0,30},{1,31},{2,0},{3,1},{4,2},{5,3},{6,4},{7,5},{8,6},{9,7},{10,... | collective-permute-start | bytes 307208 | tf_op jit(solution)/shard_map/ppermute | solution.py:357
  67.6 13.9 %all-to-all-start.2 = ((f32[64,1,128]{2,1,0:T(1,128)}), f32[64,1,128]{2,1,0:T(1,128)S(1)}, u32[]{:S(2)}, u32[]{:S(2)}) async-start(f32[64,1,128]{2,1,0:T(1,128)} %get-tuple-element.19), calls=%async_computation.2 | async-start | bytes 65536 | tf_op jit(solution)/shard_map/all_to_all | solution.py:417
  75.7 38.2 %copy-start.1 = (f32[8,8,1024]{2,1,0:T(8,128)S(1)}, f32[8,8,1024]{2,1,0:T(8,128)}, u32[]{:S(2)}) copy-start(f32[8,8,1024]{2,1,0:T(8,128)} %param.5) | copy-start | bytes 786436
  81.6 32.3 %all-to-all-start.1 = ((f32[16,128,128]{2,1,0:T(8,128)}), f32[16,128,128]{2,1,0:T(8,128)S(1)}, u32[]{:S(2)}, u32[]{:S(2)}) async-start(f32[16,128,128]{2,1,0:T(8,128)} %shard_map.71), calls=%async_computation.1 | async-start | bytes 2097152 | tf_op jit(solution)/shard_map/all_to_all | solution.py:419
  86.0 4.3 %collective-permute-start.4 = (f32[1,128]{1,0:T(1,128)S(1)}, f32[1,128]{1,0:T(1,128)S(1)}, u32[]{:S(2)}, u32[]{:S(2)}) collective-permute-start(f32[1,128]{1,0:T(1,128)S(1)} %bitcast.11), channel_id=1, source_target_pairs={{0,4},{1,5},{2,6},{3,7},{4,0},{5,1},{6,2},{7,3},{8,12},{9,13},{10,... | collective-permute-start | bytes 1544 | tf_op jit(solution)/shard_map/ppermute | solution.py:423
  90.3 5.5 %collective-permute-start.5 = (f32[1,128]{1,0:T(1,128)S(1)}, f32[1,128]{1,0:T(1,128)S(1)}, u32[]{:S(2)}, u32[]{:S(2)}) collective-permute-start(f32[1,128]{1,0:T(1,128)S(1)} %bitcast_add_fusion), channel_id=1, source_target_pairs={{0,8},{1,9},{2,10},{3,11},{4,12},{5,13},{6,14},{7,15},{8,0},{9,1},... | collective-permute-start | bytes 1544 | tf_op jit(solution)/shard_map/ppermute | solution.py:423
  95.7 8.2 %collective-permute-start.6 = (f32[1,128]{1,0:T(1,128)S(1)}, f32[1,128]{1,0:T(1,128)S(1)}, u32[]{:S(2)}, u32[]{:S(2)}) collective-permute-start(f32[1,128]{1,0:T(1,128)S(1)} %add.14), channel_id=1, source_target_pairs={{0,16},{1,17},{2,18},{3,19},{4,20},{5,21},{6,22},{7,23},{8,24},{9,... | collective-permute-start | bytes 1544 | tf_op jit(solution)/shard_map/ppermute | solution.py:423

commit v6 on v5

--- a/solution.py
+++ b/solution.py
@@ -292,32 +292,15 @@
     sums_ref[...] = jnp.broadcast_to(line[None], sums_ref.shape)
 
 
-def inverse_kernel(rows, times, length, cas_ref, one_ref, two_ref, three_ref, four_ref, out_ref, line_ref):
+def inverse_kernel(
+    rows, times, length, cas_ref, sums_ref, one_ref, two_ref, three_ref, four_ref, out_ref, line_ref
+):
     half = LANES // 2
     span = half + 2 * SIDE
     skip = (span - WINDOW) // 2
-    refs = (one_ref, two_ref, three_ref, four_ref)
-    for row in range(rows):
-        for index, ref in enumerate(refs):
-            for column in range(BLOCK):
-                start = (row * len(refs) + index) * span + skip + column
-                line_ref[pl.ds(start, SUB, stride=BLOCK), :] = ref[row, column]
-    for row in range(rows):
-        for pair in range(2):
-            start = (row * len(refs) + 2 * pair) * span + SIDE
-            points = jnp.concatenate(
-                [line_ref[start : start + half, :], line_ref[start + span : start + span + half, :]],
-                axis=0,
-            )
-            back = exact_dot(cas_ref[...], points, 1, 1).reshape(length // times, times, LANES)
-            place = (pair * rows + row) * times
-            out_ref[:, place : place + times, :] = back
-
-
-def final_kernel(rows, times, tiles, source_ref, field_ref, sums_ref, solution_ref, residual_ref):
-    line = sums_ref[...]
+    line = jnp.sum(sums_ref[...].reshape(sums_ref.shape[0], LANES), axis=0, keepdims=True)
     gamma, curved, cross, last = (
-        jnp.broadcast_to(line[:, index : index + 1], (times, LANES)) for index in range(4)
+        jnp.broadcast_to(line[:, index : index + 1], (SUB, LANES)) for index in range(4)
     )
     step = gamma / curved
     gamma_next = step * step * cross - gamma
@@ -325,22 +308,37 @@
     grown = 1.0 + turn
     next_curved = grown * grown * curved - 2.0 * step * grown * cross + step * step * last
     next_step = gamma_next / next_curved
-    low = lane_index((times, LANES)) < LANES // 2
-    scale = jnp.where(low, step + next_step * grown, -next_step * step)
+    first = step + next_step * grown
+    second = -next_step * step
+    for row in range(rows):
+        for index, (left_ref, right_ref) in enumerate(((one_ref, two_ref), (three_ref, four_ref))):
+            for column in range(BLOCK):
+                start = (2 * row + index) * span + skip + column
+                value = first * left_ref[row, column] + second * right_ref[row, column]
+                line_ref[pl.ds(start, SUB, stride=BLOCK), :] = value
+    for row in range(rows):
+        start = 2 * row * span + SIDE
+        points = jnp.concatenate(
+            [line_ref[start : start + half, :], line_ref[start + span : start + span + half, :]],
+            axis=0,
+        )
+        back = exact_dot(cas_ref[...], points, 1, 1).reshape(length // times, times, LANES)
+        out_ref[:, row * times : (row + 1) * times, :] = back
+
+
+def final_kernel(rows, times, tiles, source_ref, field_ref, solution_ref, residual_ref):
+    half = LANES // 2
+    low = lane_index((rows, LANES)) < half
     for time in range(times):
         place = slice(time * rows, (time + 1) * rows)
+        taken = pl.ds(time, rows, stride=times)
         for pair in range(tiles // 2):
             columns = slice(pair * LANES, (pair + 1) * LANES)
-            merged = []
-            for part in range(2):
-                taken = pl.ds(part * rows * times + time, rows, stride=times)
-                left = scale * source_ref[2 * pair, taken, :]
-                right = scale * source_ref[2 * pair + 1, taken, :]
-                left = left + pltpu.roll(left, LANES // 2, 1)
-                right = right + pltpu.roll(right, LANES // 2, 1)
-                merged.append(jnp.where(low, left, right))
-            solution_ref[place, columns] = merged[0]
-            residual_ref[place, columns] = field_ref[place, columns] - merged[1]
+            left = source_ref[2 * pair, taken, :]
+            right = source_ref[2 * pair + 1, taken, :]
+            solution_ref[place, columns] = jnp.where(low, left, pltpu.roll(right, half, 1))
+            change = jnp.where(low, pltpu.roll(left, half, 1), right)
+            residual_ref[place, columns] = field_ref[place, columns] - change
 
 
 def call(kernel, out_shape, scratch=()):
@@ -409,24 +407,22 @@
             (LANES, LANES),
         ],
     )(top_far, top, freq, bottom, bottom_far, coef_table)
+    sums = lax.all_to_all(sums, ("tm", "space"), 0, 0, axis_index_groups=groups)
+    planes = spaces // NEAR
+    groups = [[first + NEAR * i for i in range(planes)] for first in range(NEAR)]
+    sums = jnp.broadcast_to(jnp.sum(sums, axis=0)[None], (planes, 1, LANES))
+    sums = lax.all_to_all(sums, "space", 0, 0, axis_index_groups=groups)
     packed = call(
         functools.partial(inverse_kernel, rows, times, length),
-        [(tiles, 2 * rows * times, LANES)],
-        [(rows * 4 * span, LANES)],
-    )(cas_table, solved, solved_two, applied, applied_two)
-    sums = lax.all_to_all(sums, ("tm", "space"), 0, 0, axis_index_groups=groups)
-    sums = jnp.sum(sums, axis=0)
+        [(tiles, rows * times, LANES)],
+        [(rows * 2 * span, LANES)],
+    )(cas_table, sums, solved, solved_two, applied, applied_two)
     returned = lax.all_to_all(packed, "tm", 0, 0)
-    distance = NEAR
-    while distance < spaces:
-        pairs = [(i, i ^ distance) for i in range(spaces)]
-        sums = sums + lax.ppermute(sums, "space", pairs)
-        distance *= 2
 
     solution, residual = call(
         functools.partial(final_kernel, rows, times, tiles),
         [(times * rows, width), (times * rows, width)],
-    )(returned, field, sums)
+    )(returned, field)
     shape = right_side.shape
     return solution.reshape(shape), residual.reshape(shape)
 

time: 116 us -> 114 us (0.983)
  blocking collectives: 0 us -> 44.1 us
  waiting for transfers between devices: 50.6 us -> 22.6 us
  starting transfers between devices: 47.2 us -> 32.4 us
  Pallas kernels: 14.4 us -> 11.6 us
    all_to_all x0 -> x3, blocking collectives: none -> 44.1 us  [the longest x1 22 us: shards(): returned = lax.all_to_all(packed, 'tm', 0, 0)]
    all_to_all x2 -> x0, waiting for transfers between devices: 15.8 us -> none  [the longest x1 9.96 us: shards(): returned = lax.all_to_all(packed, 'tm', 0, 0)]
    ppermute x3 -> x0, waiting for transfers between devices: 12.2 us -> none  [shards(): sums = sums + lax.ppermute(sums, 'space', pairs)]
    all_to_all x2 -> x0, starting transfers between devices: 9.05 us -> none  [the longest x1 4.71 us: shards(): sums = lax.all_to_all(sums, ('tm', 'space'), 0, 0, axis_index_groups=groups)]
    ppermute x3 -> x0, starting transfers between devices: 5.73 us -> none  [shards(): sums = sums + lax.ppermute(sums, 'space', pairs)]
    pallas_call x1, Pallas kernels: 3.33 us -> 1.34 us  [shards(): call(functools.partial(inverse_kernel, rows, times, length), [(tiles, row...]
  transfers between devices with their start and end apart: 10 -> 5, of which waited for: 9 -> 4; matrix products, arithmetic and copies ran while one was open for 0% -> 0% of each run, Pallas kernels for 3% -> 0%
where the time goes in v6:
time: 114 us
  blocking collectives  44.1 us (39%)
  starting transfers between devices  32.4 us (28%)
  waiting for transfers between devices  22.6 us (20%)
  Pallas kernels  11.6 us (10%)
  local copies, waits for them, and re-layouts  1.97 us (2%)
    ppermute x4, starting transfers between devices, shift(): lax.ppermute(value, 'space', [(i, (i + distance) % spaces) for i in range...  22.1 us
    all_to_all x1, blocking collectives, shards(): returned = lax.all_to_all(packed, 'tm', 0, 0)  22 us
    all_to_all x1, waiting for transfers between devices, shards(): gathered = lax.all_to_all(windows, 'tm', 0, 0)  13.5 us
    all_to_all x1, blocking collectives, shards(): sums = lax.all_to_all(sums, ('tm', 'space'), 0, 0, axis_index_groups=groups)  13.2 us
    all_to_all x1, starting transfers between devices, shards(): gathered = lax.all_to_all(windows, 'tm', 0, 0)  10.3 us
    ppermute x4, waiting for transfers between devices, shift(): lax.ppermute(value, 'space', [(i, (i + distance) % spaces) for i in range...  9.14 us
    all_to_all x1, blocking collectives, shards(): sums = lax.all_to_all(sums, 'space', 0, 0, axis_index_groups=groups)  8.89 us
    pallas_call x1, Pallas kernels, shards(): call(functools.partial(stencil_kernel, rows), [tile_shape] * 4 + [(tiles...  7.65 us
  transfers between devices with their start and end apart: 5, of which 4 were waited for; matrix products, arithmetic and copies ran while one was open for 0% of the time, Pallas kernels for 0%

profile of v6, /device:TPU:1, one launch (start us, length us, event | category | flops | bytes accessed | tf_op | source)
XLA Modules:
  0.0 113.5 jit_solution(18242236342192082578)
XLA Ops:
  0.6 0.0 copy-start
  0.6 0.9 copy-done
  1.6 1.0 shard_map.68
  2.6 0.0 copy-start.4
  2.6 10.3 %all-to-all-start = ((f32[16,48,128]{2,1,0:T(8,128)}), f32[16,48,128]{2,1,0:T(8,128)S(1)}, u32[]{:S(2)}, u32[]{:S(2)}) async-start(f32[16,48,128]{2,1,0:T(8,128)} %shard_map.68), calls=%async_computation | async-start | bytes 786432 | tf_op jit(solution)/shard_map/all_to_all | solution.py:374
  13.0 0.0 copy-done.4
  13.0 0.0 copy-start.5
  13.0 0.7 copy-done.5
  13.8 0.1 fusion
  13.8 0.0 copy-start.2
  13.8 0.1 concatenate.7
  14.0 0.1 constant_dynamic-slice_fusion.local_ref
  14.0 0.0 copy-start.3
  14.0 13.5 %all-to-all-done.field_ref = f32[16,48,128]{2,1,0:T(8,128)S(1)} async-done(((f32[16,48,128]{2,1,0:T(8,128)}), f32[16,48,128]{2,1,0:T(8,128)S(1)}, u32[]{:S(2)}, u32[]{:S(2)}) %all-to-all-start) | async-done | bytes 393248 | tf_op jit(solution)/shard_map/all_to_all | solution.py:374
  27.5 0.0 copy-done.2
  27.5 0.6 shard_map.69
  28.1 11.3 %collective-permute-start.2 = (f32[91,8,128]{2,1,0:T(8,128)S(1)}, f32[91,8,128]{2,1,0:T(8,128)S(1)}, u32[]{:S(2)}, u32[]{:S(2)}) collective-permute-start(f32[91,8,128]{2,1,0:T(8,128)S(1)} %get-tuple-element.13.field_ref), channel_id=1, source_target_pairs={{0,31},{1,0},{2,1},{3,2},{4,3},{5,4},{6,5},{7,6},{8,7},{9,8},{10,9... | collective-permute-start | bytes 1118216 | tf_op jit(solution)/shard_map/ppermute | solution.py:355
  39.4 1.9 %collective-permute-start.1 = (f32[91,8,128]{2,1,0:T(8,128)S(1)}, f32[91,8,128]{2,1,0:T(8,128)S(1)}, u32[]{:S(2)}, u32[]{:S(2)}) collective-permute-start(f32[91,8,128]{2,1,0:T(8,128)S(1)} %get-tuple-element.13.field_ref), channel_id=1, source_target_pairs={{0,1},{1,2},{2,3},{3,4},{4,5},{5,6},{6,7},{7,8},{8,9},{9,10},{10,1... | collective-permute-start | bytes 1118216 | tf_op jit(solution)/shard_map/ppermute | solution.py:355
  41.3 1.9 %collective-permute-start = (f32[25,8,128]{2,1,0:T(8,128)S(1)}, f32[25,8,128]{2,1,0:T(8,128)S(1)}, u32[]{:S(2)}, u32[]{:S(2)}) collective-permute-start(f32[25,8,128]{2,1,0:T(8,128)S(1)} %get-tuple-element.12), channel_id=1, source_target_pairs={{0,2},{1,3},{2,4},{3,5},{4,6},{5,7},{6,8},{7,9},{8,10},{9,11},{10,... | collective-permute-start | bytes 307208 | tf_op jit(solution)/shard_map/ppermute | solution.py:355
  43.2 7.0 %collective-permute-start.3 = (f32[25,8,128]{2,1,0:T(8,128)S(1)}, f32[25,8,128]{2,1,0:T(8,128)S(1)}, u32[]{:S(2)}, u32[]{:S(2)}) collective-permute-start(f32[25,8,128]{2,1,0:T(8,128)S(1)} %get-tuple-element.14), channel_id=1, source_target_pairs={{0,30},{1,31},{2,0},{3,1},{4,2},{5,3},{6,4},{7,5},{8,6},{9,7},{10,... | collective-permute-start | bytes 307208 | tf_op jit(solution)/shard_map/ppermute | solution.py:355
  50.2 4.0 %collective-permute-done.top_far_ref = f32[25,8,128]{2,1,0:T(8,128)S(1)} collective-permute-done((f32[25,8,128]{2,1,0:T(8,128)S(1)}, f32[25,8,128]{2,1,0:T(8,128)S(1)}, u32[]{:S(2)}, u32[]{:S(2)}) %collective-permute-start) | collective-permute-done | bytes 102432 | tf_op jit(solution)/shard_map/ppermute | solution.py:355
  54.2 5.1 %collective-permute-done.3.bottom_far_ref = f32[25,8,128]{2,1,0:T(8,128)S(1)} collective-permute-done((f32[25,8,128]{2,1,0:T(8,128)S(1)}, f32[25,8,128]{2,1,0:T(8,128)S(1)}, u32[]{:S(2)}, u32[]{:S(2)}) %collective-permute-start.3) | collective-permute-done | bytes 102432 | tf_op jit(solution)/shard_map/ppermute | solution.py:355
  59.3 0.0 collective-permute-done.2.bottom_ref
  59.3 0.1 collective-permute-done.1.top_ref
  59.4 0.0 copy-done.3
  59.4 7.6 %shard_map.70 = (f32[8,11,8,128]{3,2,1,0:T(8,128)S(1)}, f32[8,11,8,128]{3,2,1,0:T(8,128)S(1)}, f32[8,11,8,128]{3,2,1,0:T(8,128)S(1)}, f32[8,11,8,128]{3,2,1,0:T(8,128)S(1)}, f32[64,1,128]{2,1,0:T(1,128)S(1)}) custom-call(f32[25,8,128]{2,1,0:T(8,128)S(1)} %collective-permute-done.top_far_ref, f32[91,8,128]{2,1,0:T(8,128)S(1)} %collective-permute-done.1.top_ref, ...), custom_call_target="tpu_custom_call" | custom-call | tf_op jit(solution)/shard_map/pallas_call | solution.py:398
  67.0 13.2 %all_to_all.20 = f32[64,1,128]{2,1,0:T(1,128)S(1)} all-to-all(f32[64,1,128]{2,1,0:T(1,128)S(1)} %get-tuple-element.15), channel_id=1, replica_groups={{0,1,2,3,32,33,34,35,64,65,66,67,96,97,98,99,128,129,130,131,160,161,16..., dimensions={0} | all-to-all | bytes 65536 | tf_op jit(solution)/shard_map/all_to_all | solution.py:410
  80.2 0.1 reduce_sum.9
  80.3 8.9 %all_to_all.21.sums_ref = f32[8,1,128]{2,1,0:T(1,128)S(1)} all-to-all(f32[8,1,128]{2,1,0:T(1,128)S(1)} %broadcast_in_dim.2), channel_id=1, replica_groups={{0,4,8,12,16,20,24,28},{1,5,9,13,17,21,25,29},{2,6,10,14,18,22,26,30},{..., dimensions={0} | all-to-all | bytes 8192 | tf_op jit(solution)/shard_map/all_to_all | solution.py:414
  89.2 1.3 %shard_map.71 = f32[16,64,128]{2,1,0:T(8,128)S(1)} custom-call(f32[128,128]{1,0:T(8,128)S(1)} %copy-done.2, f32[8,1,128]{2,1,0:T(1,128)S(1)} %all_to_all.21.sums_ref, f32[8,11,8,128]{3,2,1,0:T(8,128)S(1)} %get-tuple-element.16.one_ref, f32[8,11,8,128]{3,2,1,0:T(8,128)S(1)} %get-tuple-element.17.two_ref, f32[8,11,8,128]{3,2,1,0:T(8,128)S(1)} %get-tuple-element.18.three_ref, ...), custom_call_target="tpu_custom_call" | custom-call | tf_op jit(solution)/shard_map/pallas_call | solution.py:415
  90.5 0.0 copy-start.1
  90.5 22.0 %all_to_all.22.source_ref = f32[16,64,128]{2,1,0:T(8,128)S(1)} all-to-all(f32[16,64,128]{2,1,0:T(8,128)S(1)} %shard_map.71), channel_id=1, replica_groups=mesh['tm'=16,'space'=32] {'tm'}, dimensions={0} | all-to-all | bytes 1048576 | tf_op jit(solution)/shard_map/all_to_all | solution.py:420
  112.5 0.0 copy-done.1
  112.5 1.0 shard_map.72
  (4 shorter events, 0.0 us)
Async XLA Ops:
  0.6 1.0 copy-start
  2.6 10.4 %copy-start.4 = (s32[2,8,1024]{2,1,0:T(8,128)S(1)}, s32[2,8,1024]{2,1,0:T(8,128)}, u32[]{:S(2)}) copy-start(s32[2,8,1024]{2,1,0:T(8,128)} %param.7) | copy-start | bytes 196612
  2.6 24.9 %all-to-all-start = ((f32[16,48,128]{2,1,0:T(8,128)}), f32[16,48,128]{2,1,0:T(8,128)S(1)}, u32[]{:S(2)}, u32[]{:S(2)}) async-start(f32[16,48,128]{2,1,0:T(8,128)} %shard_map.68), calls=%async_computation | async-start | bytes 786432 | tf_op jit(solution)/shard_map/all_to_all | solution.py:374
  13.0 0.8 copy-start.5
  13.8 13.7 %copy-start.2 = (f32[128,128]{1,0:T(8,128)S(1)}, f32[128,128]{1,0:T(8,128)}, u32[]{:S(2)}) copy-start(f32[128,128]{1,0:T(8,128)} %constant.18.clone.cas_ref) | copy-start | bytes 196612
  14.0 45.3 %copy-start.3 = (f32[10,8,128]{2,1,0:T(8,128)S(1)}, f32[10,8,128]{2,1,0:T(8,128)}, u32[]{:S(2)}) copy-start(f32[10,8,128]{2,1,0:T(8,128)} %constant.19.clone.coef_ref) | copy-start | bytes 122884
  28.1 31.2 %collective-permute-start.2 = (f32[91,8,128]{2,1,0:T(8,128)S(1)}, f32[91,8,128]{2,1,0:T(8,128)S(1)}, u32[]{:S(2)}, u32[]{:S(2)}) collective-permute-start(f32[91,8,128]{2,1,0:T(8,128)S(1)} %get-tuple-element.13.field_ref), channel_id=1, source_target_pairs={{0,31},{1,0},{2,1},{3,2},{4,3},{5,4},{6,5},{7,6},{8,7},{9,8},{10,9... | collective-permute-start | bytes 1118216 | tf_op jit(solution)/shard_map/ppermute | solution.py:355
  39.4 20.0 %collective-permute-start.1 = (f32[91,8,128]{2,1,0:T(8,128)S(1)}, f32[91,8,128]{2,1,0:T(8,128)S(1)}, u32[]{:S(2)}, u32[]{:S(2)}) collective-permute-start(f32[91,8,128]{2,1,0:T(8,128)S(1)} %get-tuple-element.13.field_ref), channel_id=1, source_target_pairs={{0,1},{1,2},{2,3},{3,4},{4,5},{5,6},{6,7},{7,8},{8,9},{9,10},{10,1... | collective-permute-start | bytes 1118216 | tf_op jit(solution)/shard_map/ppermute | solution.py:355
  41.3 12.9 %collective-permute-start = (f32[25,8,128]{2,1,0:T(8,128)S(1)}, f32[25,8,128]{2,1,0:T(8,128)S(1)}, u32[]{:S(2)}, u32[]{:S(2)}) collective-permute-start(f32[25,8,128]{2,1,0:T(8,128)S(1)} %get-tuple-element.12), channel_id=1, source_target_pairs={{0,2},{1,3},{2,4},{3,5},{4,6},{5,7},{6,8},{7,9},{8,10},{9,11},{10,... | collective-permute-start | bytes 307208 | tf_op jit(solution)/shard_map/ppermute | solution.py:355
  43.2 16.0 %collective-permute-start.3 = (f32[25,8,128]{2,1,0:T(8,128)S(1)}, f32[25,8,128]{2,1,0:T(8,128)S(1)}, u32[]{:S(2)}, u32[]{:S(2)}) collective-permute-start(f32[25,8,128]{2,1,0:T(8,128)S(1)} %get-tuple-element.14), channel_id=1, source_target_pairs={{0,30},{1,31},{2,0},{3,1},{4,2},{5,3},{6,4},{7,5},{8,6},{9,7},{10,... | collective-permute-start | bytes 307208 | tf_op jit(solution)/shard_map/ppermute | solution.py:355
  90.5 22.0 %copy-start.1 = (f32[8,8,1024]{2,1,0:T(8,128)S(1)}, f32[8,8,1024]{2,1,0:T(8,128)}, u32[]{:S(2)}) copy-start(f32[8,8,1024]{2,1,0:T(8,128)} %param.5) | copy-start | bytes 786436

commit v7 on v6

--- a/solution.py
+++ b/solution.py
@@ -145,7 +145,7 @@
             ref[first + plane] = local_ref[plane * rows : (plane + 1) * rows, :]
 
 
-def weight_step(rows, refs, wide_ref, scratch_ref):
+def weight_lines(rows, refs, scratch_ref):
     planes = []
     for plane in range(3):
         blocks = [ref[ref.shape[0] - 3 + plane] for ref in refs]
@@ -158,14 +158,7 @@
     zero = jnp.zeros((LANES - 3 * total, LANES), jnp.float32)
     scratch_ref[...] = jnp.transpose(jnp.concatenate([planes[0], east, north, zero], axis=0))
     skip = (LANES - WINDOW) // 2
-    for column in range(BLOCK):
-        lines = scratch_ref[pl.ds(skip + column, SUB, stride=BLOCK), :]
-        for row in range(total):
-            for plane in range(3):
-                index = plane * total + row
-                wide_ref[row, plane * BLOCK + column] = jnp.broadcast_to(
-                    lines[:, index : index + 1], (SUB, LANES)
-                )
+    return [scratch_ref[pl.ds(skip + column, SUB, stride=BLOCK), :] for column in range(BLOCK)]
 
 
 def own_columns(column):
@@ -174,121 +167,124 @@
     return (place >= first) & (place < first + LANES // 2)
 
 
-def passes(edge, own, sources, wide_ref, coef_ref, step_ref, remain_ref, solved_ref, emit):
-    total = step_ref.shape[0]
+def passes(edge, own, total, source, weight, coef, step_ref, remain_ref, solved_ref, emit):
     columns = range(BLOCK)
 
     for turn in range(CHEB + 1):
         first, last = edge + turn + 1, total - edge - turn - 1
 
-        def row_step(row, carry, *, turn, place):
-            here, flux = carry[:BLOCK], carry[BLOCK:]
-            after = [step_ref[row + 1, column] for column in columns]
-            ahead = [wide_ref[row, BLOCK + column] * (here[column] - after[column]) for column in columns]
-            beside = list(here[1:]) + [pltpu.roll(here[0], SUB - 1, 0)]
-            side = [wide_ref[row, 2 * BLOCK + column] * (here[column] - beside[column]) for column in columns]
-            behind = [pltpu.roll(side[-1], 1, 0)] + side[:-1]
-            inside = place == 1
-            results = []
-            for column in columns:
-                applied = (
-                    (wide_ref[row, column] + coef_ref[0]) * here[column]
-                    + (ahead[column] - flux[column])
-                    + (side[column] - behind[column])
-                )
-                left = remain_ref[row, column] - applied
-                if turn < CHEB:
-                    remain_ref[row, column] = left
-                    step_ref[row, column] = (
-                        coef_ref[2 + 2 * turn] * here[column] + coef_ref[3 + 2 * turn] * left
+        def load(row, turn=turn):
+            if turn == 0:
+                return [coef[1] * source(row, column) for column in columns]
+            return [step_ref[row, column] for column in columns]
+
+        here = load(first - 1)
+        flux = None
+        for row in range(first - 1, last):
+            after = load(row + 1)
+            ahead = [weight(1, row, column) * (here[column] - after[column]) for column in columns]
+            if row >= first:
+                beside = here[1:] + [pltpu.roll(here[0], SUB - 1, 0)]
+                side = [weight(2, row, column) * (here[column] - beside[column]) for column in columns]
+                behind = [pltpu.roll(side[-1], 1, 0)] + side[:-1]
+                inside = row in range(*own)
+                results = []
+                for column in columns:
+                    applied = (
+                        weight(0, row, column) * here[column]
+                        + (ahead[column] - flux[column])
+                        + (side[column] - behind[column])
                     )
-                solved = here[column]
-                if inside and turn > 0:
-                    solved = solved_ref[row - own[0], column] + solved
-                if inside and turn < CHEB:
-                    solved_ref[row - own[0], column] = solved
+                    before = source(row, column) if turn == 0 else remain_ref[row, column]
+                    left = before - applied
+                    if turn < CHEB:
+                        remain_ref[row, column] = left
+                        step_ref[row, column] = (
+                            coef[2 + 2 * turn] * here[column] + coef[3 + 2 * turn] * left
+                        )
+                    solved = None
+                    if inside:
+                        place = row - own[0]
+                        solved = here[column]
+                        if turn > 0:
+                            solved = solved_ref[place, column] + solved
+                        if turn < CHEB:
+                            solved_ref[place, column] = solved
+                    if turn == CHEB:
+                        begun = source(row, column)
+                        results.append((begun, solved, begun - left))
                 if turn == CHEB:
-                    source = sources[place](row, column)
-                    results.append((source, solved, source - left))
-            if turn == CHEB:
-                emit(row, inside, *zip(*results))
-            return (*after, *ahead)
-
-        here = [step_ref[first, column] for column in columns]
-        flux = [
-            wide_ref[first - 1, BLOCK + column] * (step_ref[first - 1, column] - here[column])
-            for column in columns
-        ]
-        carry = (*here, *flux)
-        for place, (low, high) in enumerate(((first, own[0]), own, (own[1], last))):
-            if low < high:
-                step = functools.partial(row_step, turn=turn, place=place)
-                carry = lax.fori_loop(low, high, step, carry)
+                    emit(row, *zip(*results))
+            here, flux = after, ahead
 
 
 def stencil_kernel(
     rows, top_far_ref, top_ref, field_ref, bottom_ref, bottom_far_ref, coef_ref,
     solved_ref, applied_ref, solved_two_ref, applied_two_ref, sums_ref,
-    step_ref, remain_ref, part_ref, line_ref, wide_ref, scratch_ref,
+    step_ref, remain_ref, part_ref, middle_ref, wide_ref, scratch_ref,
 ):
     columns = range(BLOCK)
     refs = (top_far_ref, top_ref, field_ref, bottom_ref, bottom_far_ref)
-    weight_step(rows, refs, wide_ref, scratch_ref)
-    offset = 0
-    for ref in refs:
-        count = (ref.shape[0] - 3) // BLOCK
-
-        @pl.loop(0, count)
-        def _(row, ref=ref, offset=offset):
-            for column in columns:
-                value = ref[row * BLOCK + column]
-                remain_ref[offset + row, column] = value
-                step_ref[offset + row, column] = coef_ref[1] * value
-
-        offset += count
-
+    lines = weight_lines(rows, refs, scratch_ref)
+    coef = [coef_ref[index] for index in range(2 + 2 * CHEB)]
+    places = [
+        (ref, row) for ref in refs for row in range((ref.shape[0] - 3) // BLOCK)
+    ]
+    total = len(places)
     own = (FAR + rows, FAR + 2 * rows)
-    line_ref[...] = jnp.zeros_like(line_ref)
+    made = set()
+
+    def weight(plane, row, column):
+        place = plane * BLOCK + column
+        if (row, place) in made:
+            return wide_ref[row, place]
+        index = plane * total + row
+        value = jnp.broadcast_to(lines[column][:, index : index + 1], (SUB, LANES))
+        if plane == 0:
+            value = value + coef[0]
+        wide_ref[row, place] = value
+        made.add((row, place))
+        return value
+
+    def first_source(row, column):
+        ref, place = places[row]
+        return ref[place * BLOCK + column]
+
+    def second_source(row, column):
+        return middle_ref[row, column]
+
+    sums = [jnp.zeros((SUB, LANES), jnp.float32) for _ in range(4)]
 
     def add(index, one, two):
-        total = None
         for column in columns:
-            product = jnp.where(own_columns(column), one[column] * two[column], 0.0)
-            total = product if total is None else total + product
-        line_ref[index] = line_ref[index] + total
-
-    def emit_first(row, inside, source, solved, applied):
+            product = one[column] * two[column]
+            sums[index] = sums[index] + jnp.where(own_columns(column), product, 0.0)
+
+    def emit_first(row, source, solved, applied):
         for column in columns:
-            remain_ref[row, column] = applied[column]
-            step_ref[row, column] = coef_ref[1] * applied[column]
-        if inside:
+            middle_ref[row, column] = applied[column]
+        if row in range(*own):
             for column in columns:
                 solved_ref[row - own[0], column] = solved[column]
                 applied_ref[row - own[0], column] = applied[column]
             add(0, source, solved)
             add(1, solved, applied)
 
-    def emit_second(row, inside, source, solved, applied):
+    def emit_second(row, source, solved, applied):
         for column in columns:
             solved_two_ref[row - own[0], column] = solved[column]
             applied_two_ref[row - own[0], column] = applied[column]
         add(2, source, solved)
         add(3, solved, applied)
 
-    work = (wide_ref, coef_ref, step_ref, remain_ref, part_ref)
-    sources = (
-        lambda row, column: top_ref[(row - FAR) * BLOCK + column],
-        lambda row, column: field_ref[(row - own[0]) * BLOCK + column],
-        lambda row, column: bottom_ref[(row - own[1]) * BLOCK + column],
-    )
-    passes(0, own, sources, *work, emit_first)
-    sources = (None, lambda row, column: applied_ref[row - own[0], column], None)
-    passes(HALO, own, sources, *work, emit_second)
+    work = (weight, coef, step_ref, remain_ref, part_ref)
+    passes(0, own, total, first_source, *work, emit_first)
+    passes(HALO, own, total, second_source, *work, emit_second)
 
     lane = lane_index((1, LANES))
     line = jnp.zeros((1, LANES), jnp.float32)
     for index in range(4):
-        line = jnp.where(lane == index, jnp.sum(line_ref[index]), line)
+        line = jnp.where(lane == index, jnp.sum(sums[index]), line)
     sums_ref[...] = jnp.broadcast_to(line[None], sums_ref.shape)
 
 
@@ -402,7 +398,7 @@
             work,
             work,
             tile_shape,
-            (4, SUB, LANES),
+            work,
             (total, 3 * BLOCK, SUB, LANES),
             (LANES, LANES),
         ],

time: 114 us -> 111 us (0.974)
  Pallas kernels: 11.6 us -> 8.56 us
    pallas_call x1, Pallas kernels: 7.65 us -> 4.65 us  [shards(): call(functools.partial(stencil_kernel, rows), [tile_shape] * 4 + [(tiles...]
where the time goes in v7:
time: 111 us
  blocking collectives  44.1 us (40%)
  starting transfers between devices  32.4 us (29%)
  waiting for transfers between devices  22.6 us (20%)
  Pallas kernels  8.56 us (8%)
  local copies, waits for them, and re-layouts  1.98 us (2%)
    ppermute x4, starting transfers between devices, shift(): lax.ppermute(value, 'space', [(i, (i + distance) % spaces) for i in range...  22.1 us
    all_to_all x1, blocking collectives, shards(): returned = lax.all_to_all(packed, 'tm', 0, 0)  22 us
    all_to_all x1, waiting for transfers between devices, shards(): gathered = lax.all_to_all(windows, 'tm', 0, 0)  13.5 us
    all_to_all x1, blocking collectives, shards(): sums = lax.all_to_all(sums, ('tm', 'space'), 0, 0, axis_index_groups=groups)  13.2 us
    all_to_all x1, starting transfers between devices, shards(): gathered = lax.all_to_all(windows, 'tm', 0, 0)  10.3 us
    ppermute x4, waiting for transfers between devices, shift(): lax.ppermute(value, 'space', [(i, (i + distance) % spaces) for i in range...  9.14 us
    all_to_all x1, blocking collectives, shards(): sums = lax.all_to_all(sums, 'space', 0, 0, axis_index_groups=groups)  8.89 us
    pallas_call x1, Pallas kernels, shards(): call(functools.partial(stencil_kernel, rows), [tile_shape] * 4 + [(tiles...  4.65 us
  transfers between devices with their start and end apart: 5, of which 4 were waited for; matrix products, arithmetic and copies ran while one was open for 0% of the time, Pallas kernels for 0%

profile of v7, /device:TPU:1, one launch (start us, length us, event | category | flops | bytes accessed | tf_op | source)
XLA Modules:
  0.0 110.5 jit_solution(16955254937310235816)
XLA Ops:
  0.6 0.0 copy-start
  0.6 0.9 copy-done
  1.6 1.0 shard_map.68
  2.6 0.0 copy-start.4
  2.6 10.3 %all-to-all-start = ((f32[16,48,128]{2,1,0:T(8,128)}), f32[16,48,128]{2,1,0:T(8,128)S(1)}, u32[]{:S(2)}, u32[]{:S(2)}) async-start(f32[16,48,128]{2,1,0:T(8,128)} %shard_map.68), calls=%async_computation | async-start | bytes 786432 | tf_op jit(solution)/shard_map/all_to_all | solution.py:370
  13.0 0.0 copy-done.4
  13.0 0.0 copy-start.5
  13.0 0.7 copy-done.5
  13.8 0.1 fusion
  13.8 0.0 copy-start.2
  13.8 0.1 concatenate.7
  14.0 0.1 constant_dynamic-slice_fusion.local_ref
  14.0 0.0 copy-start.3
  14.0 13.5 %all-to-all-done.field_ref = f32[16,48,128]{2,1,0:T(8,128)S(1)} async-done(((f32[16,48,128]{2,1,0:T(8,128)}), f32[16,48,128]{2,1,0:T(8,128)S(1)}, u32[]{:S(2)}, u32[]{:S(2)}) %all-to-all-start) | async-done | bytes 393248 | tf_op jit(solution)/shard_map/all_to_all | solution.py:370
  27.5 0.0 copy-done.2
  27.5 0.6 shard_map.69
  28.1 11.3 %collective-permute-start.2 = (f32[91,8,128]{2,1,0:T(8,128)S(1)}, f32[91,8,128]{2,1,0:T(8,128)S(1)}, u32[]{:S(2)}, u32[]{:S(2)}) collective-permute-start(f32[91,8,128]{2,1,0:T(8,128)S(1)} %get-tuple-element.13.field_ref), channel_id=1, source_target_pairs={{0,31},{1,0},{2,1},{3,2},{4,3},{5,4},{6,5},{7,6},{8,7},{9,8},{10,9... | collective-permute-start | bytes 1118216 | tf_op jit(solution)/shard_map/ppermute | solution.py:351
  39.4 1.9 %collective-permute-start.1 = (f32[91,8,128]{2,1,0:T(8,128)S(1)}, f32[91,8,128]{2,1,0:T(8,128)S(1)}, u32[]{:S(2)}, u32[]{:S(2)}) collective-permute-start(f32[91,8,128]{2,1,0:T(8,128)S(1)} %get-tuple-element.13.field_ref), channel_id=1, source_target_pairs={{0,1},{1,2},{2,3},{3,4},{4,5},{5,6},{6,7},{7,8},{8,9},{9,10},{10,1... | collective-permute-start | bytes 1118216 | tf_op jit(solution)/shard_map/ppermute | solution.py:351
  41.3 1.9 %collective-permute-start = (f32[25,8,128]{2,1,0:T(8,128)S(1)}, f32[25,8,128]{2,1,0:T(8,128)S(1)}, u32[]{:S(2)}, u32[]{:S(2)}) collective-permute-start(f32[25,8,128]{2,1,0:T(8,128)S(1)} %get-tuple-element.12), channel_id=1, source_target_pairs={{0,2},{1,3},{2,4},{3,5},{4,6},{5,7},{6,8},{7,9},{8,10},{9,11},{10,... | collective-permute-start | bytes 307208 | tf_op jit(solution)/shard_map/ppermute | solution.py:351
  43.2 7.0 %collective-permute-start.3 = (f32[25,8,128]{2,1,0:T(8,128)S(1)}, f32[25,8,128]{2,1,0:T(8,128)S(1)}, u32[]{:S(2)}, u32[]{:S(2)}) collective-permute-start(f32[25,8,128]{2,1,0:T(8,128)S(1)} %get-tuple-element.14), channel_id=1, source_target_pairs={{0,30},{1,31},{2,0},{3,1},{4,2},{5,3},{6,4},{7,5},{8,6},{9,7},{10,... | collective-permute-start | bytes 307208 | tf_op jit(solution)/shard_map/ppermute | solution.py:351
  50.2 4.0 %collective-permute-done.top_far_ref = f32[25,8,128]{2,1,0:T(8,128)S(1)} collective-permute-done((f32[25,8,128]{2,1,0:T(8,128)S(1)}, f32[25,8,128]{2,1,0:T(8,128)S(1)}, u32[]{:S(2)}, u32[]{:S(2)}) %collective-permute-start) | collective-permute-done | bytes 102432 | tf_op jit(solution)/shard_map/ppermute | solution.py:351
  54.2 5.1 %collective-permute-done.3.bottom_far_ref = f32[25,8,128]{2,1,0:T(8,128)S(1)} collective-permute-done((f32[25,8,128]{2,1,0:T(8,128)S(1)}, f32[25,8,128]{2,1,0:T(8,128)S(1)}, u32[]{:S(2)}, u32[]{:S(2)}) %collective-permute-start.3) | collective-permute-done | bytes 102432 | tf_op jit(solution)/shard_map/ppermute | solution.py:351
  59.3 0.0 collective-permute-done.2.bottom_ref
  59.3 0.1 collective-permute-done.1.top_ref
  59.4 0.0 copy-done.3
  59.4 4.6 %shard_map.70 = (f32[8,11,8,128]{3,2,1,0:T(8,128)S(1)}, f32[8,11,8,128]{3,2,1,0:T(8,128)S(1)}, f32[8,11,8,128]{3,2,1,0:T(8,128)S(1)}, f32[8,11,8,128]{3,2,1,0:T(8,128)S(1)}, f32[64,1,128]{2,1,0:T(1,128)S(1)}) custom-call(f32[25,8,128]{2,1,0:T(8,128)S(1)} %collective-permute-done.top_far_ref, f32[91,8,128]{2,1,0:T(8,128)S(1)} %collective-permute-done.1.top_ref, ...), custom_call_target="tpu_custom_call" | custom-call | tf_op jit(solution)/shard_map/pallas_call | solution.py:394
  64.0 13.2 %all_to_all.20 = f32[64,1,128]{2,1,0:T(1,128)S(1)} all-to-all(f32[64,1,128]{2,1,0:T(1,128)S(1)} %get-tuple-element.15), channel_id=1, replica_groups={{0,1,2,3,32,33,34,35,64,65,66,67,96,97,98,99,128,129,130,131,160,161,16..., dimensions={0} | all-to-all | bytes 65536 | tf_op jit(solution)/shard_map/all_to_all | solution.py:406
  77.2 0.1 reduce_sum.9
  77.3 8.9 %all_to_all.21.sums_ref = f32[8,1,128]{2,1,0:T(1,128)S(1)} all-to-all(f32[8,1,128]{2,1,0:T(1,128)S(1)} %broadcast_in_dim.2), channel_id=1, replica_groups={{0,4,8,12,16,20,24,28},{1,5,9,13,17,21,25,29},{2,6,10,14,18,22,26,30},{..., dimensions={0} | all-to-all | bytes 8192 | tf_op jit(solution)/shard_map/all_to_all | solution.py:410
  86.2 1.3 %shard_map.71 = f32[16,64,128]{2,1,0:T(8,128)S(1)} custom-call(f32[128,128]{1,0:T(8,128)S(1)} %copy-done.2, f32[8,1,128]{2,1,0:T(1,128)S(1)} %all_to_all.21.sums_ref, f32[8,11,8,128]{3,2,1,0:T(8,128)S(1)} %get-tuple-element.16.one_ref, f32[8,11,8,128]{3,2,1,0:T(8,128)S(1)} %get-tuple-element.17.two_ref, f32[8,11,8,128]{3,2,1,0:T(8,128)S(1)} %get-tuple-element.18.three_ref, ...), custom_call_target="tpu_custom_call" | custom-call | tf_op jit(solution)/shard_map/pallas_call | solution.py:411
  87.5 0.0 copy-start.1
  87.5 22.0 %all_to_all.22.source_ref = f32[16,64,128]{2,1,0:T(8,128)S(1)} all-to-all(f32[16,64,128]{2,1,0:T(8,128)S(1)} %shard_map.71), channel_id=1, replica_groups=mesh['tm'=16,'space'=32] {'tm'}, dimensions={0} | all-to-all | bytes 1048576 | tf_op jit(solution)/shard_map/all_to_all | solution.py:416
  109.5 0.0 copy-done.1
  109.5 1.0 shard_map.72
  (4 shorter events, 0.0 us)
Async XLA Ops:
  0.6 1.0 copy-start
  2.6 10.4 %copy-start.4 = (s32[2,8,1024]{2,1,0:T(8,128)S(1)}, s32[2,8,1024]{2,1,0:T(8,128)}, u32[]{:S(2)}) copy-start(s32[2,8,1024]{2,1,0:T(8,128)} %param.7) | copy-start | bytes 196612
  2.6 24.9 %all-to-all-start = ((f32[16,48,128]{2,1,0:T(8,128)}), f32[16,48,128]{2,1,0:T(8,128)S(1)}, u32[]{:S(2)}, u32[]{:S(2)}) async-start(f32[16,48,128]{2,1,0:T(8,128)} %shard_map.68), calls=%async_computation | async-start | bytes 786432 | tf_op jit(solution)/shard_map/all_to_all | solution.py:370
  13.0 0.8 copy-start.5
  13.8 13.7 %copy-start.2 = (f32[128,128]{1,0:T(8,128)S(1)}, f32[128,128]{1,0:T(8,128)}, u32[]{:S(2)}) copy-start(f32[128,128]{1,0:T(8,128)} %constant.18.clone.cas_ref) | copy-start | bytes 196612
  14.0 45.3 %copy-start.3 = (f32[10,8,128]{2,1,0:T(8,128)S(1)}, f32[10,8,128]{2,1,0:T(8,128)}, u32[]{:S(2)}) copy-start(f32[10,8,128]{2,1,0:T(8,128)} %constant.19.clone.coef_ref) | copy-start | bytes 122884
  28.1 31.2 %collective-permute-start.2 = (f32[91,8,128]{2,1,0:T(8,128)S(1)}, f32[91,8,128]{2,1,0:T(8,128)S(1)}, u32[]{:S(2)}, u32[]{:S(2)}) collective-permute-start(f32[91,8,128]{2,1,0:T(8,128)S(1)} %get-tuple-element.13.field_ref), channel_id=1, source_target_pairs={{0,31},{1,0},{2,1},{3,2},{4,3},{5,4},{6,5},{7,6},{8,7},{9,8},{10,9... | collective-permute-start | bytes 1118216 | tf_op jit(solution)/shard_map/ppermute | solution.py:351
  39.4 20.0 %collective-permute-start.1 = (f32[91,8,128]{2,1,0:T(8,128)S(1)}, f32[91,8,128]{2,1,0:T(8,128)S(1)}, u32[]{:S(2)}, u32[]{:S(2)}) collective-permute-start(f32[91,8,128]{2,1,0:T(8,128)S(1)} %get-tuple-element.13.field_ref), channel_id=1, source_target_pairs={{0,1},{1,2},{2,3},{3,4},{4,5},{5,6},{6,7},{7,8},{8,9},{9,10},{10,1... | collective-permute-start | bytes 1118216 | tf_op jit(solution)/shard_map/ppermute | solution.py:351
  41.3 12.9 %collective-permute-start = (f32[25,8,128]{2,1,0:T(8,128)S(1)}, f32[25,8,128]{2,1,0:T(8,128)S(1)}, u32[]{:S(2)}, u32[]{:S(2)}) collective-permute-start(f32[25,8,128]{2,1,0:T(8,128)S(1)} %get-tuple-element.12), channel_id=1, source_target_pairs={{0,2},{1,3},{2,4},{3,5},{4,6},{5,7},{6,8},{7,9},{8,10},{9,11},{10,... | collective-permute-start | bytes 307208 | tf_op jit(solution)/shard_map/ppermute | solution.py:351
  43.2 16.0 %collective-permute-start.3 = (f32[25,8,128]{2,1,0:T(8,128)S(1)}, f32[25,8,128]{2,1,0:T(8,128)S(1)}, u32[]{:S(2)}, u32[]{:S(2)}) collective-permute-start(f32[25,8,128]{2,1,0:T(8,128)S(1)} %get-tuple-element.14), channel_id=1, source_target_pairs={{0,30},{1,31},{2,0},{3,1},{4,2},{5,3},{6,4},{7,5},{8,6},{9,7},{10,... | collective-permute-start | bytes 307208 | tf_op jit(solution)/shard_map/ppermute | solution.py:351
  87.5 22.0 %copy-start.1 = (f32[8,8,1024]{2,1,0:T(8,128)S(1)}, f32[8,8,1024]{2,1,0:T(8,128)}, u32[]{:S(2)}) copy-start(f32[8,8,1024]{2,1,0:T(8,128)} %param.5) | copy-start | bytes 786436

commit v8 on v7

--- a/solution.py
+++ b/solution.py
@@ -109,8 +109,9 @@
 
 
 def forward_kernel(
-    rows, times, length, cas_ref, field_ref, local_ref, out_ref, low_ref, high_ref, line_ref
+    rows, times, length, cas_ref, field_ref, local_ref, place_ref, out_ref, one_ref, two_ref, line_ref
 ):
+    second = place_ref[1] == 1
     half = LANES // 2
     span = half + 2 * SIDE
     pieces = field_ref.shape[1] // times
@@ -135,20 +136,21 @@
         for column in range(BLOCK):
             value = line_ref[pl.ds(row * span + skip + column, SUB, stride=BLOCK), :]
             out_ref[row * BLOCK + column] = value
-            if row < FAR:
-                low_ref[row * BLOCK + column] = value
-            if row >= rows - FAR:
-                high_ref[(row - (rows - FAR)) * BLOCK + column] = value
-    for ref in (out_ref, low_ref, high_ref):
+    for index in range(FAR * BLOCK):
+        low = out_ref[index]
+        high = out_ref[(rows - FAR) * BLOCK + index]
+        one_ref[index] = jnp.where(second, low, high)
+        two_ref[index] = jnp.where(second, high, low)
+    for ref in (out_ref, one_ref, two_ref):
         first = ref.shape[0] - 3
         for plane in range(3):
             ref[first + plane] = local_ref[plane * rows : (plane + 1) * rows, :]
 
 
-def weight_lines(rows, refs, scratch_ref):
+def weight_lines(rows, parts, scratch_ref):
     planes = []
     for plane in range(3):
-        blocks = [ref[ref.shape[0] - 3 + plane] for ref in refs]
+        blocks = [part[plane] for part in parts]
         blocks[0] = blocks[0][rows - FAR :]
         blocks[-1] = blocks[-1][:FAR]
         planes.append(jnp.concatenate(blocks, axis=0))
@@ -219,13 +221,22 @@
 
 
 def stencil_kernel(
-    rows, top_far_ref, top_ref, field_ref, bottom_ref, bottom_far_ref, coef_ref,
+    rows, one_ref, two_ref, one_far_ref, two_far_ref, field_ref, coef_ref, place_ref,
     solved_ref, applied_ref, solved_two_ref, applied_two_ref, sums_ref,
-    step_ref, remain_ref, part_ref, middle_ref, wide_ref, scratch_ref,
+    step_ref, remain_ref, part_ref, middle_ref, wide_ref, scratch_ref, near_ref, far_ref,
 ):
     columns = range(BLOCK)
-    refs = (top_far_ref, top_ref, field_ref, bottom_ref, bottom_far_ref)
-    lines = weight_lines(rows, refs, scratch_ref)
+    for ref, above, target_ref in (
+        (one_ref, place_ref[0], near_ref),
+        (two_ref, 1 - place_ref[0], near_ref),
+        (one_far_ref, place_ref[1], far_ref),
+        (two_far_ref, 1 - place_ref[1], far_ref),
+    ):
+        for index in range(ref.shape[0]):
+            target_ref[1 - above, index] = ref[index]
+    refs = (far_ref.at[0], near_ref.at[0], field_ref, near_ref.at[1], far_ref.at[1])
+    parts = [[ref[ref.shape[0] - 3 + plane] for plane in range(3)] for ref in refs]
+    lines = weight_lines(rows, parts, scratch_ref)
     coef = [coef_ref[index] for index in range(2 + 2 * CHEB)]
     places = [
         (ref, row) for ref in refs for row in range((ref.shape[0] - 3) // BLOCK)
@@ -337,18 +348,24 @@
             residual_ref[place, columns] = field_ref[place, columns] - change
 
 
-def call(kernel, out_shape, scratch=()):
+def call(kernel, out_shape, scratch=(), inputs=0):
     shapes = [jax.ShapeDtypeStruct(shape, jnp.float32) for shape in out_shape]
+    specs = {}
+    if inputs:
+        whole = pl.BlockSpec(memory_space=pltpu.VMEM)
+        specs["in_specs"] = [whole] * (inputs - 1) + [pl.BlockSpec(memory_space=pltpu.SMEM)]
     return pl.pallas_call(
         kernel,
         out_shape=shapes[0] if len(shapes) == 1 else shapes,
         scratch_shapes=[pltpu.VMEM(shape, jnp.float32) for shape in scratch],
         compiler_params=PARAMS,
+        **specs,
     )
 
 
-def shift(value, distance, spaces):
-    return lax.ppermute(value, "space", [(i, (i + distance) % spaces) for i in range(spaces)])
+def swap(value, distance, offset, spaces):
+    pairs = [(i, (((i - offset) % spaces ^ distance) + offset) % spaces) for i in range(spaces)]
+    return lax.ppermute(value, "space", pairs)
 
 
 def shards(right_side, kappa, velocity):
@@ -378,13 +395,18 @@
     row_shape = (rows * BLOCK + 3, SUB, LANES)
     far_shape = (FAR * BLOCK + 3, SUB, LANES)
     span = LANES // 2 + 2 * SIDE
-    freq, low, high = call(
+    index = lax.axis_index("space")
+    place = jnp.stack([index % 2, index // 2 % 2]).astype(jnp.int32)
+    freq, inner_far, outer_far = call(
         functools.partial(forward_kernel, rows, times, length),
         [row_shape, far_shape, far_shape],
         [(rows * span, LANES)],
-    )(cas_table, gathered, local)
-    top, bottom = shift(freq, 1, spaces), shift(freq, -1, spaces)
-    top_far, bottom_far = shift(high, 2, spaces), shift(low, -2, spaces)
+        inputs=4,
+    )(cas_table, gathered, local, place)
+    outer = swap(freq, 1, 1, spaces)
+    inner = swap(freq, 1, 0, spaces)
+    outer_far = swap(outer_far, 2, 2, spaces)
+    inner_far = swap(inner_far, 2, 0, spaces)
 
     groups = [
         [i * spaces + first + j for i in range(tiles) for j in range(NEAR)]
@@ -401,8 +423,11 @@
             work,
             (total, 3 * BLOCK, SUB, LANES),
             (LANES, LANES),
+            (2, *row_shape),
+            (2, *far_shape),
         ],
-    )(top_far, top, freq, bottom, bottom_far, coef_table)
+        inputs=7,
+    )(inner, outer, inner_far, outer_far, freq, coef_table, place)
     sums = lax.all_to_all(sums, ("tm", "space"), 0, 0, axis_index_groups=groups)
     planes = spaces // NEAR
     groups = [[first + NEAR * i for i in range(planes)] for first in range(NEAR)]

time: 111 us -> 110 us (level)
  waiting for transfers between devices: 22.6 us -> 18.6 us
  blocking collectives: 44.1 us -> 47.6 us
  starting transfers between devices: 32.4 us -> 30.2 us
    all_to_all x1, blocking collectives: 13.2 us -> 16.7 us  [shards(): sums = lax.all_to_all(sums, ('tm', 'space'), 0, 0, axis_index_groups=groups)]
    ppermute x4, waiting for transfers between devices: 9.14 us -> 6.02 us  [swap(): return lax.ppermute(value, 'space', pairs)]
    ppermute x4, starting transfers between devices: 22.1 us -> 20 us  [swap(): return lax.ppermute(value, 'space', pairs)]
  transfers between devices with their start and end apart: 5 -> 5, of which waited for: 4 -> 3; matrix products, arithmetic and copies ran while one was open for 0% -> 0% of each run, Pallas kernels for 0% -> 0%
where the time goes in v8:
time: 110 us
  blocking collectives  47.6 us (43%)
  starting transfers between devices  30.2 us (27%)
  waiting for transfers between devices  18.6 us (17%)
  Pallas kernels  9.64 us (9%)
  local copies, waits for them, and re-layouts  2.76 us (3%)
    all_to_all x1, blocking collectives, shards(): returned = lax.all_to_all(packed, 'tm', 0, 0)  22 us
    ppermute x4, starting transfers between devices, swap(): return lax.ppermute(value, 'space', pairs)  20 us
    all_to_all x1, blocking collectives, shards(): sums = lax.all_to_all(sums, ('tm', 'space'), 0, 0, axis_index_groups=groups)  16.7 us
    all_to_all x1, waiting for transfers between devices, shards(): gathered = lax.all_to_all(windows, 'tm', 0, 0)  12.6 us
    all_to_all x1, starting transfers between devices, shards(): gathered = lax.all_to_all(windows, 'tm', 0, 0)  10.2 us
    all_to_all x1, blocking collectives, shards(): sums = lax.all_to_all(sums, 'space', 0, 0, axis_index_groups=groups)  8.89 us
    ppermute x4, waiting for transfers between devices, swap(): return lax.ppermute(value, 'space', pairs)  6.02 us
    pallas_call x1, Pallas kernels, shards(): call(functools.partial(stencil_kernel, rows), [tile_shape] * 4 + [(tiles...  5.18 us
  transfers between devices with their start and end apart: 5, of which 3 were waited for; matrix products, arithmetic and copies ran while one was open for 0% of the time, Pallas kernels for 0%

profile of v8, /device:TPU:1, one launch (start us, length us, event | category | flops | bytes accessed | tf_op | source)
XLA Modules:
  0.0 109.8 jit_solution(5533825870364157307)
XLA Ops:
  0.6 0.0 copy-start
  0.6 0.9 copy-done
  1.6 1.0 shard_map.68
  2.6 10.2 %all-to-all-start = ((f32[16,48,128]{2,1,0:T(8,128)}), f32[16,48,128]{2,1,0:T(8,128)S(1)}, u32[]{:S(2)}, u32[]{:S(2)}) async-start(f32[16,48,128]{2,1,0:T(8,128)} %shard_map.68), calls=%async_computation | async-start | bytes 786432 | tf_op jit(solution)/shard_map/all_to_all | solution.py:387
  12.8 0.0 copy-start.4
  12.9 0.8 copy-done.4
  13.7 0.0 copy-start.5
  13.7 0.7 copy-done.5
  14.4 0.1 fusion
  14.5 0.0 copy-start.2
  14.5 0.1 concatenate.7
  14.6 0.1 pad_add_fusion.place_ref
  14.7 0.1 constant_dynamic-slice_fusion.local_ref
  14.8 0.0 copy-start.3
  14.8 12.6 %all-to-all-done.field_ref = f32[16,48,128]{2,1,0:T(8,128)S(1)} async-done(((f32[16,48,128]{2,1,0:T(8,128)}), f32[16,48,128]{2,1,0:T(8,128)S(1)}, u32[]{:S(2)}, u32[]{:S(2)}) %all-to-all-start) | async-done | bytes 393248 | tf_op jit(solution)/shard_map/all_to_all | solution.py:387
  27.4 0.0 copy-done.2
  27.4 1.1 %shard_map.69 = (f32[91,8,128]{2,1,0:T(8,128)S(1)}, f32[25,8,128]{2,1,0:T(8,128)S(1)}, f32[25,8,128]{2,1,0:T(8,128)S(1)}) custom-call(f32[128,128]{1,0:T(8,128)S(1)} %copy-done.2, f32[16,48,128]{2,1,0:T(8,128)S(1)} %all-to-all-done.field_ref, f32[24,128]{1,0:T(8,128)S(1)} %constant_dynamic-slice_fusion.local_ref, s32[2]{0:T(128)S(1)} %pad_add_fusion.place_ref), custom_call_target="tpu_custom_call" | custom-call | tf_op jit(solution)/shard_map/pallas_call | solution.py:400
  28.5 11.3 %collective-permute-start.1 = (f32[91,8,128]{2,1,0:T(8,128)S(1)}, f32[91,8,128]{2,1,0:T(8,128)S(1)}, u32[]{:S(2)}, u32[]{:S(2)}) collective-permute-start(f32[91,8,128]{2,1,0:T(8,128)S(1)} %get-tuple-element.12.field_ref), channel_id=1, source_target_pairs={{0,31},{1,2},{2,1},{3,4},{4,3},{5,6},{6,5},{7,8},{8,7},{9,10},{10,... | collective-permute-start | bytes 1118216 | tf_op jit(solution)/shard_map/ppermute | solution.py:368
  39.8 1.9 %collective-permute-start = (f32[91,8,128]{2,1,0:T(8,128)S(1)}, f32[91,8,128]{2,1,0:T(8,128)S(1)}, u32[]{:S(2)}, u32[]{:S(2)}) collective-permute-start(f32[91,8,128]{2,1,0:T(8,128)S(1)} %get-tuple-element.12.field_ref), channel_id=1, source_target_pairs={{0,1},{1,0},{2,3},{3,2},{4,5},{5,4},{6,7},{7,6},{8,9},{9,8},{10,11... | collective-permute-start | bytes 1118216 | tf_op jit(solution)/shard_map/ppermute | solution.py:368
  41.7 1.9 %collective-permute-start.2 = (f32[25,8,128]{2,1,0:T(8,128)S(1)}, f32[25,8,128]{2,1,0:T(8,128)S(1)}, u32[]{:S(2)}, u32[]{:S(2)}) collective-permute-start(f32[25,8,128]{2,1,0:T(8,128)S(1)} %get-tuple-element.13), channel_id=1, source_target_pairs={{0,2},{1,3},{2,0},{3,1},{4,6},{5,7},{6,4},{7,5},{8,10},{9,11},{10,... | collective-permute-start | bytes 307208 | tf_op jit(solution)/shard_map/ppermute | solution.py:368
  43.6 4.9 %collective-permute-start.3 = (f32[25,8,128]{2,1,0:T(8,128)S(1)}, f32[25,8,128]{2,1,0:T(8,128)S(1)}, u32[]{:S(2)}, u32[]{:S(2)}) collective-permute-start(f32[25,8,128]{2,1,0:T(8,128)S(1)} %get-tuple-element.14), channel_id=1, source_target_pairs={{0,30},{1,31},{2,4},{3,5},{4,2},{5,3},{6,8},{7,9},{8,6},{9,7},{10,... | collective-permute-start | bytes 307208 | tf_op jit(solution)/shard_map/ppermute | solution.py:368
  48.5 5.8 %collective-permute-done.2.one_far_ref = f32[25,8,128]{2,1,0:T(8,128)S(1)} collective-permute-done((f32[25,8,128]{2,1,0:T(8,128)S(1)}, f32[25,8,128]{2,1,0:T(8,128)S(1)}, u32[]{:S(2)}, u32[]{:S(2)}) %collective-permute-start.2) | collective-permute-done | bytes 102432 | tf_op jit(solution)/shard_map/ppermute | solution.py:368
  54.3 0.0 collective-permute-done.3.two_far_ref
  54.3 0.0 collective-permute-done.1.two_ref
  54.3 0.2 collective-permute-done.one_ref
  54.5 0.0 copy-done.3
  54.5 5.2 %shard_map.70 = (f32[8,11,8,128]{3,2,1,0:T(8,128)S(1)}, f32[8,11,8,128]{3,2,1,0:T(8,128)S(1)}, f32[8,11,8,128]{3,2,1,0:T(8,128)S(1)}, f32[8,11,8,128]{3,2,1,0:T(8,128)S(1)}, f32[64,1,128]{2,1,0:T(1,128)S(1)}) custom-call(f32[91,8,128]{2,1,0:T(8,128)S(1)} %collective-permute-done.one_ref, f32[91,8,128]{2,1,0:T(8,128)S(1)} %collective-permute-done.1.two_ref, ...), custom_call_target="tpu_custom_call" | custom-call | tf_op jit(solution)/shard_map/pallas_call | solution.py:416
  59.7 16.7 %all_to_all.20 = f32[64,1,128]{2,1,0:T(1,128)S(1)} all-to-all(f32[64,1,128]{2,1,0:T(1,128)S(1)} %get-tuple-element.15), channel_id=1, replica_groups={{0,1,2,3,32,33,34,35,64,65,66,67,96,97,98,99,128,129,130,131,160,161,16..., dimensions={0} | all-to-all | bytes 65536 | tf_op jit(solution)/shard_map/all_to_all | solution.py:431
  76.4 0.1 reduce_sum.9
  76.5 8.9 %all_to_all.21.sums_ref = f32[8,1,128]{2,1,0:T(1,128)S(1)} all-to-all(f32[8,1,128]{2,1,0:T(1,128)S(1)} %broadcast_in_dim.2), channel_id=1, replica_groups={{0,4,8,12,16,20,24,28},{1,5,9,13,17,21,25,29},{2,6,10,14,18,22,26,30},{..., dimensions={0} | all-to-all | bytes 8192 | tf_op jit(solution)/shard_map/all_to_all | solution.py:435
  85.4 1.3 %shard_map.71 = f32[16,64,128]{2,1,0:T(8,128)S(1)} custom-call(f32[128,128]{1,0:T(8,128)S(1)} %copy-done.2, f32[8,1,128]{2,1,0:T(1,128)S(1)} %all_to_all.21.sums_ref, f32[8,11,8,128]{3,2,1,0:T(8,128)S(1)} %get-tuple-element.16.one_ref, f32[8,11,8,128]{3,2,1,0:T(8,128)S(1)} %get-tuple-element.17.two_ref, f32[8,11,8,128]{3,2,1,0:T(8,128)S(1)} %get-tuple-element.18.three_ref, ...), custom_call_target="tpu_custom_call" | custom-call | tf_op jit(solution)/shard_map/pallas_call | solution.py:436
  86.8 0.0 copy-start.1
  86.8 22.0 %all_to_all.22.source_ref = f32[16,64,128]{2,1,0:T(8,128)S(1)} all-to-all(f32[16,64,128]{2,1,0:T(8,128)S(1)} %shard_map.71), channel_id=1, replica_groups=mesh['tm'=16,'space'=32] {'tm'}, dimensions={0} | all-to-all | bytes 1048576 | tf_op jit(solution)/shard_map/all_to_all | solution.py:441
  108.8 0.0 copy-done.1
  108.8 1.0 shard_map.72
  (4 shorter events, 0.0 us)
Async XLA Ops:
  0.6 1.0 copy-start
  2.6 24.8 %all-to-all-start = ((f32[16,48,128]{2,1,0:T(8,128)}), f32[16,48,128]{2,1,0:T(8,128)S(1)}, u32[]{:S(2)}, u32[]{:S(2)}) async-start(f32[16,48,128]{2,1,0:T(8,128)} %shard_map.68), calls=%async_computation | async-start | bytes 786432 | tf_op jit(solution)/shard_map/all_to_all | solution.py:387
  12.8 0.8 copy-start.4
  13.7 0.8 copy-start.5
  14.5 12.9 %copy-start.2 = (f32[128,128]{1,0:T(8,128)S(1)}, f32[128,128]{1,0:T(8,128)}, u32[]{:S(2)}) copy-start(f32[128,128]{1,0:T(8,128)} %constant.48.clone.cas_ref) | copy-start | bytes 196612
  14.8 39.7 %copy-start.3 = (f32[10,8,128]{2,1,0:T(8,128)S(1)}, f32[10,8,128]{2,1,0:T(8,128)}, u32[]{:S(2)}) copy-start(f32[10,8,128]{2,1,0:T(8,128)} %constant.49.clone.coef_ref) | copy-start | bytes 122884
  28.5 25.8 %collective-permute-start.1 = (f32[91,8,128]{2,1,0:T(8,128)S(1)}, f32[91,8,128]{2,1,0:T(8,128)S(1)}, u32[]{:S(2)}, u32[]{:S(2)}) collective-permute-start(f32[91,8,128]{2,1,0:T(8,128)S(1)} %get-tuple-element.12.field_ref), channel_id=1, source_target_pairs={{0,31},{1,2},{2,1},{3,4},{4,3},{5,6},{6,5},{7,8},{8,7},{9,10},{10,... | collective-permute-start | bytes 1118216 | tf_op jit(solution)/shard_map/ppermute | solution.py:368
  39.8 14.7 %collective-permute-start = (f32[91,8,128]{2,1,0:T(8,128)S(1)}, f32[91,8,128]{2,1,0:T(8,128)S(1)}, u32[]{:S(2)}, u32[]{:S(2)}) collective-permute-start(f32[91,8,128]{2,1,0:T(8,128)S(1)} %get-tuple-element.12.field_ref), channel_id=1, source_target_pairs={{0,1},{1,0},{2,3},{3,2},{4,5},{5,4},{6,7},{7,6},{8,9},{9,8},{10,11... | collective-permute-start | bytes 1118216 | tf_op jit(solution)/shard_map/ppermute | solution.py:368
  41.7 12.6 %collective-permute-start.2 = (f32[25,8,128]{2,1,0:T(8,128)S(1)}, f32[25,8,128]{2,1,0:T(8,128)S(1)}, u32[]{:S(2)}, u32[]{:S(2)}) collective-permute-start(f32[25,8,128]{2,1,0:T(8,128)S(1)} %get-tuple-element.13), channel_id=1, source_target_pairs={{0,2},{1,3},{2,0},{3,1},{4,6},{5,7},{6,4},{7,5},{8,10},{9,11},{10,... | collective-permute-start | bytes 307208 | tf_op jit(solution)/shard_map/ppermute | solution.py:368
  43.6 10.6 %collective-permute-start.3 = (f32[25,8,128]{2,1,0:T(8,128)S(1)}, f32[25,8,128]{2,1,0:T(8,128)S(1)}, u32[]{:S(2)}, u32[]{:S(2)}) collective-permute-start(f32[25,8,128]{2,1,0:T(8,128)S(1)} %get-tuple-element.14), channel_id=1, source_target_pairs={{0,30},{1,31},{2,4},{3,5},{4,2},{5,3},{6,8},{7,9},{8,6},{9,7},{10,... | collective-permute-start | bytes 307208 | tf_op jit(solution)/shard_map/ppermute | solution.py:368
  86.8 22.0 %copy-start.1 = (f32[8,8,1024]{2,1,0:T(8,128)S(1)}, f32[8,8,1024]{2,1,0:T(8,128)}, u32[]{:S(2)}) copy-start(f32[8,8,1024]{2,1,0:T(8,128)} %param.5) | copy-start | bytes 786436

commit v9 on v8

--- a/solution.py
+++ b/solution.py
@@ -111,7 +111,7 @@
 def forward_kernel(
     rows, times, length, cas_ref, field_ref, local_ref, place_ref, out_ref, one_ref, two_ref, line_ref
 ):
-    second = place_ref[1] == 1
+    second = place_ref[1]
     half = LANES // 2
     span = half + 2 * SIDE
     pieces = field_ref.shape[1] // times
@@ -136,11 +136,10 @@
         for column in range(BLOCK):
             value = line_ref[pl.ds(row * span + skip + column, SUB, stride=BLOCK), :]
             out_ref[row * BLOCK + column] = value
+    last = (rows - FAR) * BLOCK
     for index in range(FAR * BLOCK):
-        low = out_ref[index]
-        high = out_ref[(rows - FAR) * BLOCK + index]
-        one_ref[index] = jnp.where(second, low, high)
-        two_ref[index] = jnp.where(second, high, low)
+        one_ref[index] = out_ref[last - last * second + index]
+        two_ref[index] = out_ref[last * second + index]
     for ref in (out_ref, one_ref, two_ref):
         first = ref.shape[0] - 3
         for plane in range(3):
@@ -221,7 +220,7 @@
 
 
 def stencil_kernel(
-    rows, one_ref, two_ref, one_far_ref, two_far_ref, field_ref, coef_ref, place_ref,
+    rows, two_ref, one_ref, one_far_ref, two_far_ref, field_ref, coef_ref, place_ref,
     solved_ref, applied_ref, solved_two_ref, applied_two_ref, sums_ref,
     step_ref, remain_ref, part_ref, middle_ref, wide_ref, scratch_ref, near_ref, far_ref,
 ):
@@ -427,7 +426,7 @@
             (2, *far_shape),
         ],
         inputs=7,
-    )(inner, outer, inner_far, outer_far, freq, coef_table, place)
+    )(outer, inner, inner_far, outer_far, freq, coef_table, place)
     sums = lax.all_to_all(sums, ("tm", "space"), 0, 0, axis_index_groups=groups)
     planes = spaces // NEAR
     groups = [[first + NEAR * i for i in range(planes)] for first in range(NEAR)]

time: 110 us -> 111 us (level)
    all_to_all x1, blocking collectives: 8.89 us -> 12 us  [shards(): sums = lax.all_to_all(sums, 'space', 0, 0, axis_index_groups=groups)]
    all_to_all x1, blocking collectives: 16.7 us -> 13.7 us  [shards(): sums = lax.all_to_all(sums, ('tm', 'space'), 0, 0, axis_index_groups=groups)]
where the time goes in v9:
time: 111 us
  blocking collectives  48 us (43%)
  starting transfers between devices  30.7 us (28%)
  waiting for transfers between devices  18.9 us (17%)
  Pallas kernels  9.65 us (9%)
  local copies, waits for them, and re-layouts  2.77 us (2%)
    all_to_all x1, blocking collectives, shards(): returned = lax.all_to_all(packed, 'tm', 0, 0)  22.3 us
    ppermute x4, starting transfers between devices, swap(): return lax.ppermute(value, 'space', pairs)  20.5 us
    all_to_all x1, blocking collectives, shards(): sums = lax.all_to_all(sums, ('tm', 'space'), 0, 0, axis_index_groups=groups)  13.7 us
    all_to_all x1, waiting for transfers between devices, shards(): gathered = lax.all_to_all(windows, 'tm', 0, 0)  12.6 us
    all_to_all x1, blocking collectives, shards(): sums = lax.all_to_all(sums, 'space', 0, 0, axis_index_groups=groups)  12 us
    all_to_all x1, starting transfers between devices, shards(): gathered = lax.all_to_all(windows, 'tm', 0, 0)  10.2 us
    ppermute x4, waiting for transfers between devices, swap(): return lax.ppermute(value, 'space', pairs)  6.28 us
    pallas_call x1, Pallas kernels, shards(): call(functools.partial(stencil_kernel, rows), [tile_shape] * 4 + [(tiles...  5.19 us
  transfers between devices with their start and end apart: 5, of which 3 were waited for; matrix products, arithmetic and copies ran while one was open for 0% of the time, Pallas kernels for 0%

profile of v9, /device:TPU:1, one launch (start us, length us, event | category | flops | bytes accessed | tf_op | source)
XLA Modules:
  0.0 110.9 jit_solution(15122574286389270683)
XLA Ops:
  0.6 0.0 copy-start
  0.6 0.9 copy-done
  1.6 1.0 shard_map.68
  2.6 10.2 %all-to-all-start = ((f32[16,48,128]{2,1,0:T(8,128)}), f32[16,48,128]{2,1,0:T(8,128)S(1)}, u32[]{:S(2)}, u32[]{:S(2)}) async-start(f32[16,48,128]{2,1,0:T(8,128)} %shard_map.68), calls=%async_computation | async-start | bytes 786432 | tf_op jit(solution)/shard_map/all_to_all | solution.py:386
  12.8 0.0 copy-start.4
  12.9 0.8 copy-done.4
  13.7 0.0 copy-start.5
  13.7 0.7 copy-done.5
  14.4 0.1 fusion
  14.5 0.0 copy-start.2
  14.5 0.1 concatenate.7
  14.6 0.1 pad_add_fusion.place_ref
  14.7 0.1 constant_dynamic-slice_fusion.local_ref
  14.8 0.0 copy-start.3
  14.8 12.6 %all-to-all-done.field_ref = f32[16,48,128]{2,1,0:T(8,128)S(1)} async-done(((f32[16,48,128]{2,1,0:T(8,128)}), f32[16,48,128]{2,1,0:T(8,128)S(1)}, u32[]{:S(2)}, u32[]{:S(2)}) %all-to-all-start) | async-done | bytes 393248 | tf_op jit(solution)/shard_map/all_to_all | solution.py:386
  27.4 0.0 copy-done.2
  27.4 1.1 %shard_map.69 = (f32[91,8,128]{2,1,0:T(8,128)S(1)}, f32[25,8,128]{2,1,0:T(8,128)S(1)}, f32[25,8,128]{2,1,0:T(8,128)S(1)}) custom-call(f32[128,128]{1,0:T(8,128)S(1)} %copy-done.2, f32[16,48,128]{2,1,0:T(8,128)S(1)} %all-to-all-done.field_ref, f32[24,128]{1,0:T(8,128)S(1)} %constant_dynamic-slice_fusion.local_ref, s32[2]{0:T(128)S(1)} %pad_add_fusion.place_ref), custom_call_target="tpu_custom_call" | custom-call | tf_op jit(solution)/shard_map/pallas_call | solution.py:399
  28.5 1.9 %collective-permute-start.1 = (f32[91,8,128]{2,1,0:T(8,128)S(1)}, f32[91,8,128]{2,1,0:T(8,128)S(1)}, u32[]{:S(2)}, u32[]{:S(2)}) collective-permute-start(f32[91,8,128]{2,1,0:T(8,128)S(1)} %get-tuple-element.12.field_ref), channel_id=1, source_target_pairs={{0,1},{1,0},{2,3},{3,2},{4,5},{5,4},{6,7},{7,6},{8,9},{9,8},{10,11... | collective-permute-start | bytes 1118216 | tf_op jit(solution)/shard_map/ppermute | solution.py:367
  30.4 11.8 %collective-permute-start = (f32[91,8,128]{2,1,0:T(8,128)S(1)}, f32[91,8,128]{2,1,0:T(8,128)S(1)}, u32[]{:S(2)}, u32[]{:S(2)}) collective-permute-start(f32[91,8,128]{2,1,0:T(8,128)S(1)} %get-tuple-element.12.field_ref), channel_id=1, source_target_pairs={{0,31},{1,2},{2,1},{3,4},{4,3},{5,6},{6,5},{7,8},{8,7},{9,10},{10,... | collective-permute-start | bytes 1118216 | tf_op jit(solution)/shard_map/ppermute | solution.py:367
  42.2 1.9 %collective-permute-start.2 = (f32[25,8,128]{2,1,0:T(8,128)S(1)}, f32[25,8,128]{2,1,0:T(8,128)S(1)}, u32[]{:S(2)}, u32[]{:S(2)}) collective-permute-start(f32[25,8,128]{2,1,0:T(8,128)S(1)} %get-tuple-element.13), channel_id=1, source_target_pairs={{0,2},{1,3},{2,0},{3,1},{4,6},{5,7},{6,4},{7,5},{8,10},{9,11},{10,... | collective-permute-start | bytes 307208 | tf_op jit(solution)/shard_map/ppermute | solution.py:367
  44.2 4.9 %collective-permute-start.3 = (f32[25,8,128]{2,1,0:T(8,128)S(1)}, f32[25,8,128]{2,1,0:T(8,128)S(1)}, u32[]{:S(2)}, u32[]{:S(2)}) collective-permute-start(f32[25,8,128]{2,1,0:T(8,128)S(1)} %get-tuple-element.14), channel_id=1, source_target_pairs={{0,30},{1,31},{2,4},{3,5},{4,2},{5,3},{6,8},{7,9},{8,6},{9,7},{10,... | collective-permute-start | bytes 307208 | tf_op jit(solution)/shard_map/ppermute | solution.py:367
  49.0 3.5 %collective-permute-done.2.one_far_ref = f32[25,8,128]{2,1,0:T(8,128)S(1)} collective-permute-done((f32[25,8,128]{2,1,0:T(8,128)S(1)}, f32[25,8,128]{2,1,0:T(8,128)S(1)}, u32[]{:S(2)}, u32[]{:S(2)}) %collective-permute-start.2) | collective-permute-done | bytes 102432 | tf_op jit(solution)/shard_map/ppermute | solution.py:367
  52.5 2.8 %collective-permute-done.3.two_far_ref = f32[25,8,128]{2,1,0:T(8,128)S(1)} collective-permute-done((f32[25,8,128]{2,1,0:T(8,128)S(1)}, f32[25,8,128]{2,1,0:T(8,128)S(1)}, u32[]{:S(2)}, u32[]{:S(2)}) %collective-permute-start.3) | collective-permute-done | bytes 102432 | tf_op jit(solution)/shard_map/ppermute | solution.py:367
  55.3 0.0 collective-permute-done.1.one_ref
  55.3 0.0 collective-permute-done.two_ref
  55.3 0.0 copy-done.3
  55.3 5.2 %shard_map.70 = (f32[8,11,8,128]{3,2,1,0:T(8,128)S(1)}, f32[8,11,8,128]{3,2,1,0:T(8,128)S(1)}, f32[8,11,8,128]{3,2,1,0:T(8,128)S(1)}, f32[8,11,8,128]{3,2,1,0:T(8,128)S(1)}, f32[64,1,128]{2,1,0:T(1,128)S(1)}) custom-call(f32[91,8,128]{2,1,0:T(8,128)S(1)} %collective-permute-done.two_ref, f32[91,8,128]{2,1,0:T(8,128)S(1)} %collective-permute-done.1.one_ref, ...), custom_call_target="tpu_custom_call" | custom-call | tf_op jit(solution)/shard_map/pallas_call | solution.py:415
  60.5 13.7 %all_to_all.20 = f32[64,1,128]{2,1,0:T(1,128)S(1)} all-to-all(f32[64,1,128]{2,1,0:T(1,128)S(1)} %get-tuple-element.15), channel_id=1, replica_groups={{0,1,2,3,32,33,34,35,64,65,66,67,96,97,98,99,128,129,130,131,160,161,16..., dimensions={0} | all-to-all | bytes 65536 | tf_op jit(solution)/shard_map/all_to_all | solution.py:430
  74.2 0.1 reduce_sum.9
  74.3 12.0 %all_to_all.21.sums_ref = f32[8,1,128]{2,1,0:T(1,128)S(1)} all-to-all(f32[8,1,128]{2,1,0:T(1,128)S(1)} %broadcast_in_dim.2), channel_id=1, replica_groups={{0,4,8,12,16,20,24,28},{1,5,9,13,17,21,25,29},{2,6,10,14,18,22,26,30},{..., dimensions={0} | all-to-all | bytes 8192 | tf_op jit(solution)/shard_map/all_to_all | solution.py:434
  86.3 1.3 %shard_map.71 = f32[16,64,128]{2,1,0:T(8,128)S(1)} custom-call(f32[128,128]{1,0:T(8,128)S(1)} %copy-done.2, f32[8,1,128]{2,1,0:T(1,128)S(1)} %all_to_all.21.sums_ref, f32[8,11,8,128]{3,2,1,0:T(8,128)S(1)} %get-tuple-element.16.one_ref, f32[8,11,8,128]{3,2,1,0:T(8,128)S(1)} %get-tuple-element.17.two_ref, f32[8,11,8,128]{3,2,1,0:T(8,128)S(1)} %get-tuple-element.18.three_ref, ...), custom_call_target="tpu_custom_call" | custom-call | tf_op jit(solution)/shard_map/pallas_call | solution.py:435
  87.6 0.0 copy-start.1
  87.6 22.3 %all_to_all.22.source_ref = f32[16,64,128]{2,1,0:T(8,128)S(1)} all-to-all(f32[16,64,128]{2,1,0:T(8,128)S(1)} %shard_map.71), channel_id=1, replica_groups=mesh['tm'=16,'space'=32] {'tm'}, dimensions={0} | all-to-all | bytes 1048576 | tf_op jit(solution)/shard_map/all_to_all | solution.py:440
  109.9 0.0 copy-done.1
  109.9 1.0 shard_map.72
  (4 shorter events, 0.0 us)
Async XLA Ops:
  0.6 1.0 copy-start
  2.6 24.8 %all-to-all-start = ((f32[16,48,128]{2,1,0:T(8,128)}), f32[16,48,128]{2,1,0:T(8,128)S(1)}, u32[]{:S(2)}, u32[]{:S(2)}) async-start(f32[16,48,128]{2,1,0:T(8,128)} %shard_map.68), calls=%async_computation | async-start | bytes 786432 | tf_op jit(solution)/shard_map/all_to_all | solution.py:386
  12.8 0.8 copy-start.4
  13.7 0.8 copy-start.5
  14.5 12.9 %copy-start.2 = (f32[128,128]{1,0:T(8,128)S(1)}, f32[128,128]{1,0:T(8,128)}, u32[]{:S(2)}) copy-start(f32[128,128]{1,0:T(8,128)} %constant.48.clone.cas_ref) | copy-start | bytes 196612
  14.8 40.5 %copy-start.3 = (f32[10,8,128]{2,1,0:T(8,128)S(1)}, f32[10,8,128]{2,1,0:T(8,128)}, u32[]{:S(2)}) copy-start(f32[10,8,128]{2,1,0:T(8,128)} %constant.49.clone.coef_ref) | copy-start | bytes 122884
  28.5 26.8 %collective-permute-start.1 = (f32[91,8,128]{2,1,0:T(8,128)S(1)}, f32[91,8,128]{2,1,0:T(8,128)S(1)}, u32[]{:S(2)}, u32[]{:S(2)}) collective-permute-start(f32[91,8,128]{2,1,0:T(8,128)S(1)} %get-tuple-element.12.field_ref), channel_id=1, source_target_pairs={{0,1},{1,0},{2,3},{3,2},{4,5},{5,4},{6,7},{7,6},{8,9},{9,8},{10,11... | collective-permute-start | bytes 1118216 | tf_op jit(solution)/shard_map/ppermute | solution.py:367
  30.4 24.9 %collective-permute-start = (f32[91,8,128]{2,1,0:T(8,128)S(1)}, f32[91,8,128]{2,1,0:T(8,128)S(1)}, u32[]{:S(2)}, u32[]{:S(2)}) collective-permute-start(f32[91,8,128]{2,1,0:T(8,128)S(1)} %get-tuple-element.12.field_ref), channel_id=1, source_target_pairs={{0,31},{1,2},{2,1},{3,4},{4,3},{5,6},{6,5},{7,8},{8,7},{9,10},{10,... | collective-permute-start | bytes 1118216 | tf_op jit(solution)/shard_map/ppermute | solution.py:367
  42.2 10.3 %collective-permute-start.2 = (f32[25,8,128]{2,1,0:T(8,128)S(1)}, f32[25,8,128]{2,1,0:T(8,128)S(1)}, u32[]{:S(2)}, u32[]{:S(2)}) collective-permute-start(f32[25,8,128]{2,1,0:T(8,128)S(1)} %get-tuple-element.13), channel_id=1, source_target_pairs={{0,2},{1,3},{2,0},{3,1},{4,6},{5,7},{6,4},{7,5},{8,10},{9,11},{10,... | collective-permute-start | bytes 307208 | tf_op jit(solution)/shard_map/ppermute | solution.py:367
  44.2 11.2 %collective-permute-start.3 = (f32[25,8,128]{2,1,0:T(8,128)S(1)}, f32[25,8,128]{2,1,0:T(8,128)S(1)}, u32[]{:S(2)}, u32[]{:S(2)}) collective-permute-start(f32[25,8,128]{2,1,0:T(8,128)S(1)} %get-tuple-element.14), channel_id=1, source_target_pairs={{0,30},{1,31},{2,4},{3,5},{4,2},{5,3},{6,8},{7,9},{8,6},{9,7},{10,... | collective-permute-start | bytes 307208 | tf_op jit(solution)/shard_map/ppermute | solution.py:367
  87.6 22.3 %copy-start.1 = (f32[8,8,1024]{2,1,0:T(8,128)S(1)}, f32[8,8,1024]{2,1,0:T(8,128)}, u32[]{:S(2)}) copy-start(f32[8,8,1024]{2,1,0:T(8,128)} %param.5) | copy-start | bytes 786436

commit v10 on v7

--- a/solution.py
+++ b/solution.py
@@ -145,20 +145,23 @@
             ref[first + plane] = local_ref[plane * rows : (plane + 1) * rows, :]
 
 
-def weight_lines(rows, refs, scratch_ref):
-    planes = []
-    for plane in range(3):
-        blocks = [ref[ref.shape[0] - 3 + plane] for ref in refs]
-        blocks[0] = blocks[0][rows - FAR :]
-        blocks[-1] = blocks[-1][:FAR]
-        planes.append(jnp.concatenate(blocks, axis=0))
+def weight_lines(parts, scratch_ref):
+    planes = [jnp.concatenate(blocks, axis=0) for blocks in zip(*parts)]
     east = 1.0 + 0.125 * (planes[1] + jnp.concatenate([planes[1][1:], planes[1][:1]], axis=0))
     north = 1.0 + 0.125 * (planes[2] + pltpu.roll(planes[2], LANES - 1, 1))
-    total = planes[0].shape[0]
-    zero = jnp.zeros((LANES - 3 * total, LANES), jnp.float32)
+    zero = jnp.zeros((LANES - 3 * planes[0].shape[0], LANES), jnp.float32)
     scratch_ref[...] = jnp.transpose(jnp.concatenate([planes[0], east, north, zero], axis=0))
     skip = (LANES - WINDOW) // 2
     return [scratch_ref[pl.ds(skip + column, SUB, stride=BLOCK), :] for column in range(BLOCK)]
+
+
+def weight_part(ref):
+    return [ref[ref.shape[0] - 3 + plane] for plane in range(3)]
+
+
+def spread(lines, index, plane, coef):
+    value = jnp.broadcast_to(lines[:, index : index + 1], (SUB, LANES))
+    return value + coef[0] if plane == 0 else value
 
 
 def own_columns(column):
@@ -167,7 +170,26 @@
     return (place >= first) & (place < first + LANES // 2)
 
 
-def passes(edge, own, total, source, weight, coef, step_ref, remain_ref, solved_ref, emit):
+def stencil(weight, row, above, here, below, flux=None):
+    columns = range(BLOCK)
+    if flux is None:
+        flux = [weight(1, row - 1, column) * (above[column] - here[column]) for column in columns]
+    ahead = [weight(1, row, column) * (here[column] - below[column]) for column in columns]
+    beside = here[1:] + [pltpu.roll(here[0], SUB - 1, 0)]
+    side = [weight(2, row, column) * (here[column] - beside[column]) for column in columns]
+    behind = [pltpu.roll(side[-1], 1, 0)] + side[:-1]
+    applied = [
+        weight(0, row, column) * here[column]
+        + (ahead[column] - flux[column])
+        + (side[column] - behind[column])
+        for column in columns
+    ]
+    return applied, ahead
+
+
+def passes(
+    edge, own, total, source, weight, coef, step_ref, remain_ref, solved_ref, emit, border=None
+):
     columns = range(BLOCK)
 
     for turn in range(CHEB + 1):
@@ -178,108 +200,179 @@
                 return [coef[1] * source(row, column) for column in columns]
             return [step_ref[row, column] for column in columns]
 
-        here = load(first - 1)
+        above, here = load(first - 1), load(first)
         flux = None
-        for row in range(first - 1, last):
-            after = load(row + 1)
-            ahead = [weight(1, row, column) * (here[column] - after[column]) for column in columns]
-            if row >= first:
-                beside = here[1:] + [pltpu.roll(here[0], SUB - 1, 0)]
-                side = [weight(2, row, column) * (here[column] - beside[column]) for column in columns]
-                behind = [pltpu.roll(side[-1], 1, 0)] + side[:-1]
-                inside = row in range(*own)
-                results = []
-                for column in columns:
-                    applied = (
-                        weight(0, row, column) * here[column]
-                        + (ahead[column] - flux[column])
-                        + (side[column] - behind[column])
+        for row in range(first, last):
+            below = load(row + 1)
+            if border and row == first:
+                border(0, turn, here)
+            if border and row == last - 1:
+                border(1, turn, here)
+            applied, flux = stencil(weight, row, above, here, below, flux)
+            inside = row in range(*own)
+            results = []
+            for column in columns:
+                before = source(row, column) if turn == 0 else remain_ref[row, column]
+                left = before - applied[column]
+                if turn < CHEB:
+                    remain_ref[row, column] = left
+                    step_ref[row, column] = (
+                        coef[2 + 2 * turn] * here[column] + coef[3 + 2 * turn] * left
                     )
-                    before = source(row, column) if turn == 0 else remain_ref[row, column]
-                    left = before - applied
+                solved = None
+                if inside:
+                    place = row - own[0]
+                    solved = here[column]
+                    if turn > 0:
+                        solved = solved_ref[place, column] + solved
                     if turn < CHEB:
-                        remain_ref[row, column] = left
-                        step_ref[row, column] = (
-                            coef[2 + 2 * turn] * here[column] + coef[3 + 2 * turn] * left
-                        )
-                    solved = None
-                    if inside:
-                        place = row - own[0]
-                        solved = here[column]
-                        if turn > 0:
-                            solved = solved_ref[place, column] + solved
-                        if turn < CHEB:
-                            solved_ref[place, column] = solved
-                    if turn == CHEB:
-                        begun = source(row, column)
-                        results.append((begun, solved, begun - left))
+                        solved_ref[place, column] = solved
                 if turn == CHEB:
-                    emit(row, *zip(*results))
-            here, flux = after, ahead
-
-
-def stencil_kernel(
+                    begun = source(row, column)
+                    results.append((begun, solved, begun - left))
+            if turn == CHEB:
+                emit(row, *zip(*results))
+            above, here = here, below
+
+
+def add_products(sums, index, one, two):
+    for column in range(BLOCK):
+        product = one[column] * two[column]
+        sums[index] = sums[index] + jnp.where(own_columns(column), product, 0.0)
+
+
+def near_kernel(
+    rows, top_ref, field_ref, bottom_ref, coef_ref,
+    solved_ref, middle_ref, step_ref, remain_ref, border_ref, wide_ref, early_ref,
+    part_ref, scratch_ref,
+):
+    refs = (top_ref, field_ref, bottom_ref)
+    lines = weight_lines([weight_part(ref) for ref in refs], scratch_ref)
+    coef = [coef_ref[index] for index in range(2 + 2 * CHEB)]
+    places = [None] * FAR + [(ref, row) for ref in refs for row in range(rows)]
+    total = 3 * rows + 2 * FAR
+    own = (FAR + rows, FAR + 2 * rows)
+    made = set()
+
+    def weight(plane, row, column):
+        place = plane * BLOCK + column
+        if (row, place) not in made:
+            made.add((row, place))
+            wide_ref[row, place] = spread(lines[column], plane * 3 * rows + row - FAR, plane, coef)
+        return wide_ref[row, place]
+
+    def source(row, column):
+        ref, place = places[row]
+        return ref[place * BLOCK + column]
+
+    sums = [jnp.zeros((SUB, LANES), jnp.float32) for _ in range(2)]
+
+    def emit(row, begun, solved, applied):
+        for column in range(BLOCK):
+            middle_ref[row, column] = applied[column]
+        if row in range(*own):
+            for column in range(BLOCK):
+                solved_ref[row - own[0], column] = solved[column]
+            add_products(sums, 0, begun, solved)
+            add_products(sums, 1, solved, applied)
+
+    def border(side, turn, step):
+        for column in range(BLOCK):
+            border_ref[side, turn, column] = step[column]
+
+    passes(
+        FAR, own, total, source, weight, coef, step_ref, remain_ref, part_ref, emit, border
+    )
+    early_ref[0] = sums[0]
+    early_ref[1] = sums[1]
+
+
+def far_kernel(
     rows, top_far_ref, top_ref, field_ref, bottom_ref, bottom_far_ref, coef_ref,
-    solved_ref, applied_ref, solved_two_ref, applied_two_ref, sums_ref,
-    step_ref, remain_ref, part_ref, middle_ref, wide_ref, scratch_ref,
+    middle_ref, frozen_step_ref, frozen_remain_ref, border_ref, wide_ref, early_ref,
+    solved_ref, applied_ref, sums_ref,
+    step_ref, remain_ref, part_ref, outer_ref, scratch_ref,
 ):
     columns = range(BLOCK)
     refs = (top_far_ref, top_ref, field_ref, bottom_ref, bottom_far_ref)
-    lines = weight_lines(rows, refs, scratch_ref)
+    parts = [weight_part(ref) for ref in refs]
+    parts[0] = [block[rows - FAR :] for block in parts[0]]
+    parts[-1] = [block[:FAR] for block in parts[-1]]
+    lines = weight_lines(parts, scratch_ref)
     coef = [coef_ref[index] for index in range(2 + 2 * CHEB)]
+    total = 3 * rows + 2 * FAR
+    own = (FAR + rows, FAR + 2 * rows)
     places = [
         (ref, row) for ref in refs for row in range((ref.shape[0] - 3) // BLOCK)
     ]
-    total = len(places)
-    own = (FAR + rows, FAR + 2 * rows)
-    made = set()
+    made = {}
 
     def weight(plane, row, column):
-        place = plane * BLOCK + column
-        if (row, place) in made:
-            return wide_ref[row, place]
-        index = plane * total + row
-        value = jnp.broadcast_to(lines[column][:, index : index + 1], (SUB, LANES))
-        if plane == 0:
-            value = value + coef[0]
-        wide_ref[row, place] = value
-        made.add((row, place))
-        return value
-
-    def first_source(row, column):
+        if FAR < row < total - FAR - 1 or (plane == 1 and row == FAR):
+            return wide_ref[row, plane * BLOCK + column]
+        key = (plane, row, column)
+        if key not in made:
+            made[key] = spread(lines[column], plane * total + row, plane, coef)
+        return made[key]
+
+    def source(row):
         ref, place = places[row]
-        return ref[place * BLOCK + column]
-
-    def second_source(row, column):
+        return [ref[place * BLOCK + column] for column in columns]
+
+    for side in range(2):
+
+        def at(index, side=side):
+            return total - 1 - index if side else index
+
+        ends = [[coef[1] * value for value in source(at(index))] for index in range(FAR)]
+        rest = source(at(1))
+        for turn in range(CHEB + 1):
+            edge_row = at(turn + 2)
+            if turn == 0:
+                inner = [coef[1] * value for value in source(edge_row)]
+                inner_rest = source(edge_row)
+            else:
+                inner = [frozen_step_ref[edge_row, column] for column in columns]
+                inner_rest = [frozen_remain_ref[edge_row, column] for column in columns]
+            steps = ends + [inner, [border_ref[side, turn, column] for column in columns]]
+            new_ends, new_rest = [], []
+            for index, before in ((1, rest), (2, inner_rest)):
+                row = at(turn + index)
+                near, away = steps[index - 1], steps[index + 1]
+                above, below = (away, near) if side else (near, away)
+                here = steps[index]
+                applied, _ = stencil(weight, row, above, here, below)
+                left = [before[column] - applied[column] for column in columns]
+                new_rest.append(left)
+                if turn < CHEB:
+                    new_ends.append(
+                        [
+                            coef[2 + 2 * turn] * here[column] + coef[3 + 2 * turn] * left[column]
+                            for column in columns
+                        ]
+                    )
+                else:
+                    begun = source(row)
+                    for column in columns:
+                        outer_ref[side * FAR + index - 1, column] = begun[column] - left[column]
+            ends, rest = new_ends, new_rest[1]
+
+    def middle(row, column):
+        index = min(row, total - 1 - row)
+        if index < HALO + FAR:
+            return outer_ref[FAR * (row > index) + index - HALO, column]
         return middle_ref[row, column]
 
-    sums = [jnp.zeros((SUB, LANES), jnp.float32) for _ in range(4)]
-
-    def add(index, one, two):
+    sums = [early_ref[0], early_ref[1]] + [jnp.zeros((SUB, LANES), jnp.float32) for _ in range(2)]
+
+    def emit(row, begun, solved, applied):
         for column in columns:
-            product = one[column] * two[column]
-            sums[index] = sums[index] + jnp.where(own_columns(column), product, 0.0)
-
-    def emit_first(row, source, solved, applied):
-        for column in columns:
-            middle_ref[row, column] = applied[column]
-        if row in range(*own):
-            for column in columns:
-                solved_ref[row - own[0], column] = solved[column]
-                applied_ref[row - own[0], column] = applied[column]
-            add(0, source, solved)
-            add(1, solved, applied)
-
-    def emit_second(row, source, solved, applied):
-        for column in columns:
-            solved_two_ref[row - own[0], column] = solved[column]
-            applied_two_ref[row - own[0], column] = applied[column]
-        add(2, source, solved)
-        add(3, solved, applied)
-
-    work = (weight, coef, step_ref, remain_ref, part_ref)
-    passes(0, own, total, first_source, *work, emit_first)
-    passes(HALO, own, total, second_source, *work, emit_second)
+            solved_ref[row - own[0], column] = solved[column]
+            applied_ref[row - own[0], column] = applied[column]
+        add_products(sums, 2, begun, solved)
+        add_products(sums, 3, solved, applied)
+
+    passes(HALO, own, total, middle, weight, coef, step_ref, remain_ref, part_ref, emit)
 
     lane = lane_index((1, LANES))
     line = jnp.zeros((1, LANES), jnp.float32)
@@ -308,9 +401,10 @@
     second = -next_step * step
     for row in range(rows):
         for index, (left_ref, right_ref) in enumerate(((one_ref, two_ref), (three_ref, four_ref))):
+            offset = left_ref.shape[0] // 2 - rows // 2
             for column in range(BLOCK):
                 start = (2 * row + index) * span + skip + column
-                value = first * left_ref[row, column] + second * right_ref[row, column]
+                value = first * left_ref[offset + row, column] + second * right_ref[row, column]
                 line_ref[pl.ds(start, SUB, stride=BLOCK), :] = value
     for row in range(rows):
         start = 2 * row * span + SIDE
@@ -391,18 +485,26 @@
         for first in range(0, spaces, NEAR)
     ]
     work = (total, BLOCK, SUB, LANES)
-    solved, applied, solved_two, applied_two, sums = call(
-        functools.partial(stencil_kernel, rows),
-        [tile_shape] * 4 + [(tiles * NEAR, 1, LANES)],
+    solved, middle, step, remain, border, wide, early = call(
+        functools.partial(near_kernel, rows),
         [
+            tile_shape,
             work,
             work,
-            tile_shape,
             work,
+            (2, CHEB + 1, BLOCK, SUB, LANES),
             (total, 3 * BLOCK, SUB, LANES),
-            (LANES, LANES),
+            (2, SUB, LANES),
         ],
-    )(top_far, top, freq, bottom, bottom_far, coef_table)
+        [tile_shape, (LANES, LANES)],
+    )(top, freq, bottom, coef_table)
+    solved_two, applied_two, sums = call(
+        functools.partial(far_kernel, rows),
+        [tile_shape, tile_shape, (tiles * NEAR, 1, LANES)],
+        [work, work, tile_shape, (2 * FAR, BLOCK, SUB, LANES), (LANES, LANES)],
+    )(
+        top_far, top, freq, bottom, bottom_far, coef_table, middle, step, remain, border, wide, early
+    )
     sums = lax.all_to_all(sums, ("tm", "space"), 0, 0, axis_index_groups=groups)
     planes = spaces // NEAR
     groups = [[first + NEAR * i for i in range(planes)] for first in range(NEAR)]
@@ -412,7 +514,7 @@
         functools.partial(inverse_kernel, rows, times, length),
         [(tiles, rows * times, LANES)],
         [(rows * 2 * span, LANES)],
-    )(cas_table, sums, solved, solved_two, applied, applied_two)
+    )(cas_table, sums, solved, solved_two, middle, applied_two)
     returned = lax.all_to_all(packed, "tm", 0, 0)
 
     solution, residual = call(

time: 111 us -> 112 us (level)
    pallas_call x1 -> x2, Pallas kernels: 4.65 us -> 5.54 us  [the longest x1 3 us: shards(): call(functools.partial(near_kernel, rows), [tile_shape, work, work, work,...]
  transfers between devices with their start and end apart: 5 -> 5, of which waited for: 4 -> 2; matrix products, arithmetic and copies ran while one was open for 0% -> 0% of each run, Pallas kernels for 0% -> 3%
where the time goes in v10:
time: 112 us; the launch traced here: 111 us
  blocking collectives  43.9 us (39%)
  starting transfers between devices  32.3 us (29%)
  waiting for transfers between devices  23.4 us (21%)
  Pallas kernels  9.48 us (8%)
  local copies, waits for them, and re-layouts  1.24 us (1%)
    ppermute x4, starting transfers between devices, shift(): lax.ppermute(value, 'space', [(i, (i + distance) % spaces) for i in range...  22.1 us
    all_to_all x1, blocking collectives, shards(): returned = lax.all_to_all(packed, 'tm', 0, 0)  21.8 us
    all_to_all x1, waiting for transfers between devices, shards(): gathered = lax.all_to_all(windows, 'tm', 0, 0)  14.2 us
    all_to_all x1, blocking collectives, shards(): sums = lax.all_to_all(sums, ('tm', 'space'), 0, 0, axis_index_groups=groups)  13.2 us
    all_to_all x1, starting transfers between devices, shards(): gathered = lax.all_to_all(windows, 'tm', 0, 0)  10.2 us
    ppermute x4, waiting for transfers between devices, shift(): lax.ppermute(value, 'space', [(i, (i + distance) % spaces) for i in range...  9.14 us
    all_to_all x1, blocking collectives, shards(): sums = lax.all_to_all(sums, 'space', 0, 0, axis_index_groups=groups)  8.89 us
    pallas_call x1, Pallas kernels, shards(): call(functools.partial(near_kernel, rows), [tile_shape, work, work, work,...  3 us
  transfers between devices with their start and end apart: 5, of which 2 were waited for; matrix products, arithmetic and copies ran while one was open for 0% of the time, Pallas kernels for 3%

profile of v10, /device:TPU:1, one launch (start us, length us, event | category | flops | bytes accessed | tf_op | source)
XLA Modules:
  0.0 111.2 jit_solution(3023261426852139462)
XLA Ops:
  0.6 0.0 copy-start
  0.6 0.9 copy-done
  1.6 0.0 copy-start.4
  1.6 0.0 copy-start.5
  1.6 0.0 copy-start.2
  1.6 0.0 copy-start.3
  1.6 1.0 shard_map.68
  2.6 10.2 %all-to-all-start = ((f32[16,48,128]{2,1,0:T(8,128)}), f32[16,48,128]{2,1,0:T(8,128)S(1)}, u32[]{:S(2)}, u32[]{:S(2)}) async-start(f32[16,48,128]{2,1,0:T(8,128)} %shard_map.68), calls=%async_computation | async-start | bytes 786432 | tf_op jit(solution)/shard_map/all_to_all | solution.py:464
  12.9 0.0 copy-done.4
  12.9 0.0 copy-done.5
  12.9 0.1 fusion
  13.0 0.1 concatenate.7
  13.1 0.1 constant_dynamic-slice_fusion.local_ref
  13.2 14.2 %all-to-all-done.field_ref = f32[16,48,128]{2,1,0:T(8,128)S(1)} async-done(((f32[16,48,128]{2,1,0:T(8,128)}), f32[16,48,128]{2,1,0:T(8,128)S(1)}, u32[]{:S(2)}, u32[]{:S(2)}) %all-to-all-start) | async-done | bytes 393248 | tf_op jit(solution)/shard_map/all_to_all | solution.py:464
  27.4 0.0 copy-done.2
  27.4 0.6 shard_map.69
  28.0 11.3 %collective-permute-start.2 = (f32[91,8,128]{2,1,0:T(8,128)S(1)}, f32[91,8,128]{2,1,0:T(8,128)S(1)}, u32[]{:S(2)}, u32[]{:S(2)}) collective-permute-start(f32[91,8,128]{2,1,0:T(8,128)S(1)} %get-tuple-element.18.field_ref), channel_id=1, source_target_pairs={{0,31},{1,0},{2,1},{3,2},{4,3},{5,4},{6,5},{7,6},{8,7},{9,8},{10,9... | collective-permute-start | bytes 1118216 | tf_op jit(solution)/shard_map/ppermute | solution.py:445
  39.3 1.9 %collective-permute-start.1 = (f32[91,8,128]{2,1,0:T(8,128)S(1)}, f32[91,8,128]{2,1,0:T(8,128)S(1)}, u32[]{:S(2)}, u32[]{:S(2)}) collective-permute-start(f32[91,8,128]{2,1,0:T(8,128)S(1)} %get-tuple-element.18.field_ref), channel_id=1, source_target_pairs={{0,1},{1,2},{2,3},{3,4},{4,5},{5,6},{6,7},{7,8},{8,9},{9,10},{10,1... | collective-permute-start | bytes 1118216 | tf_op jit(solution)/shard_map/ppermute | solution.py:445
  41.2 1.9 %collective-permute-start = (f32[25,8,128]{2,1,0:T(8,128)S(1)}, f32[25,8,128]{2,1,0:T(8,128)S(1)}, u32[]{:S(2)}, u32[]{:S(2)}) collective-permute-start(f32[25,8,128]{2,1,0:T(8,128)S(1)} %get-tuple-element.17), channel_id=1, source_target_pairs={{0,2},{1,3},{2,4},{3,5},{4,6},{5,7},{6,8},{7,9},{8,10},{9,11},{10,... | collective-permute-start | bytes 307208 | tf_op jit(solution)/shard_map/ppermute | solution.py:445
  43.1 7.0 %collective-permute-start.3 = (f32[25,8,128]{2,1,0:T(8,128)S(1)}, f32[25,8,128]{2,1,0:T(8,128)S(1)}, u32[]{:S(2)}, u32[]{:S(2)}) collective-permute-start(f32[25,8,128]{2,1,0:T(8,128)S(1)} %get-tuple-element.19), channel_id=1, source_target_pairs={{0,30},{1,31},{2,0},{3,1},{4,2},{5,3},{6,4},{7,5},{8,6},{9,7},{10,... | collective-permute-start | bytes 307208 | tf_op jit(solution)/shard_map/ppermute | solution.py:445
  50.1 0.0 collective-permute-done.2.bottom_ref
  50.1 9.1 %collective-permute-done.1.top_ref = f32[91,8,128]{2,1,0:T(8,128)S(1)} collective-permute-done((f32[91,8,128]{2,1,0:T(8,128)S(1)}, f32[91,8,128]{2,1,0:T(8,128)S(1)}, u32[]{:S(2)}, u32[]{:S(2)}) %collective-permute-start.1) | collective-permute-done | bytes 372768 | tf_op jit(solution)/shard_map/ppermute | solution.py:445
  59.2 0.0 copy-done.3
  59.2 3.0 %shard_map.70 = (f32[8,11,8,128]{3,2,1,0:T(8,128)S(1)}, f32[28,11,8,128]{3,2,1,0:T(8,128)S(1)}, f32[28,11,8,128]{3,2,1,0:T(8,128)S(1)}, f32[28,11,8,128]{3,2,1,0...) custom-call(f32[91,8,128]{2,1,0:T(8,128)S(1)} %collective-permute-done.1., ...), custom_call_target="tpu_custom_call" | custom-call | tf_op jit(solution)/shard_map/pallas_call | solution.py:488
  62.2 0.0 collective-permute-done.top_far_ref
  62.3 0.0 collective-permute-done.3.bottom_far_ref
  62.3 2.5 %shard_map.71 = (f32[8,11,8,128]{3,2,1,0:T(8,128)S(1)}, f32[8,11,8,128]{3,2,1,0:T(8,128)S(1)}, f32[64,1,128]{2,1,0:T(1,128)S(1)}) custom-call(f32[25,8,128]{2,1,0:T(8,128)S(1)} %collective-permute-done.top_far_ref, f32[91,8,128]{2,1,0:T(8,128)S(1)} %collective-permute-done.1.top_ref, f32[91,8,128]{2,1,0:T(8,128)S(1)} %get-tuple-element.18.field_ref, ...), custom_call_target="tpu_custom_call" | custom-call | tf_op jit(solution)/shard_map/pallas_call | solution.py:501
  64.8 13.2 %all_to_all.20 = f32[64,1,128]{2,1,0:T(1,128)S(1)} all-to-all(f32[64,1,128]{2,1,0:T(1,128)S(1)} %get-tuple-element.26), channel_id=1, replica_groups={{0,1,2,3,32,33,34,35,64,65,66,67,96,97,98,99,128,129,130,131,160,161,16..., dimensions={0} | all-to-all | bytes 65536 | tf_op jit(solution)/shard_map/all_to_all | solution.py:508
  78.0 0.1 reduce_sum.9
  78.1 8.9 %all_to_all.21.sums_ref = f32[8,1,128]{2,1,0:T(1,128)S(1)} all-to-all(f32[8,1,128]{2,1,0:T(1,128)S(1)} %broadcast_in_dim.2), channel_id=1, replica_groups={{0,4,8,12,16,20,24,28},{1,5,9,13,17,21,25,29},{2,6,10,14,18,22,26,30},{..., dimensions={0} | all-to-all | bytes 8192 | tf_op jit(solution)/shard_map/all_to_all | solution.py:512
  87.0 0.0 copy-start.1
  87.0 1.3 %shard_map.72 = f32[16,64,128]{2,1,0:T(8,128)S(1)} custom-call(f32[128,128]{1,0:T(8,128)S(1)} %copy-done.2, f32[8,1,128]{2,1,0:T(1,128)S(1)} %all_to_all.21.sums_ref, f32[8,11,8,128]{3,2,1,0:T(8,128)S(1)} %get-tuple-element.27.one_ref, f32[8,11,8,128]{3,2,1,0:T(8,128)S(1)} %get-tuple-element.28.two_ref, ...), custom_call_target="tpu_custom_call" | custom-call | tf_op jit(solution)/shard_map/pallas_call | solution.py:513
  88.3 21.8 %all_to_all.22.source_ref = f32[16,64,128]{2,1,0:T(8,128)S(1)} all-to-all(f32[16,64,128]{2,1,0:T(8,128)S(1)} %shard_map.72), channel_id=1, replica_groups=mesh['tm'=16,'space'=32] {'tm'}, dimensions={0} | all-to-all | bytes 1048576 | tf_op jit(solution)/shard_map/all_to_all | solution.py:518
  110.2 0.0 copy-done.1
  110.2 1.0 shard_map.73
  (4 shorter events, 0.0 us)
Async XLA Ops:
  0.6 1.0 copy-start
  1.6 11.3 %copy-start.4 = (s32[2,8,1024]{2,1,0:T(8,128)S(1)}, s32[2,8,1024]{2,1,0:T(8,128)}, u32[]{:S(2)}) copy-start(s32[2,8,1024]{2,1,0:T(8,128)} %param.7) | copy-start | bytes 196612
  1.6 11.3 %copy-start.5 = (f32[8,1024]{1,0:T(8,128)S(1)}, f32[8,1024]{1,0:T(8,128)}, u32[]{:S(2)}) copy-start(f32[8,1024]{1,0:T(8,128)} %param.6) | copy-start | bytes 98308
  1.6 25.8 %copy-start.2 = (f32[128,128]{1,0:T(8,128)S(1)}, f32[128,128]{1,0:T(8,128)}, u32[]{:S(2)}) copy-start(f32[128,128]{1,0:T(8,128)} %constant.18.clone.cas_ref) | copy-start | bytes 196612
  1.6 57.7 %copy-start.3 = (f32[10,8,128]{2,1,0:T(8,128)S(1)}, f32[10,8,128]{2,1,0:T(8,128)}, u32[]{:S(2)}) copy-start(f32[10,8,128]{2,1,0:T(8,128)} %constant.19.clone.coef_ref) | copy-start | bytes 122884
  2.6 24.8 %all-to-all-start = ((f32[16,48,128]{2,1,0:T(8,128)}), f32[16,48,128]{2,1,0:T(8,128)S(1)}, u32[]{:S(2)}, u32[]{:S(2)}) async-start(f32[16,48,128]{2,1,0:T(8,128)} %shard_map.68), calls=%async_computation | async-start | bytes 786432 | tf_op jit(solution)/shard_map/all_to_all | solution.py:464
  28.0 22.1 %collective-permute-start.2 = (f32[91,8,128]{2,1,0:T(8,128)S(1)}, f32[91,8,128]{2,1,0:T(8,128)S(1)}, u32[]{:S(2)}, u32[]{:S(2)}) collective-permute-start(f32[91,8,128]{2,1,0:T(8,128)S(1)} %get-tuple-element.18.field_ref), channel_id=1, source_target_pairs={{0,31},{1,0},{2,1},{3,2},{4,3},{5,4},{6,5},{7,6},{8,7},{9,8},{10,9... | collective-permute-start | bytes 1118216 | tf_op jit(solution)/shard_map/ppermute | solution.py:445
  39.3 20.0 %collective-permute-start.1 = (f32[91,8,128]{2,1,0:T(8,128)S(1)}, f32[91,8,128]{2,1,0:T(8,128)S(1)}, u32[]{:S(2)}, u32[]{:S(2)}) collective-permute-start(f32[91,8,128]{2,1,0:T(8,128)S(1)} %get-tuple-element.18.field_ref), channel_id=1, source_target_pairs={{0,1},{1,2},{2,3},{3,4},{4,5},{5,6},{6,7},{7,8},{8,9},{9,10},{10,1... | collective-permute-start | bytes 1118216 | tf_op jit(solution)/shard_map/ppermute | solution.py:445
  41.2 21.1 %collective-permute-start = (f32[25,8,128]{2,1,0:T(8,128)S(1)}, f32[25,8,128]{2,1,0:T(8,128)S(1)}, u32[]{:S(2)}, u32[]{:S(2)}) collective-permute-start(f32[25,8,128]{2,1,0:T(8,128)S(1)} %get-tuple-element.17), channel_id=1, source_target_pairs={{0,2},{1,3},{2,4},{3,5},{4,6},{5,7},{6,8},{7,9},{8,10},{9,11},{10,... | collective-permute-start | bytes 307208 | tf_op jit(solution)/shard_map/ppermute | solution.py:445
  43.1 19.1 %collective-permute-start.3 = (f32[25,8,128]{2,1,0:T(8,128)S(1)}, f32[25,8,128]{2,1,0:T(8,128)S(1)}, u32[]{:S(2)}, u32[]{:S(2)}) collective-permute-start(f32[25,8,128]{2,1,0:T(8,128)S(1)} %get-tuple-element.19), channel_id=1, source_target_pairs={{0,30},{1,31},{2,0},{3,1},{4,2},{5,3},{6,4},{7,5},{8,6},{9,7},{10,... | collective-permute-start | bytes 307208 | tf_op jit(solution)/shard_map/ppermute | solution.py:445
  87.0 23.2 %copy-start.1 = (f32[8,8,1024]{2,1,0:T(8,128)S(1)}, f32[8,8,1024]{2,1,0:T(8,128)}, u32[]{:S(2)}) copy-start(f32[8,8,1024]{2,1,0:T(8,128)} %param.5) | copy-start | bytes 786436

commit v11 on v10

--- a/solution.py
+++ b/solution.py
@@ -242,7 +242,7 @@
 
 
 def near_kernel(
-    rows, top_ref, field_ref, bottom_ref, coef_ref,
+    rows, bottom_ref, field_ref, top_ref, coef_ref,
     solved_ref, middle_ref, step_ref, remain_ref, border_ref, wide_ref, early_ref,
     part_ref, scratch_ref,
 ):
@@ -497,7 +497,7 @@
             (2, SUB, LANES),
         ],
         [tile_shape, (LANES, LANES)],
-    )(top, freq, bottom, coef_table)
+    )(bottom, freq, top, coef_table)
     solved_two, applied_two, sums = call(
         functools.partial(far_kernel, rows),
         [tile_shape, tile_shape, (tiles * NEAR, 1, LANES)],

time: 112 us -> 112 us (level)
  no operation moved by 1% of the time
where the time goes in v11:
time: 112 us; the launch traced here: 111 us
  blocking collectives  43.9 us (39%)
  starting transfers between devices  32.3 us (29%)
  waiting for transfers between devices  23.4 us (21%)
  Pallas kernels  9.48 us (8%)
  local copies, waits for them, and re-layouts  1.24 us (1%)
    ppermute x4, starting transfers between devices, shift(): lax.ppermute(value, 'space', [(i, (i + distance) % spaces) for i in range...  22.1 us
    all_to_all x1, blocking collectives, shards(): returned = lax.all_to_all(packed, 'tm', 0, 0)  21.8 us
    all_to_all x1, waiting for transfers between devices, shards(): gathered = lax.all_to_all(windows, 'tm', 0, 0)  14.2 us
    all_to_all x1, blocking collectives, shards(): sums = lax.all_to_all(sums, ('tm', 'space'), 0, 0, axis_index_groups=groups)  13.2 us
    all_to_all x1, starting transfers between devices, shards(): gathered = lax.all_to_all(windows, 'tm', 0, 0)  10.2 us
    ppermute x4, waiting for transfers between devices, shift(): lax.ppermute(value, 'space', [(i, (i + distance) % spaces) for i in range...  9.14 us
    all_to_all x1, blocking collectives, shards(): sums = lax.all_to_all(sums, 'space', 0, 0, axis_index_groups=groups)  8.89 us
    pallas_call x1, Pallas kernels, shards(): call(functools.partial(near_kernel, rows), [tile_shape, work, work, work,...  3 us
  transfers between devices with their start and end apart: 5, of which 2 were waited for; matrix products, arithmetic and copies ran while one was open for 0% of the time, Pallas kernels for 3%

profile of v11, /device:TPU:1, one launch (start us, length us, event | category | flops | bytes accessed | tf_op | source)
XLA Modules:
  0.0 111.2 jit_solution(11894743793458896636)
XLA Ops:
  0.6 0.0 copy-start
  0.6 0.9 copy-done
  1.6 0.0 copy-start.4
  1.6 0.0 copy-start.5
  1.6 0.0 copy-start.2
  1.6 0.0 copy-start.3
  1.6 1.0 shard_map.68
  2.6 10.2 %all-to-all-start = ((f32[16,48,128]{2,1,0:T(8,128)}), f32[16,48,128]{2,1,0:T(8,128)S(1)}, u32[]{:S(2)}, u32[]{:S(2)}) async-start(f32[16,48,128]{2,1,0:T(8,128)} %shard_map.68), calls=%async_computation | async-start | bytes 786432 | tf_op jit(solution)/shard_map/all_to_all | solution.py:464
  12.9 0.0 copy-done.4
  12.9 0.0 copy-done.5
  12.9 0.1 fusion
  13.0 0.1 concatenate.7
  13.1 0.1 constant_dynamic-slice_fusion.local_ref
  13.2 14.2 %all-to-all-done.field_ref = f32[16,48,128]{2,1,0:T(8,128)S(1)} async-done(((f32[16,48,128]{2,1,0:T(8,128)}), f32[16,48,128]{2,1,0:T(8,128)S(1)}, u32[]{:S(2)}, u32[]{:S(2)}) %all-to-all-start) | async-done | bytes 393248 | tf_op jit(solution)/shard_map/all_to_all | solution.py:464
  27.4 0.0 copy-done.2
  27.4 0.6 shard_map.69
  28.0 11.3 %collective-permute-start.2 = (f32[91,8,128]{2,1,0:T(8,128)S(1)}, f32[91,8,128]{2,1,0:T(8,128)S(1)}, u32[]{:S(2)}, u32[]{:S(2)}) collective-permute-start(f32[91,8,128]{2,1,0:T(8,128)S(1)} %get-tuple-element.18.field_ref), channel_id=1, source_target_pairs={{0,31},{1,0},{2,1},{3,2},{4,3},{5,4},{6,5},{7,6},{8,7},{9,8},{10,9... | collective-permute-start | bytes 1118216 | tf_op jit(solution)/shard_map/ppermute | solution.py:445
  39.3 1.9 %collective-permute-start.1 = (f32[91,8,128]{2,1,0:T(8,128)S(1)}, f32[91,8,128]{2,1,0:T(8,128)S(1)}, u32[]{:S(2)}, u32[]{:S(2)}) collective-permute-start(f32[91,8,128]{2,1,0:T(8,128)S(1)} %get-tuple-element.18.field_ref), channel_id=1, source_target_pairs={{0,1},{1,2},{2,3},{3,4},{4,5},{5,6},{6,7},{7,8},{8,9},{9,10},{10,1... | collective-permute-start | bytes 1118216 | tf_op jit(solution)/shard_map/ppermute | solution.py:445
  41.2 1.9 %collective-permute-start = (f32[25,8,128]{2,1,0:T(8,128)S(1)}, f32[25,8,128]{2,1,0:T(8,128)S(1)}, u32[]{:S(2)}, u32[]{:S(2)}) collective-permute-start(f32[25,8,128]{2,1,0:T(8,128)S(1)} %get-tuple-element.17), channel_id=1, source_target_pairs={{0,2},{1,3},{2,4},{3,5},{4,6},{5,7},{6,8},{7,9},{8,10},{9,11},{10,... | collective-permute-start | bytes 307208 | tf_op jit(solution)/shard_map/ppermute | solution.py:445
  43.1 7.0 %collective-permute-start.3 = (f32[25,8,128]{2,1,0:T(8,128)S(1)}, f32[25,8,128]{2,1,0:T(8,128)S(1)}, u32[]{:S(2)}, u32[]{:S(2)}) collective-permute-start(f32[25,8,128]{2,1,0:T(8,128)S(1)} %get-tuple-element.19), channel_id=1, source_target_pairs={{0,30},{1,31},{2,0},{3,1},{4,2},{5,3},{6,4},{7,5},{8,6},{9,7},{10,... | collective-permute-start | bytes 307208 | tf_op jit(solution)/shard_map/ppermute | solution.py:445
  50.1 0.0 collective-permute-done.2.bottom_ref
  50.1 9.1 %collective-permute-done.1.top_ref = f32[91,8,128]{2,1,0:T(8,128)S(1)} collective-permute-done((f32[91,8,128]{2,1,0:T(8,128)S(1)}, f32[91,8,128]{2,1,0:T(8,128)S(1)}, u32[]{:S(2)}, u32[]{:S(2)}) %collective-permute-start.1) | collective-permute-done | bytes 372768 | tf_op jit(solution)/shard_map/ppermute | solution.py:445
  59.2 0.0 copy-done.3
  59.2 3.0 %shard_map.70 = (f32[8,11,8,128]{3,2,1,0:T(8,128)S(1)}, f32[28,11,8,128]{3,2,1,0:T(8,128)S(1)}, f32[28,11,8,128]{3,2,1,0:T(8,128)S(1)}, f32[28,11,8,128]{3,2,1,0...) custom-call(f32[91,8,128]{2,1,0:T(8,128)S(1)} %collective-permute-done.2., ...), custom_call_target="tpu_custom_call" | custom-call | tf_op jit(solution)/shard_map/pallas_call | solution.py:488
  62.2 0.0 collective-permute-done.top_far_ref
  62.3 0.0 collective-permute-done.3.bottom_far_ref
  62.3 2.5 %shard_map.71 = (f32[8,11,8,128]{3,2,1,0:T(8,128)S(1)}, f32[8,11,8,128]{3,2,1,0:T(8,128)S(1)}, f32[64,1,128]{2,1,0:T(1,128)S(1)}) custom-call(f32[25,8,128]{2,1,0:T(8,128)S(1)} %collective-permute-done.top_far_ref, f32[91,8,128]{2,1,0:T(8,128)S(1)} %collective-permute-done.1.top_ref, f32[91,8,128]{2,1,0:T(8,128)S(1)} %get-tuple-element.18.field_ref, ...), custom_call_target="tpu_custom_call" | custom-call | tf_op jit(solution)/shard_map/pallas_call | solution.py:501
  64.8 13.2 %all_to_all.20 = f32[64,1,128]{2,1,0:T(1,128)S(1)} all-to-all(f32[64,1,128]{2,1,0:T(1,128)S(1)} %get-tuple-element.26), channel_id=1, replica_groups={{0,1,2,3,32,33,34,35,64,65,66,67,96,97,98,99,128,129,130,131,160,161,16..., dimensions={0} | all-to-all | bytes 65536 | tf_op jit(solution)/shard_map/all_to_all | solution.py:508
  78.0 0.1 reduce_sum.9
  78.1 8.9 %all_to_all.21.sums_ref = f32[8,1,128]{2,1,0:T(1,128)S(1)} all-to-all(f32[8,1,128]{2,1,0:T(1,128)S(1)} %broadcast_in_dim.2), channel_id=1, replica_groups={{0,4,8,12,16,20,24,28},{1,5,9,13,17,21,25,29},{2,6,10,14,18,22,26,30},{..., dimensions={0} | all-to-all | bytes 8192 | tf_op jit(solution)/shard_map/all_to_all | solution.py:512
  87.0 0.0 copy-start.1
  87.0 1.3 %shard_map.72 = f32[16,64,128]{2,1,0:T(8,128)S(1)} custom-call(f32[128,128]{1,0:T(8,128)S(1)} %copy-done.2, f32[8,1,128]{2,1,0:T(1,128)S(1)} %all_to_all.21.sums_ref, f32[8,11,8,128]{3,2,1,0:T(8,128)S(1)} %get-tuple-element.27.one_ref, f32[8,11,8,128]{3,2,1,0:T(8,128)S(1)} %get-tuple-element.28.two_ref, ...), custom_call_target="tpu_custom_call" | custom-call | tf_op jit(solution)/shard_map/pallas_call | solution.py:513
  88.3 21.8 %all_to_all.22.source_ref = f32[16,64,128]{2,1,0:T(8,128)S(1)} all-to-all(f32[16,64,128]{2,1,0:T(8,128)S(1)} %shard_map.72), channel_id=1, replica_groups=mesh['tm'=16,'space'=32] {'tm'}, dimensions={0} | all-to-all | bytes 1048576 | tf_op jit(solution)/shard_map/all_to_all | solution.py:518
  110.2 0.0 copy-done.1
  110.2 1.0 shard_map.73
  (4 shorter events, 0.0 us)
Async XLA Ops:
  0.6 1.0 copy-start
  1.6 11.3 %copy-start.4 = (s32[2,8,1024]{2,1,0:T(8,128)S(1)}, s32[2,8,1024]{2,1,0:T(8,128)}, u32[]{:S(2)}) copy-start(s32[2,8,1024]{2,1,0:T(8,128)} %param.7) | copy-start | bytes 196612
  1.6 11.3 %copy-start.5 = (f32[8,1024]{1,0:T(8,128)S(1)}, f32[8,1024]{1,0:T(8,128)}, u32[]{:S(2)}) copy-start(f32[8,1024]{1,0:T(8,128)} %param.6) | copy-start | bytes 98308
  1.6 25.8 %copy-start.2 = (f32[128,128]{1,0:T(8,128)S(1)}, f32[128,128]{1,0:T(8,128)}, u32[]{:S(2)}) copy-start(f32[128,128]{1,0:T(8,128)} %constant.18.clone.cas_ref) | copy-start | bytes 196612
  1.6 57.7 %copy-start.3 = (f32[10,8,128]{2,1,0:T(8,128)S(1)}, f32[10,8,128]{2,1,0:T(8,128)}, u32[]{:S(2)}) copy-start(f32[10,8,128]{2,1,0:T(8,128)} %constant.19.clone.coef_ref) | copy-start | bytes 122884
  2.6 24.8 %all-to-all-start = ((f32[16,48,128]{2,1,0:T(8,128)}), f32[16,48,128]{2,1,0:T(8,128)S(1)}, u32[]{:S(2)}, u32[]{:S(2)}) async-start(f32[16,48,128]{2,1,0:T(8,128)} %shard_map.68), calls=%async_computation | async-start | bytes 786432 | tf_op jit(solution)/shard_map/all_to_all | solution.py:464
  28.0 22.1 %collective-permute-start.2 = (f32[91,8,128]{2,1,0:T(8,128)S(1)}, f32[91,8,128]{2,1,0:T(8,128)S(1)}, u32[]{:S(2)}, u32[]{:S(2)}) collective-permute-start(f32[91,8,128]{2,1,0:T(8,128)S(1)} %get-tuple-element.18.field_ref), channel_id=1, source_target_pairs={{0,31},{1,0},{2,1},{3,2},{4,3},{5,4},{6,5},{7,6},{8,7},{9,8},{10,9... | collective-permute-start | bytes 1118216 | tf_op jit(solution)/shard_map/ppermute | solution.py:445
  39.3 20.0 %collective-permute-start.1 = (f32[91,8,128]{2,1,0:T(8,128)S(1)}, f32[91,8,128]{2,1,0:T(8,128)S(1)}, u32[]{:S(2)}, u32[]{:S(2)}) collective-permute-start(f32[91,8,128]{2,1,0:T(8,128)S(1)} %get-tuple-element.18.field_ref), channel_id=1, source_target_pairs={{0,1},{1,2},{2,3},{3,4},{4,5},{5,6},{6,7},{7,8},{8,9},{9,10},{10,1... | collective-permute-start | bytes 1118216 | tf_op jit(solution)/shard_map/ppermute | solution.py:445
  41.2 21.1 %collective-permute-start = (f32[25,8,128]{2,1,0:T(8,128)S(1)}, f32[25,8,128]{2,1,0:T(8,128)S(1)}, u32[]{:S(2)}, u32[]{:S(2)}) collective-permute-start(f32[25,8,128]{2,1,0:T(8,128)S(1)} %get-tuple-element.17), channel_id=1, source_target_pairs={{0,2},{1,3},{2,4},{3,5},{4,6},{5,7},{6,8},{7,9},{8,10},{9,11},{10,... | collective-permute-start | bytes 307208 | tf_op jit(solution)/shard_map/ppermute | solution.py:445
  43.1 19.1 %collective-permute-start.3 = (f32[25,8,128]{2,1,0:T(8,128)S(1)}, f32[25,8,128]{2,1,0:T(8,128)S(1)}, u32[]{:S(2)}, u32[]{:S(2)}) collective-permute-start(f32[25,8,128]{2,1,0:T(8,128)S(1)} %get-tuple-element.19), channel_id=1, source_target_pairs={{0,30},{1,31},{2,0},{3,1},{4,2},{5,3},{6,4},{7,5},{8,6},{9,7},{10,... | collective-permute-start | bytes 307208 | tf_op jit(solution)/shard_map/ppermute | solution.py:445
  87.0 23.2 %copy-start.1 = (f32[8,8,1024]{2,1,0:T(8,128)S(1)}, f32[8,8,1024]{2,1,0:T(8,128)}, u32[]{:S(2)}) copy-start(f32[8,8,1024]{2,1,0:T(8,128)} %param.5) | copy-start | bytes 786436

commit v12 on v11

--- a/solution.py
+++ b/solution.py
@@ -288,7 +288,7 @@
 
 
 def far_kernel(
-    rows, top_far_ref, top_ref, field_ref, bottom_ref, bottom_far_ref, coef_ref,
+    rows, top_far_ref, bottom_ref, field_ref, top_ref, bottom_far_ref, coef_ref,
     middle_ref, frozen_step_ref, frozen_remain_ref, border_ref, wide_ref, early_ref,
     solved_ref, applied_ref, sums_ref,
     step_ref, remain_ref, part_ref, outer_ref, scratch_ref,
@@ -503,7 +503,7 @@
         [tile_shape, tile_shape, (tiles * NEAR, 1, LANES)],
         [work, work, tile_shape, (2 * FAR, BLOCK, SUB, LANES), (LANES, LANES)],
     )(
-        top_far, top, freq, bottom, bottom_far, coef_table, middle, step, remain, border, wide, early
+        top_far, bottom, freq, top, bottom_far, coef_table, middle, step, remain, border, wide, early
     )
     sums = lax.all_to_all(sums, ("tm", "space"), 0, 0, axis_index_groups=groups)
     planes = spaces // NEAR

time: 112 us -> 110 us (0.982)
  waiting for transfers between devices: 23.4 us -> 14.6 us
  blocking collectives: 43.9 us -> 51.3 us
    ppermute x4, waiting for transfers between devices: 9.14 us -> 0.41 us  [shift(): lax.ppermute(value, 'space', [(i, (i + distance) % spaces) for i in range...]
    all_to_all x1, blocking collectives: 8.89 us -> 16.3 us  [shards(): sums = lax.all_to_all(sums, 'space', 0, 0, axis_index_groups=groups)]
where the time goes in v12:
time: 110 us
  blocking collectives  51.3 us (47%)
  starting transfers between devices  32.3 us (29%)
  waiting for transfers between devices  14.6 us (13%)
  Pallas kernels  9.49 us (9%)
  local copies, waits for them, and re-layouts  1.24 us (1%)
    all_to_all x1, blocking collectives, shards(): returned = lax.all_to_all(packed, 'tm', 0, 0)  22.2 us
    ppermute x4, starting transfers between devices, shift(): lax.ppermute(value, 'space', [(i, (i + distance) % spaces) for i in range...  22.1 us
    all_to_all x1, blocking collectives, shards(): sums = lax.all_to_all(sums, 'space', 0, 0, axis_index_groups=groups)  16.3 us
    all_to_all x1, waiting for transfers between devices, shards(): gathered = lax.all_to_all(windows, 'tm', 0, 0)  14.2 us
    all_to_all x1, blocking collectives, shards(): sums = lax.all_to_all(sums, ('tm', 'space'), 0, 0, axis_index_groups=groups)  12.9 us
    all_to_all x1, starting transfers between devices, shards(): gathered = lax.all_to_all(windows, 'tm', 0, 0)  10.2 us
    pallas_call x1, Pallas kernels, shards(): call(functools.partial(near_kernel, rows), [tile_shape, work, work, work,...  3.02 us
    pallas_call x1, Pallas kernels, shards(): call(functools.partial(far_kernel, rows), [tile_shape, tile_shape, (tiles...  2.54 us
  transfers between devices with their start and end apart: 5, of which 2 were waited for; matrix products, arithmetic and copies ran while one was open for 0% of the time, Pallas kernels for 3%

profile of v12, /device:TPU:1, one launch (start us, length us, event | category | flops | bytes accessed | tf_op | source)
XLA Modules:
  0.0 109.9 jit_solution(3429126444117128105)
XLA Ops:
  0.6 0.0 copy-start
  0.6 0.9 copy-done
  1.6 0.0 copy-start.4
  1.6 0.0 copy-start.5
  1.6 0.0 copy-start.2
  1.6 0.0 copy-start.3
  1.6 1.0 shard_map.68
  2.6 10.2 %all-to-all-start = ((f32[16,48,128]{2,1,0:T(8,128)}), f32[16,48,128]{2,1,0:T(8,128)S(1)}, u32[]{:S(2)}, u32[]{:S(2)}) async-start(f32[16,48,128]{2,1,0:T(8,128)} %shard_map.68), calls=%async_computation | async-start | bytes 786432 | tf_op jit(solution)/shard_map/all_to_all | solution.py:464
  12.9 0.0 copy-done.4
  12.9 0.0 copy-done.5
  12.9 0.1 fusion
  13.0 0.1 concatenate.7
  13.1 0.1 constant_dynamic-slice_fusion.local_ref
  13.2 14.2 %all-to-all-done.field_ref = f32[16,48,128]{2,1,0:T(8,128)S(1)} async-done(((f32[16,48,128]{2,1,0:T(8,128)}), f32[16,48,128]{2,1,0:T(8,128)S(1)}, u32[]{:S(2)}, u32[]{:S(2)}) %all-to-all-start) | async-done | bytes 393248 | tf_op jit(solution)/shard_map/all_to_all | solution.py:464
  27.4 0.0 copy-done.2
  27.4 0.6 shard_map.69
  28.0 1.9 %collective-permute-start.2 = (f32[91,8,128]{2,1,0:T(8,128)S(1)}, f32[91,8,128]{2,1,0:T(8,128)S(1)}, u32[]{:S(2)}, u32[]{:S(2)}) collective-permute-start(f32[91,8,128]{2,1,0:T(8,128)S(1)} %get-tuple-element.18.field_ref), channel_id=1, source_target_pairs={{0,1},{1,2},{2,3},{3,4},{4,5},{5,6},{6,7},{7,8},{8,9},{9,10},{10,1... | collective-permute-start | bytes 1118216 | tf_op jit(solution)/shard_map/ppermute | solution.py:445
  29.9 11.3 %collective-permute-start.1 = (f32[91,8,128]{2,1,0:T(8,128)S(1)}, f32[91,8,128]{2,1,0:T(8,128)S(1)}, u32[]{:S(2)}, u32[]{:S(2)}) collective-permute-start(f32[91,8,128]{2,1,0:T(8,128)S(1)} %get-tuple-element.18.field_ref), channel_id=1, source_target_pairs={{0,31},{1,0},{2,1},{3,2},{4,3},{5,4},{6,5},{7,6},{8,7},{9,8},{10,9... | collective-permute-start | bytes 1118216 | tf_op jit(solution)/shard_map/ppermute | solution.py:445
  41.2 1.9 %collective-permute-start = (f32[25,8,128]{2,1,0:T(8,128)S(1)}, f32[25,8,128]{2,1,0:T(8,128)S(1)}, u32[]{:S(2)}, u32[]{:S(2)}) collective-permute-start(f32[25,8,128]{2,1,0:T(8,128)S(1)} %get-tuple-element.17), channel_id=1, source_target_pairs={{0,2},{1,3},{2,4},{3,5},{4,6},{5,7},{6,8},{7,9},{8,10},{9,11},{10,... | collective-permute-start | bytes 307208 | tf_op jit(solution)/shard_map/ppermute | solution.py:445
  43.1 7.0 %collective-permute-start.3 = (f32[25,8,128]{2,1,0:T(8,128)S(1)}, f32[25,8,128]{2,1,0:T(8,128)S(1)}, u32[]{:S(2)}, u32[]{:S(2)}) collective-permute-start(f32[25,8,128]{2,1,0:T(8,128)S(1)} %get-tuple-element.19), channel_id=1, source_target_pairs={{0,30},{1,31},{2,0},{3,1},{4,2},{5,3},{6,4},{7,5},{8,6},{9,7},{10,... | collective-permute-start | bytes 307208 | tf_op jit(solution)/shard_map/ppermute | solution.py:445
  50.1 0.0 collective-permute-done.2.top_ref
  50.1 0.0 collective-permute-done.1.bottom_ref
  50.1 0.0 copy-done.3
  50.1 3.0 %shard_map.70 = (f32[8,11,8,128]{3,2,1,0:T(8,128)S(1)}, f32[28,11,8,128]{3,2,1,0:T(8,128)S(1)}, f32[28,11,8,128]{3,2,1,0:T(8,128)S(1)}, f32[28,11,8,128]{3,2,1,0...) custom-call(f32[91,8,128]{2,1,0:T(8,128)S(1)} %collective-permute-done.1., ...), custom_call_target="tpu_custom_call" | custom-call | tf_op jit(solution)/shard_map/pallas_call | solution.py:488
  53.1 0.0 collective-permute-done.top_far_ref
  53.2 0.4 collective-permute-done.3.bottom_far_ref
  53.6 2.5 %shard_map.71 = (f32[8,11,8,128]{3,2,1,0:T(8,128)S(1)}, f32[8,11,8,128]{3,2,1,0:T(8,128)S(1)}, f32[64,1,128]{2,1,0:T(1,128)S(1)}) custom-call(f32[25,8,128]{2,1,0:T(8,128)S(1)} %collective-permute-done.top_far_ref, f32[91,8,128]{2,1,0:T(8,128)S(1)} %collective-permute-done.1.bottom_ref, f32[91,8,128]{2,1,0:T(8,128)S(1)} %get-tuple-element.18.field_ref, ...), custom_call_target="tpu_custom_call" | custom-call | tf_op jit(solution)/shard_map/pallas_call | solution.py:501
  56.1 12.9 %all_to_all.20 = f32[64,1,128]{2,1,0:T(1,128)S(1)} all-to-all(f32[64,1,128]{2,1,0:T(1,128)S(1)} %get-tuple-element.26), channel_id=1, replica_groups={{0,1,2,3,32,33,34,35,64,65,66,67,96,97,98,99,128,129,130,131,160,161,16..., dimensions={0} | all-to-all | bytes 65536 | tf_op jit(solution)/shard_map/all_to_all | solution.py:508
  69.0 0.1 reduce_sum.9
  69.1 16.3 %all_to_all.21.sums_ref = f32[8,1,128]{2,1,0:T(1,128)S(1)} all-to-all(f32[8,1,128]{2,1,0:T(1,128)S(1)} %broadcast_in_dim.2), channel_id=1, replica_groups={{0,4,8,12,16,20,24,28},{1,5,9,13,17,21,25,29},{2,6,10,14,18,22,26,30},{..., dimensions={0} | all-to-all | bytes 8192 | tf_op jit(solution)/shard_map/all_to_all | solution.py:512
  85.4 0.0 copy-start.1
  85.4 1.3 %shard_map.72 = f32[16,64,128]{2,1,0:T(8,128)S(1)} custom-call(f32[128,128]{1,0:T(8,128)S(1)} %copy-done.2, f32[8,1,128]{2,1,0:T(1,128)S(1)} %all_to_all.21.sums_ref, f32[8,11,8,128]{3,2,1,0:T(8,128)S(1)} %get-tuple-element.27.one_ref, f32[8,11,8,128]{3,2,1,0:T(8,128)S(1)} %get-tuple-element.28.two_ref, ...), custom_call_target="tpu_custom_call" | custom-call | tf_op jit(solution)/shard_map/pallas_call | solution.py:513
  86.7 22.2 %all_to_all.22.source_ref = f32[16,64,128]{2,1,0:T(8,128)S(1)} all-to-all(f32[16,64,128]{2,1,0:T(8,128)S(1)} %shard_map.72), channel_id=1, replica_groups=mesh['tm'=16,'space'=32] {'tm'}, dimensions={0} | all-to-all | bytes 1048576 | tf_op jit(solution)/shard_map/all_to_all | solution.py:518
  108.9 0.0 copy-done.1
  108.9 1.0 shard_map.73
  (4 shorter events, 0.0 us)
Async XLA Ops:
  0.6 1.0 copy-start
  1.6 11.3 %copy-start.4 = (s32[2,8,1024]{2,1,0:T(8,128)S(1)}, s32[2,8,1024]{2,1,0:T(8,128)}, u32[]{:S(2)}) copy-start(s32[2,8,1024]{2,1,0:T(8,128)} %param.7) | copy-start | bytes 196612
  1.6 11.3 %copy-start.5 = (f32[8,1024]{1,0:T(8,128)S(1)}, f32[8,1024]{1,0:T(8,128)}, u32[]{:S(2)}) copy-start(f32[8,1024]{1,0:T(8,128)} %param.6) | copy-start | bytes 98308
  1.6 25.8 %copy-start.2 = (f32[128,128]{1,0:T(8,128)S(1)}, f32[128,128]{1,0:T(8,128)}, u32[]{:S(2)}) copy-start(f32[128,128]{1,0:T(8,128)} %constant.18.clone.cas_ref) | copy-start | bytes 196612
  1.6 48.5 %copy-start.3 = (f32[10,8,128]{2,1,0:T(8,128)S(1)}, f32[10,8,128]{2,1,0:T(8,128)}, u32[]{:S(2)}) copy-start(f32[10,8,128]{2,1,0:T(8,128)} %constant.19.clone.coef_ref) | copy-start | bytes 122884
  2.6 24.8 %all-to-all-start = ((f32[16,48,128]{2,1,0:T(8,128)}), f32[16,48,128]{2,1,0:T(8,128)S(1)}, u32[]{:S(2)}, u32[]{:S(2)}) async-start(f32[16,48,128]{2,1,0:T(8,128)} %shard_map.68), calls=%async_computation | async-start | bytes 786432 | tf_op jit(solution)/shard_map/all_to_all | solution.py:464
  28.0 22.1 %collective-permute-start.2 = (f32[91,8,128]{2,1,0:T(8,128)S(1)}, f32[91,8,128]{2,1,0:T(8,128)S(1)}, u32[]{:S(2)}, u32[]{:S(2)}) collective-permute-start(f32[91,8,128]{2,1,0:T(8,128)S(1)} %get-tuple-element.18.field_ref), channel_id=1, source_target_pairs={{0,1},{1,2},{2,3},{3,4},{4,5},{5,6},{6,7},{7,8},{8,9},{9,10},{10,1... | collective-permute-start | bytes 1118216 | tf_op jit(solution)/shard_map/ppermute | solution.py:445
  29.9 20.2 %collective-permute-start.1 = (f32[91,8,128]{2,1,0:T(8,128)S(1)}, f32[91,8,128]{2,1,0:T(8,128)S(1)}, u32[]{:S(2)}, u32[]{:S(2)}) collective-permute-start(f32[91,8,128]{2,1,0:T(8,128)S(1)} %get-tuple-element.18.field_ref), channel_id=1, source_target_pairs={{0,31},{1,0},{2,1},{3,2},{4,3},{5,4},{6,5},{7,6},{8,7},{9,8},{10,9... | collective-permute-start | bytes 1118216 | tf_op jit(solution)/shard_map/ppermute | solution.py:445
  41.2 12.0 %collective-permute-start = (f32[25,8,128]{2,1,0:T(8,128)S(1)}, f32[25,8,128]{2,1,0:T(8,128)S(1)}, u32[]{:S(2)}, u32[]{:S(2)}) collective-permute-start(f32[25,8,128]{2,1,0:T(8,128)S(1)} %get-tuple-element.17), channel_id=1, source_target_pairs={{0,2},{1,3},{2,4},{3,5},{4,6},{5,7},{6,8},{7,9},{8,10},{9,11},{10,... | collective-permute-start | bytes 307208 | tf_op jit(solution)/shard_map/ppermute | solution.py:445
  43.1 10.4 %collective-permute-start.3 = (f32[25,8,128]{2,1,0:T(8,128)S(1)}, f32[25,8,128]{2,1,0:T(8,128)S(1)}, u32[]{:S(2)}, u32[]{:S(2)}) collective-permute-start(f32[25,8,128]{2,1,0:T(8,128)S(1)} %get-tuple-element.19), channel_id=1, source_target_pairs={{0,30},{1,31},{2,0},{3,1},{4,2},{5,3},{6,4},{7,5},{8,6},{9,7},{10,... | collective-permute-start | bytes 307208 | tf_op jit(solution)/shard_map/ppermute | solution.py:445
  85.4 23.5 %copy-start.1 = (f32[8,8,1024]{2,1,0:T(8,128)S(1)}, f32[8,8,1024]{2,1,0:T(8,128)}, u32[]{:S(2)}) copy-start(f32[8,8,1024]{2,1,0:T(8,128)} %param.5) | copy-start | bytes 786436

commit v13 on v7

--- a/solution.py
+++ b/solution.py
@@ -219,7 +219,7 @@
 
 
 def stencil_kernel(
-    rows, top_far_ref, top_ref, field_ref, bottom_ref, bottom_far_ref, coef_ref,
+    rows, top_far_ref, bottom_ref, field_ref, top_ref, bottom_far_ref, coef_ref,
     solved_ref, applied_ref, solved_two_ref, applied_two_ref, sums_ref,
     step_ref, remain_ref, part_ref, middle_ref, wide_ref, scratch_ref,
 ):
@@ -402,7 +402,7 @@
             (total, 3 * BLOCK, SUB, LANES),
             (LANES, LANES),
         ],
-    )(top_far, top, freq, bottom, bottom_far, coef_table)
+    )(top_far, bottom, freq, top, bottom_far, coef_table)
     sums = lax.all_to_all(sums, ("tm", "space"), 0, 0, axis_index_groups=groups)
     planes = spaces // NEAR
     groups = [[first + NEAR * i for i in range(planes)] for first in range(NEAR)]

time: 111 us -> 110 us (level)
  waiting for transfers between devices: 22.6 us -> 17 us
  blocking collectives: 44.1 us -> 48.5 us
    ppermute x4, waiting for transfers between devices: 9.14 us -> 3.48 us  [shift(): lax.ppermute(value, 'space', [(i, (i + distance) % spaces) for i in range...]
    all_to_all x1, blocking collectives: 8.89 us -> 13.2 us  [shards(): sums = lax.all_to_all(sums, 'space', 0, 0, axis_index_groups=groups)]
  transfers between devices with their start and end apart: 5 -> 5, of which waited for: 4 -> 3; matrix products, arithmetic and copies ran while one was open for 0% -> 0% of each run, Pallas kernels for 0% -> 0%
where the time goes in v13:
time: 110 us; the launch traced here: 109 us
  blocking collectives  48.5 us (44%)
  starting transfers between devices  32.4 us (29%)
  waiting for transfers between devices  17 us (15%)
  Pallas kernels  8.58 us (8%)
  local copies, waits for them, and re-layouts  1.97 us (2%)
    all_to_all x1, blocking collectives, shards(): returned = lax.all_to_all(packed, 'tm', 0, 0)  22.3 us
    ppermute x4, starting transfers between devices, shift(): lax.ppermute(value, 'space', [(i, (i + distance) % spaces) for i in range...  22.1 us
    all_to_all x1, waiting for transfers between devices, shards(): gathered = lax.all_to_all(windows, 'tm', 0, 0)  13.5 us
    all_to_all x1, blocking collectives, shards(): sums = lax.all_to_all(sums, 'space', 0, 0, axis_index_groups=groups)  13.2 us
    all_to_all x1, blocking collectives, shards(): sums = lax.all_to_all(sums, ('tm', 'space'), 0, 0, axis_index_groups=groups)  12.9 us
    all_to_all x1, starting transfers between devices, shards(): gathered = lax.all_to_all(windows, 'tm', 0, 0)  10.3 us
    pallas_call x1, Pallas kernels, shards(): call(functools.partial(stencil_kernel, rows), [tile_shape] * 4 + [(tiles...  4.66 us
    ppermute x4, waiting for transfers between devices, shift(): lax.ppermute(value, 'space', [(i, (i + distance) % spaces) for i in range...  3.48 us
  transfers between devices with their start and end apart: 5, of which 3 were waited for; matrix products, arithmetic and copies ran while one was open for 0% of the time, Pallas kernels for 0%

profile of v13, /device:TPU:1, one launch (start us, length us, event | category | flops | bytes accessed | tf_op | source)
XLA Modules:
  0.0 109.2 jit_solution(9551440853026760024)
XLA Ops:
  0.6 0.0 copy-start
  0.6 0.9 copy-done
  1.6 1.0 shard_map.68
  2.6 0.0 copy-start.4
  2.6 10.3 %all-to-all-start = ((f32[16,48,128]{2,1,0:T(8,128)}), f32[16,48,128]{2,1,0:T(8,128)S(1)}, u32[]{:S(2)}, u32[]{:S(2)}) async-start(f32[16,48,128]{2,1,0:T(8,128)} %shard_map.68), calls=%async_computation | async-start | bytes 786432 | tf_op jit(solution)/shard_map/all_to_all | solution.py:370
  13.0 0.0 copy-done.4
  13.0 0.0 copy-start.5
  13.0 0.7 copy-done.5
  13.8 0.1 fusion
  13.8 0.0 copy-start.2
  13.8 0.1 concatenate.7
  14.0 0.1 constant_dynamic-slice_fusion.local_ref
  14.0 0.0 copy-start.3
  14.0 13.5 %all-to-all-done.field_ref = f32[16,48,128]{2,1,0:T(8,128)S(1)} async-done(((f32[16,48,128]{2,1,0:T(8,128)}), f32[16,48,128]{2,1,0:T(8,128)S(1)}, u32[]{:S(2)}, u32[]{:S(2)}) %all-to-all-start) | async-done | bytes 393248 | tf_op jit(solution)/shard_map/all_to_all | solution.py:370
  27.5 0.0 copy-done.2
  27.5 0.6 shard_map.69
  28.1 1.9 %collective-permute-start.2 = (f32[91,8,128]{2,1,0:T(8,128)S(1)}, f32[91,8,128]{2,1,0:T(8,128)S(1)}, u32[]{:S(2)}, u32[]{:S(2)}) collective-permute-start(f32[91,8,128]{2,1,0:T(8,128)S(1)} %get-tuple-element.13.field_ref), channel_id=1, source_target_pairs={{0,1},{1,2},{2,3},{3,4},{4,5},{5,6},{6,7},{7,8},{8,9},{9,10},{10,1... | collective-permute-start | bytes 1118216 | tf_op jit(solution)/shard_map/ppermute | solution.py:351
  30.0 11.3 %collective-permute-start.1 = (f32[91,8,128]{2,1,0:T(8,128)S(1)}, f32[91,8,128]{2,1,0:T(8,128)S(1)}, u32[]{:S(2)}, u32[]{:S(2)}) collective-permute-start(f32[91,8,128]{2,1,0:T(8,128)S(1)} %get-tuple-element.13.field_ref), channel_id=1, source_target_pairs={{0,31},{1,0},{2,1},{3,2},{4,3},{5,4},{6,5},{7,6},{8,7},{9,8},{10,9... | collective-permute-start | bytes 1118216 | tf_op jit(solution)/shard_map/ppermute | solution.py:351
  41.3 1.9 %collective-permute-start = (f32[25,8,128]{2,1,0:T(8,128)S(1)}, f32[25,8,128]{2,1,0:T(8,128)S(1)}, u32[]{:S(2)}, u32[]{:S(2)}) collective-permute-start(f32[25,8,128]{2,1,0:T(8,128)S(1)} %get-tuple-element.12), channel_id=1, source_target_pairs={{0,2},{1,3},{2,4},{3,5},{4,6},{5,7},{6,8},{7,9},{8,10},{9,11},{10,... | collective-permute-start | bytes 307208 | tf_op jit(solution)/shard_map/ppermute | solution.py:351
  43.2 7.0 %collective-permute-start.3 = (f32[25,8,128]{2,1,0:T(8,128)S(1)}, f32[25,8,128]{2,1,0:T(8,128)S(1)}, u32[]{:S(2)}, u32[]{:S(2)}) collective-permute-start(f32[25,8,128]{2,1,0:T(8,128)S(1)} %get-tuple-element.14), channel_id=1, source_target_pairs={{0,30},{1,31},{2,0},{3,1},{4,2},{5,3},{6,4},{7,5},{8,6},{9,7},{10,... | collective-permute-start | bytes 307208 | tf_op jit(solution)/shard_map/ppermute | solution.py:351
  50.2 1.5 %collective-permute-done.top_far_ref = f32[25,8,128]{2,1,0:T(8,128)S(1)} collective-permute-done((f32[25,8,128]{2,1,0:T(8,128)S(1)}, f32[25,8,128]{2,1,0:T(8,128)S(1)}, u32[]{:S(2)}, u32[]{:S(2)}) %collective-permute-start) | collective-permute-done | bytes 102432 | tf_op jit(solution)/shard_map/ppermute | solution.py:351
  51.7 2.0 %collective-permute-done.3.bottom_far_ref = f32[25,8,128]{2,1,0:T(8,128)S(1)} collective-permute-done((f32[25,8,128]{2,1,0:T(8,128)S(1)}, f32[25,8,128]{2,1,0:T(8,128)S(1)}, u32[]{:S(2)}, u32[]{:S(2)}) %collective-permute-start.3) | collective-permute-done | bytes 102432 | tf_op jit(solution)/shard_map/ppermute | solution.py:351
  53.7 0.0 collective-permute-done.2.top_ref
  53.7 0.0 collective-permute-done.1.bottom_ref
  53.7 0.0 copy-done.3
  53.7 4.7 %shard_map.70 = (f32[8,11,8,128]{3,2,1,0:T(8,128)S(1)}, f32[8,11,8,128]{3,2,1,0:T(8,128)S(1)}, f32[8,11,8,128]{3,2,1,0:T(8,128)S(1)}, f32[8,11,8,128]{3,2,1,0:T(8,128)S(1)}, f32[64,1,128]{2,1,0:T(1,128)S(1)}) custom-call(f32[25,8,128]{2,1,0:T(8,128)S(1)} %collective-permute-done.top_far_ref, f32[91,8,128]{2,1,0:T(8,128)S(1)} %collective-permute-done.1.bottom_ref, ...), custom_call_target="tpu_custom_call" | custom-call | tf_op jit(solution)/shard_map/pallas_call | solution.py:394
  58.4 12.9 %all_to_all.20 = f32[64,1,128]{2,1,0:T(1,128)S(1)} all-to-all(f32[64,1,128]{2,1,0:T(1,128)S(1)} %get-tuple-element.15), channel_id=1, replica_groups={{0,1,2,3,32,33,34,35,64,65,66,67,96,97,98,99,128,129,130,131,160,161,16..., dimensions={0} | all-to-all | bytes 65536 | tf_op jit(solution)/shard_map/all_to_all | solution.py:406
  71.3 0.1 reduce_sum.9
  71.4 13.2 %all_to_all.21.sums_ref = f32[8,1,128]{2,1,0:T(1,128)S(1)} all-to-all(f32[8,1,128]{2,1,0:T(1,128)S(1)} %broadcast_in_dim.2), channel_id=1, replica_groups={{0,4,8,12,16,20,24,28},{1,5,9,13,17,21,25,29},{2,6,10,14,18,22,26,30},{..., dimensions={0} | all-to-all | bytes 8192 | tf_op jit(solution)/shard_map/all_to_all | solution.py:410
  84.6 1.3 %shard_map.71 = f32[16,64,128]{2,1,0:T(8,128)S(1)} custom-call(f32[128,128]{1,0:T(8,128)S(1)} %copy-done.2, f32[8,1,128]{2,1,0:T(1,128)S(1)} %all_to_all.21.sums_ref, f32[8,11,8,128]{3,2,1,0:T(8,128)S(1)} %get-tuple-element.16.one_ref, f32[8,11,8,128]{3,2,1,0:T(8,128)S(1)} %get-tuple-element.17.two_ref, f32[8,11,8,128]{3,2,1,0:T(8,128)S(1)} %get-tuple-element.18.three_ref, ...), custom_call_target="tpu_custom_call" | custom-call | tf_op jit(solution)/shard_map/pallas_call | solution.py:411
  86.0 0.0 copy-start.1
  86.0 22.3 %all_to_all.22.source_ref = f32[16,64,128]{2,1,0:T(8,128)S(1)} all-to-all(f32[16,64,128]{2,1,0:T(8,128)S(1)} %shard_map.71), channel_id=1, replica_groups=mesh['tm'=16,'space'=32] {'tm'}, dimensions={0} | all-to-all | bytes 1048576 | tf_op jit(solution)/shard_map/all_to_all | solution.py:416
  108.3 0.0 copy-done.1
  108.3 1.0 shard_map.72
  (4 shorter events, 0.0 us)
Async XLA Ops:
  0.6 1.0 copy-start
  2.6 10.4 %copy-start.4 = (s32[2,8,1024]{2,1,0:T(8,128)S(1)}, s32[2,8,1024]{2,1,0:T(8,128)}, u32[]{:S(2)}) copy-start(s32[2,8,1024]{2,1,0:T(8,128)} %param.7) | copy-start | bytes 196612
  2.6 24.9 %all-to-all-start = ((f32[16,48,128]{2,1,0:T(8,128)}), f32[16,48,128]{2,1,0:T(8,128)S(1)}, u32[]{:S(2)}, u32[]{:S(2)}) async-start(f32[16,48,128]{2,1,0:T(8,128)} %shard_map.68), calls=%async_computation | async-start | bytes 786432 | tf_op jit(solution)/shard_map/all_to_all | solution.py:370
  13.0 0.8 copy-start.5
  13.8 13.7 %copy-start.2 = (f32[128,128]{1,0:T(8,128)S(1)}, f32[128,128]{1,0:T(8,128)}, u32[]{:S(2)}) copy-start(f32[128,128]{1,0:T(8,128)} %constant.18.clone.cas_ref) | copy-start | bytes 196612
  14.0 39.6 %copy-start.3 = (f32[10,8,128]{2,1,0:T(8,128)S(1)}, f32[10,8,128]{2,1,0:T(8,128)}, u32[]{:S(2)}) copy-start(f32[10,8,128]{2,1,0:T(8,128)} %constant.19.clone.coef_ref) | copy-start | bytes 122884
  28.1 25.6 %collective-permute-start.2 = (f32[91,8,128]{2,1,0:T(8,128)S(1)}, f32[91,8,128]{2,1,0:T(8,128)S(1)}, u32[]{:S(2)}, u32[]{:S(2)}) collective-permute-start(f32[91,8,128]{2,1,0:T(8,128)S(1)} %get-tuple-element.13.field_ref), channel_id=1, source_target_pairs={{0,1},{1,2},{2,3},{3,4},{4,5},{5,6},{6,7},{7,8},{8,9},{9,10},{10,1... | collective-permute-start | bytes 1118216 | tf_op jit(solution)/shard_map/ppermute | solution.py:351
  30.0 23.7 %collective-permute-start.1 = (f32[91,8,128]{2,1,0:T(8,128)S(1)}, f32[91,8,128]{2,1,0:T(8,128)S(1)}, u32[]{:S(2)}, u32[]{:S(2)}) collective-permute-start(f32[91,8,128]{2,1,0:T(8,128)S(1)} %get-tuple-element.13.field_ref), channel_id=1, source_target_pairs={{0,31},{1,0},{2,1},{3,2},{4,3},{5,4},{6,5},{7,6},{8,7},{9,8},{10,9... | collective-permute-start | bytes 1118216 | tf_op jit(solution)/shard_map/ppermute | solution.py:351
  41.3 10.4 %collective-permute-start = (f32[25,8,128]{2,1,0:T(8,128)S(1)}, f32[25,8,128]{2,1,0:T(8,128)S(1)}, u32[]{:S(2)}, u32[]{:S(2)}) collective-permute-start(f32[25,8,128]{2,1,0:T(8,128)S(1)} %get-tuple-element.12), channel_id=1, source_target_pairs={{0,2},{1,3},{2,4},{3,5},{4,6},{5,7},{6,8},{7,9},{8,10},{9,11},{10,... | collective-permute-start | bytes 307208 | tf_op jit(solution)/shard_map/ppermute | solution.py:351
  43.2 10.5 %collective-permute-start.3 = (f32[25,8,128]{2,1,0:T(8,128)S(1)}, f32[25,8,128]{2,1,0:T(8,128)S(1)}, u32[]{:S(2)}, u32[]{:S(2)}) collective-permute-start(f32[25,8,128]{2,1,0:T(8,128)S(1)} %get-tuple-element.14), channel_id=1, source_target_pairs={{0,30},{1,31},{2,0},{3,1},{4,2},{5,3},{6,4},{7,5},{8,6},{9,7},{10,... | collective-permute-start | bytes 307208 | tf_op jit(solution)/shard_map/ppermute | solution.py:351
  86.0 22.3 %copy-start.1 = (f32[8,8,1024]{2,1,0:T(8,128)S(1)}, f32[8,8,1024]{2,1,0:T(8,128)}, u32[]{:S(2)}) copy-start(f32[8,8,1024]{2,1,0:T(8,128)} %param.5) | copy-start | bytes 786436

commit v14 on v7

--- a/solution.py
+++ b/solution.py
@@ -108,8 +108,33 @@
             out_ref[2 * part + 1, start : start + times, :] = odd[part]
 
 
+def reach(distance):
+    halo = 2 * HALO - distance
+    margin = 0 if halo == 0 else 4 if halo <= 4 else 8 if halo <= 8 else 12
+    return SIDE - margin, SIDE + LANES // 2 + margin
+
+
+def sent_places(distances, start):
+    places = {}
+    for distance in distances:
+        places[distance] = start
+        first, last = reach(distance)
+        start += last - first
+    return places, start
+
+
+def near_places(rows):
+    return sent_places(range(rows, 0, -1), 3 * rows)
+
+
+def far_places(rows):
+    places, end = sent_places(range(rows + 1, rows + FAR + 1), SUB)
+    return places, end + SIDE
+
+
 def forward_kernel(
-    rows, times, length, cas_ref, field_ref, local_ref, out_ref, low_ref, high_ref, line_ref
+    rows, times, length, cas_ref, field_ref, local_ref,
+    out_ref, up_ref, down_ref, far_up_ref, far_down_ref, line_ref,
 ):
     half = LANES // 2
     span = half + 2 * SIDE
@@ -135,23 +160,30 @@
         for column in range(BLOCK):
             value = line_ref[pl.ds(row * span + skip + column, SUB, stride=BLOCK), :]
             out_ref[row * BLOCK + column] = value
-            if row < FAR:
-                low_ref[row * BLOCK + column] = value
-            if row >= rows - FAR:
-                high_ref[(row - (rows - FAR)) * BLOCK + column] = value
-    for ref in (out_ref, low_ref, high_ref):
-        first = ref.shape[0] - 3
-        for plane in range(3):
-            ref[first + plane] = local_ref[plane * rows : (plane + 1) * rows, :]
-
-
-def weight_lines(rows, refs, scratch_ref):
-    planes = []
     for plane in range(3):
-        blocks = [ref[ref.shape[0] - 3 + plane] for ref in refs]
-        blocks[0] = blocks[0][rows - FAR :]
-        blocks[-1] = blocks[-1][:FAR]
-        planes.append(jnp.concatenate(blocks, axis=0))
+        out_ref[rows * BLOCK + plane] = local_ref[plane * rows : (plane + 1) * rows, :]
+    near, far = near_places(rows)[0], far_places(rows)[0]
+    for ref, places, row_of in (
+        (up_ref, near, lambda distance: rows - distance),
+        (down_ref, near, lambda distance: distance - 1),
+        (far_up_ref, far, lambda distance: 2 * rows - distance),
+        (far_down_ref, far, lambda distance: distance - 1 - rows),
+    ):
+        for distance, place in places.items():
+            first, last = reach(distance)
+            start = row_of(distance) * span
+            ref[place : place + last - first, :] = line_ref[start + first : start + last, :]
+    up_ref[: 3 * rows, :] = local_ref[...]
+    down_ref[: 3 * rows, :] = local_ref[...]
+    for ref, first in ((far_up_ref, rows - FAR), (far_down_ref, 0)):
+        ref[ref.shape[0] - SIDE :, :] = jnp.zeros((SIDE, LANES), jnp.float32)
+        kept = [local_ref[plane * rows + first : plane * rows + first + FAR, :] for plane in range(3)]
+        kept.append(jnp.zeros((SUB - 3 * FAR, LANES), jnp.float32))
+        ref[:SUB, :] = jnp.concatenate(kept, axis=0)
+
+
+def weight_lines(parts, scratch_ref):
+    planes = [jnp.concatenate(blocks, axis=0) for blocks in zip(*parts)]
     east = 1.0 + 0.125 * (planes[1] + jnp.concatenate([planes[1][1:], planes[1][:1]], axis=0))
     north = 1.0 + 0.125 * (planes[2] + pltpu.roll(planes[2], LANES - 1, 1))
     total = planes[0].shape[0]
@@ -224,13 +256,18 @@
     step_ref, remain_ref, part_ref, middle_ref, wide_ref, scratch_ref,
 ):
     columns = range(BLOCK)
-    refs = (top_far_ref, top_ref, field_ref, bottom_ref, bottom_far_ref)
-    lines = weight_lines(rows, refs, scratch_ref)
+    parts = [
+        [top_far_ref[plane * FAR : (plane + 1) * FAR, :] for plane in range(3)],
+        [top_ref[plane * rows : (plane + 1) * rows, :] for plane in range(3)],
+        [field_ref[rows * BLOCK + plane] for plane in range(3)],
+        [bottom_ref[plane * rows : (plane + 1) * rows, :] for plane in range(3)],
+        [bottom_far_ref[plane * FAR : (plane + 1) * FAR, :] for plane in range(3)],
+    ]
+    lines = weight_lines(parts, scratch_ref)
     coef = [coef_ref[index] for index in range(2 + 2 * CHEB)]
-    places = [
-        (ref, row) for ref in refs for row in range((ref.shape[0] - 3) // BLOCK)
-    ]
-    total = len(places)
+    total = 3 * rows + 2 * FAR
+    skip = (LANES // 2 + 2 * SIDE - WINDOW) // 2
+    near, far = near_places(rows)[0], far_places(rows)[0]
     own = (FAR + rows, FAR + 2 * rows)
     made = set()
 
@@ -247,8 +284,15 @@
         return value
 
     def first_source(row, column):
-        ref, place = places[row]
-        return ref[place * BLOCK + column]
+        if row in range(*own):
+            return field_ref[(row - own[0]) * BLOCK + column]
+        distance = own[0] - row if row < own[0] else row - own[1] + 1
+        if distance > rows:
+            ref, place = (top_far_ref if row < own[0] else bottom_far_ref), far[distance]
+        else:
+            ref, place = (top_ref if row < own[0] else bottom_ref), near[distance]
+        start = place - reach(distance)[0] + skip + column
+        return ref[pl.ds(start, SUB, stride=BLOCK), :]
 
     def second_source(row, column):
         return middle_ref[row, column]
@@ -375,16 +419,16 @@
     local = lax.dynamic_slice_in_dim(planes, lax.axis_index("tm") * tile, LANES, 1)
     total = 3 * rows + 2 * FAR
     tile_shape = (rows, BLOCK, SUB, LANES)
-    row_shape = (rows * BLOCK + 3, SUB, LANES)
-    far_shape = (FAR * BLOCK + 3, SUB, LANES)
+    near_shape = (near_places(rows)[1], LANES)
+    far_shape = (far_places(rows)[1], LANES)
     span = LANES // 2 + 2 * SIDE
-    freq, low, high = call(
+    freq, up, down, far_up, far_down = call(
         functools.partial(forward_kernel, rows, times, length),
-        [row_shape, far_shape, far_shape],
+        [(rows * BLOCK + 3, SUB, LANES), near_shape, near_shape, far_shape, far_shape],
         [(rows * span, LANES)],
     )(cas_table, gathered, local)
-    top, bottom = shift(freq, 1, spaces), shift(freq, -1, spaces)
-    top_far, bottom_far = shift(high, 2, spaces), shift(low, -2, spaces)
+    top, bottom = shift(up, 1, spaces), shift(down, -1, spaces)
+    top_far, bottom_far = shift(far_up, 2, spaces), shift(far_down, -2, spaces)
 
     groups = [
         [i * spaces + first + j for i in range(tiles) for j in range(NEAR)]

time: 111 us -> 109 us (0.982)
  waiting for transfers between devices: 22.6 us -> 16.1 us
  blocking collectives: 44.1 us -> 48.7 us
    ppermute x4, waiting for transfers between devices: 9.14 us -> 2.6 us  [shift(): lax.ppermute(value, 'space', [(i, (i + distance) % spaces) for i in range...]
    all_to_all x1, blocking collectives: 8.89 us -> 13.5 us  [shards(): sums = lax.all_to_all(sums, 'space', 0, 0, axis_index_groups=groups)]
  transfers between devices with their start and end apart: 5 -> 5, of which waited for: 4 -> 3; matrix products, arithmetic and copies ran while one was open for 0% -> 0% of each run, Pallas kernels for 0% -> 0%
where the time goes in v14:
time: 109 us
  blocking collectives  48.7 us (45%)
  starting transfers between devices  32.4 us (30%)
  waiting for transfers between devices  16.1 us (15%)
  Pallas kernels  8.61 us (8%)
  local copies, waits for them, and re-layouts  1.98 us (2%)
    all_to_all x1, blocking collectives, shards(): returned = lax.all_to_all(packed, 'tm', 0, 0)  22.3 us
    ppermute x4, starting transfers between devices, shift(): lax.ppermute(value, 'space', [(i, (i + distance) % spaces) for i in range...  22.1 us
    all_to_all x1, blocking collectives, shards(): sums = lax.all_to_all(sums, 'space', 0, 0, axis_index_groups=groups)  13.5 us
    all_to_all x1, waiting for transfers between devices, shards(): gathered = lax.all_to_all(windows, 'tm', 0, 0)  13.5 us
    all_to_all x1, blocking collectives, shards(): sums = lax.all_to_all(sums, ('tm', 'space'), 0, 0, axis_index_groups=groups)  12.9 us
    all_to_all x1, starting transfers between devices, shards(): gathered = lax.all_to_all(windows, 'tm', 0, 0)  10.3 us
    pallas_call x1, Pallas kernels, shards(): call(functools.partial(stencil_kernel, rows), [tile_shape] * 4 + [(tiles...  4.67 us
    ppermute x4, waiting for transfers between devices, shift(): lax.ppermute(value, 'space', [(i, (i + distance) % spaces) for i in range...  2.6 us
  transfers between devices with their start and end apart: 5, of which 3 were waited for; matrix products, arithmetic and copies ran while one was open for 0% of the time, Pallas kernels for 0%

profile of v14, /device:TPU:1, one launch (start us, length us, event | category | flops | bytes accessed | tf_op | source)
XLA Modules:
  0.0 108.6 jit_solution(3485992714582822180)
XLA Ops:
  0.6 0.0 copy-start
  0.6 0.9 copy-done
  1.6 1.0 shard_map.68
  2.6 0.0 copy-start.4
  2.6 10.3 %all-to-all-start = ((f32[16,48,128]{2,1,0:T(8,128)}), f32[16,48,128]{2,1,0:T(8,128)S(1)}, u32[]{:S(2)}, u32[]{:S(2)}) async-start(f32[16,48,128]{2,1,0:T(8,128)} %shard_map.68), calls=%async_computation | async-start | bytes 786432 | tf_op jit(solution)/shard_map/all_to_all | solution.py:414
  13.0 0.0 copy-done.4
  13.0 0.0 copy-start.5
  13.0 0.7 copy-done.5
  13.8 0.1 fusion
  13.8 0.0 copy-start.2
  13.8 0.1 concatenate.7
  14.0 0.1 constant_dynamic-slice_fusion.local_ref
  14.0 0.0 copy-start.3
  14.0 13.5 %all-to-all-done.field_ref = f32[16,48,128]{2,1,0:T(8,128)S(1)} async-done(((f32[16,48,128]{2,1,0:T(8,128)}), f32[16,48,128]{2,1,0:T(8,128)S(1)}, u32[]{:S(2)}, u32[]{:S(2)}) %all-to-all-start) | async-done | bytes 393248 | tf_op jit(solution)/shard_map/all_to_all | solution.py:414
  27.5 0.0 copy-done.2
  27.5 0.6 shard_map.69
  28.1 1.9 %collective-permute-start.1 = (f32[648,128]{1,0:T(8,128)S(1)}, f32[648,128]{1,0:T(8,128)S(1)}, u32[]{:S(2)}, u32[]{:S(2)}) collective-permute-start(f32[648,128]{1,0:T(8,128)S(1)} %get-tuple-element.15), channel_id=1, source_target_pairs={{0,1},{1,2},{2,3},{3,4},{4,5},{5,6},{6,7},{7,8},{8,9},{9,10},{10,1... | collective-permute-start | bytes 995336 | tf_op jit(solution)/shard_map/ppermute | solution.py:395
  30.1 11.3 %collective-permute-start.2 = (f32[648,128]{1,0:T(8,128)S(1)}, f32[648,128]{1,0:T(8,128)S(1)}, u32[]{:S(2)}, u32[]{:S(2)}) collective-permute-start(f32[648,128]{1,0:T(8,128)S(1)} %get-tuple-element.17), channel_id=1, source_target_pairs={{0,31},{1,0},{2,1},{3,2},{4,3},{5,4},{6,5},{7,6},{8,7},{9,8},{10,9... | collective-permute-start | bytes 995336 | tf_op jit(solution)/shard_map/ppermute | solution.py:395
  41.3 1.9 %collective-permute-start = (f32[160,128]{1,0:T(8,128)S(1)}, f32[160,128]{1,0:T(8,128)S(1)}, u32[]{:S(2)}, u32[]{:S(2)}) collective-permute-start(f32[160,128]{1,0:T(8,128)S(1)} %get-tuple-element.14), channel_id=1, source_target_pairs={{0,2},{1,3},{2,4},{3,5},{4,6},{5,7},{6,8},{7,9},{8,10},{9,11},{10,... | collective-permute-start | bytes 245768 | tf_op jit(solution)/shard_map/ppermute | solution.py:395
  43.2 7.0 %collective-permute-start.3 = (f32[160,128]{1,0:T(8,128)S(1)}, f32[160,128]{1,0:T(8,128)S(1)}, u32[]{:S(2)}, u32[]{:S(2)}) collective-permute-start(f32[160,128]{1,0:T(8,128)S(1)} %get-tuple-element.18), channel_id=1, source_target_pairs={{0,30},{1,31},{2,0},{3,1},{4,2},{5,3},{6,4},{7,5},{8,6},{9,7},{10,... | collective-permute-start | bytes 245768 | tf_op jit(solution)/shard_map/ppermute | solution.py:395
  50.2 1.0 collective-permute-done.top_far_ref
  51.3 1.6 %collective-permute-done.3.bottom_far_ref = f32[160,128]{1,0:T(8,128)S(1)} collective-permute-done((f32[160,128]{1,0:T(8,128)S(1)}, f32[160,128]{1,0:T(8,128)S(1)}, u32[]{:S(2)}, u32[]{:S(2)}) %collective-permute-start.3) | collective-permute-done | bytes 81952 | tf_op jit(solution)/shard_map/ppermute | solution.py:395
  52.8 0.0 collective-permute-done.1.top_ref
  52.8 0.0 collective-permute-done.2.bottom_ref
  52.8 0.0 copy-done.3
  52.8 4.7 %shard_map.70 = (f32[8,11,8,128]{3,2,1,0:T(8,128)S(1)}, f32[8,11,8,128]{3,2,1,0:T(8,128)S(1)}, f32[8,11,8,128]{3,2,1,0:T(8,128)S(1)}, f32[8,11,8,128]{3,2,1,0:T(8,128)S(1)}, f32[64,1,128]{2,1,0:T(1,128)S(1)}) custom-call(f32[160,128]{1,0:T(8,128)S(1)} %collective-permute-done.top_far_ref, f32[648,128]{1,0:T(8,128)S(1)} %collective-permute-done.1.top_ref, ...), custom_call_target="tpu_custom_call" | custom-call | tf_op jit(solution)/shard_map/pallas_call | solution.py:438
  57.5 12.9 %all_to_all.20 = f32[64,1,128]{2,1,0:T(1,128)S(1)} all-to-all(f32[64,1,128]{2,1,0:T(1,128)S(1)} %get-tuple-element.19), channel_id=1, replica_groups={{0,1,2,3,32,33,34,35,64,65,66,67,96,97,98,99,128,129,130,131,160,161,16..., dimensions={0} | all-to-all | bytes 65536 | tf_op jit(solution)/shard_map/all_to_all | solution.py:450
  70.4 0.1 reduce_sum.9
  70.5 13.5 %all_to_all.21.sums_ref = f32[8,1,128]{2,1,0:T(1,128)S(1)} all-to-all(f32[8,1,128]{2,1,0:T(1,128)S(1)} %broadcast_in_dim.2), channel_id=1, replica_groups={{0,4,8,12,16,20,24,28},{1,5,9,13,17,21,25,29},{2,6,10,14,18,22,26,30},{..., dimensions={0} | all-to-all | bytes 8192 | tf_op jit(solution)/shard_map/all_to_all | solution.py:454
  84.0 1.3 %shard_map.71 = f32[16,64,128]{2,1,0:T(8,128)S(1)} custom-call(f32[128,128]{1,0:T(8,128)S(1)} %copy-done.2, f32[8,1,128]{2,1,0:T(1,128)S(1)} %all_to_all.21.sums_ref, f32[8,11,8,128]{3,2,1,0:T(8,128)S(1)} %get-tuple-element.20.one_ref, f32[8,11,8,128]{3,2,1,0:T(8,128)S(1)} %get-tuple-element.21.two_ref, f32[8,11,8,128]{3,2,1,0:T(8,128)S(1)} %get-tuple-element.22.three_ref, ...), custom_call_target="tpu_custom_call" | custom-call | tf_op jit(solution)/shard_map/pallas_call | solution.py:455
  85.4 0.0 copy-start.1
  85.4 22.3 %all_to_all.22.source_ref = f32[16,64,128]{2,1,0:T(8,128)S(1)} all-to-all(f32[16,64,128]{2,1,0:T(8,128)S(1)} %shard_map.71), channel_id=1, replica_groups=mesh['tm'=16,'space'=32] {'tm'}, dimensions={0} | all-to-all | bytes 1048576 | tf_op jit(solution)/shard_map/all_to_all | solution.py:460
  107.7 0.0 copy-done.1
  107.7 1.0 shard_map.72
  (4 shorter events, 0.0 us)
Async XLA Ops:
  0.6 1.0 copy-start
  2.6 10.4 %copy-start.4 = (s32[2,8,1024]{2,1,0:T(8,128)S(1)}, s32[2,8,1024]{2,1,0:T(8,128)}, u32[]{:S(2)}) copy-start(s32[2,8,1024]{2,1,0:T(8,128)} %param.7) | copy-start | bytes 196612
  2.6 24.9 %all-to-all-start = ((f32[16,48,128]{2,1,0:T(8,128)}), f32[16,48,128]{2,1,0:T(8,128)S(1)}, u32[]{:S(2)}, u32[]{:S(2)}) async-start(f32[16,48,128]{2,1,0:T(8,128)} %shard_map.68), calls=%async_computation | async-start | bytes 786432 | tf_op jit(solution)/shard_map/all_to_all | solution.py:414
  13.0 0.8 copy-start.5
  13.8 13.7 %copy-start.2 = (f32[128,128]{1,0:T(8,128)S(1)}, f32[128,128]{1,0:T(8,128)}, u32[]{:S(2)}) copy-start(f32[128,128]{1,0:T(8,128)} %constant.18.clone.cas_ref) | copy-start | bytes 196612
  14.0 38.8 %copy-start.3 = (f32[10,8,128]{2,1,0:T(8,128)S(1)}, f32[10,8,128]{2,1,0:T(8,128)}, u32[]{:S(2)}) copy-start(f32[10,8,128]{2,1,0:T(8,128)} %constant.19.clone.coef_ref) | copy-start | bytes 122884
  28.1 24.7 %collective-permute-start.1 = (f32[648,128]{1,0:T(8,128)S(1)}, f32[648,128]{1,0:T(8,128)S(1)}, u32[]{:S(2)}, u32[]{:S(2)}) collective-permute-start(f32[648,128]{1,0:T(8,128)S(1)} %get-tuple-element.15), channel_id=1, source_target_pairs={{0,1},{1,2},{2,3},{3,4},{4,5},{5,6},{6,7},{7,8},{8,9},{9,10},{10,1... | collective-permute-start | bytes 995336 | tf_op jit(solution)/shard_map/ppermute | solution.py:395
  30.1 22.8 %collective-permute-start.2 = (f32[648,128]{1,0:T(8,128)S(1)}, f32[648,128]{1,0:T(8,128)S(1)}, u32[]{:S(2)}, u32[]{:S(2)}) collective-permute-start(f32[648,128]{1,0:T(8,128)S(1)} %get-tuple-element.17), channel_id=1, source_target_pairs={{0,31},{1,0},{2,1},{3,2},{4,3},{5,4},{6,5},{7,6},{8,7},{9,8},{10,9... | collective-permute-start | bytes 995336 | tf_op jit(solution)/shard_map/ppermute | solution.py:395
  41.3 9.9 %collective-permute-start = (f32[160,128]{1,0:T(8,128)S(1)}, f32[160,128]{1,0:T(8,128)S(1)}, u32[]{:S(2)}, u32[]{:S(2)}) collective-permute-start(f32[160,128]{1,0:T(8,128)S(1)} %get-tuple-element.14), channel_id=1, source_target_pairs={{0,2},{1,3},{2,4},{3,5},{4,6},{5,7},{6,8},{7,9},{8,10},{9,11},{10,... | collective-permute-start | bytes 245768 | tf_op jit(solution)/shard_map/ppermute | solution.py:395
  43.2 9.6 %collective-permute-start.3 = (f32[160,128]{1,0:T(8,128)S(1)}, f32[160,128]{1,0:T(8,128)S(1)}, u32[]{:S(2)}, u32[]{:S(2)}) collective-permute-start(f32[160,128]{1,0:T(8,128)S(1)} %get-tuple-element.18), channel_id=1, source_target_pairs={{0,30},{1,31},{2,0},{3,1},{4,2},{5,3},{6,4},{7,5},{8,6},{9,7},{10,... | collective-permute-start | bytes 245768 | tf_op jit(solution)/shard_map/ppermute | solution.py:395
  85.4 22.3 %copy-start.1 = (f32[8,8,1024]{2,1,0:T(8,128)S(1)}, f32[8,8,1024]{2,1,0:T(8,128)}, u32[]{:S(2)}) copy-start(f32[8,8,1024]{2,1,0:T(8,128)} %param.5) | copy-start | bytes 786436

commit v15 on v14

--- a/solution.py
+++ b/solution.py
@@ -60,11 +60,19 @@
     )
 
 
-def window_kernel(rows, times, tiles, source_ref, out_ref, scratch_ref):
+def window_kernel(rows, times, tiles, source_ref, out_ref, scratch_ref, arrived):
     half = LANES // 2
     parts = source_ref.shape[1] // LANES
-    for part in range(parts):
-        scratch_ref[part] = source_ref[:, part * LANES : (part + 1) * LANES]
+    copies = [
+        pltpu.make_async_copy(
+            source_ref.at[:, pl.ds(part * LANES, LANES)], scratch_ref.at[part], arrived.at[part]
+        )
+        for part in range(parts)
+    ]
+    for copy in copies:
+        copy.start()
+    for copy in copies:
+        copy.wait()
     lane = lane_index((times, LANES))
     fields = [
         [scratch_ref[part, pl.ds(row, times, stride=rows), :] for part in range(parts)]
@@ -251,7 +259,7 @@
 
 
 def stencil_kernel(
-    rows, top_far_ref, top_ref, field_ref, bottom_ref, bottom_far_ref, coef_ref,
+    rows, bottom_far_ref, top_ref, field_ref, bottom_ref, top_far_ref, coef_ref,
     solved_ref, applied_ref, solved_two_ref, applied_two_ref, sums_ref,
     step_ref, remain_ref, part_ref, middle_ref, wide_ref, scratch_ref,
 ):
@@ -406,10 +414,15 @@
     coef_table = jnp.asarray(chebyshev_table(length))
 
     field = right_side.reshape(times * rows, width)
-    windows = call(
+    windows = pl.pallas_call(
         functools.partial(window_kernel, rows, times, tiles),
-        [(tiles, 6 * times, LANES)],
-        [(width // LANES, times * rows, LANES)],
+        out_shape=jax.ShapeDtypeStruct((tiles, 6 * times, LANES), jnp.float32),
+        in_specs=[pl.BlockSpec(memory_space=pl.ANY)],
+        scratch_shapes=[
+            pltpu.VMEM((width // LANES, times * rows, LANES), jnp.float32),
+            pltpu.SemaphoreType.DMA((width // LANES,)),
+        ],
+        compiler_params=PARAMS,
     )(field)
     gathered = lax.all_to_all(windows, "tm", 0, 0)
 
@@ -446,7 +459,7 @@
             (total, 3 * BLOCK, SUB, LANES),
             (LANES, LANES),
         ],
-    )(top_far, top, freq, bottom, bottom_far, coef_table)
+    )(bottom_far, top, freq, bottom, top_far, coef_table)
     sums = lax.all_to_all(sums, ("tm", "space"), 0, 0, axis_index_groups=groups)
     planes = spaces // NEAR
     groups = [[first + NEAR * i for i in range(planes)] for first in range(NEAR)]

time: 109 us -> 109 us (level)
  waiting for transfers between devices: 16.1 us -> 19.8 us
  blocking collectives: 48.7 us -> 46.5 us
  starting transfers between devices: 32.4 us -> 30.3 us
    ppermute x4, waiting for transfers between devices: 2.6 us -> 6.35 us  [shift(): lax.ppermute(value, 'space', [(i, (i + distance) % spaces) for i in range...]
    all_to_all x1, blocking collectives: 13.5 us -> 10.6 us  [shards(): sums = lax.all_to_all(sums, 'space', 0, 0, axis_index_groups=groups)]
    ppermute x4, starting transfers between devices: 22.1 us -> 20 us  [shift(): lax.ppermute(value, 'space', [(i, (i + distance) % spaces) for i in range...]
where the time goes in v15:
time: 109 us; the launch traced here: 108 us
  blocking collectives  46.5 us (43%)
  starting transfers between devices  30.3 us (28%)
  waiting for transfers between devices  19.8 us (18%)
  Pallas kernels  8.72 us (8%)
  local copies, waits for them, and re-layouts  1.98 us (2%)
    all_to_all x1, blocking collectives, shards(): returned = lax.all_to_all(packed, 'tm', 0, 0)  22.3 us
    ppermute x4, starting transfers between devices, shift(): lax.ppermute(value, 'space', [(i, (i + distance) % spaces) for i in range...  20 us
    all_to_all x1, blocking collectives, shards(): sums = lax.all_to_all(sums, ('tm', 'space'), 0, 0, axis_index_groups=groups)  13.7 us
    all_to_all x1, waiting for transfers between devices, shards(): gathered = lax.all_to_all(windows, 'tm', 0, 0)  13.5 us
    all_to_all x1, blocking collectives, shards(): sums = lax.all_to_all(sums, 'space', 0, 0, axis_index_groups=groups)  10.6 us
    all_to_all x1, starting transfers between devices, shards(): gathered = lax.all_to_all(windows, 'tm', 0, 0)  10.4 us
    ppermute x4, waiting for transfers between devices, shift(): lax.ppermute(value, 'space', [(i, (i + distance) % spaces) for i in range...  6.35 us
    pallas_call x1, Pallas kernels, shards(): call(functools.partial(stencil_kernel, rows), [tile_shape] * 4 + [(tiles...  4.67 us
  transfers between devices with their start and end apart: 5, of which 3 were waited for; matrix products, arithmetic and copies ran while one was open for 0% of the time, Pallas kernels for 0%

profile of v15, /device:TPU:1, one launch (start us, length us, event | category | flops | bytes accessed | tf_op | source)
XLA Modules:
  0.0 108.3 jit_solution(14531447013038891652)
XLA Ops:
  0.6 0.0 copy-start
  0.6 0.9 copy-done
  1.6 1.1 %shard_map.68 = f32[16,48,128]{2,1,0:T(8,128)} custom-call(f32[64,1024]{1,0:T(8,128)S(1)} %bitcast.7), custom_call_target="tpu_custom_call" | custom-call | tf_op jit(solution)/shard_map/pallas_call | solution.py:417
  2.7 0.0 copy-start.4
  2.7 10.4 %all-to-all-start = ((f32[16,48,128]{2,1,0:T(8,128)}), f32[16,48,128]{2,1,0:T(8,128)S(1)}, u32[]{:S(2)}, u32[]{:S(2)}) async-start(f32[16,48,128]{2,1,0:T(8,128)} %shard_map.68), calls=%async_computation | async-start | bytes 786432 | tf_op jit(solution)/shard_map/all_to_all | solution.py:427
  13.1 0.0 copy-done.4
  13.1 0.0 copy-start.5
  13.2 0.7 copy-done.5
  13.9 0.1 fusion
  14.0 0.0 copy-start.2
  14.0 0.1 concatenate.7
  14.1 0.1 constant_dynamic-slice_fusion.local_ref
  14.2 0.0 copy-start.3
  14.2 13.5 %all-to-all-done.field_ref = f32[16,48,128]{2,1,0:T(8,128)S(1)} async-done(((f32[16,48,128]{2,1,0:T(8,128)}), f32[16,48,128]{2,1,0:T(8,128)S(1)}, u32[]{:S(2)}, u32[]{:S(2)}) %all-to-all-start) | async-done | bytes 393248 | tf_op jit(solution)/shard_map/all_to_all | solution.py:427
  27.7 0.0 copy-done.2
  27.7 0.6 shard_map.69
  28.3 1.9 %collective-permute-start.1 = (f32[648,128]{1,0:T(8,128)S(1)}, f32[648,128]{1,0:T(8,128)S(1)}, u32[]{:S(2)}, u32[]{:S(2)}) collective-permute-start(f32[648,128]{1,0:T(8,128)S(1)} %get-tuple-element.15), channel_id=1, source_target_pairs={{0,1},{1,2},{2,3},{3,4},{4,5},{5,6},{6,7},{7,8},{8,9},{9,10},{10,1... | collective-permute-start | bytes 995336 | tf_op jit(solution)/shard_map/ppermute | solution.py:403
  30.2 11.3 %collective-permute-start.2 = (f32[648,128]{1,0:T(8,128)S(1)}, f32[648,128]{1,0:T(8,128)S(1)}, u32[]{:S(2)}, u32[]{:S(2)}) collective-permute-start(f32[648,128]{1,0:T(8,128)S(1)} %get-tuple-element.17), channel_id=1, source_target_pairs={{0,31},{1,0},{2,1},{3,2},{4,3},{5,4},{6,5},{7,6},{8,7},{9,8},{10,9... | collective-permute-start | bytes 995336 | tf_op jit(solution)/shard_map/ppermute | solution.py:403
  41.5 3.6 %collective-permute-start = (f32[160,128]{1,0:T(8,128)S(1)}, f32[160,128]{1,0:T(8,128)S(1)}, u32[]{:S(2)}, u32[]{:S(2)}) collective-permute-start(f32[160,128]{1,0:T(8,128)S(1)} %get-tuple-element.14), channel_id=1, source_target_pairs={{0,30},{1,31},{2,0},{3,1},{4,2},{5,3},{6,4},{7,5},{8,6},{9,7},{10,... | collective-permute-start | bytes 245768 | tf_op jit(solution)/shard_map/ppermute | solution.py:403
  45.1 3.2 %collective-permute-start.3 = (f32[160,128]{1,0:T(8,128)S(1)}, f32[160,128]{1,0:T(8,128)S(1)}, u32[]{:S(2)}, u32[]{:S(2)}) collective-permute-start(f32[160,128]{1,0:T(8,128)S(1)} %get-tuple-element.18), channel_id=1, source_target_pairs={{0,2},{1,3},{2,4},{3,5},{4,6},{5,7},{6,8},{7,9},{8,10},{9,11},{10,... | collective-permute-start | bytes 245768 | tf_op jit(solution)/shard_map/ppermute | solution.py:403
  48.3 2.8 %collective-permute-done.bottom_far_ref = f32[160,128]{1,0:T(8,128)S(1)} collective-permute-done((f32[160,128]{1,0:T(8,128)S(1)}, f32[160,128]{1,0:T(8,128)S(1)}, u32[]{:S(2)}, u32[]{:S(2)}) %collective-permute-start) | collective-permute-done | bytes 81952 | tf_op jit(solution)/shard_map/ppermute | solution.py:403
  51.1 3.5 %collective-permute-done.3.top_far_ref = f32[160,128]{1,0:T(8,128)S(1)} collective-permute-done((f32[160,128]{1,0:T(8,128)S(1)}, f32[160,128]{1,0:T(8,128)S(1)}, u32[]{:S(2)}, u32[]{:S(2)}) %collective-permute-start.3) | collective-permute-done | bytes 81952 | tf_op jit(solution)/shard_map/ppermute | solution.py:403
  54.6 0.0 collective-permute-done.1.top_ref
  54.6 0.0 collective-permute-done.2.bottom_ref
  54.6 0.0 copy-done.3
  54.6 4.7 %shard_map.70 = (f32[8,11,8,128]{3,2,1,0:T(8,128)S(1)}, f32[8,11,8,128]{3,2,1,0:T(8,128)S(1)}, f32[8,11,8,128]{3,2,1,0:T(8,128)S(1)}, f32[8,11,8,128]{3,2,1,0:T(8,128)S(1)}, f32[64,1,128]{2,1,0:T(1,128)S(1)}) custom-call(f32[160,128]{1,0:T(8,128)S(1)} %collective-permute-done.bottom_far_ref, f32[648,128]{1,0:T(8,128)S(1)} %collective-permute-done.1.top_ref, ...), custom_call_target="tpu_custom_call" | custom-call | tf_op jit(solution)/shard_map/pallas_call | solution.py:451
  59.3 13.7 %all_to_all.20 = f32[64,1,128]{2,1,0:T(1,128)S(1)} all-to-all(f32[64,1,128]{2,1,0:T(1,128)S(1)} %get-tuple-element.19), channel_id=1, replica_groups={{0,1,2,3,32,33,34,35,64,65,66,67,96,97,98,99,128,129,130,131,160,161,16..., dimensions={0} | all-to-all | bytes 65536 | tf_op jit(solution)/shard_map/all_to_all | solution.py:463
  73.0 0.1 reduce_sum.9
  73.1 10.6 %all_to_all.21.sums_ref = f32[8,1,128]{2,1,0:T(1,128)S(1)} all-to-all(f32[8,1,128]{2,1,0:T(1,128)S(1)} %broadcast_in_dim.2), channel_id=1, replica_groups={{0,4,8,12,16,20,24,28},{1,5,9,13,17,21,25,29},{2,6,10,14,18,22,26,30},{..., dimensions={0} | all-to-all | bytes 8192 | tf_op jit(solution)/shard_map/all_to_all | solution.py:467
  83.6 1.3 %shard_map.71 = f32[16,64,128]{2,1,0:T(8,128)S(1)} custom-call(f32[128,128]{1,0:T(8,128)S(1)} %copy-done.2, f32[8,1,128]{2,1,0:T(1,128)S(1)} %all_to_all.21.sums_ref, f32[8,11,8,128]{3,2,1,0:T(8,128)S(1)} %get-tuple-element.20.one_ref, f32[8,11,8,128]{3,2,1,0:T(8,128)S(1)} %get-tuple-element.21.two_ref, f32[8,11,8,128]{3,2,1,0:T(8,128)S(1)} %get-tuple-element.22.three_ref, ...), custom_call_target="tpu_custom_call" | custom-call | tf_op jit(solution)/shard_map/pallas_call | solution.py:468
  85.0 0.0 copy-start.1
  85.0 22.3 %all_to_all.22.source_ref = f32[16,64,128]{2,1,0:T(8,128)S(1)} all-to-all(f32[16,64,128]{2,1,0:T(8,128)S(1)} %shard_map.71), channel_id=1, replica_groups=mesh['tm'=16,'space'=32] {'tm'}, dimensions={0} | all-to-all | bytes 1048576 | tf_op jit(solution)/shard_map/all_to_all | solution.py:473
  107.3 0.0 copy-done.1
  107.3 1.0 shard_map.72
  (4 shorter events, 0.0 us)
Async XLA Ops:
  0.6 1.0 copy-start
  2.7 10.4 %copy-start.4 = (s32[2,8,1024]{2,1,0:T(8,128)S(1)}, s32[2,8,1024]{2,1,0:T(8,128)}, u32[]{:S(2)}) copy-start(s32[2,8,1024]{2,1,0:T(8,128)} %param.7) | copy-start | bytes 196612
  2.7 24.9 %all-to-all-start = ((f32[16,48,128]{2,1,0:T(8,128)}), f32[16,48,128]{2,1,0:T(8,128)S(1)}, u32[]{:S(2)}, u32[]{:S(2)}) async-start(f32[16,48,128]{2,1,0:T(8,128)} %shard_map.68), calls=%async_computation | async-start | bytes 786432 | tf_op jit(solution)/shard_map/all_to_all | solution.py:427
  13.1 0.8 copy-start.5
  14.0 13.7 %copy-start.2 = (f32[128,128]{1,0:T(8,128)S(1)}, f32[128,128]{1,0:T(8,128)}, u32[]{:S(2)}) copy-start(f32[128,128]{1,0:T(8,128)} %constant.18.clone.cas_ref) | copy-start | bytes 196612
  14.2 40.4 %copy-start.3 = (f32[10,8,128]{2,1,0:T(8,128)S(1)}, f32[10,8,128]{2,1,0:T(8,128)}, u32[]{:S(2)}) copy-start(f32[10,8,128]{2,1,0:T(8,128)} %constant.19.clone.coef_ref) | copy-start | bytes 122884
  28.3 26.4 %collective-permute-start.1 = (f32[648,128]{1,0:T(8,128)S(1)}, f32[648,128]{1,0:T(8,128)S(1)}, u32[]{:S(2)}, u32[]{:S(2)}) collective-permute-start(f32[648,128]{1,0:T(8,128)S(1)} %get-tuple-element.15), channel_id=1, source_target_pairs={{0,1},{1,2},{2,3},{3,4},{4,5},{5,6},{6,7},{7,8},{8,9},{9,10},{10,1... | collective-permute-start | bytes 995336 | tf_op jit(solution)/shard_map/ppermute | solution.py:403
  30.2 24.4 %collective-permute-start.2 = (f32[648,128]{1,0:T(8,128)S(1)}, f32[648,128]{1,0:T(8,128)S(1)}, u32[]{:S(2)}, u32[]{:S(2)}) collective-permute-start(f32[648,128]{1,0:T(8,128)S(1)} %get-tuple-element.17), channel_id=1, source_target_pairs={{0,31},{1,0},{2,1},{3,2},{4,3},{5,4},{6,5},{7,6},{8,7},{9,8},{10,9... | collective-permute-start | bytes 995336 | tf_op jit(solution)/shard_map/ppermute | solution.py:403
  41.5 9.6 %collective-permute-start = (f32[160,128]{1,0:T(8,128)S(1)}, f32[160,128]{1,0:T(8,128)S(1)}, u32[]{:S(2)}, u32[]{:S(2)}) collective-permute-start(f32[160,128]{1,0:T(8,128)S(1)} %get-tuple-element.14), channel_id=1, source_target_pairs={{0,30},{1,31},{2,0},{3,1},{4,2},{5,3},{6,4},{7,5},{8,6},{9,7},{10,... | collective-permute-start | bytes 245768 | tf_op jit(solution)/shard_map/ppermute | solution.py:403
  45.1 9.5 %collective-permute-start.3 = (f32[160,128]{1,0:T(8,128)S(1)}, f32[160,128]{1,0:T(8,128)S(1)}, u32[]{:S(2)}, u32[]{:S(2)}) collective-permute-start(f32[160,128]{1,0:T(8,128)S(1)} %get-tuple-element.18), channel_id=1, source_target_pairs={{0,2},{1,3},{2,4},{3,5},{4,6},{5,7},{6,8},{7,9},{8,10},{9,11},{10,... | collective-permute-start | bytes 245768 | tf_op jit(solution)/shard_map/ppermute | solution.py:403
  85.0 22.3 %copy-start.1 = (f32[8,8,1024]{2,1,0:T(8,128)S(1)}, f32[8,8,1024]{2,1,0:T(8,128)}, u32[]{:S(2)}) copy-start(f32[8,8,1024]{2,1,0:T(8,128)} %param.5) | copy-start | bytes 786436

commit v16 on v10

--- a/solution.py
+++ b/solution.py
@@ -108,8 +108,33 @@
             out_ref[2 * part + 1, start : start + times, :] = odd[part]
 
 
+def reach(distance):
+    halo = 2 * HALO - distance
+    margin = 0 if halo == 0 else 4 if halo <= 4 else 8 if halo <= 8 else 12
+    return SIDE - margin, SIDE + LANES // 2 + margin
+
+
+def sent_places(distances, start):
+    places = {}
+    for distance in distances:
+        places[distance] = start
+        first, last = reach(distance)
+        start += last - first
+    return places, start
+
+
+def near_places(rows):
+    return sent_places(range(rows, 0, -1), 3 * rows)
+
+
+def far_places(rows):
+    places, end = sent_places(range(rows + 1, rows + FAR + 1), SUB)
+    return places, end + SIDE
+
+
 def forward_kernel(
-    rows, times, length, cas_ref, field_ref, local_ref, out_ref, low_ref, high_ref, line_ref
+    rows, times, length, cas_ref, field_ref, local_ref,
+    out_ref, up_ref, down_ref, far_up_ref, far_down_ref, line_ref,
 ):
     half = LANES // 2
     span = half + 2 * SIDE
@@ -135,14 +160,26 @@
         for column in range(BLOCK):
             value = line_ref[pl.ds(row * span + skip + column, SUB, stride=BLOCK), :]
             out_ref[row * BLOCK + column] = value
-            if row < FAR:
-                low_ref[row * BLOCK + column] = value
-            if row >= rows - FAR:
-                high_ref[(row - (rows - FAR)) * BLOCK + column] = value
-    for ref in (out_ref, low_ref, high_ref):
-        first = ref.shape[0] - 3
-        for plane in range(3):
-            ref[first + plane] = local_ref[plane * rows : (plane + 1) * rows, :]
+    for plane in range(3):
+        out_ref[rows * BLOCK + plane] = local_ref[plane * rows : (plane + 1) * rows, :]
+    near, far = near_places(rows)[0], far_places(rows)[0]
+    for ref, places, row_of in (
+        (up_ref, near, lambda distance: rows - distance),
+        (down_ref, near, lambda distance: distance - 1),
+        (far_up_ref, far, lambda distance: 2 * rows - distance),
+        (far_down_ref, far, lambda distance: distance - 1 - rows),
+    ):
+        for distance, place in places.items():
+            first, last = reach(distance)
+            start = row_of(distance) * span
+            ref[place : place + last - first, :] = line_ref[start + first : start + last, :]
+    up_ref[: 3 * rows, :] = local_ref[...]
+    down_ref[: 3 * rows, :] = local_ref[...]
+    for ref, first in ((far_up_ref, rows - FAR), (far_down_ref, 0)):
+        ref[ref.shape[0] - SIDE :, :] = jnp.zeros((SIDE, LANES), jnp.float32)
+        kept = [local_ref[plane * rows + first : plane * rows + first + FAR, :] for plane in range(3)]
+        kept.append(jnp.zeros((SUB - 3 * FAR, LANES), jnp.float32))
+        ref[:SUB, :] = jnp.concatenate(kept, axis=0)
 
 
 def weight_lines(parts, scratch_ref):
@@ -155,8 +192,18 @@
     return [scratch_ref[pl.ds(skip + column, SUB, stride=BLOCK), :] for column in range(BLOCK)]
 
 
-def weight_part(ref):
-    return [ref[ref.shape[0] - 3 + plane] for plane in range(3)]
+def weight_part(ref, rows):
+    return [ref[plane * rows : (plane + 1) * rows, :] for plane in range(3)]
+
+
+def own_weight_part(field_ref, rows):
+    return [field_ref[rows * BLOCK + plane] for plane in range(3)]
+
+
+def received(ref, places, distance, column):
+    skip = (LANES // 2 + 2 * SIDE - WINDOW) // 2
+    start = places[distance] - reach(distance)[0] + skip + column
+    return ref[pl.ds(start, SUB, stride=BLOCK), :]
 
 
 def spread(lines, index, plane, coef):
@@ -246,10 +293,14 @@
     solved_ref, middle_ref, step_ref, remain_ref, border_ref, wide_ref, early_ref,
     part_ref, scratch_ref,
 ):
-    refs = (top_ref, field_ref, bottom_ref)
-    lines = weight_lines([weight_part(ref) for ref in refs], scratch_ref)
+    parts = [
+        weight_part(top_ref, rows),
+        own_weight_part(field_ref, rows),
+        weight_part(bottom_ref, rows),
+    ]
+    lines = weight_lines(parts, scratch_ref)
+    places = near_places(rows)[0]
     coef = [coef_ref[index] for index in range(2 + 2 * CHEB)]
-    places = [None] * FAR + [(ref, row) for ref in refs for row in range(rows)]
     total = 3 * rows + 2 * FAR
     own = (FAR + rows, FAR + 2 * rows)
     made = set()
@@ -262,8 +313,11 @@
         return wide_ref[row, place]
 
     def source(row, column):
-        ref, place = places[row]
-        return ref[place * BLOCK + column]
+        if row < own[0]:
+            return received(top_ref, places, own[0] - row, column)
+        if row >= own[1]:
+            return received(bottom_ref, places, row - own[1] + 1, column)
+        return field_ref[(row - own[0]) * BLOCK + column]
 
     sums = [jnp.zeros((SUB, LANES), jnp.float32) for _ in range(2)]
 
@@ -294,17 +348,18 @@
     step_ref, remain_ref, part_ref, outer_ref, scratch_ref,
 ):
     columns = range(BLOCK)
-    refs = (top_far_ref, top_ref, field_ref, bottom_ref, bottom_far_ref)
-    parts = [weight_part(ref) for ref in refs]
-    parts[0] = [block[rows - FAR :] for block in parts[0]]
-    parts[-1] = [block[:FAR] for block in parts[-1]]
+    parts = [
+        weight_part(top_far_ref, FAR),
+        weight_part(top_ref, rows),
+        own_weight_part(field_ref, rows),
+        weight_part(bottom_ref, rows),
+        weight_part(bottom_far_ref, FAR),
+    ]
     lines = weight_lines(parts, scratch_ref)
     coef = [coef_ref[index] for index in range(2 + 2 * CHEB)]
     total = 3 * rows + 2 * FAR
     own = (FAR + rows, FAR + 2 * rows)
-    places = [
-        (ref, row) for ref in refs for row in range((ref.shape[0] - 3) // BLOCK)
-    ]
+    near, far = near_places(rows)[0], far_places(rows)[0]
     made = {}
 
     def weight(plane, row, column):
@@ -316,8 +371,12 @@
         return made[key]
 
     def source(row):
-        ref, place = places[row]
-        return [ref[place * BLOCK + column] for column in columns]
+        distance = own[0] - row if row < own[0] else row - own[1] + 1
+        if distance > rows:
+            ref, places = (top_far_ref if row < own[0] else bottom_far_ref), far
+        else:
+            ref, places = (top_ref if row < own[0] else bottom_ref), near
+        return [received(ref, places, distance, column) for column in columns]
 
     for side in range(2):
 
@@ -338,8 +397,8 @@
             new_ends, new_rest = [], []
             for index, before in ((1, rest), (2, inner_rest)):
                 row = at(turn + index)
-                near, away = steps[index - 1], steps[index + 1]
-                above, below = (away, near) if side else (near, away)
+                outside, inside = steps[index - 1], steps[index + 1]
+                above, below = (inside, outside) if side else (outside, inside)
                 here = steps[index]
                 applied, _ = stencil(weight, row, above, here, below)
                 left = [before[column] - applied[column] for column in columns]
@@ -469,16 +528,16 @@
     local = lax.dynamic_slice_in_dim(planes, lax.axis_index("tm") * tile, LANES, 1)
     total = 3 * rows + 2 * FAR
     tile_shape = (rows, BLOCK, SUB, LANES)
-    row_shape = (rows * BLOCK + 3, SUB, LANES)
-    far_shape = (FAR * BLOCK + 3, SUB, LANES)
+    near_shape = (near_places(rows)[1], LANES)
+    far_shape = (far_places(rows)[1], LANES)
     span = LANES // 2 + 2 * SIDE
-    freq, low, high = call(
+    freq, up, down, far_up, far_down = call(
         functools.partial(forward_kernel, rows, times, length),
-        [row_shape, far_shape, far_shape],
+        [(rows * BLOCK + 3, SUB, LANES), near_shape, near_shape, far_shape, far_shape],
         [(rows * span, LANES)],
     )(cas_table, gathered, local)
-    top, bottom = shift(freq, 1, spaces), shift(freq, -1, spaces)
-    top_far, bottom_far = shift(high, 2, spaces), shift(low, -2, spaces)
+    top, bottom = shift(up, 1, spaces), shift(down, -1, spaces)
+    top_far, bottom_far = shift(far_up, 2, spaces), shift(far_down, -2, spaces)
 
     groups = [
         [i * spaces + first + j for i in range(tiles) for j in range(NEAR)]

time: 112 us -> 108 us (0.964)
  waiting for transfers between devices: 23.4 us -> 14.2 us
  blocking collectives: 43.9 us -> 49.7 us
    ppermute x4, waiting for transfers between devices: 9.14 us -> 0.01 us  [shift(): lax.ppermute(value, 'space', [(i, (i + distance) % spaces) for i in range...]
    all_to_all x1, blocking collectives: 8.89 us -> 14.3 us  [shards(): sums = lax.all_to_all(sums, 'space', 0, 0, axis_index_groups=groups)]
  transfers between devices with their start and end apart: 5 -> 5, of which waited for: 2 -> 1; matrix products, arithmetic and copies ran while one was open for 0% -> 0% of each run, Pallas kernels for 3% -> 3%
where the time goes in v16:
time: 108 us
  blocking collectives  49.7 us (46%)
  starting transfers between devices  32.3 us (30%)
  waiting for transfers between devices  14.2 us (13%)
  Pallas kernels  9.48 us (9%)
  local copies, waits for them, and re-layouts  1.24 us (1%)
    all_to_all x1, blocking collectives, shards(): returned = lax.all_to_all(packed, 'tm', 0, 0)  22.2 us
    ppermute x4, starting transfers between devices, shift(): lax.ppermute(value, 'space', [(i, (i + distance) % spaces) for i in range...  22.1 us
    all_to_all x1, blocking collectives, shards(): sums = lax.all_to_all(sums, 'space', 0, 0, axis_index_groups=groups)  14.3 us
    all_to_all x1, waiting for transfers between devices, shards(): gathered = lax.all_to_all(windows, 'tm', 0, 0)  14.2 us
    all_to_all x1, blocking collectives, shards(): sums = lax.all_to_all(sums, ('tm', 'space'), 0, 0, axis_index_groups=groups)  13.2 us
    all_to_all x1, starting transfers between devices, shards(): gathered = lax.all_to_all(windows, 'tm', 0, 0)  10.2 us
    pallas_call x1, Pallas kernels, shards(): call(functools.partial(near_kernel, rows), [tile_shape, work, work, work,...  2.99 us
    pallas_call x1, Pallas kernels, shards(): call(functools.partial(far_kernel, rows), [tile_shape, tile_shape, (tiles...  2.53 us
  transfers between devices with their start and end apart: 5, of which 1 were waited for; matrix products, arithmetic and copies ran while one was open for 0% of the time, Pallas kernels for 3%

profile of v16, /device:TPU:1, one launch (start us, length us, event | category | flops | bytes accessed | tf_op | source)
XLA Modules:
  0.0 107.8 jit_solution(8967696054279061340)
XLA Ops:
  0.6 0.0 copy-start
  0.6 0.9 copy-done
  1.6 0.0 copy-start.4
  1.6 0.0 copy-start.5
  1.6 0.0 copy-start.2
  1.6 0.0 copy-start.3
  1.6 1.0 shard_map.68
  2.6 10.2 %all-to-all-start = ((f32[16,48,128]{2,1,0:T(8,128)}), f32[16,48,128]{2,1,0:T(8,128)S(1)}, u32[]{:S(2)}, u32[]{:S(2)}) async-start(f32[16,48,128]{2,1,0:T(8,128)} %shard_map.68), calls=%async_computation | async-start | bytes 786432 | tf_op jit(solution)/shard_map/all_to_all | solution.py:523
  12.9 0.0 copy-done.4
  12.9 0.0 copy-done.5
  12.9 0.1 fusion
  13.0 0.1 concatenate.7
  13.1 0.1 constant_dynamic-slice_fusion.local_ref
  13.2 14.2 %all-to-all-done.field_ref = f32[16,48,128]{2,1,0:T(8,128)S(1)} async-done(((f32[16,48,128]{2,1,0:T(8,128)}), f32[16,48,128]{2,1,0:T(8,128)S(1)}, u32[]{:S(2)}, u32[]{:S(2)}) %all-to-all-start) | async-done | bytes 393248 | tf_op jit(solution)/shard_map/all_to_all | solution.py:523
  27.4 0.0 copy-done.2
  27.4 0.6 shard_map.69
  28.0 1.9 %collective-permute-start.1 = (f32[648,128]{1,0:T(8,128)S(1)}, f32[648,128]{1,0:T(8,128)S(1)}, u32[]{:S(2)}, u32[]{:S(2)}) collective-permute-start(f32[648,128]{1,0:T(8,128)S(1)} %get-tuple-element.20), channel_id=1, source_target_pairs={{0,1},{1,2},{2,3},{3,4},{4,5},{5,6},{6,7},{7,8},{8,9},{9,10},{10,1... | collective-permute-start | bytes 995336 | tf_op jit(solution)/shard_map/ppermute | solution.py:504
  29.9 11.3 %collective-permute-start.2 = (f32[648,128]{1,0:T(8,128)S(1)}, f32[648,128]{1,0:T(8,128)S(1)}, u32[]{:S(2)}, u32[]{:S(2)}) collective-permute-start(f32[648,128]{1,0:T(8,128)S(1)} %get-tuple-element.22), channel_id=1, source_target_pairs={{0,31},{1,0},{2,1},{3,2},{4,3},{5,4},{6,5},{7,6},{8,7},{9,8},{10,9... | collective-permute-start | bytes 995336 | tf_op jit(solution)/shard_map/ppermute | solution.py:504
  41.2 1.9 %collective-permute-start = (f32[160,128]{1,0:T(8,128)S(1)}, f32[160,128]{1,0:T(8,128)S(1)}, u32[]{:S(2)}, u32[]{:S(2)}) collective-permute-start(f32[160,128]{1,0:T(8,128)S(1)} %get-tuple-element.19), channel_id=1, source_target_pairs={{0,2},{1,3},{2,4},{3,5},{4,6},{5,7},{6,8},{7,9},{8,10},{9,11},{10,... | collective-permute-start | bytes 245768 | tf_op jit(solution)/shard_map/ppermute | solution.py:504
  43.1 7.0 %collective-permute-start.3 = (f32[160,128]{1,0:T(8,128)S(1)}, f32[160,128]{1,0:T(8,128)S(1)}, u32[]{:S(2)}, u32[]{:S(2)}) collective-permute-start(f32[160,128]{1,0:T(8,128)S(1)} %get-tuple-element.23), channel_id=1, source_target_pairs={{0,30},{1,31},{2,0},{3,1},{4,2},{5,3},{6,4},{7,5},{8,6},{9,7},{10,... | collective-permute-start | bytes 245768 | tf_op jit(solution)/shard_map/ppermute | solution.py:504
  50.1 0.0 collective-permute-done.1.top_ref
  50.1 0.0 collective-permute-done.2.bottom_ref
  50.1 0.0 copy-done.3
  50.2 3.0 %shard_map.70 = (f32[8,11,8,128]{3,2,1,0:T(8,128)S(1)}, f32[28,11,8,128]{3,2,1,0:T(8,128)S(1)}, f32[28,11,8,128]{3,2,1,0:T(8,128)S(1)}, f32[28,11,8,128]{3,2,1,0...) custom-call(f32[648,128]{1,0:T(8,128)S(1)} %collective-permute-done.1.top, ...), custom_call_target="tpu_custom_call" | custom-call | tf_op jit(solution)/shard_map/pallas_call | solution.py:547
  53.1 0.0 collective-permute-done.top_far_ref
  53.1 0.0 collective-permute-done.3.bottom_far_ref
  53.2 2.5 %shard_map.71 = (f32[8,11,8,128]{3,2,1,0:T(8,128)S(1)}, f32[8,11,8,128]{3,2,1,0:T(8,128)S(1)}, f32[64,1,128]{2,1,0:T(1,128)S(1)}) custom-call(f32[160,128]{1,0:T(8,128)S(1)} %collective-permute-done.top_far_ref, f32[648,128]{1,0:T(8,128)S(1)} %collective-permute-done.1.top_ref, f32[91,8,128]{2,1,0:T(8,128)S(1)} %get-tuple-element.21.field_ref, ...), custom_call_target="tpu_custom_call" | custom-call | tf_op jit(solution)/shard_map/pallas_call | solution.py:560
  55.7 13.2 %all_to_all.20 = f32[64,1,128]{2,1,0:T(1,128)S(1)} all-to-all(f32[64,1,128]{2,1,0:T(1,128)S(1)} %get-tuple-element.30), channel_id=1, replica_groups={{0,1,2,3,32,33,34,35,64,65,66,67,96,97,98,99,128,129,130,131,160,161,16..., dimensions={0} | all-to-all | bytes 65536 | tf_op jit(solution)/shard_map/all_to_all | solution.py:567
  68.9 0.1 reduce_sum.9
  69.0 14.3 %all_to_all.21.sums_ref = f32[8,1,128]{2,1,0:T(1,128)S(1)} all-to-all(f32[8,1,128]{2,1,0:T(1,128)S(1)} %broadcast_in_dim.2), channel_id=1, replica_groups={{0,4,8,12,16,20,24,28},{1,5,9,13,17,21,25,29},{2,6,10,14,18,22,26,30},{..., dimensions={0} | all-to-all | bytes 8192 | tf_op jit(solution)/shard_map/all_to_all | solution.py:571
  83.3 0.0 copy-start.1
  83.3 1.3 %shard_map.72 = f32[16,64,128]{2,1,0:T(8,128)S(1)} custom-call(f32[128,128]{1,0:T(8,128)S(1)} %copy-done.2, f32[8,1,128]{2,1,0:T(1,128)S(1)} %all_to_all.21.sums_ref, f32[8,11,8,128]{3,2,1,0:T(8,128)S(1)} %get-tuple-element.31.one_ref, f32[8,11,8,128]{3,2,1,0:T(8,128)S(1)} %get-tuple-element.32.two_ref, ...), custom_call_target="tpu_custom_call" | custom-call | tf_op jit(solution)/shard_map/pallas_call | solution.py:572
  84.7 22.2 %all_to_all.22.source_ref = f32[16,64,128]{2,1,0:T(8,128)S(1)} all-to-all(f32[16,64,128]{2,1,0:T(8,128)S(1)} %shard_map.72), channel_id=1, replica_groups=mesh['tm'=16,'space'=32] {'tm'}, dimensions={0} | all-to-all | bytes 1048576 | tf_op jit(solution)/shard_map/all_to_all | solution.py:577
  106.8 0.0 copy-done.1
  106.8 1.0 shard_map.73
  (4 shorter events, 0.0 us)
Async XLA Ops:
  0.6 1.0 copy-start
  1.6 11.3 %copy-start.4 = (s32[2,8,1024]{2,1,0:T(8,128)S(1)}, s32[2,8,1024]{2,1,0:T(8,128)}, u32[]{:S(2)}) copy-start(s32[2,8,1024]{2,1,0:T(8,128)} %param.7) | copy-start | bytes 196612
  1.6 11.3 %copy-start.5 = (f32[8,1024]{1,0:T(8,128)S(1)}, f32[8,1024]{1,0:T(8,128)}, u32[]{:S(2)}) copy-start(f32[8,1024]{1,0:T(8,128)} %param.6) | copy-start | bytes 98308
  1.6 25.8 %copy-start.2 = (f32[128,128]{1,0:T(8,128)S(1)}, f32[128,128]{1,0:T(8,128)}, u32[]{:S(2)}) copy-start(f32[128,128]{1,0:T(8,128)} %constant.18.clone.cas_ref) | copy-start | bytes 196612
  1.6 48.6 %copy-start.3 = (f32[10,8,128]{2,1,0:T(8,128)S(1)}, f32[10,8,128]{2,1,0:T(8,128)}, u32[]{:S(2)}) copy-start(f32[10,8,128]{2,1,0:T(8,128)} %constant.19.clone.coef_ref) | copy-start | bytes 122884
  2.6 24.8 %all-to-all-start = ((f32[16,48,128]{2,1,0:T(8,128)}), f32[16,48,128]{2,1,0:T(8,128)S(1)}, u32[]{:S(2)}, u32[]{:S(2)}) async-start(f32[16,48,128]{2,1,0:T(8,128)} %shard_map.68), calls=%async_computation | async-start | bytes 786432 | tf_op jit(solution)/shard_map/all_to_all | solution.py:523
  28.0 22.1 %collective-permute-start.1 = (f32[648,128]{1,0:T(8,128)S(1)}, f32[648,128]{1,0:T(8,128)S(1)}, u32[]{:S(2)}, u32[]{:S(2)}) collective-permute-start(f32[648,128]{1,0:T(8,128)S(1)} %get-tuple-element.20), channel_id=1, source_target_pairs={{0,1},{1,2},{2,3},{3,4},{4,5},{5,6},{6,7},{7,8},{8,9},{9,10},{10,1... | collective-permute-start | bytes 995336 | tf_op jit(solution)/shard_map/ppermute | solution.py:504
  29.9 20.2 %collective-permute-start.2 = (f32[648,128]{1,0:T(8,128)S(1)}, f32[648,128]{1,0:T(8,128)S(1)}, u32[]{:S(2)}, u32[]{:S(2)}) collective-permute-start(f32[648,128]{1,0:T(8,128)S(1)} %get-tuple-element.22), channel_id=1, source_target_pairs={{0,31},{1,0},{2,1},{3,2},{4,3},{5,4},{6,5},{7,6},{8,7},{9,8},{10,9... | collective-permute-start | bytes 995336 | tf_op jit(solution)/shard_map/ppermute | solution.py:504
  41.2 11.9 %collective-permute-start = (f32[160,128]{1,0:T(8,128)S(1)}, f32[160,128]{1,0:T(8,128)S(1)}, u32[]{:S(2)}, u32[]{:S(2)}) collective-permute-start(f32[160,128]{1,0:T(8,128)S(1)} %get-tuple-element.19), channel_id=1, source_target_pairs={{0,2},{1,3},{2,4},{3,5},{4,6},{5,7},{6,8},{7,9},{8,10},{9,11},{10,... | collective-permute-start | bytes 245768 | tf_op jit(solution)/shard_map/ppermute | solution.py:504
  43.1 10.0 %collective-permute-start.3 = (f32[160,128]{1,0:T(8,128)S(1)}, f32[160,128]{1,0:T(8,128)S(1)}, u32[]{:S(2)}, u32[]{:S(2)}) collective-permute-start(f32[160,128]{1,0:T(8,128)S(1)} %get-tuple-element.23), channel_id=1, source_target_pairs={{0,30},{1,31},{2,0},{3,1},{4,2},{5,3},{6,4},{7,5},{8,6},{9,7},{10,... | collective-permute-start | bytes 245768 | tf_op jit(solution)/shard_map/ppermute | solution.py:504
  83.3 23.5 %copy-start.1 = (f32[8,8,1024]{2,1,0:T(8,128)S(1)}, f32[8,8,1024]{2,1,0:T(8,128)}, u32[]{:S(2)}) copy-start(f32[8,8,1024]{2,1,0:T(8,128)} %param.5) | copy-start | bytes 786436

commit v17 on v16

--- a/solution.py
+++ b/solution.py
@@ -465,14 +465,17 @@
                 start = (2 * row + index) * span + skip + column
                 value = first * left_ref[offset + row, column] + second * right_ref[row, column]
                 line_ref[pl.ds(start, SUB, stride=BLOCK), :] = value
+    points = jnp.concatenate(
+        [
+            line_ref[index * span + SIDE : index * span + SIDE + half, :]
+            for index in range(2 * rows)
+        ],
+        axis=0,
+    )
+    back = exact_dot(cas_ref[...], points, 1, 1)
     for row in range(rows):
-        start = 2 * row * span + SIDE
-        points = jnp.concatenate(
-            [line_ref[start : start + half, :], line_ref[start + span : start + span + half, :]],
-            axis=0,
-        )
-        back = exact_dot(cas_ref[...], points, 1, 1).reshape(length // times, times, LANES)
-        out_ref[:, row * times : (row + 1) * times, :] = back
+        piece = back[:, row * LANES : (row + 1) * LANES].reshape(length // times, times, LANES)
+        out_ref[:, row * times : (row + 1) * times, :] = piece
 
 
 def final_kernel(rows, times, tiles, source_ref, field_ref, solution_ref, residual_ref):

time: 108 us -> 108 us (level)
  no operation moved by 1% of the time
where the time goes in v17:
time: 108 us; the launch traced here: 107 us
  blocking collectives  49.7 us (46%)
  starting transfers between devices  32.3 us (30%)
  waiting for transfers between devices  14.2 us (13%)
  Pallas kernels  8.91 us (8%)
  local copies, waits for them, and re-layouts  1.24 us (1%)
    all_to_all x1, blocking collectives, shards(): returned = lax.all_to_all(packed, 'tm', 0, 0)  22.2 us
    ppermute x4, starting transfers between devices, shift(): lax.ppermute(value, 'space', [(i, (i + distance) % spaces) for i in range...  22.1 us
    all_to_all x1, blocking collectives, shards(): sums = lax.all_to_all(sums, 'space', 0, 0, axis_index_groups=groups)  14.3 us
    all_to_all x1, waiting for transfers between devices, shards(): gathered = lax.all_to_all(windows, 'tm', 0, 0)  14.2 us
    all_to_all x1, blocking collectives, shards(): sums = lax.all_to_all(sums, ('tm', 'space'), 0, 0, axis_index_groups=groups)  13.2 us
    all_to_all x1, starting transfers between devices, shards(): gathered = lax.all_to_all(windows, 'tm', 0, 0)  10.2 us
    pallas_call x1, Pallas kernels, shards(): call(functools.partial(near_kernel, rows), [tile_shape, work, work, work,...  2.99 us
    pallas_call x1, Pallas kernels, shards(): call(functools.partial(far_kernel, rows), [tile_shape, tile_shape, (tiles...  2.53 us
  transfers between devices with their start and end apart: 5, of which 1 were waited for; matrix products, arithmetic and copies ran while one was open for 0% of the time, Pallas kernels for 3%

profile of v17, /device:TPU:1, one launch (start us, length us, event | category | flops | bytes accessed | tf_op | source)
XLA Modules:
  0.0 107.2 jit_solution(10355684367604757798)
XLA Ops:
  0.6 0.0 copy-start
  0.6 0.9 copy-done
  1.6 0.0 copy-start.4
  1.6 0.0 copy-start.5
  1.6 0.0 copy-start.2
  1.6 0.0 copy-start.3
  1.6 1.0 shard_map.68
  2.6 10.2 %all-to-all-start = ((f32[16,48,128]{2,1,0:T(8,128)}), f32[16,48,128]{2,1,0:T(8,128)S(1)}, u32[]{:S(2)}, u32[]{:S(2)}) async-start(f32[16,48,128]{2,1,0:T(8,128)} %shard_map.68), calls=%async_computation | async-start | bytes 786432 | tf_op jit(solution)/shard_map/all_to_all | solution.py:526
  12.9 0.0 copy-done.4
  12.9 0.0 copy-done.5
  12.9 0.1 fusion
  13.0 0.1 concatenate.7
  13.1 0.1 constant_dynamic-slice_fusion.local_ref
  13.2 14.2 %all-to-all-done.field_ref = f32[16,48,128]{2,1,0:T(8,128)S(1)} async-done(((f32[16,48,128]{2,1,0:T(8,128)}), f32[16,48,128]{2,1,0:T(8,128)S(1)}, u32[]{:S(2)}, u32[]{:S(2)}) %all-to-all-start) | async-done | bytes 393248 | tf_op jit(solution)/shard_map/all_to_all | solution.py:526
  27.4 0.0 copy-done.2
  27.4 0.6 shard_map.69
  28.0 1.9 %collective-permute-start.1 = (f32[648,128]{1,0:T(8,128)S(1)}, f32[648,128]{1,0:T(8,128)S(1)}, u32[]{:S(2)}, u32[]{:S(2)}) collective-permute-start(f32[648,128]{1,0:T(8,128)S(1)} %get-tuple-element.20), channel_id=1, source_target_pairs={{0,1},{1,2},{2,3},{3,4},{4,5},{5,6},{6,7},{7,8},{8,9},{9,10},{10,1... | collective-permute-start | bytes 995336 | tf_op jit(solution)/shard_map/ppermute | solution.py:507
  29.9 11.3 %collective-permute-start.2 = (f32[648,128]{1,0:T(8,128)S(1)}, f32[648,128]{1,0:T(8,128)S(1)}, u32[]{:S(2)}, u32[]{:S(2)}) collective-permute-start(f32[648,128]{1,0:T(8,128)S(1)} %get-tuple-element.22), channel_id=1, source_target_pairs={{0,31},{1,0},{2,1},{3,2},{4,3},{5,4},{6,5},{7,6},{8,7},{9,8},{10,9... | collective-permute-start | bytes 995336 | tf_op jit(solution)/shard_map/ppermute | solution.py:507
  41.2 1.9 %collective-permute-start = (f32[160,128]{1,0:T(8,128)S(1)}, f32[160,128]{1,0:T(8,128)S(1)}, u32[]{:S(2)}, u32[]{:S(2)}) collective-permute-start(f32[160,128]{1,0:T(8,128)S(1)} %get-tuple-element.19), channel_id=1, source_target_pairs={{0,2},{1,3},{2,4},{3,5},{4,6},{5,7},{6,8},{7,9},{8,10},{9,11},{10,... | collective-permute-start | bytes 245768 | tf_op jit(solution)/shard_map/ppermute | solution.py:507
  43.1 7.0 %collective-permute-start.3 = (f32[160,128]{1,0:T(8,128)S(1)}, f32[160,128]{1,0:T(8,128)S(1)}, u32[]{:S(2)}, u32[]{:S(2)}) collective-permute-start(f32[160,128]{1,0:T(8,128)S(1)} %get-tuple-element.23), channel_id=1, source_target_pairs={{0,30},{1,31},{2,0},{3,1},{4,2},{5,3},{6,4},{7,5},{8,6},{9,7},{10,... | collective-permute-start | bytes 245768 | tf_op jit(solution)/shard_map/ppermute | solution.py:507
  50.1 0.0 collective-permute-done.1.top_ref
  50.1 0.0 collective-permute-done.2.bottom_ref
  50.1 0.0 copy-done.3
  50.2 3.0 %shard_map.70 = (f32[8,11,8,128]{3,2,1,0:T(8,128)S(1)}, f32[28,11,8,128]{3,2,1,0:T(8,128)S(1)}, f32[28,11,8,128]{3,2,1,0:T(8,128)S(1)}, f32[28,11,8,128]{3,2,1,0...) custom-call(f32[648,128]{1,0:T(8,128)S(1)} %collective-permute-done.1.top, ...), custom_call_target="tpu_custom_call" | custom-call | tf_op jit(solution)/shard_map/pallas_call | solution.py:550
  53.1 0.0 collective-permute-done.top_far_ref
  53.1 0.0 collective-permute-done.3.bottom_far_ref
  53.2 2.5 %shard_map.71 = (f32[8,11,8,128]{3,2,1,0:T(8,128)S(1)}, f32[8,11,8,128]{3,2,1,0:T(8,128)S(1)}, f32[64,1,128]{2,1,0:T(1,128)S(1)}) custom-call(f32[160,128]{1,0:T(8,128)S(1)} %collective-permute-done.top_far_ref, f32[648,128]{1,0:T(8,128)S(1)} %collective-permute-done.1.top_ref, f32[91,8,128]{2,1,0:T(8,128)S(1)} %get-tuple-element.21.field_ref, ...), custom_call_target="tpu_custom_call" | custom-call | tf_op jit(solution)/shard_map/pallas_call | solution.py:563
  55.7 13.2 %all_to_all.20 = f32[64,1,128]{2,1,0:T(1,128)S(1)} all-to-all(f32[64,1,128]{2,1,0:T(1,128)S(1)} %get-tuple-element.30), channel_id=1, replica_groups={{0,1,2,3,32,33,34,35,64,65,66,67,96,97,98,99,128,129,130,131,160,161,16..., dimensions={0} | all-to-all | bytes 65536 | tf_op jit(solution)/shard_map/all_to_all | solution.py:570
  68.9 0.1 reduce_sum.9
  69.0 14.3 %all_to_all.21.sums_ref = f32[8,1,128]{2,1,0:T(1,128)S(1)} all-to-all(f32[8,1,128]{2,1,0:T(1,128)S(1)} %broadcast_in_dim.2), channel_id=1, replica_groups={{0,4,8,12,16,20,24,28},{1,5,9,13,17,21,25,29},{2,6,10,14,18,22,26,30},{..., dimensions={0} | all-to-all | bytes 8192 | tf_op jit(solution)/shard_map/all_to_all | solution.py:574
  83.3 0.0 copy-start.1
  83.3 0.8 shard_map.72
  84.1 22.2 %all_to_all.22.source_ref = f32[16,64,128]{2,1,0:T(8,128)S(1)} all-to-all(f32[16,64,128]{2,1,0:T(8,128)S(1)} %shard_map.72), channel_id=1, replica_groups=mesh['tm'=16,'space'=32] {'tm'}, dimensions={0} | all-to-all | bytes 1048576 | tf_op jit(solution)/shard_map/all_to_all | solution.py:580
  106.3 0.0 copy-done.1
  106.3 1.0 shard_map.73
  (4 shorter events, 0.0 us)
Async XLA Ops:
  0.6 1.0 copy-start
  1.6 11.3 %copy-start.4 = (s32[2,8,1024]{2,1,0:T(8,128)S(1)}, s32[2,8,1024]{2,1,0:T(8,128)}, u32[]{:S(2)}) copy-start(s32[2,8,1024]{2,1,0:T(8,128)} %param.7) | copy-start | bytes 196612
  1.6 11.3 %copy-start.5 = (f32[8,1024]{1,0:T(8,128)S(1)}, f32[8,1024]{1,0:T(8,128)}, u32[]{:S(2)}) copy-start(f32[8,1024]{1,0:T(8,128)} %param.6) | copy-start | bytes 98308
  1.6 25.8 %copy-start.2 = (f32[128,128]{1,0:T(8,128)S(1)}, f32[128,128]{1,0:T(8,128)}, u32[]{:S(2)}) copy-start(f32[128,128]{1,0:T(8,128)} %constant.18.clone.cas_ref) | copy-start | bytes 196612
  1.6 48.6 %copy-start.3 = (f32[10,8,128]{2,1,0:T(8,128)S(1)}, f32[10,8,128]{2,1,0:T(8,128)}, u32[]{:S(2)}) copy-start(f32[10,8,128]{2,1,0:T(8,128)} %constant.19.clone.coef_ref) | copy-start | bytes 122884
  2.6 24.8 %all-to-all-start = ((f32[16,48,128]{2,1,0:T(8,128)}), f32[16,48,128]{2,1,0:T(8,128)S(1)}, u32[]{:S(2)}, u32[]{:S(2)}) async-start(f32[16,48,128]{2,1,0:T(8,128)} %shard_map.68), calls=%async_computation | async-start | bytes 786432 | tf_op jit(solution)/shard_map/all_to_all | solution.py:526
  28.0 22.1 %collective-permute-start.1 = (f32[648,128]{1,0:T(8,128)S(1)}, f32[648,128]{1,0:T(8,128)S(1)}, u32[]{:S(2)}, u32[]{:S(2)}) collective-permute-start(f32[648,128]{1,0:T(8,128)S(1)} %get-tuple-element.20), channel_id=1, source_target_pairs={{0,1},{1,2},{2,3},{3,4},{4,5},{5,6},{6,7},{7,8},{8,9},{9,10},{10,1... | collective-permute-start | bytes 995336 | tf_op jit(solution)/shard_map/ppermute | solution.py:507
  29.9 20.2 %collective-permute-start.2 = (f32[648,128]{1,0:T(8,128)S(1)}, f32[648,128]{1,0:T(8,128)S(1)}, u32[]{:S(2)}, u32[]{:S(2)}) collective-permute-start(f32[648,128]{1,0:T(8,128)S(1)} %get-tuple-element.22), channel_id=1, source_target_pairs={{0,31},{1,0},{2,1},{3,2},{4,3},{5,4},{6,5},{7,6},{8,7},{9,8},{10,9... | collective-permute-start | bytes 995336 | tf_op jit(solution)/shard_map/ppermute | solution.py:507
  41.2 11.9 %collective-permute-start = (f32[160,128]{1,0:T(8,128)S(1)}, f32[160,128]{1,0:T(8,128)S(1)}, u32[]{:S(2)}, u32[]{:S(2)}) collective-permute-start(f32[160,128]{1,0:T(8,128)S(1)} %get-tuple-element.19), channel_id=1, source_target_pairs={{0,2},{1,3},{2,4},{3,5},{4,6},{5,7},{6,8},{7,9},{8,10},{9,11},{10,... | collective-permute-start | bytes 245768 | tf_op jit(solution)/shard_map/ppermute | solution.py:507
  43.1 10.0 %collective-permute-start.3 = (f32[160,128]{1,0:T(8,128)S(1)}, f32[160,128]{1,0:T(8,128)S(1)}, u32[]{:S(2)}, u32[]{:S(2)}) collective-permute-start(f32[160,128]{1,0:T(8,128)S(1)} %get-tuple-element.23), channel_id=1, source_target_pairs={{0,30},{1,31},{2,0},{3,1},{4,2},{5,3},{6,4},{7,5},{8,6},{9,7},{10,... | collective-permute-start | bytes 245768 | tf_op jit(solution)/shard_map/ppermute | solution.py:507
  83.3 22.9 %copy-start.1 = (f32[8,8,1024]{2,1,0:T(8,128)S(1)}, f32[8,8,1024]{2,1,0:T(8,128)}, u32[]{:S(2)}) copy-start(f32[8,8,1024]{2,1,0:T(8,128)} %param.5) | copy-start | bytes 786436

commit v18 on v17

--- a/solution.py
+++ b/solution.py
@@ -288,8 +288,20 @@
         sums[index] = sums[index] + jnp.where(own_columns(column), product, 0.0)
 
 
+def own_kernel(rows, local_ref, coef_ref, wide_ref, scratch_ref):
+    lines = weight_lines([weight_part(local_ref, rows)], scratch_ref)
+    coef = [coef_ref[0]]
+    for row in range(rows):
+        for plane in range(3):
+            for column in range(BLOCK):
+                value = jnp.zeros((SUB, LANES), jnp.float32)
+                if plane != 1 or row < rows - 1:
+                    value = spread(lines[column], plane * rows + row, plane, coef)
+                wide_ref[row, plane * BLOCK + column] = value
+
+
 def near_kernel(
-    rows, top_ref, field_ref, bottom_ref, coef_ref,
+    rows, top_ref, field_ref, bottom_ref, coef_ref, own_wide_ref,
     solved_ref, middle_ref, step_ref, remain_ref, border_ref, wide_ref, early_ref,
     part_ref, scratch_ref,
 ):
@@ -307,6 +319,8 @@
 
     def weight(plane, row, column):
         place = plane * BLOCK + column
+        if own[0] <= row < own[1] - (plane == 1):
+            return own_wide_ref[row - own[0], place]
         if (row, place) not in made:
             made.add((row, place))
             wide_ref[row, place] = spread(lines[column], plane * 3 * rows + row - FAR, plane, coef)
@@ -343,7 +357,7 @@
 
 def far_kernel(
     rows, top_far_ref, top_ref, field_ref, bottom_ref, bottom_far_ref, coef_ref,
-    middle_ref, frozen_step_ref, frozen_remain_ref, border_ref, wide_ref, early_ref,
+    middle_ref, frozen_step_ref, frozen_remain_ref, border_ref, wide_ref, own_wide_ref, early_ref,
     solved_ref, applied_ref, sums_ref,
     step_ref, remain_ref, part_ref, outer_ref, scratch_ref,
 ):
@@ -363,6 +377,8 @@
     made = {}
 
     def weight(plane, row, column):
+        if own[0] <= row < own[1] - (plane == 1):
+            return own_wide_ref[row - own[0], plane * BLOCK + column]
         if FAR < row < total - FAR - 1 or (plane == 1 and row == FAR):
             return wide_ref[row, plane * BLOCK + column]
         key = (plane, row, column)
@@ -529,6 +545,12 @@
     planes = jnp.concatenate([kappa, squares[0], squares[1]], axis=0)
     planes = jnp.concatenate([planes[:, -around:], planes, planes[:, :around]], axis=1)
     local = lax.dynamic_slice_in_dim(planes, lax.axis_index("tm") * tile, LANES, 1)
+    own_wide = call(
+        functools.partial(own_kernel, rows),
+        [(rows, 3 * BLOCK, SUB, LANES)],
+        [(LANES, LANES)],
+    )(local, coef_table)
+
     total = 3 * rows + 2 * FAR
     tile_shape = (rows, BLOCK, SUB, LANES)
     near_shape = (near_places(rows)[1], LANES)
@@ -559,13 +581,14 @@
             (2, SUB, LANES),
         ],
         [tile_shape, (LANES, LANES)],
-    )(top, freq, bottom, coef_table)
+    )(top, freq, bottom, coef_table, own_wide)
     solved_two, applied_two, sums = call(
         functools.partial(far_kernel, rows),
         [tile_shape, tile_shape, (tiles * NEAR, 1, LANES)],
         [work, work, tile_shape, (2 * FAR, BLOCK, SUB, LANES), (LANES, LANES)],
     )(
-        top_far, top, freq, bottom, bottom_far, coef_table, middle, step, remain, border, wide, early
+        top_far, top, freq, bottom, bottom_far, coef_table, middle, step, remain, border, wide,
+        own_wide, early,
     )
     sums = lax.all_to_all(sums, ("tm", "space"), 0, 0, axis_index_groups=groups)
     planes = spaces // NEAR

time: 108 us -> 108 us (level)
  no operation moved by 1% of the time
where the time goes in v18:
time: 108 us; the launch traced here: 107 us
  blocking collectives  49.1 us (45%)
  starting transfers between devices  32.3 us (30%)
  waiting for transfers between devices  14.2 us (13%)
  Pallas kernels  9.43 us (9%)
  local copies, waits for them, and re-layouts  1.24 us (1%)
    all_to_all x1, blocking collectives, shards(): returned = lax.all_to_all(packed, 'tm', 0, 0)  22.2 us
    ppermute x4, starting transfers between devices, shift(): lax.ppermute(value, 'space', [(i, (i + distance) % spaces) for i in range...  22.1 us
    all_to_all x1, waiting for transfers between devices, shards(): gathered = lax.all_to_all(windows, 'tm', 0, 0)  14.2 us
    all_to_all x1, blocking collectives, shards(): sums = lax.all_to_all(sums, 'space', 0, 0, axis_index_groups=groups)  13.7 us
    all_to_all x1, blocking collectives, shards(): sums = lax.all_to_all(sums, ('tm', 'space'), 0, 0, axis_index_groups=groups)  13.2 us
    all_to_all x1, starting transfers between devices, shards(): gathered = lax.all_to_all(windows, 'tm', 0, 0)  10.2 us
    pallas_call x1, Pallas kernels, shards(): call(functools.partial(near_kernel, rows), [tile_shape, work, work, work,...  2.91 us
    pallas_call x1, Pallas kernels, shards(): call(functools.partial(far_kernel, rows), [tile_shape, tile_shape, (tiles...  2.55 us
  transfers between devices with their start and end apart: 5, of which 1 were waited for; matrix products, arithmetic and copies ran while one was open for 0% of the time, Pallas kernels for 3%

profile of v18, /device:TPU:1, one launch (start us, length us, event | category | flops | bytes accessed | tf_op | source)
XLA Modules:
  0.0 107.2 jit_solution(950621640900218310)
XLA Ops:
  0.6 0.0 copy-start
  0.6 0.9 copy-done
  1.6 0.0 copy-start.4
  1.6 0.0 copy-start.5
  1.6 0.0 copy-start.3
  1.6 0.0 copy-start.2
  1.6 1.0 shard_map.68
  2.6 10.2 %all-to-all-start = ((f32[16,48,128]{2,1,0:T(8,128)}), f32[16,48,128]{2,1,0:T(8,128)S(1)}, u32[]{:S(2)}, u32[]{:S(2)}) async-start(f32[16,48,128]{2,1,0:T(8,128)} %shard_map.68), calls=%async_computation | async-start | bytes 786432 | tf_op jit(solution)/shard_map/all_to_all | solution.py:542
  12.9 0.0 copy-done.4
  12.9 0.0 copy-done.5
  12.9 0.1 fusion
  13.0 0.1 concatenate.7
  13.1 0.1 constant_dynamic-slice_fusion.local_ref
  13.2 14.2 %all-to-all-done.field_ref = f32[16,48,128]{2,1,0:T(8,128)S(1)} async-done(((f32[16,48,128]{2,1,0:T(8,128)}), f32[16,48,128]{2,1,0:T(8,128)S(1)}, u32[]{:S(2)}, u32[]{:S(2)}) %all-to-all-start) | async-done | bytes 393248 | tf_op jit(solution)/shard_map/all_to_all | solution.py:542
  27.4 0.0 copy-done.3
  27.4 0.6 shard_map.69
  28.0 1.9 %collective-permute-start.1 = (f32[648,128]{1,0:T(8,128)S(1)}, f32[648,128]{1,0:T(8,128)S(1)}, u32[]{:S(2)}, u32[]{:S(2)}) collective-permute-start(f32[648,128]{1,0:T(8,128)S(1)} %get-tuple-element.20), channel_id=1, source_target_pairs={{0,1},{1,2},{2,3},{3,4},{4,5},{5,6},{6,7},{7,8},{8,9},{9,10},{10,1... | collective-permute-start | bytes 995336 | tf_op jit(solution)/shard_map/ppermute | solution.py:523
  29.9 11.3 %collective-permute-start.2 = (f32[648,128]{1,0:T(8,128)S(1)}, f32[648,128]{1,0:T(8,128)S(1)}, u32[]{:S(2)}, u32[]{:S(2)}) collective-permute-start(f32[648,128]{1,0:T(8,128)S(1)} %get-tuple-element.22), channel_id=1, source_target_pairs={{0,31},{1,0},{2,1},{3,2},{4,3},{5,4},{6,5},{7,6},{8,7},{9,8},{10,9... | collective-permute-start | bytes 995336 | tf_op jit(solution)/shard_map/ppermute | solution.py:523
  41.2 1.9 %collective-permute-start = (f32[160,128]{1,0:T(8,128)S(1)}, f32[160,128]{1,0:T(8,128)S(1)}, u32[]{:S(2)}, u32[]{:S(2)}) collective-permute-start(f32[160,128]{1,0:T(8,128)S(1)} %get-tuple-element.19), channel_id=1, source_target_pairs={{0,2},{1,3},{2,4},{3,5},{4,6},{5,7},{6,8},{7,9},{8,10},{9,11},{10,... | collective-permute-start | bytes 245768 | tf_op jit(solution)/shard_map/ppermute | solution.py:523
  43.1 7.0 %collective-permute-start.3 = (f32[160,128]{1,0:T(8,128)S(1)}, f32[160,128]{1,0:T(8,128)S(1)}, u32[]{:S(2)}, u32[]{:S(2)}) collective-permute-start(f32[160,128]{1,0:T(8,128)S(1)} %get-tuple-element.23), channel_id=1, source_target_pairs={{0,30},{1,31},{2,0},{3,1},{4,2},{5,3},{6,4},{7,5},{8,6},{9,7},{10,... | collective-permute-start | bytes 245768 | tf_op jit(solution)/shard_map/ppermute | solution.py:523
  50.1 0.0 copy-done.2
  50.1 0.6 shard_map.70.own_wide_ref
  50.7 0.0 collective-permute-done.1.top_ref
  50.7 0.0 collective-permute-done.2.bottom_ref
  50.7 2.9 %shard_map.71 = (f32[8,11,8,128]{3,2,1,0:T(8,128)S(1)}, f32[28,11,8,128]{3,2,1,0:T(8,128)S(1)}, f32[28,11,8,128]{3,2,1,0:T(8,128)S(1)}, f32[28,11,8,128]{3,2,1,0...) custom-call(f32[648,128]{1,0:T(8,128)S(1)} %collective-permute-done.1.top, ...), custom_call_target="tpu_custom_call" | custom-call | tf_op jit(solution)/shard_map/pallas_call | solution.py:572
  53.6 0.0 collective-permute-done.top_far_ref
  53.7 0.0 collective-permute-done.3.bottom_far_ref
  53.7 2.5 %shard_map.72 = (f32[8,11,8,128]{3,2,1,0:T(8,128)S(1)}, f32[8,11,8,128]{3,2,1,0:T(8,128)S(1)}, f32[64,1,128]{2,1,0:T(1,128)S(1)}) custom-call(f32[160,128]{1,0:T(8,128)S(1)} %collective-permute-done.top_far_ref, f32[648,128]{1,0:T(8,128)S(1)} %collective-permute-done.1.top_ref, f32[91,8,128]{2,1,0:T(8,128)S(1)} %get-tuple-element.21.field_ref, ...), custom_call_target="tpu_custom_call" | custom-call | tf_op jit(solution)/shard_map/pallas_call | solution.py:585
  56.2 13.2 %all_to_all.20 = f32[64,1,128]{2,1,0:T(1,128)S(1)} all-to-all(f32[64,1,128]{2,1,0:T(1,128)S(1)} %get-tuple-element.30), channel_id=1, replica_groups={{0,1,2,3,32,33,34,35,64,65,66,67,96,97,98,99,128,129,130,131,160,161,16..., dimensions={0} | all-to-all | bytes 65536 | tf_op jit(solution)/shard_map/all_to_all | solution.py:593
  69.4 0.1 reduce_sum.9
  69.5 13.7 %all_to_all.21.sums_ref = f32[8,1,128]{2,1,0:T(1,128)S(1)} all-to-all(f32[8,1,128]{2,1,0:T(1,128)S(1)} %broadcast_in_dim.2), channel_id=1, replica_groups={{0,4,8,12,16,20,24,28},{1,5,9,13,17,21,25,29},{2,6,10,14,18,22,26,30},{..., dimensions={0} | all-to-all | bytes 8192 | tf_op jit(solution)/shard_map/all_to_all | solution.py:597
  83.3 0.0 copy-start.1
  83.3 0.8 shard_map.73
  84.1 22.2 %all_to_all.22.source_ref = f32[16,64,128]{2,1,0:T(8,128)S(1)} all-to-all(f32[16,64,128]{2,1,0:T(8,128)S(1)} %shard_map.73), channel_id=1, replica_groups=mesh['tm'=16,'space'=32] {'tm'}, dimensions={0} | all-to-all | bytes 1048576 | tf_op jit(solution)/shard_map/all_to_all | solution.py:603
  106.2 0.0 copy-done.1
  106.2 1.0 shard_map.74
  (4 shorter events, 0.0 us)
Async XLA Ops:
  0.6 1.0 copy-start
  1.6 11.3 %copy-start.4 = (s32[2,8,1024]{2,1,0:T(8,128)S(1)}, s32[2,8,1024]{2,1,0:T(8,128)}, u32[]{:S(2)}) copy-start(s32[2,8,1024]{2,1,0:T(8,128)} %param.7) | copy-start | bytes 196612
  1.6 11.3 %copy-start.5 = (f32[8,1024]{1,0:T(8,128)S(1)}, f32[8,1024]{1,0:T(8,128)}, u32[]{:S(2)}) copy-start(f32[8,1024]{1,0:T(8,128)} %param.6) | copy-start | bytes 98308
  1.6 25.8 %copy-start.3 = (f32[128,128]{1,0:T(8,128)S(1)}, f32[128,128]{1,0:T(8,128)}, u32[]{:S(2)}) copy-start(f32[128,128]{1,0:T(8,128)} %constant.18.clone.cas_ref) | copy-start | bytes 196612
  1.6 48.5 %copy-start.2 = (f32[10,8,128]{2,1,0:T(8,128)S(1)}, f32[10,8,128]{2,1,0:T(8,128)}, u32[]{:S(2)}) copy-start(f32[10,8,128]{2,1,0:T(8,128)} %constant.19.clone.coef_ref) | copy-start | bytes 122884
  2.6 24.8 %all-to-all-start = ((f32[16,48,128]{2,1,0:T(8,128)}), f32[16,48,128]{2,1,0:T(8,128)S(1)}, u32[]{:S(2)}, u32[]{:S(2)}) async-start(f32[16,48,128]{2,1,0:T(8,128)} %shard_map.68), calls=%async_computation | async-start | bytes 786432 | tf_op jit(solution)/shard_map/all_to_all | solution.py:542
  28.0 22.7 %collective-permute-start.1 = (f32[648,128]{1,0:T(8,128)S(1)}, f32[648,128]{1,0:T(8,128)S(1)}, u32[]{:S(2)}, u32[]{:S(2)}) collective-permute-start(f32[648,128]{1,0:T(8,128)S(1)} %get-tuple-element.20), channel_id=1, source_target_pairs={{0,1},{1,2},{2,3},{3,4},{4,5},{5,6},{6,7},{7,8},{8,9},{9,10},{10,1... | collective-permute-start | bytes 995336 | tf_op jit(solution)/shard_map/ppermute | solution.py:523
  29.9 20.8 %collective-permute-start.2 = (f32[648,128]{1,0:T(8,128)S(1)}, f32[648,128]{1,0:T(8,128)S(1)}, u32[]{:S(2)}, u32[]{:S(2)}) collective-permute-start(f32[648,128]{1,0:T(8,128)S(1)} %get-tuple-element.22), channel_id=1, source_target_pairs={{0,31},{1,0},{2,1},{3,2},{4,3},{5,4},{6,5},{7,6},{8,7},{9,8},{10,9... | collective-permute-start | bytes 995336 | tf_op jit(solution)/shard_map/ppermute | solution.py:523
  41.2 12.4 %collective-permute-start = (f32[160,128]{1,0:T(8,128)S(1)}, f32[160,128]{1,0:T(8,128)S(1)}, u32[]{:S(2)}, u32[]{:S(2)}) collective-permute-start(f32[160,128]{1,0:T(8,128)S(1)} %get-tuple-element.19), channel_id=1, source_target_pairs={{0,2},{1,3},{2,4},{3,5},{4,6},{5,7},{6,8},{7,9},{8,10},{9,11},{10,... | collective-permute-start | bytes 245768 | tf_op jit(solution)/shard_map/ppermute | solution.py:523
  43.1 10.5 %collective-permute-start.3 = (f32[160,128]{1,0:T(8,128)S(1)}, f32[160,128]{1,0:T(8,128)S(1)}, u32[]{:S(2)}, u32[]{:S(2)}) collective-permute-start(f32[160,128]{1,0:T(8,128)S(1)} %get-tuple-element.23), channel_id=1, source_target_pairs={{0,30},{1,31},{2,0},{3,1},{4,2},{5,3},{6,4},{7,5},{8,6},{9,7},{10,... | collective-permute-start | bytes 245768 | tf_op jit(solution)/shard_map/ppermute | solution.py:523
  83.3 22.9 %copy-start.1 = (f32[8,8,1024]{2,1,0:T(8,128)S(1)}, f32[8,8,1024]{2,1,0:T(8,128)}, u32[]{:S(2)}) copy-start(f32[8,8,1024]{2,1,0:T(8,128)} %param.5) | copy-start | bytes 786436

commit v19 on v18

--- a/solution.py
+++ b/solution.py
@@ -494,9 +494,13 @@
         out_ref[:, row * times : (row + 1) * times, :] = piece
 
 
-def final_kernel(rows, times, tiles, source_ref, field_ref, solution_ref, residual_ref):
+def final_kernel(
+    rows, times, tiles, source_ref, field_ref, solution_ref, residual_ref,
+    solution_part, residual_part, sent,
+):
     half = LANES // 2
     low = lane_index((rows, LANES)) < half
+    copies = []
     for time in range(times):
         place = slice(time * rows, (time + 1) * rows)
         taken = pl.ds(time, rows, stride=times)
@@ -504,9 +508,19 @@
             columns = slice(pair * LANES, (pair + 1) * LANES)
             left = source_ref[2 * pair, taken, :]
             right = source_ref[2 * pair + 1, taken, :]
-            solution_ref[place, columns] = jnp.where(low, left, pltpu.roll(right, half, 1))
+            solution_part[place, columns] = jnp.where(low, left, pltpu.roll(right, half, 1))
             change = jnp.where(low, pltpu.roll(left, half, 1), right)
-            residual_ref[place, columns] = field_ref[place, columns] - change
+            residual_part[place, columns] = field_ref[place, columns] - change
+        for index, (part_ref, whole_ref) in enumerate(
+            ((solution_part, solution_ref), (residual_part, residual_ref))
+        ):
+            span = pl.ds(time * rows, rows)
+            copies.append(
+                pltpu.make_async_copy(part_ref.at[span], whole_ref.at[span], sent.at[index, time])
+            )
+            copies[-1].start()
+    for copy in copies:
+        copy.wait()
 
 
 def call(kernel, out_shape, scratch=()):
@@ -602,9 +616,17 @@
     )(cas_table, sums, solved, solved_two, middle, applied_two)
     returned = lax.all_to_all(packed, "tm", 0, 0)
 
-    solution, residual = call(
+    whole = jax.ShapeDtypeStruct((times * rows, width), jnp.float32)
+    solution, residual = pl.pallas_call(
         functools.partial(final_kernel, rows, times, tiles),
-        [(times * rows, width), (times * rows, width)],
+        out_shape=[whole, whole],
+        out_specs=[pl.BlockSpec(memory_space=pl.ANY)] * 2,
+        scratch_shapes=[
+            pltpu.VMEM(whole.shape, jnp.float32),
+            pltpu.VMEM(whole.shape, jnp.float32),
+            pltpu.SemaphoreType.DMA((2, times)),
+        ],
+        compiler_params=PARAMS,
     )(returned, field)
     shape = right_side.shape
     return solution.reshape(shape), residual.reshape(shape)

time: 108 us -> 108 us (level)
  no operation moved by 1% of the time
where the time goes in v19:
time: 108 us; the launch traced here: 107 us
  blocking collectives  49.1 us (45%)
  starting transfers between devices  32.3 us (30%)
  waiting for transfers between devices  14.2 us (13%)
  Pallas kernels  9.45 us (9%)
  local copies, waits for them, and re-layouts  1.24 us (1%)
    all_to_all x1, blocking collectives, shards(): returned = lax.all_to_all(packed, 'tm', 0, 0)  22.2 us
    ppermute x4, starting transfers between devices, shift(): lax.ppermute(value, 'space', [(i, (i + distance) % spaces) for i in range...  22.1 us
    all_to_all x1, waiting for transfers between devices, shards(): gathered = lax.all_to_all(windows, 'tm', 0, 0)  14.2 us
    all_to_all x1, blocking collectives, shards(): sums = lax.all_to_all(sums, 'space', 0, 0, axis_index_groups=groups)  13.7 us
    all_to_all x1, blocking collectives, shards(): sums = lax.all_to_all(sums, ('tm', 'space'), 0, 0, axis_index_groups=groups)  13.2 us
    all_to_all x1, starting transfers between devices, shards(): gathered = lax.all_to_all(windows, 'tm', 0, 0)  10.2 us
    pallas_call x1, Pallas kernels, shards(): call(functools.partial(near_kernel, rows), [tile_shape, work, work, work,...  2.91 us
    pallas_call x1, Pallas kernels, shards(): call(functools.partial(far_kernel, rows), [tile_shape, tile_shape, (tiles...  2.55 us
  transfers between devices with their start and end apart: 5, of which 1 were waited for; matrix products, arithmetic and copies ran while one was open for 0% of the time, Pallas kernels for 3%

profile of v19, /device:TPU:1, one launch (start us, length us, event | category | flops | bytes accessed | tf_op | source)
XLA Modules:
  0.0 107.2 jit_solution(7262031705584883449)
XLA Ops:
  0.6 0.0 copy-start
  0.6 0.9 copy-done
  1.6 0.0 copy-start.4
  1.6 0.0 copy-start.5
  1.6 0.0 copy-start.3
  1.6 0.0 copy-start.2
  1.6 1.0 shard_map.68
  2.6 10.2 %all-to-all-start = ((f32[16,48,128]{2,1,0:T(8,128)}), f32[16,48,128]{2,1,0:T(8,128)S(1)}, u32[]{:S(2)}, u32[]{:S(2)}) async-start(f32[16,48,128]{2,1,0:T(8,128)} %shard_map.68), calls=%async_computation | async-start | bytes 786432 | tf_op jit(solution)/shard_map/all_to_all | solution.py:556
  12.9 0.0 copy-done.4
  12.9 0.0 copy-done.5
  12.9 0.1 fusion
  13.0 0.1 concatenate.7
  13.1 0.1 constant_dynamic-slice_fusion.local_ref
  13.2 14.2 %all-to-all-done.field_ref = f32[16,48,128]{2,1,0:T(8,128)S(1)} async-done(((f32[16,48,128]{2,1,0:T(8,128)}), f32[16,48,128]{2,1,0:T(8,128)S(1)}, u32[]{:S(2)}, u32[]{:S(2)}) %all-to-all-start) | async-done | bytes 393248 | tf_op jit(solution)/shard_map/all_to_all | solution.py:556
  27.4 0.0 copy-done.3
  27.4 0.6 shard_map.69
  28.0 1.9 %collective-permute-start.1 = (f32[648,128]{1,0:T(8,128)S(1)}, f32[648,128]{1,0:T(8,128)S(1)}, u32[]{:S(2)}, u32[]{:S(2)}) collective-permute-start(f32[648,128]{1,0:T(8,128)S(1)} %get-tuple-element.20), channel_id=1, source_target_pairs={{0,1},{1,2},{2,3},{3,4},{4,5},{5,6},{6,7},{7,8},{8,9},{9,10},{10,1... | collective-permute-start | bytes 995336 | tf_op jit(solution)/shard_map/ppermute | solution.py:537
  29.9 11.3 %collective-permute-start.2 = (f32[648,128]{1,0:T(8,128)S(1)}, f32[648,128]{1,0:T(8,128)S(1)}, u32[]{:S(2)}, u32[]{:S(2)}) collective-permute-start(f32[648,128]{1,0:T(8,128)S(1)} %get-tuple-element.22), channel_id=1, source_target_pairs={{0,31},{1,0},{2,1},{3,2},{4,3},{5,4},{6,5},{7,6},{8,7},{9,8},{10,9... | collective-permute-start | bytes 995336 | tf_op jit(solution)/shard_map/ppermute | solution.py:537
  41.2 1.9 %collective-permute-start = (f32[160,128]{1,0:T(8,128)S(1)}, f32[160,128]{1,0:T(8,128)S(1)}, u32[]{:S(2)}, u32[]{:S(2)}) collective-permute-start(f32[160,128]{1,0:T(8,128)S(1)} %get-tuple-element.19), channel_id=1, source_target_pairs={{0,2},{1,3},{2,4},{3,5},{4,6},{5,7},{6,8},{7,9},{8,10},{9,11},{10,... | collective-permute-start | bytes 245768 | tf_op jit(solution)/shard_map/ppermute | solution.py:537
  43.1 7.0 %collective-permute-start.3 = (f32[160,128]{1,0:T(8,128)S(1)}, f32[160,128]{1,0:T(8,128)S(1)}, u32[]{:S(2)}, u32[]{:S(2)}) collective-permute-start(f32[160,128]{1,0:T(8,128)S(1)} %get-tuple-element.23), channel_id=1, source_target_pairs={{0,30},{1,31},{2,0},{3,1},{4,2},{5,3},{6,4},{7,5},{8,6},{9,7},{10,... | collective-permute-start | bytes 245768 | tf_op jit(solution)/shard_map/ppermute | solution.py:537
  50.1 0.0 copy-done.2
  50.1 0.6 shard_map.70.own_wide_ref
  50.7 0.0 collective-permute-done.1.top_ref
  50.7 0.0 collective-permute-done.2.bottom_ref
  50.7 2.9 %shard_map.71 = (f32[8,11,8,128]{3,2,1,0:T(8,128)S(1)}, f32[28,11,8,128]{3,2,1,0:T(8,128)S(1)}, f32[28,11,8,128]{3,2,1,0:T(8,128)S(1)}, f32[28,11,8,128]{3,2,1,0...) custom-call(f32[648,128]{1,0:T(8,128)S(1)} %collective-permute-done.1.top, ...), custom_call_target="tpu_custom_call" | custom-call | tf_op jit(solution)/shard_map/pallas_call | solution.py:586
  53.6 0.0 collective-permute-done.top_far_ref
  53.7 0.0 collective-permute-done.3.bottom_far_ref
  53.7 2.5 %shard_map.72 = (f32[8,11,8,128]{3,2,1,0:T(8,128)S(1)}, f32[8,11,8,128]{3,2,1,0:T(8,128)S(1)}, f32[64,1,128]{2,1,0:T(1,128)S(1)}) custom-call(f32[160,128]{1,0:T(8,128)S(1)} %collective-permute-done.top_far_ref, f32[648,128]{1,0:T(8,128)S(1)} %collective-permute-done.1.top_ref, f32[91,8,128]{2,1,0:T(8,128)S(1)} %get-tuple-element.21.field_ref, ...), custom_call_target="tpu_custom_call" | custom-call | tf_op jit(solution)/shard_map/pallas_call | solution.py:599
  56.2 13.2 %all_to_all.20 = f32[64,1,128]{2,1,0:T(1,128)S(1)} all-to-all(f32[64,1,128]{2,1,0:T(1,128)S(1)} %get-tuple-element.30), channel_id=1, replica_groups={{0,1,2,3,32,33,34,35,64,65,66,67,96,97,98,99,128,129,130,131,160,161,16..., dimensions={0} | all-to-all | bytes 65536 | tf_op jit(solution)/shard_map/all_to_all | solution.py:607
  69.4 0.1 reduce_sum.9
  69.5 13.7 %all_to_all.21.sums_ref = f32[8,1,128]{2,1,0:T(1,128)S(1)} all-to-all(f32[8,1,128]{2,1,0:T(1,128)S(1)} %broadcast_in_dim.2), channel_id=1, replica_groups={{0,4,8,12,16,20,24,28},{1,5,9,13,17,21,25,29},{2,6,10,14,18,22,26,30},{..., dimensions={0} | all-to-all | bytes 8192 | tf_op jit(solution)/shard_map/all_to_all | solution.py:611
  83.3 0.0 copy-start.1
  83.3 0.8 shard_map.73
  84.1 22.2 %all_to_all.22.source_ref = f32[16,64,128]{2,1,0:T(8,128)S(1)} all-to-all(f32[16,64,128]{2,1,0:T(8,128)S(1)} %shard_map.73), channel_id=1, replica_groups=mesh['tm'=16,'space'=32] {'tm'}, dimensions={0} | all-to-all | bytes 1048576 | tf_op jit(solution)/shard_map/all_to_all | solution.py:617
  106.2 0.0 copy-done.1
  106.2 1.0 shard_map.74
  (4 shorter events, 0.0 us)
Async XLA Ops:
  0.6 1.0 copy-start
  1.6 11.3 %copy-start.4 = (s32[2,8,1024]{2,1,0:T(8,128)S(1)}, s32[2,8,1024]{2,1,0:T(8,128)}, u32[]{:S(2)}) copy-start(s32[2,8,1024]{2,1,0:T(8,128)} %param.7) | copy-start | bytes 196612
  1.6 11.3 %copy-start.5 = (f32[8,1024]{1,0:T(8,128)S(1)}, f32[8,1024]{1,0:T(8,128)}, u32[]{:S(2)}) copy-start(f32[8,1024]{1,0:T(8,128)} %param.6) | copy-start | bytes 98308
  1.6 25.8 %copy-start.3 = (f32[128,128]{1,0:T(8,128)S(1)}, f32[128,128]{1,0:T(8,128)}, u32[]{:S(2)}) copy-start(f32[128,128]{1,0:T(8,128)} %constant.18.clone.cas_ref) | copy-start | bytes 196612
  1.6 48.5 %copy-start.2 = (f32[10,8,128]{2,1,0:T(8,128)S(1)}, f32[10,8,128]{2,1,0:T(8,128)}, u32[]{:S(2)}) copy-start(f32[10,8,128]{2,1,0:T(8,128)} %constant.19.clone.coef_ref) | copy-start | bytes 122884
  2.6 24.8 %all-to-all-start = ((f32[16,48,128]{2,1,0:T(8,128)}), f32[16,48,128]{2,1,0:T(8,128)S(1)}, u32[]{:S(2)}, u32[]{:S(2)}) async-start(f32[16,48,128]{2,1,0:T(8,128)} %shard_map.68), calls=%async_computation | async-start | bytes 786432 | tf_op jit(solution)/shard_map/all_to_all | solution.py:556
  28.0 22.7 %collective-permute-start.1 = (f32[648,128]{1,0:T(8,128)S(1)}, f32[648,128]{1,0:T(8,128)S(1)}, u32[]{:S(2)}, u32[]{:S(2)}) collective-permute-start(f32[648,128]{1,0:T(8,128)S(1)} %get-tuple-element.20), channel_id=1, source_target_pairs={{0,1},{1,2},{2,3},{3,4},{4,5},{5,6},{6,7},{7,8},{8,9},{9,10},{10,1... | collective-permute-start | bytes 995336 | tf_op jit(solution)/shard_map/ppermute | solution.py:537
  29.9 20.8 %collective-permute-start.2 = (f32[648,128]{1,0:T(8,128)S(1)}, f32[648,128]{1,0:T(8,128)S(1)}, u32[]{:S(2)}, u32[]{:S(2)}) collective-permute-start(f32[648,128]{1,0:T(8,128)S(1)} %get-tuple-element.22), channel_id=1, source_target_pairs={{0,31},{1,0},{2,1},{3,2},{4,3},{5,4},{6,5},{7,6},{8,7},{9,8},{10,9... | collective-permute-start | bytes 995336 | tf_op jit(solution)/shard_map/ppermute | solution.py:537
  41.2 12.4 %collective-permute-start = (f32[160,128]{1,0:T(8,128)S(1)}, f32[160,128]{1,0:T(8,128)S(1)}, u32[]{:S(2)}, u32[]{:S(2)}) collective-permute-start(f32[160,128]{1,0:T(8,128)S(1)} %get-tuple-element.19), channel_id=1, source_target_pairs={{0,2},{1,3},{2,4},{3,5},{4,6},{5,7},{6,8},{7,9},{8,10},{9,11},{10,... | collective-permute-start | bytes 245768 | tf_op jit(solution)/shard_map/ppermute | solution.py:537
  43.1 10.5 %collective-permute-start.3 = (f32[160,128]{1,0:T(8,128)S(1)}, f32[160,128]{1,0:T(8,128)S(1)}, u32[]{:S(2)}, u32[]{:S(2)}) collective-permute-start(f32[160,128]{1,0:T(8,128)S(1)} %get-tuple-element.23), channel_id=1, source_target_pairs={{0,30},{1,31},{2,0},{3,1},{4,2},{5,3},{6,4},{7,5},{8,6},{9,7},{10,... | collective-permute-start | bytes 245768 | tf_op jit(solution)/shard_map/ppermute | solution.py:537
  83.3 22.9 %copy-start.1 = (f32[8,8,1024]{2,1,0:T(8,128)S(1)}, f32[8,8,1024]{2,1,0:T(8,128)}, u32[]{:S(2)}) copy-start(f32[8,8,1024]{2,1,0:T(8,128)} %param.5) | copy-start | bytes 786436

commit v20 on v18

--- a/solution.py
+++ b/solution.py
@@ -22,7 +22,6 @@
 SIDE = 16
 BLOCK = 11
 WINDOW = SUB * BLOCK
-NEAR = 4
 PARAMS = pltpu.CompilerParams(vmem_limit_bytes=24 * 1024 * 1024)
 
 
@@ -564,10 +563,6 @@
     top, bottom = shift(up, 1, spaces), shift(down, -1, spaces)
     top_far, bottom_far = shift(far_up, 2, spaces), shift(far_down, -2, spaces)
 
-    groups = [
-        [i * spaces + first + j for i in range(tiles) for j in range(NEAR)]
-        for first in range(0, spaces, NEAR)
-    ]
     work = (total, BLOCK, SUB, LANES)
     solved, middle, step, remain, border, wide, early = call(
         functools.partial(near_kernel, rows),
@@ -584,17 +579,14 @@
     )(top, freq, bottom, coef_table, own_wide)
     solved_two, applied_two, sums = call(
         functools.partial(far_kernel, rows),
-        [tile_shape, tile_shape, (tiles * NEAR, 1, LANES)],
+        [tile_shape, tile_shape, (tiles, 1, LANES)],
         [work, work, tile_shape, (2 * FAR, BLOCK, SUB, LANES), (LANES, LANES)],
     )(
         top_far, top, freq, bottom, bottom_far, coef_table, middle, step, remain, border, wide,
         own_wide, early,
     )
-    sums = lax.all_to_all(sums, ("tm", "space"), 0, 0, axis_index_groups=groups)
-    planes = spaces // NEAR
-    groups = [[first + NEAR * i for i in range(planes)] for first in range(NEAR)]
-    sums = jnp.broadcast_to(jnp.sum(sums, axis=0)[None], (planes, 1, LANES))
-    sums = lax.all_to_all(sums, "space", 0, 0, axis_index_groups=groups)
+    sums = jnp.sum(lax.all_to_all(sums, "tm", 0, 0), axis=0)
+    sums = lax.all_to_all(jnp.broadcast_to(sums[None], (spaces, 1, LANES)), "space", 0, 0)
     packed = call(
         functools.partial(inverse_kernel, rows, times, length),
         [(tiles, rows * times, LANES)],

time: 108 us -> 107 us (level)
  no operation moved by 1% of the time
where the time goes in v20:
time: 107 us
  blocking collectives  49 us (46%)
  starting transfers between devices  32.3 us (30%)
  waiting for transfers between devices  14.2 us (13%)
  Pallas kernels  9.46 us (9%)
  local copies, waits for them, and re-layouts  1.24 us (1%)
    ppermute x4, starting transfers between devices, shift(): lax.ppermute(value, 'space', [(i, (i + distance) % spaces) for i in range...  22.1 us
    all_to_all x1, blocking collectives, shards(): returned = lax.all_to_all(packed, 'tm', 0, 0)  21.9 us
    all_to_all x1, blocking collectives, shards(): lax.all_to_all(jnp.broadcast_to(sums[None], (spaces, 1, LANES)), 'space',...  16.6 us
    all_to_all x1, waiting for transfers between devices, shards(): gathered = lax.all_to_all(windows, 'tm', 0, 0)  14.2 us
    all_to_all x1, blocking collectives, shards(): sums = jnp.sum(lax.all_to_all(sums, 'tm', 0, 0), axis=0)  10.5 us
    all_to_all x1, starting transfers between devices, shards(): gathered = lax.all_to_all(windows, 'tm', 0, 0)  10.2 us
    pallas_call x1, Pallas kernels, shards(): call(functools.partial(near_kernel, rows), [tile_shape, work, work, work,...  2.96 us
    pallas_call x1, Pallas kernels, shards(): call(functools.partial(far_kernel, rows), [tile_shape, tile_shape, (tiles...  2.53 us
  transfers between devices with their start and end apart: 5, of which 1 were waited for; matrix products, arithmetic and copies ran while one was open for 0% of the time, Pallas kernels for 3%

profile of v20, /device:TPU:1, one launch (start us, length us, event | category | flops | bytes accessed | tf_op | source)
XLA Modules:
  0.0 107.0 jit_solution(7083715198871457570)
XLA Ops:
  0.6 0.0 copy-start
  0.6 0.9 copy-done
  1.6 0.0 copy-start.4
  1.6 0.0 copy-start.5
  1.6 0.0 copy-start.3
  1.6 0.0 copy-start.2
  1.6 1.0 shard_map.68
  2.6 10.2 %all-to-all-start = ((f32[16,48,128]{2,1,0:T(8,128)}), f32[16,48,128]{2,1,0:T(8,128)S(1)}, u32[]{:S(2)}, u32[]{:S(2)}) async-start(f32[16,48,128]{2,1,0:T(8,128)} %shard_map.68), calls=%async_computation | async-start | bytes 786432 | tf_op jit(solution)/shard_map/all_to_all | solution.py:541
  12.9 0.0 copy-done.4
  12.9 0.0 copy-done.5
  12.9 0.1 fusion
  13.0 0.1 concatenate.7
  13.1 0.1 constant_dynamic-slice_fusion.local_ref
  13.2 14.2 %all-to-all-done.field_ref = f32[16,48,128]{2,1,0:T(8,128)S(1)} async-done(((f32[16,48,128]{2,1,0:T(8,128)}), f32[16,48,128]{2,1,0:T(8,128)S(1)}, u32[]{:S(2)}, u32[]{:S(2)}) %all-to-all-start) | async-done | bytes 393248 | tf_op jit(solution)/shard_map/all_to_all | solution.py:541
  27.4 0.0 copy-done.3
  27.4 0.6 shard_map.69
  28.0 1.9 %collective-permute-start.1 = (f32[648,128]{1,0:T(8,128)S(1)}, f32[648,128]{1,0:T(8,128)S(1)}, u32[]{:S(2)}, u32[]{:S(2)}) collective-permute-start(f32[648,128]{1,0:T(8,128)S(1)} %get-tuple-element.20), channel_id=1, source_target_pairs={{0,1},{1,2},{2,3},{3,4},{4,5},{5,6},{6,7},{7,8},{8,9},{9,10},{10,1... | collective-permute-start | bytes 995336 | tf_op jit(solution)/shard_map/ppermute | solution.py:522
  29.9 11.3 %collective-permute-start.2 = (f32[648,128]{1,0:T(8,128)S(1)}, f32[648,128]{1,0:T(8,128)S(1)}, u32[]{:S(2)}, u32[]{:S(2)}) collective-permute-start(f32[648,128]{1,0:T(8,128)S(1)} %get-tuple-element.22), channel_id=1, source_target_pairs={{0,31},{1,0},{2,1},{3,2},{4,3},{5,4},{6,5},{7,6},{8,7},{9,8},{10,9... | collective-permute-start | bytes 995336 | tf_op jit(solution)/shard_map/ppermute | solution.py:522
  41.2 1.9 %collective-permute-start = (f32[160,128]{1,0:T(8,128)S(1)}, f32[160,128]{1,0:T(8,128)S(1)}, u32[]{:S(2)}, u32[]{:S(2)}) collective-permute-start(f32[160,128]{1,0:T(8,128)S(1)} %get-tuple-element.19), channel_id=1, source_target_pairs={{0,2},{1,3},{2,4},{3,5},{4,6},{5,7},{6,8},{7,9},{8,10},{9,11},{10,... | collective-permute-start | bytes 245768 | tf_op jit(solution)/shard_map/ppermute | solution.py:522
  43.1 7.0 %collective-permute-start.3 = (f32[160,128]{1,0:T(8,128)S(1)}, f32[160,128]{1,0:T(8,128)S(1)}, u32[]{:S(2)}, u32[]{:S(2)}) collective-permute-start(f32[160,128]{1,0:T(8,128)S(1)} %get-tuple-element.23), channel_id=1, source_target_pairs={{0,30},{1,31},{2,0},{3,1},{4,2},{5,3},{6,4},{7,5},{8,6},{9,7},{10,... | collective-permute-start | bytes 245768 | tf_op jit(solution)/shard_map/ppermute | solution.py:522
  50.1 0.0 copy-done.2
  50.1 0.6 shard_map.70.own_wide_ref
  50.7 0.0 collective-permute-done.1.top_ref
  50.7 0.0 collective-permute-done.2.bottom_ref
  50.7 3.0 %shard_map.71 = (f32[8,11,8,128]{3,2,1,0:T(8,128)S(1)}, f32[28,11,8,128]{3,2,1,0:T(8,128)S(1)}, f32[28,11,8,128]{3,2,1,0:T(8,128)S(1)}, f32[28,11,8,128]{3,2,1,0...) custom-call(f32[648,128]{1,0:T(8,128)S(1)} %collective-permute-done.1.top, ...), custom_call_target="tpu_custom_call" | custom-call | tf_op jit(solution)/shard_map/pallas_call | solution.py:567
  53.7 0.0 collective-permute-done.top_far_ref
  53.7 0.0 collective-permute-done.3.bottom_far_ref
  53.7 2.5 %shard_map.72 = (f32[8,11,8,128]{3,2,1,0:T(8,128)S(1)}, f32[8,11,8,128]{3,2,1,0:T(8,128)S(1)}, f32[16,1,128]{2,1,0:T(1,128)S(1)}) custom-call(f32[160,128]{1,0:T(8,128)S(1)} %collective-permute-done.top_far_ref, f32[648,128]{1,0:T(8,128)S(1)} %collective-permute-done.1.top_ref, f32[91,8,128]{2,1,0:T(8,128)S(1)} %get-tuple-element.21.field_ref, ...), custom_call_target="tpu_custom_call" | custom-call | tf_op jit(solution)/shard_map/pallas_call | solution.py:580
  56.2 10.5 %all_to_all.20 = f32[16,1,128]{2,1,0:T(1,128)S(1)} all-to-all(f32[16,1,128]{2,1,0:T(1,128)S(1)} %get-tuple-element.30), channel_id=1, replica_groups=mesh['tm'=16,'space'=32] {'tm'}, dimensions={0} | all-to-all | bytes 16384 | tf_op jit(solution)/shard_map/all_to_all | solution.py:588
  66.8 16.6 %all_to_all.21.sums_ref = f32[32,1,128]{2,1,0:T(1,128)S(1)} all-to-all(f32[32,1,128]{2,1,0:T(1,128)S(1)} %broadcast_in_dim.2), channel_id=1, replica_groups=mesh['tm'=16,'space'=32] {'space'}, dimensions={0} | all-to-all | bytes 32768 | tf_op jit(solution)/shard_map/all_to_all | solution.py:589
  83.4 0.0 copy-start.1
  83.4 0.8 shard_map.73
  84.2 21.9 %all_to_all.22.source_ref = f32[16,64,128]{2,1,0:T(8,128)S(1)} all-to-all(f32[16,64,128]{2,1,0:T(8,128)S(1)} %shard_map.73), channel_id=1, replica_groups=mesh['tm'=16,'space'=32] {'tm'}, dimensions={0} | all-to-all | bytes 1048576 | tf_op jit(solution)/shard_map/all_to_all | solution.py:595
  106.1 0.0 copy-done.1
  106.1 1.0 shard_map.74
  (5 shorter events, 0.1 us)
Async XLA Ops:
  0.6 1.0 copy-start
  1.6 11.3 %copy-start.4 = (s32[2,8,1024]{2,1,0:T(8,128)S(1)}, s32[2,8,1024]{2,1,0:T(8,128)}, u32[]{:S(2)}) copy-start(s32[2,8,1024]{2,1,0:T(8,128)} %param.7) | copy-start | bytes 196612
  1.6 11.3 %copy-start.5 = (f32[8,1024]{1,0:T(8,128)S(1)}, f32[8,1024]{1,0:T(8,128)}, u32[]{:S(2)}) copy-start(f32[8,1024]{1,0:T(8,128)} %param.6) | copy-start | bytes 98308
  1.6 25.8 %copy-start.3 = (f32[128,128]{1,0:T(8,128)S(1)}, f32[128,128]{1,0:T(8,128)}, u32[]{:S(2)}) copy-start(f32[128,128]{1,0:T(8,128)} %constant.18.clone.cas_ref) | copy-start | bytes 196612
  1.6 48.5 %copy-start.2 = (f32[10,8,128]{2,1,0:T(8,128)S(1)}, f32[10,8,128]{2,1,0:T(8,128)}, u32[]{:S(2)}) copy-start(f32[10,8,128]{2,1,0:T(8,128)} %constant.19.clone.coef_ref) | copy-start | bytes 122884
  2.6 24.8 %all-to-all-start = ((f32[16,48,128]{2,1,0:T(8,128)}), f32[16,48,128]{2,1,0:T(8,128)S(1)}, u32[]{:S(2)}, u32[]{:S(2)}) async-start(f32[16,48,128]{2,1,0:T(8,128)} %shard_map.68), calls=%async_computation | async-start | bytes 786432 | tf_op jit(solution)/shard_map/all_to_all | solution.py:541
  28.0 22.7 %collective-permute-start.1 = (f32[648,128]{1,0:T(8,128)S(1)}, f32[648,128]{1,0:T(8,128)S(1)}, u32[]{:S(2)}, u32[]{:S(2)}) collective-permute-start(f32[648,128]{1,0:T(8,128)S(1)} %get-tuple-element.20), channel_id=1, source_target_pairs={{0,1},{1,2},{2,3},{3,4},{4,5},{5,6},{6,7},{7,8},{8,9},{9,10},{10,1... | collective-permute-start | bytes 995336 | tf_op jit(solution)/shard_map/ppermute | solution.py:522
  29.9 20.8 %collective-permute-start.2 = (f32[648,128]{1,0:T(8,128)S(1)}, f32[648,128]{1,0:T(8,128)S(1)}, u32[]{:S(2)}, u32[]{:S(2)}) collective-permute-start(f32[648,128]{1,0:T(8,128)S(1)} %get-tuple-element.22), channel_id=1, source_target_pairs={{0,31},{1,0},{2,1},{3,2},{4,3},{5,4},{6,5},{7,6},{8,7},{9,8},{10,9... | collective-permute-start | bytes 995336 | tf_op jit(solution)/shard_map/ppermute | solution.py:522
  41.2 12.5 %collective-permute-start = (f32[160,128]{1,0:T(8,128)S(1)}, f32[160,128]{1,0:T(8,128)S(1)}, u32[]{:S(2)}, u32[]{:S(2)}) collective-permute-start(f32[160,128]{1,0:T(8,128)S(1)} %get-tuple-element.19), channel_id=1, source_target_pairs={{0,2},{1,3},{2,4},{3,5},{4,6},{5,7},{6,8},{7,9},{8,10},{9,11},{10,... | collective-permute-start | bytes 245768 | tf_op jit(solution)/shard_map/ppermute | solution.py:522
  43.1 10.6 %collective-permute-start.3 = (f32[160,128]{1,0:T(8,128)S(1)}, f32[160,128]{1,0:T(8,128)S(1)}, u32[]{:S(2)}, u32[]{:S(2)}) collective-permute-start(f32[160,128]{1,0:T(8,128)S(1)} %get-tuple-element.23), channel_id=1, source_target_pairs={{0,30},{1,31},{2,0},{3,1},{4,2},{5,3},{6,4},{7,5},{8,6},{9,7},{10,... | collective-permute-start | bytes 245768 | tf_op jit(solution)/shard_map/ppermute | solution.py:522
  83.4 22.7 %copy-start.1 = (f32[8,8,1024]{2,1,0:T(8,128)S(1)}, f32[8,8,1024]{2,1,0:T(8,128)}, u32[]{:S(2)}) copy-start(f32[8,8,1024]{2,1,0:T(8,128)} %param.5) | copy-start | bytes 786436
